TPU v7x, 32 devices: a whole 2x2x4 slice. The times are simulated.
32 devices in a mesh: groups: 2 (over x), row: 8 (over z, y), col: 2 (over core).
Axes of the slice: x: 2, y: 2, z: 4, core: 2. Of those that a mesh axis runs over, the one named last changes fastest.
Arguments:
- vectors: bfloat16 [1024, 16, 64], P(('groups', 'row', 'col')), parts along dimension 0, may hold values from -6 to 6
- leaf_basis: bfloat16 [1024, 64, 64], P(('groups', 'row', 'col')), parts along dimension 0, may hold values from -0.75 to 0.75
- leaf_transfer: bfloat16 [1024, 64, 64], P(('groups', 'row', 'col')), parts along dimension 0, may hold values from -0.5 to 0.5
- pair_transfer: bfloat16 [512, 64, 64], P(('groups', 'row', 'col')), parts along dimension 0, may hold values from -0.5 to 0.5
- near_blocks: bfloat16 [3, 1024, 3, 64, 64], P(None, ('groups', 'row', 'col')), parts along dimension 1, may hold values from -0.4375 to 0.4375
- near_offset: int32 [1024, 3], P(('groups', 'row', 'col')), parts along dimension 0, may hold values from -2 to 2
- leaf_send: int32 [32, 5, 8], P(('groups', 'row', 'col')), parts along dimension 0, may hold values from 0 to 31
- leaf_list: int32 [1024, 4], P(('groups', 'row', 'col')), parts along dimension 0, may hold values from 0 to 39
- leaf_coupling: bfloat16 [3, 1024, 4, 64, 64], P(None, ('groups', 'row', 'col')), parts along dimension 1, may hold values from -0.375 to 0.375
- pair_send: int32 [32, 5, 2], P(('groups', 'row', 'col')), parts along dimension 0, may hold values from 0 to 15
- pair_list: int32 [512, 4], P(('groups', 'row', 'col')), parts along dimension 0, may hold values from 0 to 9
- pair_coupling: bfloat16 [3, 512, 4, 64, 64], P(None, ('groups', 'row', 'col')), parts along dimension 1, may hold values from -0.375 to 0.375
- top_list: int32 [256, 8], P(('groups', 'row', 'col')), parts along dimension 0, may hold values from 0 to 127
- top_coupling: bfloat16 [3, 256, 8, 64, 64], P(None, ('groups', 'row', 'col')), parts along dimension 1, may hold values from -0.25 to 0.25
Outputs:
- potential: bfloat16 [3, 1024, 16, 64], P(None, ('groups', 'row', 'col')), parts along dimension 1
There are 2 independent parts, one for each index of `groups`. A program takes and returns all parts, laid end to end along the dimension named above; each array names one. Nothing has to cross between parts.
All inputs are finite; a program needn't handle non-finite values.
Results may differ from a plain program's by a relative error of at most 0.0058.
Values may be sent and summed in bfloat16 or wider, within the bound.
No kernel may reach another device: no remote copies, remote signals or barrier semaphores. Data moves between devices by JAX's collectives and lax.ppermute only.
A program may use at most 64 MiB of HBM per device.

v0:
```python
import jax
import jax.numpy as jnp
from jax import lax
from jax.sharding import PartitionSpec as P

RANK = 64
VECS = 16
LEAVES_DEV = 32
MT = 8
REACH = 2
CAP0 = 8
CAP1 = 2
HW = 2


def passed_along(shard, axis, by):
    length = lax.axis_size(axis)
    return lax.ppermute(shard, axis, [(i, (i + by) % length) for i in range(length)])


def extended(block, sides, width):
    for axis, dim in sides:
        count = lax.axis_size(axis)
        forward = [(i, i + 1) for i in range(count - 1)]
        backward = [(target, source) for source, target in forward]
        low = lax.ppermute(
            lax.slice_in_dim(block, block.shape[dim] - width, None, axis=dim), axis, forward
        )
        high = lax.ppermute(lax.slice_in_dim(block, 0, width, axis=dim), axis, backward)
        block = jnp.concatenate([low, block, high], axis=dim)
    return block


def hop_once(leaf_part, pair_part, step):
    return passed_along((leaf_part, pair_part), ("row", "col"), step)


def on_device(
    vectors,
    leaf_basis,
    leaf_transfer,
    pair_transfer,
    near_blocks,
    near_offset,
    leaf_send,
    leaf_list,
    leaf_coupling,
    pair_send,
    pair_list,
    pair_coupling,
    top_list,
    top_coupling,
):
    f32 = jnp.float32
    bf = jnp.bfloat16
    pairs = LEAVES_DEV // 2
    tops = LEAVES_DEV // 4
    window = 2 * REACH + 1
    up0 = jnp.einsum("tvp,tpr->tvr", vectors, leaf_basis, preferred_element_type=f32).astype(bf)
    up1 = (
        jnp.einsum("tvr,trs->tvs", up0, leaf_transfer, preferred_element_type=f32)
        .reshape(pairs, 2, VECS, RANK)
        .sum(1)
        .astype(bf)
    )
    up2 = (
        jnp.einsum("tvr,trs->tvs", up1, pair_transfer, preferred_element_type=f32)
        .reshape(tops, 2, VECS, RANK)
        .sum(1)
        .astype(bf)
    )
    leaf_blocks = jnp.take(up0, leaf_send.reshape(window * CAP0), axis=0).reshape(
        window, CAP0, VECS, RANK
    )
    pair_blocks = jnp.take(up1, pair_send.reshape(window * CAP1), axis=0).reshape(
        window, CAP1, VECS, RANK
    )
    leaf_parts = [None] * window
    pair_parts = [None] * window
    leaf_parts[REACH] = leaf_blocks[REACH]
    pair_parts[REACH] = pair_blocks[REACH]
    for side in (1, -1):
        places = [REACH + side * (hop + 1) for hop in range(REACH)]
        carry_leaf = jnp.stack([leaf_blocks[place] for place in places], axis=0)
        carry_pair = jnp.stack([pair_blocks[place] for place in places], axis=0)
        for hop in range(REACH):
            carry_leaf, carry_pair = hop_once(carry_leaf, carry_pair, -side)
            leaf_parts[places[hop]] = carry_leaf[0]
            pair_parts[places[hop]] = carry_pair[0]
            carry_leaf = carry_leaf[1:]
            carry_pair = carry_pair[1:]
    leaf_window = jnp.stack(leaf_parts, axis=0).reshape(window * CAP0, VECS, RANK)
    pair_window = jnp.stack(pair_parts, axis=0).reshape(window * CAP1, VECS, RANK)
    piece = lax.all_gather(up2, ("row", "col"), axis=0, tiled=True)
    count = piece.shape[0]
    inside = (top_list >= 0) & (top_list < count)
    taken = jnp.take(piece, jnp.clip(top_list, 0, count - 1), axis=0)
    top_rows = jnp.where(inside[:, :, None, None], taken, jnp.zeros((tops, MT, VECS, RANK), bf))
    leaf_rows = jnp.take(leaf_window, leaf_list, axis=0)
    pair_rows = jnp.take(pair_window, pair_list, axis=0)
    far0 = jnp.einsum("ktmrs,tmvs->ktvr", leaf_coupling, leaf_rows, preferred_element_type=f32)
    far1 = jnp.einsum("ktmrs,tmvs->ktvr", pair_coupling, pair_rows, preferred_element_type=f32)
    far2 = jnp.einsum("ktmrs,tmvs->ktvr", top_coupling, top_rows, preferred_element_type=f32)
    down2 = far2.astype(bf)
    down1 = (
        far1
        + jnp.einsum(
            "trs,ktvs->ktvr",
            pair_transfer,
            jnp.repeat(down2, 2, axis=1),
            preferred_element_type=f32,
        )
    ).astype(bf)
    down0 = (
        far0
        + jnp.einsum(
            "trs,ktvs->ktvr",
            leaf_transfer,
            jnp.repeat(down1, 2, axis=1),
            preferred_element_type=f32,
        )
    ).astype(bf)
    far_points = jnp.einsum("tpr,ktvr->ktvp", leaf_basis, down0, preferred_element_type=f32)
    padded = extended(vectors, ((("row", "col"), 0),), HW)
    near_index = jnp.arange(LEAVES_DEV, dtype=jnp.int32)[:, None] + HW + near_offset
    neighbours = jnp.take(padded, near_index, axis=0)
    near = jnp.einsum("ktnpq,tnvq->ktvp", near_blocks, neighbours, preferred_element_type=f32)
    return (far_points + near).astype(bf)


def solution(mesh):
    placed = (
        P(("groups", "row", "col"), None, None),
        P(("groups", "row", "col"), None, None),
        P(("groups", "row", "col"), None, None),
        P(("groups", "row", "col"), None, None),
        P(None, ("groups", "row", "col"), None, None, None),
        P(("groups", "row", "col"), None),
        P(("groups", "row", "col"), None, None),
        P(("groups", "row", "col"), None),
        P(None, ("groups", "row", "col"), None, None, None),
        P(("groups", "row", "col"), None, None),
        P(("groups", "row", "col"), None),
        P(None, ("groups", "row", "col"), None, None, None),
        P(("groups", "row", "col"), None),
        P(None, ("groups", "row", "col"), None, None, None),
    )
    return jax.shard_map(
        on_device,
        mesh=mesh,
        in_specs=placed,
        out_specs=P(None, ("groups", "row", "col"), None, None),
        check_vma=False,
    )
```

profile of v0, /device:TPU:0, one launch (start us, length us, event | category | flops | bytes accessed | tf_op | source)
XLA Modules:
  0.0 98.0 jit_solution(11515107297071385768)
XLA Ops:
  0.0 0.9 copy.45
  1.1 0.7 reduce
  1.9 1.4 %convolution_convert_fusion = bf16[32,16,64]{2,1,0:T(8,128)(2,1)S(1)} fusion(bf16[32,16,64]{2,1,0:T(8,128)(2,1)} %param.14, bf16[32,64,64]{2,1,0:T(8,128)(2,1)} %param.15), kind=kOutput, calls=%fused_computation.26 | convolution fusion | flops 4227072 | bytes 393216 | tf_op jit(solution)/shard_map/tvp,tpr->tvr/dot_general | solution.py:59
  3.3 1.3 %bitcast_reduce_fusion = bf16[16,16,64]{2,1,0:T(8,128)(2,1)S(1)} fusion(bf16[32,16,64]{2,1,0:T(8,128)(2,1)S(1)} %convolution_convert_fusion, bf16[32,64,64]{2,1,0:T(8,128)(2,1)} %param.16), kind=kOutput, calls=%fused_computation.41 | convolution fusion | flops 4210688 | bytes 360448 | tf_op jit(solution)/shard_map/tvr,trs->tvs/dot_general | solution.py:61
  4.6 0.6 gather_fusion.2
  5.2 0.6 pad_maximum_fusion.3
  6.3 0.6 pad_maximum_fusion.4
  6.9 5.0 %collective-permute-start.6 = (bf16[2,2,16,64]{3,2,1,0:T(8,128)(2,1)}, bf16[2,2,16,64]{3,2,1,0:T(8,128)(2,1)}, u32[]{:S(2)}, u32[]{:S(2)}) collective-permute-start(bf16[2,2,16,64]{3,2,1,0:T(8,128)(2,1)} %pad_maximum_fusion.4), channel_id=1, source_target_pairs={{0,15},{1,0},{2,1},{3,2},{4,3},{5,4},{6,5},{7,6},{8,7},{9,8},{10,9... | collective-permute-start | bytes 24584 | tf_op jit(solution)/shard_map/ppermute | solution.py:18
  12.0 0.6 gather_fusion
  12.7 0.6 copy-done.2
  13.4 0.6 pad_maximum_fusion.1
  14.0 0.7 fusion.63
  14.7 1.3 %collective-permute-start.8 = (bf16[2,16,64]{2,1,0:T(8,128)(2,1)S(1)}, bf16[2,16,64]{2,1,0:T(8,128)(2,1)S(1)}, u32[]{:S(2)}, u32[]{:S(2)}) collective-permute-start(bf16[2,16,64]{2,1,0:T(8,128)(2,1)S(1)} %get-tuple-element.11), channel_id=1, source_target_pairs={{0,1},{1,2},{2,3},{3,4},{4,5},{5,6},{6,7},{7,8},{8,9},{9,10},{10,1... | collective-permute-start | bytes 12296 | tf_op jit(solution)/shard_map/ppermute | solution.py:26
  16.0 1.3 %collective-permute-start.9 = (bf16[2,16,64]{2,1,0:T(8,128)(2,1)S(1)}, bf16[2,16,64]{2,1,0:T(8,128)(2,1)}, u32[]{:S(2)}, u32[]{:S(2)}) collective-permute-start(bf16[2,16,64]{2,1,0:T(8,128)(2,1)S(1)} %get-tuple-element.12), channel_id=1, source_target_pairs={{1,0},{2,1},{3,2},{4,3},{5,4},{6,5},{7,6},{8,7},{9,8},{10,9},{11,1... | collective-permute-start | bytes 12296 | tf_op jit(solution)/shard_map/ppermute | solution.py:29
  17.3 0.7 compare_select_fusion.2
  18.0 0.7 compare_and_fusion.4
  18.7 0.7 compare_select_fusion
  19.4 0.7 compare_and_fusion.1
  20.1 0.7 compare_select_fusion.3
  20.8 0.7 compare_and_fusion.6
  21.6 1.1 %bitcast_reduce_fusion.1 = bf16[8,16,64]{2,1,0:T(8,128)(2,1)S(1)} fusion(bf16[16,16,64]{2,1,0:T(8,128)(2,1)S(1)} %bitcast_reduce_fusion, bf16[16,64,64]{2,1,0:T(8,128)(2,1)} %param.17), kind=kOutput, calls=%fused_computation.52 | convolution fusion | flops 2105344 | bytes 180224 | tf_op jit(solution)/shard_map/tvr,trs->tvs/dot_general | solution.py:67
  22.8 26.2 %all_gather.3 = bf16[128,16,64]{2,1,0:T(8,128)(2,1)} all-gather(bf16[8,16,64]{2,1,0:T(8,128)(2,1)S(1)} %bitcast_reduce_fusion.1), channel_id=1, replica_groups=mesh['groups'=2,'row'=8,'col'=2] {'row','col'}, dimensions={0}, use_global_device_ids=true | all-gather | bytes 278528 | tf_op jit(solution)/shard_map/all_gather | solution.py:94
  49.3 0.7 compare_and_fusion.2
  50.2 2.4 %gather_fusion.4 = bf16[64,16,64]{2,1,0:T(8,128)(2,1)} fusion(bf16[128,16,64]{2,1,0:T(8,128)(2,1)} %all_gather.3, s32[1024]{0:T(1024)S(1)} %pad_clamp_fusion.1), kind=kCustom, calls=%fused_computation.4 | custom fusion | bytes 262400 | tf_op jit(solution)/shard_map/jit(_take)/gather | solution.py:97
  52.6 0.6 pad_maximum_fusion.2
  53.2 3.9 %fusion.29 = bf16[3,8,16,64]{3,2,0,1:T(8,128)(2,1)} fusion(bf16[3,8,8,64,64]{4,3,2,1,0:T(8,128)(2,1)} %param.27, bf16[8,8,16,64]{3,2,1,0:T(8,128)(2,1)} %bitcast.135, pred[8,8]{1,0:T(8,128)(4,1)S(1)} %get-tuple-element.22, pred[8,8]{1,0:T(8,128)(4,1)S(1)} %get-tuple-element.21), kind=kOutput, calls=%fused_computation.29 | convolution fusion | flops 25321472 | bytes 1753216 | tf_op jit(solution)/shard_map/ktmrs,tmvs->ktvr/dot_general | solution.py:103
  57.1 0.7 copy.44
  57.8 0.7 copy.41
  58.6 0.7 slice.143
  59.9 0.8 pad_maximum_fusion
  60.7 1.4 %gather_fusion.5 = bf16[96,16,64]{2,1,0:T(8,128)(2,1)} fusion(bf16[36,16,64]{2,1,0:T(8,128)(2,1)S(1)} %pad_maximum_fusion, s32[1024]{0:T(1024)S(1)} %pad_clamp_fusion), kind=kCustom, calls=%fused_computation.5 | custom fusion | bytes 393600 | tf_op jit(solution)/shard_map/jit(_take)/gather | solution.py:126
  62.1 3.0 %collective-permute-done.5 = bf16[1,2,16,64]{3,2,1,0:T(8,128)(2,1)S(1)} collective-permute-done((bf16[1,2,16,64]{3,2,1,0:T(8,128)(2,1)S(1)}, bf16[1,2,16,64]{3,2,1,0:T(8,128)(2,1)S(1)}, u32[]{:S(2)}, u32[]{:S(2)}) %collective-permute-start.5) | collective-permute-done | bytes 4128 | tf_op jit(solution)/shard_map/ppermute | solution.py:18
  65.1 0.7 constant_dynamic-update-slice_fusion.5
  65.8 0.7 fusion.65
  66.6 0.8 collective-permute-start.7
  67.4 5.7 %fusion.8 = f32[3,32,16,64]{3,2,0,1:T(8,128)} fusion(bf16[3,32,3,64,64]{4,3,2,1,0:T(8,128)(2,1)} %param.18, bf16[32,3,16,64]{3,2,1,0:T(8,128)(2,1)} %bitcast.131, pred[32,3]{1,0:T(8,128)(4,1)S(1)} %copy.50), kind=kOutput, calls=%fused_computation.14 | convolution fusion | flops 37847040 | bytes 2949216 | tf_op jit(solution)/shard_map/ktnpq,tnvq->ktvp/dot_general | solution.py:127
  73.2 0.6 gather_fusion.3
  73.8 0.8 slice.134
  74.6 1.9 %fusion.18 = f32[3,16,16,64]{3,2,0,1:T(8,128)S(1)} fusion(bf16[3,16,4,64,64]{4,3,2,1,0:T(8,128)(2,1)S(1)} %copy-done, bf16[16,4,16,64]{3,2,1,0:T(8,128)(2,1)S(1)} %bitcast.133, pred[16,4]{1,0:T(8,128)(4,1)} %copy.44), kind=kOutput, calls=%fused_computation.22 | convolution fusion | flops 25231360 | bytes 1900608 | tf_op jit(solution)/shard_map/ktmrs,tmvs->ktvr/dot_general | solution.py:102
  76.5 4.1 %collective-permute-done.1 = bf16[1,8,16,64]{3,2,1,0:T(8,128)(2,1)S(1)} collective-permute-done((bf16[1,8,16,64]{3,2,1,0:T(8,128)(2,1)S(1)}, bf16[1,8,16,64]{3,2,1,0:T(8,128)(2,1)S(1)}, u32[]{:S(2)}, u32[]{:S(2)}) %collective-permute-start.1) | collective-permute-done | bytes 16416 | tf_op jit(solution)/shard_map/ppermute | solution.py:18
  80.6 0.8 slice_dynamic-update-slice_fusion.1
  81.4 0.8 fusion.55
  82.2 0.8 fusion.64
  83.4 1.9 %fusion.22 = bf16[3,16,16,64]{3,2,0,1:T(8,128)(2,1)} fusion(f32[3,16,16,64]{3,2,0,1:T(8,128)S(1)} %fusion.18, bf16[3,16,16,64]{3,2,0,1:T(8,128)(2,1)S(1)} %bitcast.134, bf16[16,64,64]{2,1,0:T(8,128)(2,1)} %param.17), kind=kOutput, calls=%fused_computation.25 | convolution fusion | flops 6389760 | bytes 524288 | tf_op jit(solution)/shard_map/trs,ktvs->ktvr/dot_general | solution.py:107
  85.3 1.5 %gather_fusion.1 = bf16[128,16,64]{2,1,0:T(8,128)(2,1)} fusion(bf16[40,16,64]{2,1,0:T(8,128)(2,1)S(1)} %bitcast.129, s32[1024]{0:T(1024)S(1)} %pad_clamp_fusion.4), kind=kCustom, calls=%fused_computation.1 | custom fusion | bytes 524800 | tf_op jit(solution)/shard_map/jit(_take)/gather | solution.py:99
  86.8 6.3 %fusion.13 = f32[3,32,16,64]{3,2,0,1:T(8,128)} fusion(bf16[3,32,4,64,64]{4,3,2,1,0:T(8,128)(2,1)} %param.22, bf16[32,4,16,64]{3,2,1,0:T(8,128)(2,1)} %bitcast.128, pred[32,4]{1,0:T(8,128)(4,1)S(1)} %copy-done.5), kind=kOutput, calls=%fused_computation.19 | convolution fusion | flops 50462720 | bytes 3801216 | tf_op jit(solution)/shard_map/ktmrs,tmvs->ktvr/dot_general | solution.py:101
  93.1 3.1 %fusion.16 = bf16[3,32,16,64]{3,2,0,1:T(8,128)(2,1)} fusion(f32[3,32,16,64]{3,2,0,1:T(8,128)} %fusion.8, f32[3,32,16,64]{3,2,0,1:T(8,128)} %fusion.13, bf16[3,32,16,64]{3,2,0,1:T(8,128)(2,1)S(1)} %bitcast.132, bf16[32,64,64]{2,1,0:T(8,128)(2,1)} %param.15, bf16[32,64,64]{2,1,0:T(8,128)(2,1)} %param.16), kind=kOutput, calls=%fused_computation.20 | convolution fusion | flops 25559040 | bytes 1703936 | tf_op jit(solution)/shard_map/tpr,ktvr->ktvp/dot_general | solution.py:123
  96.2 1.8 %copy.53 = bf16[3,32,16,64]{3,2,1,0:T(8,128)(2,1)} copy(bf16[3,32,16,64]{3,2,0,1:T(8,128)(2,1)} %fusion.16) | data formatting | bytes 393216 | tf_op jit(solution)/shard_map/convert_element_type | solution.py:128
  (60 shorter events, 3.0 us)
Async XLA Ops:
  0.0 74.6 %copy-start = (bf16[3,16,4,64,64]{4,3,2,1,0:T(8,128)(2,1)S(1)}, bf16[3,16,4,64,64]{4,3,2,1,0:T(8,128)(2,1)}, u32[]{:S(2)}) copy-start(bf16[3,16,4,64,64]{4,3,2,1,0:T(8,128)(2,1)} %param.25) | copy-start | bytes 4718596
  5.8 52.7 %collective-permute-start.4 = (bf16[2,2,16,64]{3,2,1,0:T(8,128)(2,1)}, bf16[2,2,16,64]{3,2,1,0:T(8,128)(2,1)}, u32[]{:S(2)}, u32[]{:S(2)}) collective-permute-start(bf16[2,2,16,64]{3,2,1,0:T(8,128)(2,1)} %pad_maximum_fusion.3), channel_id=1, source_target_pairs={{0,1},{1,2},{2,3},{3,4},{4,5},{5,6},{6,7},{7,8},{8,9},{9,10},{10,1... | collective-permute-start | bytes 24584 | tf_op jit(solution)/shard_map/ppermute | solution.py:18
  6.9 58.9 %collective-permute-start.6 = (bf16[2,2,16,64]{3,2,1,0:T(8,128)(2,1)}, bf16[2,2,16,64]{3,2,1,0:T(8,128)(2,1)}, u32[]{:S(2)}, u32[]{:S(2)}) collective-permute-start(bf16[2,2,16,64]{3,2,1,0:T(8,128)(2,1)} %pad_maximum_fusion.4), channel_id=1, source_target_pairs={{0,15},{1,0},{2,1},{3,2},{4,3},{5,4},{6,5},{7,6},{8,7},{9,8},{10,9... | collective-permute-start | bytes 24584 | tf_op jit(solution)/shard_map/ppermute | solution.py:18
  12.7 0.7 copy-start.2
  13.4 46.6 %copy-start.3 = (bf16[32,16,64]{2,1,0:T(8,128)(2,1)S(1)}, bf16[32,16,64]{2,1,0:T(8,128)(2,1)}, u32[]{:S(2)}) copy-start(bf16[32,16,64]{2,1,0:T(8,128)(2,1)} %param.14) | copy-start | bytes 196612
  14.0 59.8 %collective-permute-start = (bf16[2,8,16,64]{3,2,1,0:T(8,128)(2,1)}, bf16[2,8,16,64]{3,2,1,0:T(8,128)(2,1)}, u32[]{:S(2)}, u32[]{:S(2)}) collective-permute-start(bf16[2,8,16,64]{3,2,1,0:T(8,128)(2,1)} %pad_maximum_fusion.1), channel_id=1, source_target_pairs={{0,1},{1,2},{2,3},{3,4},{4,5},{5,6},{6,7},{7,8},{8,9},{9,10},{10,1... | collective-permute-start | bytes 98312 | tf_op jit(solution)/shard_map/ppermute | solution.py:18
  14.7 44.6 %collective-permute-start.8 = (bf16[2,16,64]{2,1,0:T(8,128)(2,1)S(1)}, bf16[2,16,64]{2,1,0:T(8,128)(2,1)S(1)}, u32[]{:S(2)}, u32[]{:S(2)}) collective-permute-start(bf16[2,16,64]{2,1,0:T(8,128)(2,1)S(1)} %get-tuple-element.11), channel_id=1, source_target_pairs={{0,1},{1,2},{2,3},{3,4},{4,5},{5,6},{6,7},{7,8},{8,9},{9,10},{10,1... | collective-permute-start | bytes 12296 | tf_op jit(solution)/shard_map/ppermute | solution.py:26
  16.0 43.9 %collective-permute-start.9 = (bf16[2,16,64]{2,1,0:T(8,128)(2,1)S(1)}, bf16[2,16,64]{2,1,0:T(8,128)(2,1)}, u32[]{:S(2)}, u32[]{:S(2)}) collective-permute-start(bf16[2,16,64]{2,1,0:T(8,128)(2,1)S(1)} %get-tuple-element.12), channel_id=1, source_target_pairs={{1,0},{2,1},{3,2},{4,3},{5,4},{6,5},{7,6},{8,7},{9,8},{10,9},{11,1... | collective-permute-start | bytes 12296 | tf_op jit(solution)/shard_map/ppermute | solution.py:29
  58.6 23.6 %collective-permute-start.2 = (bf16[2,8,16,64]{3,2,1,0:T(8,128)(2,1)}, bf16[2,8,16,64]{3,2,1,0:T(8,128)(2,1)}, u32[]{:S(2)}, u32[]{:S(2)}) collective-permute-start(bf16[2,8,16,64]{3,2,1,0:T(8,128)(2,1)} %pad_maximum_fusion.2), channel_id=1, source_target_pairs={{0,15},{1,0},{2,1},{3,2},{4,3},{5,4},{6,5},{7,6},{8,7},{9,8},{10,9... | collective-permute-start | bytes 98312 | tf_op jit(solution)/shard_map/ppermute | solution.py:18
  59.3 0.6 copy-start.6
  59.3 5.8 %collective-permute-start.5 = (bf16[1,2,16,64]{3,2,1,0:T(8,128)(2,1)S(1)}, bf16[1,2,16,64]{3,2,1,0:T(8,128)(2,1)S(1)}, u32[]{:S(2)}, u32[]{:S(2)}) collective-permute-start(bf16[1,2,16,64]{3,2,1,0:T(8,128)(2,1)S(1)} %slice.143), channel_id=1, source_target_pairs={{0,1},{1,2},{2,3},{3,4},{4,5},{5,6},{6,7},{7,8},{8,9},{9,10},{10,1... | collective-permute-start | bytes 12296 | tf_op jit(solution)/shard_map/ppermute | solution.py:18
  66.6 6.6 %collective-permute-start.7 = (bf16[1,2,16,64]{3,2,1,0:T(8,128)(2,1)S(1)}, bf16[1,2,16,64]{3,2,1,0:T(8,128)(2,1)S(1)}, u32[]{:S(2)}, u32[]{:S(2)}) collective-permute-start(bf16[1,2,16,64]{3,2,1,0:T(8,128)(2,1)S(1)} %get-tuple-element.19), channel_id=1, source_target_pairs={{0,15},{1,0},{2,1},{3,2},{4,3},{5,4},{6,5},{7,6},{8,7},{9,8},{10,9... | collective-permute-start | bytes 12296 | tf_op jit(solution)/shard_map/ppermute | solution.py:18
  67.4 15.9 %copy-start.4 = (bf16[3,8,16,64]{3,2,0,1:T(8,128)(2,1)S(1)}, bf16[3,8,16,64]{3,2,0,1:T(8,128)(2,1)}, u32[]{:S(2)}) copy-start(bf16[3,8,16,64]{3,2,0,1:T(8,128)(2,1)} %fusion.29) | copy-start | bytes 147460
  73.8 13.0 %copy-start.5 = (pred[32,4]{1,0:T(8,128)(4,1)S(1)}, pred[32,4]{1,0:T(8,128)(4,1)}, u32[]{:S(2)}) copy-start(pred[32,4]{1,0:T(8,128)(4,1)} %copy.41) | copy-start | bytes 388
  74.6 6.0 %collective-permute-start.1 = (bf16[1,8,16,64]{3,2,1,0:T(8,128)(2,1)S(1)}, bf16[1,8,16,64]{3,2,1,0:T(8,128)(2,1)S(1)}, u32[]{:S(2)}, u32[]{:S(2)}) collective-permute-start(bf16[1,8,16,64]{3,2,1,0:T(8,128)(2,1)S(1)} %slice.134), channel_id=1, source_target_pairs={{0,1},{1,2},{2,3},{3,4},{4,5},{5,6},{6,7},{7,8},{8,9},{9,10},{10,1... | collective-permute-start | bytes 49160 | tf_op jit(solution)/shard_map/ppermute | solution.py:18
  82.9 2.3 %collective-permute-start.3 = (bf16[1,8,16,64]{3,2,1,0:T(8,128)(2,1)S(1)}, bf16[1,8,16,64]{3,2,1,0:T(8,128)(2,1)S(1)}, u32[]{:S(2)}, u32[]{:S(2)}) collective-permute-start(bf16[1,8,16,64]{3,2,1,0:T(8,128)(2,1)S(1)} %get-tuple-element.13), channel_id=1, source_target_pairs={{0,15},{1,0},{2,1},{3,2},{4,3},{5,4},{6,5},{7,6},{8,7},{9,8},{10,9... | collective-permute-start | bytes 49160 | tf_op jit(solution)/shard_map/ppermute | solution.py:18
  86.8 6.3 %copy-start.1 = (bf16[3,16,16,64]{3,2,0,1:T(8,128)(2,1)S(1)}, bf16[3,16,16,64]{3,2,0,1:T(8,128)(2,1)}, u32[]{:S(2)}) copy-start(bf16[3,16,16,64]{3,2,0,1:T(8,128)(2,1)} %fusion.22) | copy-start | bytes 294916
where the time goes:
time: 99.1 us; the launch traced here: 98 us
  matrix products  26.6 us (27%)
  blocking collectives  26.2 us (26%)
  local copies, waits for them, and re-layouts  19 us (19%)
  starting transfers between devices  9.8 us (10%)
  other arithmetic  9.01 us (9%)
  waiting for transfers between devices  7.18 us (7%)
    all_gather x1, blocking collectives, on_device(): piece = lax.all_gather(up2, ('row', 'col'), axis=0, tiled=True)  26.2 us
    ppermute x8, starting transfers between devices, passed_along(): lax.ppermute(shard, axis, [(i, (i + by) % length) for i in range(length)])  7.23 us
    ppermute x8, waiting for transfers between devices, passed_along(): lax.ppermute(shard, axis, [(i, (i + by) % length) for i in range(length)])  7.18 us
    dot_general x1, matrix products, on_device(): jnp.einsum('ktmrs,tmvs->ktvr', leaf_coupling, leaf_rows, preferred_elemen...  6.27 us
    dot_general x1, matrix products, on_device(): jnp.einsum('ktnpq,tnvq->ktvp', near_blocks, neighbours, preferred_element...  5.75 us
    unnamed x21, local copies, waits for them, and re-layouts  3.94 us
    dot_general x1, matrix products, on_device(): jnp.einsum('ktmrs,tmvs->ktvr', top_coupling, top_rows, preferred_element_...  3.9 us
    dot_general x1, matrix products, on_device(): jnp.einsum('tpr,ktvr->ktvp', leaf_basis, down0, preferred_element_type=f32)  3.11 us
  transfers between devices with their start and end apart: 10, of which 2 were waited for; matrix products, arithmetic and copies ran while one was open for 35% of the time, Pallas kernels for 0%

commit v1 on v0

v1 whole, which is shorter than its diff:
```python
import functools

import jax
import jax.numpy as jnp
from jax import lax
from jax.experimental import pallas as pl
from jax.experimental.pallas import tpu as pltpu
from jax.sharding import PartitionSpec as P

REACH = 2
WIN = 2 * REACH + 1
HW = 2
AXES = ("row", "col")
F32 = jnp.float32
BF = jnp.bfloat16
NT = (((1,), (1,)), ((), ()))
LIMIT = 40 * 1024 * 1024

VMEM = pltpu.VMEM
SMEM = pltpu.SMEM


def side_by_side(left, right):
    return jnp.concatenate([left, right], axis=1)


def weights_of(ref, *place):
    return jnp.concatenate([ref[(k,) + place] for k in range(ref.shape[0])], axis=0)


def by_kernel(wide, rank):
    count = wide.shape[1] // rank
    return jnp.concatenate([wide[:, k * rank:(k + 1) * rank] for k in range(count)], axis=0)


def up_body(lsend, psend, vec, basis, ltr, ptr, top, own, sib, cross, fwd, back, low, mid):
    leaves, _, rank = vec.shape
    col = lax.axis_index("col")
    cap0 = lsend.shape[2]
    cap1 = psend.shape[1]
    for t in range(leaves):
        low[t] = jnp.dot(vec[t], basis[t], preferred_element_type=F32).astype(BF)
    for j in range(leaves // 2):
        both = side_by_side(low[2 * j], low[2 * j + 1])
        weights = ltr[2 * j:2 * j + 2].reshape(2 * rank, rank)
        mid[j] = jnp.dot(both, weights, preferred_element_type=F32).astype(BF)
    for i in range(leaves // 8):
        pieces = []
        for half in range(2):
            j = 4 * i + 2 * half
            both = side_by_side(mid[j], mid[j + 1])
            weights = ptr[j:j + 2].reshape(2 * rank, rank)
            pieces.append(jnp.dot(both, weights, preferred_element_type=F32).astype(BF))
        top[i] = side_by_side(*pieces)

    def pack(out, place):
        for c in range(cap0 // 2):
            out[c] = side_by_side(low[lsend[place, 0, 2 * c]], low[lsend[place, 0, 2 * c + 1]])
        for c in range(cap1 // 2):
            out[cap0 // 2 + c] = side_by_side(
                mid[psend[0, 2 * c, place]], mid[psend[0, 2 * c + 1, place]]
            )

    def pack_halo(out, start):
        out[(cap0 + cap1) // 2] = side_by_side(vec[start], vec[start + 1])

    pack(own, REACH)
    pack(fwd, 0)
    pack(back, 4)
    pack(sib, 1 + 2 * col)
    pack_halo(sib, (1 - col) * (leaves - HW))
    pack(cross, 3 - 2 * col)
    pack_halo(cross, col * (leaves - HW))


def up_pass(lsend, psend, vec, basis, ltr, ptr):
    leaves, vecs, rank = vec.shape
    blocks = (lsend.shape[2] + psend.shape[1]) // 2
    shape = lambda n: jax.ShapeDtypeStruct((n, vecs, 2 * rank), BF)
    return pl.pallas_call(
        up_body,
        out_shape=[shape(leaves // 8), shape(blocks), shape(blocks + 1), shape(blocks + 1), shape(blocks), shape(blocks)],
        in_specs=[pl.BlockSpec(memory_space=SMEM)] * 2 + [pl.BlockSpec(memory_space=VMEM)] * 4,
        out_specs=[pl.BlockSpec(memory_space=VMEM)] * 6,
        scratch_shapes=[VMEM((leaves, vecs, rank), BF), VMEM((leaves // 2, vecs, rank), BF)],
        compiler_params=pltpu.CompilerParams(vmem_limit_bytes=LIMIT),
        cost_estimate=pl.CostEstimate(flops=10_000_000, bytes_accessed=3_000_000, transcendentals=0),
        name="up",
    )(lsend, psend, vec, basis, ltr, ptr)


def near_body(offsets, vec, blocks, out, padded):
    step = pl.program_id(0)
    count = blocks.shape[1]
    leaves, vecs, rank = vec.shape

    @pl.when(step == 0)
    def _():
        padded[0:HW] = jnp.zeros((HW, vecs, rank), BF)
        padded[HW:HW + leaves] = vec[...]
        padded[HW + leaves:] = jnp.zeros((HW, vecs, rank), BF)

    for q in range(count):
        t = step * count + q
        total = None
        for n in range(blocks.shape[2]):
            rows = padded[t + HW + offsets[n, t]]
            part = lax.dot_general(rows, weights_of(blocks, q, n), NT, preferred_element_type=F32)
            total = part if total is None else total + part
        out[q] = by_kernel(total, rank)


def near_pass(offsets, vec, blocks, per):
    kernels, leaves, near, rank, _ = blocks.shape
    vecs = vec.shape[1]
    return pl.pallas_call(
        near_body,
        grid=(leaves // per,),
        out_shape=jax.ShapeDtypeStruct((leaves, kernels * vecs, rank), F32),
        in_specs=[
            pl.BlockSpec(memory_space=SMEM),
            pl.BlockSpec(memory_space=VMEM),
            pl.BlockSpec((kernels, per, near, rank, rank), lambda i: (0, i, 0, 0, 0)),
        ],
        out_specs=pl.BlockSpec((per, kernels * vecs, rank), lambda i: (i, 0, 0)),
        scratch_shapes=[VMEM((leaves + 2 * HW, vecs, rank), BF)],
        compiler_params=pltpu.CompilerParams(vmem_limit_bytes=LIMIT),
        cost_estimate=pl.CostEstimate(flops=40_000_000, bytes_accessed=12_000_000, transcendentals=0),
        name="near",
    )(offsets, vec, blocks)


def far_body(llist, plist, offsets, own, sib, cross, fwd, back, leaf, pair, first, last, nears, far0, far1, edge,
             wleaf, wpair, halo):
    step = pl.program_id(0)
    per = leaf.shape[1]
    _, vecs, rank = wleaf.shape
    cap0 = wleaf.shape[0] // WIN
    cap1 = wpair.shape[0] // WIN
    leaves = offsets.shape[1]
    heads = first.shape[1]

    @pl.when(step == 0)
    def _():
        col = lax.axis_index("col")
        place = lax.axis_index("row") * lax.axis_size("col") + col
        last_place = lax.axis_size("row") * lax.axis_size("col") - 1

        def unpack(block, slot):
            for c in range(cap0 // 2):
                row = block[c]
                wleaf[slot * cap0 + 2 * c] = row[:, :rank]
                wleaf[slot * cap0 + 2 * c + 1] = row[:, rank:]
            for c in range(cap1 // 2):
                row = block[cap0 // 2 + c]
                wpair[slot * cap1 + 2 * c] = row[:, :rank]
                wpair[slot * cap1 + 2 * c + 1] = row[:, rank:]

        unpack(own, REACH)
        unpack(fwd, 0)
        unpack(back, 4)
        unpack(sib, 3 - 2 * col)
        unpack(cross, 1 + 2 * col)
        row = sib[(cap0 + cap1) // 2]
        halo[2 - 2 * col] = row[:, :rank]
        halo[3 - 2 * col] = row[:, rank:]
        row = cross[(cap0 + cap1) // 2]
        halo[2 * col] = row[:, :rank]
        halo[2 * col + 1] = row[:, rank:]
        zero = jnp.zeros((HW, vecs, rank), BF)
        halo[2 * HW:] = zero

        @pl.when(place == 0)
        def _():
            halo[0:HW] = zero

        @pl.when(place == last_place)
        def _():
            halo[HW:2 * HW] = zero

        for q in range(heads):
            total = None
            for n in range(first.shape[2]):
                at = q + offsets[n, q]
                rows = halo[jnp.where(at < 0, at + HW, 2 * HW)]
                part = lax.dot_general(rows, weights_of(first, q, n), NT, preferred_element_type=F32)
                total = part if total is None else total + part
            edge[q] = nears[0, q] + by_kernel(total, rank)
            total = None
            t = leaves - heads + q
            for n in range(last.shape[2]):
                at = t + offsets[n, t]
                rows = halo[jnp.where(at >= leaves, at - leaves + HW, 2 * HW)]
                part = lax.dot_general(rows, weights_of(last, q, n), NT, preferred_element_type=F32)
                total = part if total is None else total + part
            edge[heads + q] = nears[1, q] + by_kernel(total, rank)

    for q in range(per):
        t = step * per + q
        total = None
        for m in range(leaf.shape[2]):
            rows = wleaf[llist[m, t]]
            part = lax.dot_general(rows, weights_of(leaf, q, m), NT, preferred_element_type=F32)
            total = part if total is None else total + part
        far0[q] = by_kernel(total, rank)
    for q in range(per // 2):
        t = step * (per // 2) + q
        total = None
        for m in range(pair.shape[2]):
            rows = wpair[plist[m, t]]
            part = lax.dot_general(rows, weights_of(pair, q, m), NT, preferred_element_type=F32)
            total = part if total is None else total + part
        far1[q] = by_kernel(total, rank)


def far_pass(llist, plist, offsets, own, sib, cross, fwd, back, leaf, pair, near_blocks, nears, per, cap0, cap1):
    kernels, leaves, partners, rank, _ = leaf.shape
    vecs = own.shape[1]
    near = near_blocks.shape[2]
    ends = leaves // HW
    whole = pl.BlockSpec(memory_space=VMEM)
    rows = kernels * vecs
    ends_of_near = jnp.stack([nears[:HW], nears[leaves - HW:]])
    return pl.pallas_call(
        far_body,
        grid=(leaves // per,),
        out_shape=[
            jax.ShapeDtypeStruct((leaves, rows, rank), F32),
            jax.ShapeDtypeStruct((leaves // 2, rows, rank), F32),
            jax.ShapeDtypeStruct((2 * HW, rows, rank), F32),
        ],
        in_specs=[pl.BlockSpec(memory_space=SMEM)] * 3 + [whole] * 5 + [
            pl.BlockSpec((kernels, per, partners, rank, rank), lambda i: (0, i, 0, 0, 0)),
            pl.BlockSpec((kernels, per // 2, pair.shape[2], rank, rank), lambda i: (0, i, 0, 0, 0)),
            pl.BlockSpec((kernels, HW, near, rank, rank), lambda i: (0, 0, 0, 0, 0)),
            pl.BlockSpec((kernels, HW, near, rank, rank), lambda i: (0, ends - 1, 0, 0, 0)),
            whole,
        ],
        out_specs=[
            pl.BlockSpec((per, rows, rank), lambda i: (i, 0, 0)),
            pl.BlockSpec((per // 2, rows, rank), lambda i: (i, 0, 0)),
            pl.BlockSpec((2 * HW, rows, rank), lambda i: (0, 0, 0)),
        ],
        scratch_shapes=[
            VMEM((WIN * cap0, vecs, rank), BF),
            VMEM((WIN * cap1, vecs, rank), BF),
            VMEM((3 * HW, vecs, rank), BF),
        ],
        compiler_params=pltpu.CompilerParams(vmem_limit_bytes=LIMIT),
        cost_estimate=pl.CostEstimate(flops=80_000_000, bytes_accessed=18_000_000, transcendentals=0),
        name="far",
    )(llist, plist, offsets, own, sib, cross, fwd, back, leaf, pair, near_blocks, near_blocks, ends_of_near)


def down_body(tlist, tops, coupling, ptr, ltr, basis, far1, far0, nears, edge, out, held):
    step = pl.program_id(0)
    steps = pl.num_programs(0)
    per = coupling.shape[1]
    rank = basis.shape[2]
    vecs = tops.shape[1]
    kernels = coupling.shape[0]

    @pl.when(step == 0)
    def _():
        for i in range(tops.shape[0]):
            row = tops[i]
            held[2 * i] = row[:, :rank]
            held[2 * i + 1] = row[:, rank:]

    for q in range(per):
        i = step * per + q
        total = None
        for m in range(coupling.shape[2]):
            rows = held[tlist[i, m]]
            part = lax.dot_general(rows, weights_of(coupling, q, m), NT, preferred_element_type=F32)
            total = part if total is None else total + part
        down2 = by_kernel(total, rank).astype(BF)
        for a in range(2):
            j = 2 * q + a
            down1 = (far1[j] + lax.dot_general(down2, ptr[j], NT, preferred_element_type=F32)).astype(BF)
            for b in range(2):
                t = 2 * j + b
                down0 = (far0[t] + lax.dot_general(down1, ltr[t], NT, preferred_element_type=F32)).astype(BF)
                points = lax.dot_general(down0, basis[t], NT, preferred_element_type=F32)
                base = nears[t]
                if t < HW:
                    base = jnp.where(step == 0, edge[t], base)
                if t >= 4 * per - HW:
                    base = jnp.where(step == steps - 1, edge[HW + t - (4 * per - HW)], base)
                points = (points + base).astype(BF)
                for k in range(kernels):
                    out[k, t] = points[k * vecs:(k + 1) * vecs]


def down_pass(tlist, tops, coupling, ptr, ltr, basis, far1, far0, nears, edge, per):
    kernels, count, partners, rank, _ = coupling.shape
    vecs = tops.shape[1]
    leaves = basis.shape[0]
    rows = kernels * vecs
    whole = pl.BlockSpec(memory_space=VMEM)
    return pl.pallas_call(
        down_body,
        grid=(count // per,),
        out_shape=jax.ShapeDtypeStruct((kernels, leaves, vecs, rank), BF),
        in_specs=[
            pl.BlockSpec(memory_space=SMEM),
            whole,
            pl.BlockSpec((kernels, per, partners, rank, rank), lambda i: (0, i, 0, 0, 0)),
            pl.BlockSpec((2 * per, rank, rank), lambda i: (i, 0, 0)),
            pl.BlockSpec((4 * per, rank, rank), lambda i: (i, 0, 0)),
            pl.BlockSpec((4 * per, rank, rank), lambda i: (i, 0, 0)),
            pl.BlockSpec((2 * per, rows, rank), lambda i: (i, 0, 0)),
            pl.BlockSpec((4 * per, rows, rank), lambda i: (i, 0, 0)),
            pl.BlockSpec((4 * per, rows, rank), lambda i: (i, 0, 0)),
            whole,
        ],
        out_specs=pl.BlockSpec((kernels, 4 * per, vecs, rank), lambda i: (0, i, 0, 0)),
        scratch_shapes=[VMEM((2 * tops.shape[0], vecs, rank), BF)],
        compiler_params=pltpu.CompilerParams(vmem_limit_bytes=LIMIT),
        cost_estimate=pl.CostEstimate(flops=40_000_000, bytes_accessed=8_000_000, transcendentals=0),
        name="down",
    )(tlist, tops, coupling, ptr, ltr, basis, far1, far0, nears, edge)


def sent(block, pairs):
    return lax.ppermute(block, AXES, pairs)


def on_device(
    vectors,
    leaf_basis,
    leaf_transfer,
    pair_transfer,
    near_blocks,
    near_offset,
    leaf_send,
    leaf_list,
    leaf_coupling,
    pair_send,
    pair_list,
    pair_coupling,
    top_list,
    top_coupling,
):
    devs = lax.axis_size("row") * lax.axis_size("col")
    cap0, cap1 = leaf_send.shape[2], pair_send.shape[2]
    lsend = jnp.transpose(leaf_send, (1, 0, 2))
    psend = jnp.transpose(pair_send, (0, 2, 1))
    offsets = near_offset.T
    llist = leaf_list.T
    plist = pair_list.T
    top, own, sib, cross, fwd, back = up_pass(lsend, psend, vectors, leaf_basis, leaf_transfer, pair_transfer)
    ring = range(devs)
    sib = sent(sib, [(d, d ^ 1) for d in ring])
    cross = sent(cross, [(d, (d + 1 if d % 2 else d - 1) % devs) for d in ring])
    fwd = sent(fwd, [(d, (d + 2) % devs) for d in ring])
    back = sent(back, [(d, (d - 2) % devs) for d in ring])
    tops = lax.all_gather(top, AXES, axis=0, tiled=True)
    nears = near_pass(offsets, vectors, near_blocks, 4)
    far0, far1, edge = far_pass(
        llist, plist, offsets, own, sib, cross, fwd, back, leaf_coupling, pair_coupling, near_blocks, nears, 4, cap0, cap1
    )
    return down_pass(
        top_list, tops, top_coupling, pair_transfer, leaf_transfer, leaf_basis, far1, far0, nears, edge, 2
    )


def solution(mesh):
    placed = P(("groups", "row", "col"))
    behind = P(None, ("groups", "row", "col"))
    return jax.shard_map(
        on_device,
        mesh=mesh,
        in_specs=(
            placed, placed, placed, placed, behind, placed, placed, placed, behind, placed, placed, behind, placed, behind,
        ),
        out_specs=behind,
        check_vma=False,
    )
```

time: 99.1 us -> 67.8 us (0.68)
  Pallas kernels: 0 us -> 28.6 us
  matrix products: 26.6 us -> 0 us
  other arithmetic: 9.01 us -> 0.01 us
  local copies, waits for them, and re-layouts: 19 us -> 11.2 us
  waiting for transfers between devices: 7.18 us -> 0.01 us
  blocking collectives: 26.2 us -> 19.2 us
  starting transfers between devices: 9.8 us -> 8.17 us
    pallas_call x0 -> x4, Pallas kernels: none -> 28.6 us  [the longest x1 12.9 us: down_pass(): pl.pallas_call(down_body, grid=(count // per,), out_shape=jax.ShapeDtypeS...]
    dot_general x9 -> x0, matrix products: 26.6 us -> none  [the longest x1 6.27 us: on_device(): jnp.einsum('ktmrs,tmvs->ktvr', leaf_coupling, leaf_rows, preferred_elemen...]
    unnamed x21 -> x38, local copies, waits for them, and re-layouts: 3.94 us -> 11.2 us
    ppermute x10 -> x4, waiting for transfers between devices: 7.18 us -> 0.01 us  [sent(): return lax.ppermute(block, AXES, pairs)]
    gather x6 -> x0, local copies, waits for them, and re-layouts: 7.08 us -> none  [the longest x1 2.37 us: on_device(): taken = jnp.take(piece, jnp.clip(top_list, 0, count - 1), axis=0)]
    all_gather x1, blocking collectives: 26.2 us -> 19.2 us  [on_device(): tops = lax.all_gather(top, AXES, axis=0, tiled=True)]
    slice x7 -> x0, local copies, waits for them, and re-layouts: 3.7 us -> none  [the longest x2 1.55 us: on_device(): carry_leaf = carry_leaf[1:]]
    and x6 -> x0, other arithmetic: 2.78 us -> none  [the longest x1 0.69 us: on_device(): inside = (top_list >= 0) & (top_list < count)]
  transfers between devices with their start and end apart: 10 -> 4, of which waited for: 2 -> 0; matrix products, arithmetic and copies ran while one was open for 35% -> 0% of each run, Pallas kernels for 0% -> 7%
where the time goes in v1:
time: 67.8 us; the launch traced here: 67.3 us
  Pallas kernels  28.6 us (42%)
  blocking collectives  19.2 us (28%)
  local copies, waits for them, and re-layouts  11.2 us (17%)
  starting transfers between devices  8.17 us (12%)
    all_gather x1, blocking collectives, on_device(): tops = lax.all_gather(top, AXES, axis=0, tiled=True)  19.2 us
    pallas_call x1, Pallas kernels, down_pass(): pl.pallas_call(down_body, grid=(count // per,), out_shape=jax.ShapeDtypeS...  12.9 us
    unnamed x38, local copies, waits for them, and re-layouts  11.2 us
    pallas_call x1, Pallas kernels, far_pass(): pl.pallas_call(far_body, grid=(leaves // per,), out_shape=[jax.ShapeDtype...  9.54 us
    ppermute x4, starting transfers between devices, sent(): return lax.ppermute(block, AXES, pairs)  8.17 us
    pallas_call x1, Pallas kernels, near_pass(): pl.pallas_call(near_body, grid=(leaves // per,), out_shape=jax.ShapeDtype...  4.84 us
  transfers between devices with their start and end apart: 4, of which 0 were waited for; matrix products, arithmetic and copies ran while one was open for 0% of the time, Pallas kernels for 7%

profile of v1, /device:TPU:0, one launch (start us, length us, event | category | flops | bytes accessed | tf_op | source)
XLA Modules:
  0.0 67.3 jit_solution(1480346493774635877)
XLA Ops:
  0.0 0.0 copy-start.13
  0.0 0.0 copy-start.4
  0.0 1.1 %copy-done.4 = bf16[32,64,64]{2,1,0:T(8,128)(2,1)S(1)} copy-done((bf16[32,64,64]{2,1,0:T(8,128)(2,1)S(1)}, bf16[32,64,64]{2,1,0:T(8,128)(2,1)}, u32[]{:S(2)}) %copy-start.4) | copy-done | bytes 262168
  1.1 0.0 copy-start.6
  1.1 1.0 %copy-done.6 = bf16[32,64,64]{2,1,0:T(8,128)(2,1)S(1)} copy-done((bf16[32,64,64]{2,1,0:T(8,128)(2,1)S(1)}, bf16[32,64,64]{2,1,0:T(8,128)(2,1)}, u32[]{:S(2)}) %copy-start.6) | copy-done | bytes 262168
  2.1 0.0 copy-start.8
  2.1 0.9 %copy-done.8 = bf16[16,64,64]{2,1,0:T(8,128)(2,1)S(1)} copy-done((bf16[16,64,64]{2,1,0:T(8,128)(2,1)S(1)}, bf16[16,64,64]{2,1,0:T(8,128)(2,1)}, u32[]{:S(2)}) %copy-start.8) | copy-done | bytes 131096
  3.1 0.0 copy-start.10
  3.1 0.9 %copy-done.10 = bf16[32,16,64]{2,1,0:T(8,128)(2,1)S(1)} copy-done((bf16[32,16,64]{2,1,0:T(8,128)(2,1)S(1)}, bf16[32,16,64]{2,1,0:T(8,128)(2,1)}, u32[]{:S(2)}) %copy-start.10) | copy-done | bytes 65560
  4.0 0.0 copy-start.15
  4.0 0.7 %copy-done.15 = s32[1,5,8]{2,0,1:T(1,128)S(1)} copy-done((s32[1,5,8]{2,0,1:T(1,128)S(1)}, s32[1,5,8]{2,0,1:T(1,128)}, u32[]{:S(2)}) %copy-start.15) | copy-done | bytes 184
  4.6 0.0 copy-start.18
  4.6 0.7 %copy-done.18 = s32[1,5,2]{1,2,0:T(2,128)S(1)} copy-done((s32[1,5,2]{1,2,0:T(2,128)S(1)}, s32[1,5,2]{1,2,0:T(2,128)}, u32[]{:S(2)}) %copy-start.18) | copy-done | bytes 64
  5.3 0.0 copy-start.16
  5.3 0.0 copy-start.17
  5.3 1.3 %up.1 = (bf16[4,16,128]{2,1,0:T(8,128)(2,1)S(1)}, bf16[5,16,128]{2,1,0:T(8,128)(2,1)S(1)}, bf16[6,16,128]{2,1,0:T(8,128)(2,1)S(1)}, bf16[6,16,128]{2,1,0:T(8,128...) custom-call(s32[5,1,8]{2,1,0:T(1,128)S(1)} %bitcast.11, s32[1,2,5]{2,1,0:T(2,128)S(1)} %bitcast.14, ...), custom_call_target="tpu_custom_call" | custom-call | flops 10000000 | bytes 3000000 | tf_op jit(solution)/shard_map/up/pallas_call | solution.py:80
  6.6 3.0 %collective-permute-start.2 = (bf16[5,16,128]{2,1,0:T(8,128)(2,1)S(1)}, bf16[5,16,128]{2,1,0:T(8,128)(2,1)S(1)}, u32[]{:S(2)}, u32[]{:S(2)}) collective-permute-start(bf16[5,16,128]{2,1,0:T(8,128)(2,1)S(1)} %get-tuple-element.18), channel_id=1, source_target_pairs={{0,2},{1,3},{2,4},{3,5},{4,6},{5,7},{6,8},{7,9},{8,10},{9,11},{10,... | collective-permute-start | bytes 61448 | tf_op jit(solution)/shard_map/ppermute | solution.py:326
  9.6 3.1 %collective-permute-start.3 = (bf16[5,16,128]{2,1,0:T(8,128)(2,1)S(1)}, bf16[5,16,128]{2,1,0:T(8,128)(2,1)S(1)}, u32[]{:S(2)}, u32[]{:S(2)}) collective-permute-start(bf16[5,16,128]{2,1,0:T(8,128)(2,1)S(1)} %get-tuple-element.19), channel_id=1, source_target_pairs={{0,14},{1,15},{2,0},{3,1},{4,2},{5,3},{6,4},{7,5},{8,6},{9,7},{10,... | collective-permute-start | bytes 61448 | tf_op jit(solution)/shard_map/ppermute | solution.py:326
  12.7 0.0 collective-permute-start
  12.7 2.1 %collective-permute-start.1 = (bf16[6,16,128]{2,1,0:T(8,128)(2,1)S(1)}, bf16[6,16,128]{2,1,0:T(8,128)(2,1)S(1)}, u32[]{:S(2)}, u32[]{:S(2)}) collective-permute-start(bf16[6,16,128]{2,1,0:T(8,128)(2,1)S(1)} %get-tuple-element.17), channel_id=1, source_target_pairs={{0,15},{1,2},{2,1},{3,4},{4,3},{5,6},{6,5},{7,8},{8,7},{9,10},{10,... | collective-permute-start | bytes 73736 | tf_op jit(solution)/shard_map/ppermute | solution.py:326
  14.8 19.2 %all_gather.3.tops = bf16[64,16,128]{2,1,0:T(8,128)(2,1)S(1)} all-gather(bf16[4,16,128]{2,1,0:T(8,128)(2,1)S(1)} %get-tuple-element.14), channel_id=1, replica_groups=mesh['groups'=2,'row'=8,'col'=2] {'row','col'}, dimensions={0}, use_global_device_ids=true | all-gather | bytes 278528 | tf_op jit(solution)/shard_map/all_gather | solution.py:358
  34.0 0.0 copy-start
  34.0 2.3 %copy-done = bf16[3,32,3,64,64]{4,3,2,1,0:T(8,128)(2,1)S(1)} copy-done((bf16[3,32,3,64,64]{4,3,2,1,0:T(8,128)(2,1)S(1)}, bf16[3,32,3,64,64]{4,3,2,1,0:T(8,128)(2,1)}, u32[]{:S(2)}) %copy-start) | copy-done | bytes 2359320
  36.3 0.0 copy-start.11
  36.3 0.9 %copy-done.11 = bf16[32,16,64]{2,1,0:T(8,128)(2,1)S(1)} copy-done((bf16[32,16,64]{2,1,0:T(8,128)(2,1)S(1)}, bf16[32,16,64]{2,1,0:T(8,128)(2,1)}, u32[]{:S(2)}) %copy-start.11) | copy-done | bytes 65560
  37.2 0.0 copy-start.12
  37.2 0.7 %copy-done.12 = s32[32,3]{0,1:T(4,128)S(1)} copy-done((s32[32,3]{0,1:T(4,128)S(1)}, s32[32,3]{0,1:T(4,128)}, u32[]{:S(2)}) %copy-start.12) | copy-done | bytes 408
  37.9 0.0 copy-start.1
  37.9 4.8 %near.1.nears = f32[32,48,64]{2,1,0:T(8,128)S(1)} custom-call(s32[3,32]{1,0:T(4,128)S(1)} %bitcast.9, bf16[32,16,64]{2,1,0:T(8,128)(2,1)S(1)} %copy-done.11, bf16[3,32,3,64,64]{4,3,2,1,0:T(8,128)(2,1)S(1)} %copy-done), custom_call_target="tpu_custom_call" | custom-call | flops 40000000 | bytes 12000000 | tf_op jit(solution)/shard_map/near/pallas_call | solution.py:116
  42.8 0.0 collective-permute-done.2.fwd
  42.8 0.0 collective-permute-done.3.back
  42.8 0.0 collective-permute-done.sib
  42.8 0.0 collective-permute-done.1.cross
  42.8 0.0 copy-done.13
  42.9 0.0 copy-done.16
  42.9 0.0 copy-done.17
  42.9 0.0 copy-done.1
  42.9 0.0 copy-start.3
  42.9 1.9 %copy-done.3 = bf16[3,16,4,64,64]{4,3,2,1,0:T(8,128)(2,1)S(1)} copy-done((bf16[3,16,4,64,64]{4,3,2,1,0:T(8,128)(2,1)S(1)}, bf16[3,16,4,64,64]{4,3,2,1,0:T(8,128)(2,1)}, u32[]{:S(2)}) %copy-start.3) | copy-done | bytes 1572888
  44.8 0.0 copy-start.2
  44.8 0.0 copy-start.14
  44.8 9.5 %far.1 = (f32[32,48,64]{2,1,0:T(8,128)S(1)}, f32[16,48,64]{2,1,0:T(8,128)S(1)}, f32[4,48,64]{2,1,0:T(8,128)S(1)}) custom-call(s32[4,32]{1,0:T(4,128)S(1)} %bitcast.12, s32[4,16]{1,0:T(4,128)S(1)} %bitcast.13, s32[3,32]{1,0:T(4,128)S(1)} %bitcast.10, bf16[5,16,128]{2,1,0:T(8,128)(2,1)S(1)} %get-tuple-element.15.own, ...), custom_call_target="tpu_custom_call" | custom-call | flops 80000000 | bytes 18000000 | tf_op jit(solution)/shard_map/far/pallas_call | solution.py:224
  54.3 0.0 copy-done.2
  54.4 0.0 copy-done.5
  54.4 0.0 copy-done.7
  54.4 0.0 copy-done.9
  54.4 0.0 copy-done.14
  54.4 12.9 %down.1 = bf16[3,32,16,64]{3,2,1,0:T(8,128)(2,1)} custom-call(s32[8,8]{1,0:T(8,128)S(1)} %copy-done.14, bf16[64,16,128]{2,1,0:T(8,128)(2,1)S(1)} %all_gather.3.tops, bf16[3,8,8,64,64]{4,3,2,1,0:T(8,128)(2,1)S(1)} %copy-done.2, bf16[16,64,64]{2,1,0:T(8,128)(2,1)S(1)} %copy-done.9, bf16[32,64,64]{2,1,0:T(8,128)(2,1)S(1)} %copy-done.7, ...), custom_call_target="tpu_custom_call" | custom-call | flops 40000000 | bytes 8000000 | tf_op jit(solution)/shard_map/down/pallas_call | solution.py:301
  (5 shorter events, 0.1 us)
Async XLA Ops:
  0.0 42.8 %copy-start.13 = (s32[32,3]{0,1:T(4,128)S(1)}, s32[32,3]{0,1:T(4,128)}, u32[]{:S(2)}) copy-start(s32[32,3]{0,1:T(4,128)} %param.19) | copy-start | bytes 1156
  0.0 1.1 %copy-start.4 = (bf16[32,64,64]{2,1,0:T(8,128)(2,1)S(1)}, bf16[32,64,64]{2,1,0:T(8,128)(2,1)}, u32[]{:S(2)}) copy-start(bf16[32,64,64]{2,1,0:T(8,128)(2,1)} %basis.3) | copy-start | bytes 786436
  1.1 1.0 %copy-start.6 = (bf16[32,64,64]{2,1,0:T(8,128)(2,1)S(1)}, bf16[32,64,64]{2,1,0:T(8,128)(2,1)}, u32[]{:S(2)}) copy-start(bf16[32,64,64]{2,1,0:T(8,128)(2,1)} %ltr.3) | copy-start | bytes 786436
  2.1 0.9 %copy-start.8 = (bf16[16,64,64]{2,1,0:T(8,128)(2,1)S(1)}, bf16[16,64,64]{2,1,0:T(8,128)(2,1)}, u32[]{:S(2)}) copy-start(bf16[16,64,64]{2,1,0:T(8,128)(2,1)} %ptr.3) | copy-start | bytes 393220
  3.1 0.9 %copy-start.10 = (bf16[32,16,64]{2,1,0:T(8,128)(2,1)S(1)}, bf16[32,16,64]{2,1,0:T(8,128)(2,1)}, u32[]{:S(2)}) copy-start(bf16[32,16,64]{2,1,0:T(8,128)(2,1)} %vec.3) | copy-start | bytes 196612
  4.0 0.7 %copy-start.15 = (s32[1,5,8]{2,0,1:T(1,128)S(1)}, s32[1,5,8]{2,0,1:T(1,128)}, u32[]{:S(2)}) copy-start(s32[1,5,8]{2,0,1:T(1,128)} %param.20) | copy-start | bytes 484
  4.6 0.7 %copy-start.18 = (s32[1,5,2]{1,2,0:T(2,128)S(1)}, s32[1,5,2]{1,2,0:T(2,128)}, u32[]{:S(2)}) copy-start(s32[1,5,2]{1,2,0:T(2,128)} %param.23) | copy-start | bytes 124
  5.3 37.5 %copy-start.16 = (s32[32,4]{0,1:T(4,128)S(1)}, s32[32,4]{0,1:T(4,128)}, u32[]{:S(2)}) copy-start(s32[32,4]{0,1:T(4,128)} %param.21) | copy-start | bytes 1540
  5.3 37.5 %copy-start.17 = (s32[16,4]{0,1:T(4,128)S(1)}, s32[16,4]{0,1:T(4,128)}, u32[]{:S(2)}) copy-start(s32[16,4]{0,1:T(4,128)} %param.24) | copy-start | bytes 772
  6.6 36.2 %collective-permute-start.2 = (bf16[5,16,128]{2,1,0:T(8,128)(2,1)S(1)}, bf16[5,16,128]{2,1,0:T(8,128)(2,1)S(1)}, u32[]{:S(2)}, u32[]{:S(2)}) collective-permute-start(bf16[5,16,128]{2,1,0:T(8,128)(2,1)S(1)} %get-tuple-element.18), channel_id=1, source_target_pairs={{0,2},{1,3},{2,4},{3,5},{4,6},{5,7},{6,8},{7,9},{8,10},{9,11},{10,... | collective-permute-start | bytes 61448 | tf_op jit(solution)/shard_map/ppermute | solution.py:326
  9.6 33.2 %collective-permute-start.3 = (bf16[5,16,128]{2,1,0:T(8,128)(2,1)S(1)}, bf16[5,16,128]{2,1,0:T(8,128)(2,1)S(1)}, u32[]{:S(2)}, u32[]{:S(2)}) collective-permute-start(bf16[5,16,128]{2,1,0:T(8,128)(2,1)S(1)} %get-tuple-element.19), channel_id=1, source_target_pairs={{0,14},{1,15},{2,0},{3,1},{4,2},{5,3},{6,4},{7,5},{8,6},{9,7},{10,... | collective-permute-start | bytes 61448 | tf_op jit(solution)/shard_map/ppermute | solution.py:326
  12.7 30.1 %collective-permute-start = (bf16[6,16,128]{2,1,0:T(8,128)(2,1)S(1)}, bf16[6,16,128]{2,1,0:T(8,128)(2,1)S(1)}, u32[]{:S(2)}, u32[]{:S(2)}) collective-permute-start(bf16[6,16,128]{2,1,0:T(8,128)(2,1)S(1)} %get-tuple-element.16), channel_id=1, source_target_pairs={{0,1},{1,0},{2,3},{3,2},{4,5},{5,4},{6,7},{7,6},{8,9},{9,8},{10,11... | collective-permute-start | bytes 73736 | tf_op jit(solution)/shard_map/ppermute | solution.py:326
  12.7 30.1 %collective-permute-start.1 = (bf16[6,16,128]{2,1,0:T(8,128)(2,1)S(1)}, bf16[6,16,128]{2,1,0:T(8,128)(2,1)S(1)}, u32[]{:S(2)}, u32[]{:S(2)}) collective-permute-start(bf16[6,16,128]{2,1,0:T(8,128)(2,1)S(1)} %get-tuple-element.17), channel_id=1, source_target_pairs={{0,15},{1,2},{2,1},{3,4},{4,3},{5,6},{6,5},{7,8},{8,7},{9,10},{10,... | collective-permute-start | bytes 73736 | tf_op jit(solution)/shard_map/ppermute | solution.py:326
  34.0 2.3 %copy-start = (bf16[3,32,3,64,64]{4,3,2,1,0:T(8,128)(2,1)S(1)}, bf16[3,32,3,64,64]{4,3,2,1,0:T(8,128)(2,1)}, u32[]{:S(2)}) copy-start(bf16[3,32,3,64,64]{4,3,2,1,0:T(8,128)(2,1)} %last.1) | copy-start | bytes 7077892
  36.3 0.9 %copy-start.11 = (bf16[32,16,64]{2,1,0:T(8,128)(2,1)S(1)}, bf16[32,16,64]{2,1,0:T(8,128)(2,1)}, u32[]{:S(2)}) copy-start(bf16[32,16,64]{2,1,0:T(8,128)(2,1)} %vec.3) | copy-start | bytes 196612
  37.2 0.7 %copy-start.12 = (s32[32,3]{0,1:T(4,128)S(1)}, s32[32,3]{0,1:T(4,128)}, u32[]{:S(2)}) copy-start(s32[32,3]{0,1:T(4,128)} %param.19) | copy-start | bytes 1156
  37.9 5.0 %copy-start.1 = (bf16[3,32,3,64,64]{4,3,2,1,0:T(8,128)(2,1)S(1)}, bf16[3,32,3,64,64]{4,3,2,1,0:T(8,128)(2,1)}, u32[]{:S(2)}) copy-start(bf16[3,32,3,64,64]{4,3,2,1,0:T(8,128)(2,1)} %last.1) | copy-start | bytes 7077892
  42.9 1.9 %copy-start.3 = (bf16[3,16,4,64,64]{4,3,2,1,0:T(8,128)(2,1)S(1)}, bf16[3,16,4,64,64]{4,3,2,1,0:T(8,128)(2,1)}, u32[]{:S(2)}) copy-start(bf16[3,16,4,64,64]{4,3,2,1,0:T(8,128)(2,1)} %pair.1) | copy-start | bytes 4718596
  44.8 9.6 %copy-start.2 = (bf16[3,8,8,64,64]{4,3,2,1,0:T(8,128)(2,1)S(1)}, bf16[3,8,8,64,64]{4,3,2,1,0:T(8,128)(2,1)}, u32[]{:S(2)}) copy-start(bf16[3,8,8,64,64]{4,3,2,1,0:T(8,128)(2,1)} %coupling.1) | copy-start | bytes 4718596
  44.8 9.6 %copy-start.5 = (bf16[32,64,64]{2,1,0:T(8,128)(2,1)S(1)}, bf16[32,64,64]{2,1,0:T(8,128)(2,1)}, u32[]{:S(2)}) copy-start(bf16[32,64,64]{2,1,0:T(8,128)(2,1)} %basis.3) | copy-start | bytes 786436
  44.8 9.6 %copy-start.7 = (bf16[32,64,64]{2,1,0:T(8,128)(2,1)S(1)}, bf16[32,64,64]{2,1,0:T(8,128)(2,1)}, u32[]{:S(2)}) copy-start(bf16[32,64,64]{2,1,0:T(8,128)(2,1)} %ltr.3) | copy-start | bytes 786436
  44.8 9.6 %copy-start.9 = (bf16[16,64,64]{2,1,0:T(8,128)(2,1)S(1)}, bf16[16,64,64]{2,1,0:T(8,128)(2,1)}, u32[]{:S(2)}) copy-start(bf16[16,64,64]{2,1,0:T(8,128)(2,1)} %ptr.3) | copy-start | bytes 393220
  44.8 9.6 %copy-start.14 = (s32[8,8]{1,0:T(8,128)S(1)}, s32[8,8]{1,0:T(8,128)}, u32[]{:S(2)}) copy-start(s32[8,8]{1,0:T(8,128)} %tlist.1) | copy-start | bytes 772

commit v2 on v0

v2 whole, which is shorter than its diff:
```python
import jax
import jax.numpy as jnp
from jax import lax
from jax.experimental import pallas as pl
from jax.experimental.pallas import tpu as pltpu
from jax.sharding import PartitionSpec as P

REACH = 2
WIN = 2 * REACH + 1
HW = 2
AXES = ("row", "col")
F32 = jnp.float32
BF = jnp.bfloat16
LIMIT = 56 * 1024 * 1024

VMEM = pltpu.VMEM
SMEM = pltpu.SMEM
DMA = pltpu.SemaphoreType.DMA
HERE = pl.BlockSpec(memory_space=pl.ANY)
SCALARS = pl.BlockSpec(memory_space=SMEM)
WHOLE = pl.BlockSpec(memory_space=VMEM)


def dot(left, right):
    return jnp.dot(left, right, preferred_element_type=F32)


def beside(*parts):
    return jnp.concatenate(parts, axis=1)


def above(*parts):
    return jnp.concatenate(parts, axis=0)


def turned(block):
    return block.astype(F32).T.astype(BF)


def row_of_blocks(ref, q):
    kernels, _, partners, _, _ = ref.shape
    return beside(*[above(*[ref[k, q, m] for k in range(kernels)]) for m in range(partners)])


def kernels_beside(tall, rank):
    return beside(*[tall[k * rank:(k + 1) * rank] for k in range(tall.shape[0] // rank)])


def copies(pairs, sems):
    made = [pltpu.make_async_copy(src, dst, sems.at[i]) for i, (src, dst) in enumerate(pairs)]
    for copy in made:
        copy.start()
    return made


def up_body(lsend, psend, vec_h, basis_h, ltr_h, ptr_h, tops, own, sib, cross, fwd, back,
            vec, basis, ltr, ptr, low, mid, sems):
    leaves, vecs, rank = vec.shape
    col = lax.axis_index("col")
    cap0 = lsend.shape[2]
    cap1 = psend.shape[1]
    made = copies([(vec_h, vec), (basis_h, basis), (ltr_h, ltr), (ptr_h, ptr)], sems)
    made[0].wait()
    made[1].wait()
    for t in range(leaves):
        low[t] = dot(vec[t], basis[t]).astype(BF)
    made[2].wait()
    for j in range(leaves // 2):
        mid[j] = dot(
            beside(low[2 * j], low[2 * j + 1]), ltr[2 * j:2 * j + 2].reshape(2 * rank, rank)
        ).astype(BF)
    made[3].wait()
    high = []
    for i in range(leaves // 4):
        high.append(
            dot(beside(mid[2 * i], mid[2 * i + 1]), ptr[2 * i:2 * i + 2].reshape(2 * rank, rank))
        )
    turned_tops = above(*high).T.astype(BF)
    for row in range(tops.shape[0]):
        tops[row] = turned_tops

    def pack(out, place):
        out[0:rank] = turned(above(*[low[lsend[place, 0, c]] for c in range(cap0)]))
        out[rank:rank + vecs] = beside(*[mid[psend[0, c, place]] for c in range(cap1)])

    def pack_halo(out, start):
        out[rank + vecs:] = beside(*[vec[start + h] for h in range(HW)])

    pack(sib, 1 + 2 * col)
    pack_halo(sib, (1 - col) * (leaves - HW))
    pack(cross, 3 - 2 * col)
    pack_halo(cross, col * (leaves - HW))
    pack(fwd, 0)
    pack(back, 4)
    pack(own, REACH)


def up_pass(lsend, psend, vec, basis, ltr, ptr, rows):
    leaves, vecs, rank = vec.shape
    wide = lsend.shape[2] * vecs
    shape = lambda *n: jax.ShapeDtypeStruct(n, BF)
    short, tall = shape(rank + vecs, wide), shape(rank + 2 * vecs, wide)
    return pl.pallas_call(
        up_body,
        out_shape=[shape(rows, rank, leaves // 4 * vecs), short, tall, tall, short, short],
        in_specs=[SCALARS] * 2 + [HERE] * 4,
        out_specs=[WHOLE] * 6,
        scratch_shapes=[
            VMEM(vec.shape, BF), VMEM(basis.shape, BF), VMEM(ltr.shape, BF), VMEM(ptr.shape, BF),
            VMEM((leaves, vecs, rank), BF), VMEM((leaves // 2, vecs, rank), BF), DMA((4,)),
        ],
        compiler_params=pltpu.CompilerParams(vmem_limit_bytes=LIMIT),
        cost_estimate=pl.CostEstimate(flops=10_000_000, bytes_accessed=3_000_000, transcendentals=0),
        name="up",
    )(lsend, psend, vec, basis, ltr, ptr)


def near_body(offsets, vec_h, blocks_h, out, vec, blocks, padded, sems, chunk_sems):
    leaves, vecs, rank = vec.shape
    kernels = blocks.shape[0]
    chunks = chunk_sems.shape[0]
    per = leaves // chunks

    def chunk(c):
        part = pl.ds(c * per, per)
        return pltpu.make_async_copy(blocks_h.at[:, part], blocks.at[:, part], chunk_sems.at[c])

    made = copies([(vec_h, vec)], sems)
    for c in range(chunks):
        chunk(c).start()
    made[0].wait()
    zero = jnp.zeros((HW, rank, vecs), BF)
    padded[0:HW] = zero
    padded[HW + leaves:] = zero
    group = 128 // vecs
    for g in range(leaves // group):
        wide = turned(above(*[vec[g * group + c] for c in range(group)]))
        for c in range(group):
            padded[HW + g * group + c] = wide[:, c * vecs:(c + 1) * vecs]

    def body(c, _):
        chunk(c).wait()
        for q in range(per):
            t = c * per + q
            rows = above(*[padded[t + HW + offsets[n, t]] for n in range(blocks.shape[2])])
            out[t] = kernels_beside(dot(row_of_blocks(blocks, t), rows), rank)
        return 0

    lax.fori_loop(0, chunks, body, 0)


def near_pass(offsets, vec, blocks, chunks):
    kernels, leaves, near, rank, _ = blocks.shape
    vecs = vec.shape[1]
    return pl.pallas_call(
        near_body,
        out_shape=jax.ShapeDtypeStruct((leaves, rank, kernels * vecs), F32),
        in_specs=[SCALARS, HERE, HERE],
        out_specs=WHOLE,
        scratch_shapes=[
            VMEM(vec.shape, BF), VMEM(blocks.shape, BF), VMEM((leaves + 2 * HW, rank, vecs), BF), DMA((1,)), DMA((chunks,)),
        ],
        compiler_params=pltpu.CompilerParams(vmem_limit_bytes=LIMIT),
        cost_estimate=pl.CostEstimate(flops=40_000_000, bytes_accessed=12_000_000, transcendentals=0),
        name="near",
    )(offsets, vec, blocks)


def far_body(llist, plist, offsets, own_h, sib_h, cross_h, fwd_h, back_h, leaf_h, pair_h, near_h, far0, far1, edge,
             own, sib, cross, fwd, back, leaf, pair, first, last, wleaf, wpair, halo, sems, leaf_sems, pair_sems):
    leaves = offsets.shape[1]
    _, rank, vecs = wleaf.shape
    cap0 = wleaf.shape[0] // WIN
    cap1 = wpair.shape[0] // WIN
    heads = first.shape[1]
    chunks = leaf_sems.shape[0]
    per = leaves // chunks
    col = lax.axis_index("col")
    place = lax.axis_index("row") * lax.axis_size("col") + col
    last_place = lax.axis_size("row") * lax.axis_size("col") - 1

    def leaf_chunk(c):
        part = pl.ds(c * per, per)
        return pltpu.make_async_copy(leaf_h.at[:, part], leaf.at[:, part], leaf_sems.at[c])

    def pair_chunk(c):
        part = pl.ds(c * (per // 2), per // 2)
        return pltpu.make_async_copy(pair_h.at[:, part], pair.at[:, part], pair_sems.at[c])

    made = copies(
        [
            (own_h, own), (sib_h, sib), (cross_h, cross), (fwd_h, fwd), (back_h, back),
            (near_h.at[:, pl.ds(0, heads)], first), (near_h.at[:, pl.ds(leaves - heads, heads)], last),
        ],
        sems,
    )
    for c in range(chunks):
        leaf_chunk(c).start()
        pair_chunk(c).start()
    for copy in made:
        copy.wait()

    def unpack(block, slot):
        for c in range(cap0):
            wleaf[slot * cap0 + c] = block[0:rank, c * vecs:(c + 1) * vecs]
        both = turned(block[rank:rank + vecs, :])
        for c in range(cap1):
            wpair[slot * cap1 + c] = both[c * rank:(c + 1) * rank]

    unpack(own, REACH)
    unpack(fwd, 0)
    unpack(back, 4)
    unpack(sib, 3 - 2 * col)
    unpack(cross, 1 + 2 * col)
    zero = jnp.zeros((rank, vecs), BF)
    for block, slot in ((sib, HW - HW * col), (cross, HW * col)):
        both = turned(block[rank + vecs:, :])
        outside = (place == 0) & (slot == 0) | (place == last_place) & (slot == HW)
        for h in range(HW):
            halo[slot + h] = jnp.where(outside, zero, both[h * rank:(h + 1) * rank])
    halo[2 * HW] = zero

    for q in range(heads):
        spots = [q + offsets[n, q] for n in range(first.shape[2])]
        rows = above(*[halo[jnp.where(at < 0, at + HW, 2 * HW)] for at in spots])
        edge[q] = kernels_beside(dot(row_of_blocks(first, q), rows), rank)
        t = leaves - heads + q
        spots = [t + offsets[n, t] for n in range(last.shape[2])]
        rows = above(*[halo[jnp.where(at >= leaves, at - leaves + HW, 2 * HW)] for at in spots])
        edge[heads + q] = kernels_beside(dot(row_of_blocks(last, q), rows), rank)

    def body(c, _):
        leaf_chunk(c).wait()
        pair_chunk(c).wait()
        for q in range(per):
            t = c * per + q
            rows = above(*[wleaf[llist[m, t]] for m in range(leaf.shape[2])])
            far0[t] = kernels_beside(dot(row_of_blocks(leaf, t), rows), rank)
        for q in range(per // 2):
            j = c * (per // 2) + q
            rows = above(*[wpair[plist[m, j]] for m in range(pair.shape[2])])
            far1[j] = kernels_beside(dot(row_of_blocks(pair, j), rows), rank)
        return 0

    lax.fori_loop(0, chunks, body, 0)


def far_pass(llist, plist, offsets, own, sib, cross, fwd, back, leaf, pair, near, chunks, cap0, cap1):
    kernels, leaves, partners, rank, _ = leaf.shape
    vecs = own.shape[0] - rank
    lanes = kernels * vecs
    ends = (kernels, HW) + near.shape[2:]
    return pl.pallas_call(
        far_body,
        out_shape=[
            jax.ShapeDtypeStruct((leaves, rank, lanes), F32),
            jax.ShapeDtypeStruct((leaves // 2, rank, lanes), F32),
            jax.ShapeDtypeStruct((2 * HW, rank, lanes), F32),
        ],
        in_specs=[SCALARS] * 3 + [HERE] * 8,
        out_specs=[WHOLE] * 3,
        scratch_shapes=[VMEM(x.shape, BF) for x in (own, sib, cross, fwd, back, leaf, pair)] + [
            VMEM(ends, BF), VMEM(ends, BF),
            VMEM((WIN * cap0, rank, vecs), BF), VMEM((WIN * cap1, rank, vecs), BF), VMEM((2 * HW + 1, rank, vecs), BF),
            DMA((7,)), DMA((chunks,)), DMA((chunks,)),
        ],
        compiler_params=pltpu.CompilerParams(vmem_limit_bytes=LIMIT),
        cost_estimate=pl.CostEstimate(flops=80_000_000, bytes_accessed=18_000_000, transcendentals=0),
        name="far",
    )(llist, plist, offsets, own, sib, cross, fwd, back, leaf, pair, near)


def down_body(tlist, mine_h, theirs_h, coupling_h, ptr_h, ltr_h, basis_h, far1_h, far0_h, near_h, edge_h, out,
              tops, coupling, ptr, ltr, basis, far1, far0, near, edge, sems, top_sems):
    kernels, count, partners, rank, _ = coupling.shape
    leaves = basis.shape[0]
    vecs = edge.shape[2] // kernels
    per_dev = tops.shape[3] // vecs
    col = lax.axis_index("col")
    made = copies([(mine_h, tops.at[:, col]), (theirs_h, tops.at[:, 1 - col])], sems)
    chunk = [
        pltpu.make_async_copy(coupling_h.at[:, pl.ds(i, 1)], coupling.at[:, pl.ds(i, 1)], top_sems.at[i])
        for i in range(count)
    ]
    for copy in chunk:
        copy.start()
    rest = copies(
        [
            (ptr_h, ptr), (far1_h, far1), (ltr_h, ltr), (far0_h, far0), (basis_h, basis), (near_h, near), (edge_h, edge),
        ],
        sems.at[pl.ds(2, 7)],
    )
    for copy in made:
        copy.wait()

    def partner(e):
        d = e // per_dev
        block = tops[d // 2, d % 2].astype(F32)
        shift = (per_dev - e % per_dev) % per_dev * vecs
        return pltpu.roll(block, shift, 1).astype(BF)

    down2 = []
    for i in range(count):
        chunk[i].wait()
        rows = above(*[partner(tlist[i, m]) for m in range(partners)])
        total = dot(row_of_blocks(coupling, i), rows)[:, :vecs]
        down2.append(kernels_beside(total, rank).astype(BF))
    rest[0].wait()
    rest[1].wait()
    down1 = []
    for i in range(count):
        both = dot(ptr[2 * i:2 * i + 2].reshape(2 * rank, rank), down2[i])
        for a in range(2):
            down1.append((far1[2 * i + a] + both[a * rank:(a + 1) * rank]).astype(BF))
    rest[2].wait()
    rest[3].wait()
    down0 = []
    for j in range(2 * count):
        both = dot(ltr[2 * j:2 * j + 2].reshape(2 * rank, rank), down1[j])
        for a in range(2):
            down0.append((far0[2 * j + a] + both[a * rank:(a + 1) * rank]).astype(BF))
    for copy in rest[4:]:
        copy.wait()
    for t in range(leaves):
        points = dot(basis[t], down0[t]) + near[t]
        if t < HW:
            points = points + edge[t]
        if t >= leaves - HW:
            points = points + edge[HW + t - (leaves - HW)]
        points = points.T.astype(BF)
        for k in range(kernels):
            out[k, t] = points[k * vecs:(k + 1) * vecs]


def down_pass(tlist, mine, theirs, coupling, ptr, ltr, basis, far1, far0, near, edge):
    kernels, count, partners, rank, _ = coupling.shape
    leaves = basis.shape[0]
    vecs = near.shape[2] // kernels
    rows, _, wide = mine.shape
    return pl.pallas_call(
        down_body,
        out_shape=jax.ShapeDtypeStruct((kernels, leaves, vecs, rank), BF),
        in_specs=[SCALARS] + [HERE] * 10,
        out_specs=WHOLE,
        scratch_shapes=[VMEM((rows, 2, rank, wide), BF)]
        + [VMEM(x.shape, x.dtype) for x in (coupling, ptr, ltr, basis, far1, far0, near, edge)]
        + [DMA((9,)), DMA((count,))],
        compiler_params=pltpu.CompilerParams(vmem_limit_bytes=LIMIT),
        cost_estimate=pl.CostEstimate(flops=40_000_000, bytes_accessed=8_000_000, transcendentals=0),
        name="down",
    )(tlist, mine, theirs, coupling, ptr, ltr, basis, far1, far0, near, edge)


def on_device(
    vectors,
    leaf_basis,
    leaf_transfer,
    pair_transfer,
    near_blocks,
    near_offset,
    leaf_send,
    leaf_list,
    leaf_coupling,
    pair_send,
    pair_list,
    pair_coupling,
    top_list,
    top_coupling,
):
    rows = lax.axis_size("row")
    devs = rows * lax.axis_size("col")
    cap0, cap1 = leaf_send.shape[2], pair_send.shape[2]
    lsend = jnp.transpose(leaf_send, (1, 0, 2))
    psend = jnp.transpose(pair_send, (0, 2, 1))
    offsets = near_offset.T
    llist = leaf_list.T
    plist = pair_list.T
    tops, own, sib, cross, fwd, back = up_pass(
        lsend, psend, vectors, leaf_basis, leaf_transfer, pair_transfer, rows
    )
    ring = range(devs)
    sibling = [(d, d ^ 1) for d in ring]
    sib = lax.ppermute(sib, AXES, sibling)
    cross = lax.ppermute(cross, AXES, [(d, (d + 1 if d % 2 else d - 1) % devs) for d in ring])
    fwd = lax.ppermute(fwd, AXES, [(d, (d + 2) % devs) for d in ring])
    back = lax.ppermute(back, AXES, [(d, (d - 2) % devs) for d in ring])
    mine = lax.all_to_all(tops, "row", split_axis=0, concat_axis=0)
    theirs = lax.ppermute(mine, AXES, sibling)
    near = near_pass(offsets, vectors, near_blocks, 8)
    far0, far1, edge = far_pass(
        llist, plist, offsets, own, sib, cross, fwd, back, leaf_coupling, pair_coupling, near_blocks, 8, cap0, cap1
    )
    return down_pass(
        top_list, mine, theirs, top_coupling, pair_transfer, leaf_transfer, leaf_basis, far1, far0, near, edge
    )


def solution(mesh):
    placed = P(("groups", "row", "col"))
    behind = P(None, ("groups", "row", "col"))
    return jax.shard_map(
        on_device,
        mesh=mesh,
        in_specs=(
            placed, placed, placed, placed, behind, placed, placed, placed, behind, placed, placed, behind, placed, behind,
        ),
        out_specs=behind,
        check_vma=False,
    )
```

time: 99.1 us -> 50.3 us (0.51)
  Pallas kernels: 0 us -> 27.9 us
  matrix products: 26.6 us -> 0 us
  local copies, waits for them, and re-layouts: 19 us -> 1.26 us
  blocking collectives: 26.2 us -> 14.6 us
  other arithmetic: 9.01 us -> 0 us
  waiting for transfers between devices: 7.18 us -> 0.01 us
  starting transfers between devices: 9.8 us -> 5.93 us
    pallas_call x0 -> x4, Pallas kernels: none -> 27.9 us  [the longest x1 9.98 us: far_pass(): pl.pallas_call(far_body, out_shape=[jax.ShapeDtypeStruct((leaves, rank, l...]
    dot_general x9 -> x0, matrix products: 26.6 us -> none  [the longest x1 6.27 us: on_device(): jnp.einsum('ktmrs,tmvs->ktvr', leaf_coupling, leaf_rows, preferred_elemen...]
    all_gather x1 -> x0, blocking collectives: 26.2 us -> none  [on_device(): piece = lax.all_gather(up2, ('row', 'col'), axis=0, tiled=True)]
    all_to_all x0 -> x1, blocking collectives: none -> 14.6 us  [on_device(): mine = lax.all_to_all(tops, 'row', split_axis=0, concat_axis=0)]
    ppermute x10 -> x5, waiting for transfers between devices: 7.18 us -> 0.01 us  [the longest x1 0.01 us: on_device(): fwd = lax.ppermute(fwd, AXES, [(d, (d + 2) % devs) for d in ring])]
    gather x6 -> x0, local copies, waits for them, and re-layouts: 7.08 us -> none  [the longest x1 2.37 us: on_device(): taken = jnp.take(piece, jnp.clip(top_list, 0, count - 1), axis=0)]
    ppermute x10 -> x5, starting transfers between devices: 9.8 us -> 5.93 us  [the longest x1 3.78 us: on_device(): back = lax.ppermute(back, AXES, [(d, (d - 2) % devs) for d in ring])]
    slice x7 -> x0, local copies, waits for them, and re-layouts: 3.7 us -> none  [the longest x2 1.55 us: on_device(): carry_leaf = carry_leaf[1:]]
  transfers between devices with their start and end apart: 10 -> 5, of which waited for: 2 -> 0; matrix products, arithmetic and copies ran while one was open for 35% -> 0% of each run, Pallas kernels for 0% -> 35%
where the time goes in v2:
time: 50.3 us; the launch traced here: 49.9 us
  Pallas kernels  27.9 us (55%)
  blocking collectives  14.6 us (29%)
  starting transfers between devices  5.93 us (12%)
  local copies, waits for them, and re-layouts  1.26 us (3%)
    all_to_all x1, blocking collectives, on_device(): mine = lax.all_to_all(tops, 'row', split_axis=0, concat_axis=0)  14.6 us
    pallas_call x1, Pallas kernels, far_pass(): pl.pallas_call(far_body, out_shape=[jax.ShapeDtypeStruct((leaves, rank, l...  9.98 us
    pallas_call x1, Pallas kernels, near_pass(): pl.pallas_call(near_body, out_shape=jax.ShapeDtypeStruct((leaves, rank, k...  7.34 us
    pallas_call x1, Pallas kernels, down_pass(): pl.pallas_call(down_body, out_shape=jax.ShapeDtypeStruct((kernels, leaves...  7.2 us
    ppermute x1, starting transfers between devices, on_device(): back = lax.ppermute(back, AXES, [(d, (d - 2) % devs) for d in ring])  3.78 us
    pallas_call x1, Pallas kernels, up_pass(): pl.pallas_call(up_body, out_shape=[shape(rows, rank, leaves // 4 * vecs),...  3.4 us
    unnamed x12, local copies, waits for them, and re-layouts  1.26 us
  transfers between devices with their start and end apart: 5, of which 0 were waited for; matrix products, arithmetic and copies ran while one was open for 0% of the time, Pallas kernels for 35%

profile of v2, /device:TPU:0, one launch (start us, length us, event | category | flops | bytes accessed | tf_op | source)
XLA Modules:
  0.0 49.9 jit_solution(4525782627654318311)
XLA Ops:
  0.0 3.4 %up.1 = (bf16[8,64,128]{2,1,0:T(8,128)(2,1)}, bf16[80,128]{1,0:T(8,128)(2,1)}, bf16[96,128]{1,0:T(8,128)(2,1)}, bf16[96,128]{1,0:T(8,128)(2,1)}, bf16[80,128]{1,0:T(8,128)(2,1)}, /*index=5*/bf16[80,128]{1,0:T(8,128)(2,1)}) custom-call(s32[5,1,8]{2,1,0:T(1,128)} %bitcast.7, s32[1,2,5]{2,1,0:T(2,128)} %bitcast.10, bf16[32,16,64]{2,1,0:T(8,128)(2,1)} %vec_h.3, ...), custom_call_target="tpu_custom_call" | custom-call | flops 10000000 | bytes 3000000 | tf_op jit(solution)/shard_map/up/pallas_call | solution.py:103
  3.4 14.6 %all_to_all.5.mine_h = bf16[8,64,128]{2,1,0:T(8,128)(2,1)S(1)} all-to-all(bf16[8,64,128]{2,1,0:T(8,128)(2,1)} %get-tuple-element.14), channel_id=1, replica_groups=mesh['groups'=2,'row'=8,'col'=2] {'row'}, dimensions={0} | all-to-all | bytes 262144 | tf_op jit(solution)/shard_map/all_to_all | solution.py:387
  18.0 0.0 copy-start
  18.0 0.0 collective-permute-start
  18.0 0.5 %collective-permute-start.1 = (bf16[96,128]{1,0:T(8,128)(2,1)}, bf16[96,128]{1,0:T(8,128)(2,1)S(1)}, u32[]{:S(2)}, u32[]{:S(2)}) collective-permute-start(bf16[96,128]{1,0:T(8,128)(2,1)} %get-tuple-element.16), channel_id=1, source_target_pairs={{0,1},{1,0},{2,3},{3,2},{4,5},{5,4},{6,7},{7,6},{8,9},{9,8},{10,11... | collective-permute-start | bytes 73736 | tf_op jit(solution)/shard_map/ppermute | solution.py:383
  18.6 0.7 %collective-permute-start.2 = (bf16[96,128]{1,0:T(8,128)(2,1)}, bf16[96,128]{1,0:T(8,128)(2,1)S(1)}, u32[]{:S(2)}, u32[]{:S(2)}) collective-permute-start(bf16[96,128]{1,0:T(8,128)(2,1)} %get-tuple-element.17), channel_id=1, source_target_pairs={{0,15},{1,2},{2,1},{3,4},{4,3},{5,6},{6,5},{7,8},{8,7},{9,10},{10,... | collective-permute-start | bytes 73736 | tf_op jit(solution)/shard_map/ppermute | solution.py:384
  19.3 0.9 %collective-permute-start.3 = (bf16[80,128]{1,0:T(8,128)(2,1)}, bf16[80,128]{1,0:T(8,128)(2,1)S(1)}, u32[]{:S(2)}, u32[]{:S(2)}) collective-permute-start(bf16[80,128]{1,0:T(8,128)(2,1)} %get-tuple-element.18), channel_id=1, source_target_pairs={{0,2},{1,3},{2,4},{3,5},{4,6},{5,7},{6,8},{7,9},{8,10},{9,11},{10,... | collective-permute-start | bytes 61448 | tf_op jit(solution)/shard_map/ppermute | solution.py:385
  20.2 3.8 %collective-permute-start.4 = (bf16[80,128]{1,0:T(8,128)(2,1)}, bf16[80,128]{1,0:T(8,128)(2,1)S(1)}, u32[]{:S(2)}, u32[]{:S(2)}) collective-permute-start(bf16[80,128]{1,0:T(8,128)(2,1)} %get-tuple-element.19), channel_id=1, source_target_pairs={{0,14},{1,15},{2,0},{3,1},{4,2},{5,3},{6,4},{7,5},{8,6},{9,7},{10,... | collective-permute-start | bytes 61448 | tf_op jit(solution)/shard_map/ppermute | solution.py:386
  24.0 7.3 %near.1.near_h = f32[32,64,48]{2,1,0:T(8,128)} custom-call(s32[3,32]{1,0:T(4,128)} %bitcast.5, bf16[32,16,64]{2,1,0:T(8,128)(2,1)} %vec_h.3, bf16[3,32,3,64,64]{4,3,2,1,0:T(8,128)(2,1)} %blocks_h.1), custom_call_target="tpu_custom_call" | custom-call | flops 40000000 | bytes 12000000 | tf_op jit(solution)/shard_map/near/pallas_call | solution.py:155
  31.3 0.0 collective-permute-done.3.fwd_h
  31.3 0.0 copy-start.4
  31.3 0.0 collective-permute-done.4.back_h
  31.4 0.0 copy-start.5
  31.4 0.0 collective-permute-done.1.sib_h
  31.4 0.0 copy-start.2
  31.4 0.0 collective-permute-done.2.cross_h
  31.4 0.0 copy-start.3
  31.4 0.5 %copy-done.4 = bf16[80,128]{1,0:T(8,128)(2,1)} copy-done((bf16[80,128]{1,0:T(8,128)(2,1)}, bf16[80,128]{1,0:T(8,128)(2,1)S(1)}, u32[]{:S(2)}) %copy-start.4) | copy-done | bytes 20504
  31.9 0.0 copy-done.5
  32.0 0.0 copy-done.2
  32.0 0.0 copy-done.3
  32.0 10.0 %far.1 = (f32[32,64,48]{2,1,0:T(8,128)}, f32[16,64,48]{2,1,0:T(8,128)}, f32[4,64,48]{2,1,0:T(8,128)}) custom-call(s32[4,32]{1,0:T(4,128)} %bitcast.8, s32[4,16]{1,0:T(4,128)} %bitcast.9, s32[3,32]{1,0:T(4,128)} %bitcast.6, bf16[80,128]{1,0:T(8,128)(2,1)} %get-tuple-element.15.own_h, bf16[96,128]{1,0:T(8,128)(2,1)} %copy-done.2, bf16[96,128]{1,0:T(8,128)(2,1)} %copy-done.3, ...), custom_call_target="tpu_custom_call" | custom-call | flops 80000000 | bytes 18000000 | tf_op jit(solution)/shard_map/far/pallas_call | solution.py:253
  42.0 0.0 copy-done
  42.0 0.0 collective-permute-done.theirs_h
  42.0 0.0 copy-start.1
  42.0 0.7 %copy-done.1 = bf16[8,64,128]{2,1,0:T(8,128)(2,1)} copy-done((bf16[8,64,128]{2,1,0:T(8,128)(2,1)}, bf16[8,64,128]{2,1,0:T(8,128)(2,1)S(1)}, u32[]{:S(2)}) %copy-start.1) | copy-done | bytes 131096
  42.7 7.2 %down.1 = bf16[3,32,16,64]{3,2,1,0:T(8,128)(2,1)} custom-call(s32[8,8]{1,0:T(8,128)} %tlist.1, bf16[8,64,128]{2,1,0:T(8,128)(2,1)} %copy-done, bf16[8,64,128]{2,1,0:T(8,128)(2,1)} %copy-done.1, bf16[3,8,8,64,64]{4,3,2,1,0:T(8,128)(2,1)} %coupling_h.1, bf16[16,64,64]{2,1,0:T(8,128)(2,1)} %ptr_h.3, bf16[32,64,64]{2,1,0:T(8,128)(2,1)} %ltr_h.3, ...), custom_call_target="tpu_custom_call" | custom-call | flops 40000000 | bytes 8000000 | tf_op jit(solution)/shard_map/down/pallas_call | solution.py:340
Async XLA Ops:
  18.0 23.9 %copy-start = (bf16[8,64,128]{2,1,0:T(8,128)(2,1)}, bf16[8,64,128]{2,1,0:T(8,128)(2,1)S(1)}, u32[]{:S(2)}) copy-start(bf16[8,64,128]{2,1,0:T(8,128)(2,1)S(1)} %all_to_all.5.mine_h) | copy-start | bytes 393220
  18.0 24.0 %collective-permute-start = (bf16[8,64,128]{2,1,0:T(8,128)(2,1)S(1)}, bf16[8,64,128]{2,1,0:T(8,128)(2,1)S(1)}, u32[]{:S(2)}, u32[]{:S(2)}) collective-permute-start(bf16[8,64,128]{2,1,0:T(8,128)(2,1)S(1)} %all_to_all.5.mine_h), channel_id=1, source_target_pairs={{0,1},{1,0},{2,3},{3,2},{4,5},{5,4},{6,7},{7,6},{8,9},{9,8},{10,11... | collective-permute-start | bytes 393224 | tf_op jit(solution)/shard_map/ppermute | solution.py:388
  18.0 13.3 %collective-permute-start.1 = (bf16[96,128]{1,0:T(8,128)(2,1)}, bf16[96,128]{1,0:T(8,128)(2,1)S(1)}, u32[]{:S(2)}, u32[]{:S(2)}) collective-permute-start(bf16[96,128]{1,0:T(8,128)(2,1)} %get-tuple-element.16), channel_id=1, source_target_pairs={{0,1},{1,0},{2,3},{3,2},{4,5},{5,4},{6,7},{7,6},{8,9},{9,8},{10,11... | collective-permute-start | bytes 73736 | tf_op jit(solution)/shard_map/ppermute | solution.py:383
  18.6 12.8 %collective-permute-start.2 = (bf16[96,128]{1,0:T(8,128)(2,1)}, bf16[96,128]{1,0:T(8,128)(2,1)S(1)}, u32[]{:S(2)}, u32[]{:S(2)}) collective-permute-start(bf16[96,128]{1,0:T(8,128)(2,1)} %get-tuple-element.17), channel_id=1, source_target_pairs={{0,15},{1,2},{2,1},{3,4},{4,3},{5,6},{6,5},{7,8},{8,7},{9,10},{10,... | collective-permute-start | bytes 73736 | tf_op jit(solution)/shard_map/ppermute | solution.py:384
  19.3 12.1 %collective-permute-start.3 = (bf16[80,128]{1,0:T(8,128)(2,1)}, bf16[80,128]{1,0:T(8,128)(2,1)S(1)}, u32[]{:S(2)}, u32[]{:S(2)}) collective-permute-start(bf16[80,128]{1,0:T(8,128)(2,1)} %get-tuple-element.18), channel_id=1, source_target_pairs={{0,2},{1,3},{2,4},{3,5},{4,6},{5,7},{6,8},{7,9},{8,10},{9,11},{10,... | collective-permute-start | bytes 61448 | tf_op jit(solution)/shard_map/ppermute | solution.py:385
  20.2 11.2 %collective-permute-start.4 = (bf16[80,128]{1,0:T(8,128)(2,1)}, bf16[80,128]{1,0:T(8,128)(2,1)S(1)}, u32[]{:S(2)}, u32[]{:S(2)}) collective-permute-start(bf16[80,128]{1,0:T(8,128)(2,1)} %get-tuple-element.19), channel_id=1, source_target_pairs={{0,14},{1,15},{2,0},{3,1},{4,2},{5,3},{6,4},{7,5},{8,6},{9,7},{10,... | collective-permute-start | bytes 61448 | tf_op jit(solution)/shard_map/ppermute | solution.py:386
  31.3 0.6 %copy-start.4 = (bf16[80,128]{1,0:T(8,128)(2,1)}, bf16[80,128]{1,0:T(8,128)(2,1)S(1)}, u32[]{:S(2)}) copy-start(bf16[80,128]{1,0:T(8,128)(2,1)S(1)} %collective-permute-done.3.fwd_h) | copy-start | bytes 61444
  31.4 0.6 %copy-start.5 = (bf16[80,128]{1,0:T(8,128)(2,1)}, bf16[80,128]{1,0:T(8,128)(2,1)S(1)}, u32[]{:S(2)}) copy-start(bf16[80,128]{1,0:T(8,128)(2,1)S(1)} %collective-permute-done.4.back_h) | copy-start | bytes 61444
  31.4 0.6 %copy-start.2 = (bf16[96,128]{1,0:T(8,128)(2,1)}, bf16[96,128]{1,0:T(8,128)(2,1)S(1)}, u32[]{:S(2)}) copy-start(bf16[96,128]{1,0:T(8,128)(2,1)S(1)} %collective-permute-done.1.sib_h) | copy-start | bytes 73732
  31.4 0.6 %copy-start.3 = (bf16[96,128]{1,0:T(8,128)(2,1)}, bf16[96,128]{1,0:T(8,128)(2,1)S(1)}, u32[]{:S(2)}) copy-start(bf16[96,128]{1,0:T(8,128)(2,1)S(1)} %collective-permute-done.2.cross_h) | copy-start | bytes 73732
  42.0 0.7 %copy-start.1 = (bf16[8,64,128]{2,1,0:T(8,128)(2,1)}, bf16[8,64,128]{2,1,0:T(8,128)(2,1)S(1)}, u32[]{:S(2)}) copy-start(bf16[8,64,128]{2,1,0:T(8,128)(2,1)S(1)} %collective-permute-done.theirs_h) | copy-start | bytes 393220

commit v3 on v2

v3 whole, which is shorter than its diff:
```python
import functools

import jax
import jax.numpy as jnp
from jax import lax
from jax.experimental import pallas as pl
from jax.experimental.pallas import tpu as pltpu
from jax.sharding import PartitionSpec as P

REACH = 2
WIN = 2 * REACH + 1
HW = 2
AXES = ("row", "col")
F32 = jnp.float32
BF = jnp.bfloat16
LIMIT = 56 * 1024 * 1024

VMEM = pltpu.VMEM
SMEM = pltpu.SMEM
DMA = pltpu.SemaphoreType.DMA
HERE = pl.BlockSpec(memory_space=pl.ANY)
SCALARS = pl.BlockSpec(memory_space=SMEM)
WHOLE = pl.BlockSpec(memory_space=VMEM)


def dot(left, right):
    return jnp.dot(left, right, preferred_element_type=F32)


def beside(*parts):
    return jnp.concatenate(parts, axis=1)


def above(*parts):
    return jnp.concatenate(parts, axis=0)


def dot_t(left, right):
    return lax.dot_general(left, right, (((1,), (1,)), ((), ())), preferred_element_type=F32)


def row_of_blocks(ref, q):
    kernels, _, partners, _, _ = ref.shape
    return beside(*[above(*[ref[k, q, m] for k in range(kernels)]) for m in range(partners)])


def by_kernel(wide, rank):
    return above(*[wide[:, k * rank:(k + 1) * rank] for k in range(wide.shape[1] // rank)])


def copies(pairs, sems):
    made = [pltpu.make_async_copy(src, dst, sems.at[i]) for i, (src, dst) in enumerate(pairs)]
    for copy in made:
        copy.start()
    return made


def chunk_of(src, dst, sems, size):
    def chunk(c):
        part = pl.ds(c * size, size)
        return pltpu.make_async_copy(src.at[:, part], dst.at[:, part], sems.at[c])

    return chunk


def split(row, ref, at):
    rank = row.shape[1] // 2
    ref[at] = row[:, :rank]
    ref[at + 1] = row[:, rank:]


def call(body, name, scalars, arrays, out_shape, out_specs, scratch, cost):
    return pl.pallas_call(
        body,
        out_shape=out_shape,
        in_specs=[SCALARS] * len(scalars) + [HERE] * len(arrays),
        out_specs=out_specs,
        scratch_shapes=scratch,
        compiler_params=pltpu.CompilerParams(vmem_limit_bytes=LIMIT),
        cost_estimate=pl.CostEstimate(flops=cost[0], bytes_accessed=cost[1], transcendentals=0),
        name=name,
    )(*scalars, *arrays)


def like(x):
    return VMEM(x.shape, x.dtype)


def joined_shape(piece):
    return jax.ShapeDtypeStruct((2 * piece.shape[0],) + piece.shape[1:], piece.dtype)


def join(first_h, second_h, out_h, sems):
    count = first_h.shape[0]
    return copies([(first_h, out_h.at[pl.ds(0, count)]), (second_h, out_h.at[pl.ds(count, count)])], sems)


def up_body(lsend, psend, vec_h, basis_h, ltr_h, ptr_h, tops, own, sib, cross, fwd, back,
            vec, basis, ltr, ptr, low, mid, sems):
    leaves, vecs, rank = vec.shape
    col = lax.axis_index("col")
    cap0 = lsend.shape[2]
    cap1 = psend.shape[1]
    made = copies([(vec_h, vec), (basis_h, basis), (ltr_h, ltr), (ptr_h, ptr)], sems)
    made[0].wait()
    made[1].wait()
    for t in range(leaves):
        low[t] = dot(vec[t], basis[t]).astype(BF)
    made[2].wait()
    for j in range(leaves // 2):
        mid[j] = dot(
            beside(low[2 * j], low[2 * j + 1]), ltr[2 * j:2 * j + 2].reshape(2 * rank, rank)
        ).astype(BF)
    made[3].wait()
    high = []
    for i in range(leaves // 4):
        high.append(
            dot(beside(mid[2 * i], mid[2 * i + 1]), ptr[2 * i:2 * i + 2].reshape(2 * rank, rank)).astype(BF)
        )
    for i in range(leaves // 8):
        tops[0, i] = beside(high[2 * i], high[2 * i + 1])

    def pack(out, place):
        for c in range(cap0 // 2):
            out[c] = beside(low[lsend[place, 0, 2 * c]], low[lsend[place, 0, 2 * c + 1]])
        for c in range(cap1 // 2):
            out[cap0 // 2 + c] = beside(mid[psend[0, 2 * c, place]], mid[psend[0, 2 * c + 1, place]])

    def pack_halo(out, start):
        out[(cap0 + cap1) // 2] = beside(vec[start], vec[start + 1])

    pack(sib, 1 + 2 * col)
    pack_halo(sib, (1 - col) * (leaves - HW))
    pack(cross, 3 - 2 * col)
    pack_halo(cross, col * (leaves - HW))
    pack(fwd, 0)
    pack(back, 4)
    pack(own, REACH)


def up_pass(lsend, psend, vec, basis, ltr, ptr):
    leaves, vecs, rank = vec.shape
    count = (lsend.shape[2] + psend.shape[1]) // 2
    shape = lambda *n: jax.ShapeDtypeStruct(n + (vecs, 2 * rank), BF)
    return call(
        up_body, "up", (lsend, psend), (vec, basis, ltr, ptr),
        [shape(1, leaves // 8), shape(count), shape(count + 1), shape(count + 1), shape(count), shape(count)],
        [WHOLE] * 6,
        [
            like(vec), like(basis), like(ltr), like(ptr),
            VMEM((leaves, vecs, rank), BF), VMEM((leaves // 2, vecs, rank), BF), DMA((4,)),
        ],
        (10_000_000, 3_000_000),
    )


def near_body(start, offsets, vec_h, blocks_h, held_h, got_h, out, both_h, vec, blocks, padded, sems, chunk_sems, join_sems):
    leaves, vecs, rank = vec.shape
    half = blocks.shape[1]
    chunks = chunk_sems.shape[0]
    per = half // chunks
    chunk = chunk_of(blocks_h.at[:, pl.ds(start, half)], blocks, chunk_sems, per)
    joining = join(held_h, got_h, both_h, join_sems)
    made = copies([(vec_h, padded.at[pl.ds(HW, leaves)])], sems)
    for c in range(chunks):
        chunk(c).start()
    zero = jnp.zeros((HW, vecs, rank), BF)
    padded[0:HW] = zero
    padded[HW + leaves:] = zero
    made[0].wait()

    def body(c, _):
        chunk(c).wait()
        for q in range(per):
            t = c * per + q
            rows = beside(*[padded[start + t + HW + offsets[n, start + t]] for n in range(blocks.shape[2])])
            out[t] = by_kernel(dot_t(rows, row_of_blocks(blocks, t)), rank)
        return 0

    lax.fori_loop(0, chunks, body, 0)
    for copy in joining:
        copy.wait()


def near_pass(offsets, vec, blocks, held, got, half, chunks):
    kernels, leaves, near, rank, _ = blocks.shape
    vecs = vec.shape[1]
    count = leaves // 2
    return call(
        functools.partial(near_body, half * count), "near%d" % half, (offsets,), (vec, blocks, held, got),
        [jax.ShapeDtypeStruct((count, kernels * vecs, rank), F32), joined_shape(held)],
        [WHOLE, HERE],
        [
            like(vec), VMEM((kernels, count) + blocks.shape[2:], BF), VMEM((leaves + 2 * HW, vecs, rank), BF),
            DMA((1,)), DMA((chunks,)), DMA((2,)),
        ],
        (20_000_000, 6_000_000),
    )


def leaf_body(llist, own_h, sib_h, cross_h, fwd_h, back_h, leaf_h, held_h, got_h, far0, both_h,
              own, sib, cross, fwd, back, leaf, window, sems, chunk_sems, join_sems):
    _, vecs, rank = window.shape
    cap0 = window.shape[0] // WIN
    chunks = chunk_sems.shape[0]
    per = leaf.shape[1] // chunks
    col = lax.axis_index("col")
    joining = join(held_h, got_h, both_h, join_sems)
    made = copies([(own_h, own), (sib_h, sib), (cross_h, cross), (fwd_h, fwd), (back_h, back)], sems)
    chunk = chunk_of(leaf_h, leaf, chunk_sems, per)
    for c in range(chunks):
        chunk(c).start()
    for copy in made:
        copy.wait()
    for block, slot in ((own, REACH), (fwd, 0), (back, 4), (sib, 3 - 2 * col), (cross, 1 + 2 * col)):
        for c in range(cap0 // 2):
            split(block[c], window, slot * cap0 + 2 * c)

    def body(c, _):
        chunk(c).wait()
        for q in range(per):
            t = c * per + q
            rows = beside(*[window[llist[m, t]] for m in range(leaf.shape[2])])
            far0[t] = by_kernel(dot_t(rows, row_of_blocks(leaf, t)), rank)
        return 0

    lax.fori_loop(0, chunks, body, 0)
    for copy in joining:
        copy.wait()


def leaf_pass(llist, own, sib, cross, fwd, back, leaf, held, got, chunks, cap0):
    kernels, leaves, partners, rank, _ = leaf.shape
    vecs = own.shape[1]
    return call(
        leaf_body, "leaf", (llist,), (own, sib, cross, fwd, back, leaf, held, got),
        [jax.ShapeDtypeStruct((leaves, kernels * vecs, rank), F32), joined_shape(held)],
        [WHOLE, HERE],
        [like(x) for x in (own, sib, cross, fwd, back, leaf)]
        + [VMEM((WIN * cap0, vecs, rank), BF), DMA((5,)), DMA((chunks,)), DMA((2,))],
        (50_000_000, 9_000_000),
    )


def pair_body(plist, offsets, own_h, sib_h, cross_h, fwd_h, back_h, pair_h, near_h, far1, edge,
              own, sib, cross, fwd, back, pair, first, last, window, halo, sems, chunk_sems):
    leaves = offsets.shape[1]
    _, vecs, rank = window.shape
    cap1 = window.shape[0] // WIN
    base = own.shape[0] - cap1 // 2
    heads = first.shape[1]
    chunks = chunk_sems.shape[0]
    per = pair.shape[1] // chunks
    col = lax.axis_index("col")
    place = lax.axis_index("row") * lax.axis_size("col") + col
    last_place = lax.axis_size("row") * lax.axis_size("col") - 1
    made = copies(
        [
            (own_h, own), (sib_h, sib), (cross_h, cross), (fwd_h, fwd), (back_h, back),
            (near_h.at[:, pl.ds(0, heads)], first), (near_h.at[:, pl.ds(leaves - heads, heads)], last),
        ],
        sems,
    )
    chunk = chunk_of(pair_h, pair, chunk_sems, per)
    for c in range(chunks):
        chunk(c).start()
    for copy in made:
        copy.wait()
    for block, slot in ((own, REACH), (fwd, 0), (back, 4), (sib, 3 - 2 * col), (cross, 1 + 2 * col)):
        for c in range(cap1 // 2):
            split(block[base + c], window, slot * cap1 + 2 * c)
    zero = jnp.zeros((vecs, rank), BF)
    for block, slot in ((sib, HW - HW * col), (cross, HW * col)):
        row = block[base + cap1 // 2]
        outside = (place == 0) & (slot == 0) | (place == last_place) & (slot == HW)
        split(jnp.where(outside, jnp.zeros_like(row), row), halo, slot)
    halo[2 * HW] = zero

    for q in range(heads):
        spots = [q + offsets[n, q] for n in range(first.shape[2])]
        rows = beside(*[halo[jnp.where(at < 0, at + HW, 2 * HW)] for at in spots])
        edge[q] = by_kernel(dot_t(rows, row_of_blocks(first, q)), rank)
        t = leaves - heads + q
        spots = [t + offsets[n, t] for n in range(last.shape[2])]
        rows = beside(*[halo[jnp.where(at >= leaves, at - leaves + HW, 2 * HW)] for at in spots])
        edge[heads + q] = by_kernel(dot_t(rows, row_of_blocks(last, q)), rank)

    def body(c, _):
        chunk(c).wait()
        for q in range(per):
            j = c * per + q
            rows = beside(*[window[plist[m, j]] for m in range(pair.shape[2])])
            far1[j] = by_kernel(dot_t(rows, row_of_blocks(pair, j)), rank)
        return 0

    lax.fori_loop(0, chunks, body, 0)


def pair_pass(plist, offsets, own, sib, cross, fwd, back, pair, near, chunks, cap1):
    kernels, pairs, partners, rank, _ = pair.shape
    vecs = own.shape[1]
    ends = (kernels, HW) + near.shape[2:]
    return call(
        pair_body, "pair", (plist, offsets), (own, sib, cross, fwd, back, pair, near),
        [
            jax.ShapeDtypeStruct((pairs, kernels * vecs, rank), F32),
            jax.ShapeDtypeStruct((2 * HW, kernels * vecs, rank), F32),
        ],
        [WHOLE] * 2,
        [like(x) for x in (own, sib, cross, fwd, back, pair)] + [
            VMEM(ends, BF), VMEM(ends, BF),
            VMEM((WIN * cap1, vecs, rank), BF), VMEM((2 * HW + 1, vecs, rank), BF), DMA((7,)), DMA((chunks,)),
        ],
        (30_000_000, 5_000_000),
    )


def down_body(offs, tlist, mine_h, theirs_h, coupling_h, ptr_h, ltr_h, basis_h, far1_h, far0_h, near0_h, near1_h, edge_h, out,
              mine, theirs, coupling, ptr, ltr, basis, far1, far0, near, edge, tops, sems, top_sems):
    kernels, count, partners, rank, _ = coupling.shape
    leaves, vecs, _ = near.shape
    vecs //= kernels
    half = leaves // 2
    col = lax.axis_index("col")
    row = lax.axis_index("row")
    made = copies([(mine_h, mine), (theirs_h, theirs)], sems)
    chunk = chunk_of(coupling_h, coupling, top_sems, 1)
    for i in range(count):
        chunk(i).start()
    rest = copies(
        [
            (ptr_h, ptr), (far1_h, far1), (ltr_h, ltr), (far0_h, far0), (basis_h, basis),
            (near0_h, near.at[pl.ds(0, half)]), (near1_h, near.at[pl.ds(half, half)]), (edge_h, edge),
        ],
        sems.at[pl.ds(2, 8)],
    )
    for copy in made:
        copy.wait()
    for block, side in ((mine, col), (theirs, 1 - col)):
        for s, off in enumerate(offs):
            device = (row ^ off) * 2 + side
            for i in range(block.shape[1]):
                split(block[s, i], tops, device * count + 2 * i)

    down2 = []
    for i in range(count):
        chunk(i).wait()
        rows = beside(*[tops[tlist[i, m]] for m in range(partners)])
        down2.append(by_kernel(dot_t(rows, row_of_blocks(coupling, i)), rank).astype(BF))
    rest[0].wait()
    rest[1].wait()
    down1 = []
    for j in range(2 * count):
        down1.append((far1[j] + dot_t(down2[j // 2], ptr[j])).astype(BF))
    rest[2].wait()
    rest[3].wait()
    down0 = []
    for t in range(leaves):
        down0.append((far0[t] + dot_t(down1[t // 2], ltr[t])).astype(BF))
    for copy in rest[4:]:
        copy.wait()
    for t in range(leaves):
        points = dot_t(down0[t], basis[t]) + near[t]
        if t < HW:
            points = points + edge[t]
        if t >= leaves - HW:
            points = points + edge[HW + t - (leaves - HW)]
        points = points.astype(BF)
        for k in range(kernels):
            out[k, t] = points[k * vecs:(k + 1) * vecs]


def down_pass(offs, tlist, mine, theirs, coupling, ptr, ltr, basis, far1, far0, near0, near1, edge):
    kernels, count, partners, rank, _ = coupling.shape
    leaves = basis.shape[0]
    rows, _, vecs, _ = mine.shape
    return call(
        functools.partial(down_body, offs), "down", (tlist,),
        (mine, theirs, coupling, ptr, ltr, basis, far1, far0, near0, near1, edge),
        jax.ShapeDtypeStruct((kernels, leaves, vecs, rank), BF),
        WHOLE,
        [like(x) for x in (mine, theirs, coupling, ptr, ltr, basis, far1, far0)]
        + [VMEM((leaves,) + near0.shape[1:], F32), like(edge), VMEM((2 * rows * count, vecs, rank), BF), DMA((10,)), DMA((count,))],
        (40_000_000, 8_000_000),
    )


def on_device(
    vectors,
    leaf_basis,
    leaf_transfer,
    pair_transfer,
    near_blocks,
    near_offset,
    leaf_send,
    leaf_list,
    leaf_coupling,
    pair_send,
    pair_list,
    pair_coupling,
    top_list,
    top_coupling,
):
    rows = lax.axis_size("row")
    devs = rows * lax.axis_size("col")
    cap0, cap1 = leaf_send.shape[2], pair_send.shape[2]
    lsend = jnp.transpose(leaf_send, (1, 0, 2))
    psend = jnp.transpose(pair_send, (0, 2, 1))
    offsets = near_offset.T
    llist = leaf_list.T
    plist = pair_list.T
    held, own, sib, cross, fwd, back = up_pass(lsend, psend, vectors, leaf_basis, leaf_transfer, pair_transfer)
    ring = range(devs)
    sibling = [(d, d ^ 1) for d in ring]

    masks = []
    while rows >> (len(masks) + 1):
        masks.append(rows >> (len(masks) + 1))
    offs = [0]
    for mask in masks:
        offs = offs + [off ^ mask for off in offs]

    def exchanged(piece, mask):
        return lax.ppermute(piece, "row", [(r, r ^ mask) for r in range(rows)])

    for mask in masks[:-3]:
        held = jnp.concatenate([held, exchanged(held, mask)], axis=0)
    got = exchanged(held, masks[-3])
    sib = lax.ppermute(sib, AXES, sibling)
    cross = lax.ppermute(cross, AXES, [(d, (d + 1 if d % 2 else d - 1) % devs) for d in ring])
    fwd = lax.ppermute(fwd, AXES, [(d, (d + 2) % devs) for d in ring])
    back = lax.ppermute(back, AXES, [(d, (d - 2) % devs) for d in ring])
    near0, held = near_pass(offsets, vectors, near_blocks, held, got, 0, 2)
    got = exchanged(held, masks[-2])
    near1, held = near_pass(offsets, vectors, near_blocks, held, got, 1, 2)
    got = exchanged(held, masks[-1])
    far0, mine = leaf_pass(llist, own, sib, cross, fwd, back, leaf_coupling, held, got, 4, cap0)
    theirs = lax.ppermute(mine, AXES, sibling)
    far1, edge = pair_pass(plist, offsets, own, sib, cross, fwd, back, pair_coupling, near_blocks, 2, cap1)
    return down_pass(
        offs, top_list, mine, theirs, top_coupling, pair_transfer, leaf_transfer, leaf_basis, far1, far0, near0, near1, edge
    )


def solution(mesh):
    placed = P(("groups", "row", "col"))
    behind = P(None, ("groups", "row", "col"))
    return jax.shard_map(
        on_device,
        mesh=mesh,
        in_specs=(
            placed, placed, placed, placed, behind, placed, placed, placed, behind, placed, placed, behind, placed, behind,
        ),
        out_specs=behind,
        check_vma=False,
    )
```

time: 50.3 us -> 55.3 us (1.099)
  blocking collectives: 14.6 us -> 0 us
  starting transfers between devices: 5.93 us -> 16.5 us
  waiting for transfers between devices: 0.01 us -> 5.91 us
  Pallas kernels: 27.9 us -> 29.9 us
  local copies, waits for them, and re-layouts: 1.26 us -> 2.5 us
    all_to_all x1 -> x0, blocking collectives: 14.6 us -> none  [on_device(): mine = lax.all_to_all(tops, 'row', split_axis=0, concat_axis=0)]
    ppermute x0 -> x3, starting transfers between devices: none -> 8.05 us  [exchanged(): return lax.ppermute(piece, 'row', [(r, r ^ mask) for r in range(rows)])]
    ppermute x0 -> x3, waiting for transfers between devices: none -> 4.15 us  [exchanged(): return lax.ppermute(piece, 'row', [(r, r ^ mask) for r in range(rows)])]
    ppermute x1, starting transfers between devices: 0.69 us -> 3.66 us  [on_device(): lax.ppermute(cross, AXES, [(d, (d + 1 if d % 2 else d - 1) % devs) for d...]
    pallas_call x4 -> x6, Pallas kernels: 27.9 us -> 29.9 us  [call(): pl.pallas_call(body, out_shape=out_shape, in_specs=[SCALARS] * len(scalar...]
    ppermute x1, waiting for transfers between devices: 0.01 us -> 1.75 us  [on_device(): fwd = lax.ppermute(fwd, AXES, [(d, (d + 2) % devs) for d in ring])]
    unnamed x12 -> x24, local copies, waits for them, and re-layouts: 1.26 us -> 2.5 us
    ppermute x1, starting transfers between devices: 0.94 us -> 0.01 us  [on_device(): fwd = lax.ppermute(fwd, AXES, [(d, (d + 2) % devs) for d in ring])]
  transfers between devices with their start and end apart: 5 -> 8, of which waited for: 0 -> 3; matrix products, arithmetic and copies ran while one was open for 0% -> 0% of each run, Pallas kernels for 35% -> 8%
where the time goes in v3:
time: 55.3 us; the launch traced here: 54.9 us
  Pallas kernels  29.9 us (54%)
  starting transfers between devices  16.5 us (30%)
  waiting for transfers between devices  5.91 us (11%)
  local copies, waits for them, and re-layouts  2.5 us (5%)
    pallas_call x6, Pallas kernels, call(): pl.pallas_call(body, out_shape=out_shape, in_specs=[SCALARS] * len(scalar...  29.9 us
    ppermute x3, starting transfers between devices, exchanged(): return lax.ppermute(piece, 'row', [(r, r ^ mask) for r in range(rows)])  8.05 us
    ppermute x1, starting transfers between devices, on_device(): back = lax.ppermute(back, AXES, [(d, (d - 2) % devs) for d in ring])  4.72 us
    ppermute x3, waiting for transfers between devices, exchanged(): return lax.ppermute(piece, 'row', [(r, r ^ mask) for r in range(rows)])  4.15 us
    ppermute x1, starting transfers between devices, on_device(): lax.ppermute(cross, AXES, [(d, (d + 1 if d % 2 else d - 1) % devs) for d...  3.66 us
    unnamed x24, local copies, waits for them, and re-layouts  2.5 us
    ppermute x1, waiting for transfers between devices, on_device(): fwd = lax.ppermute(fwd, AXES, [(d, (d + 2) % devs) for d in ring])  1.75 us
  transfers between devices with their start and end apart: 8, of which 3 were waited for; matrix products, arithmetic and copies ran while one was open for 0% of the time, Pallas kernels for 8%

profile of v3, /device:TPU:0, one launch (start us, length us, event | category | flops | bytes accessed | tf_op | source)
XLA Modules:
  0.0 54.9 jit_solution(13564224082782052159)
XLA Ops:
  0.0 3.4 %up.1 = (bf16[1,4,16,128]{3,2,1,0:T(8,128)(2,1)}, bf16[5,16,128]{2,1,0:T(8,128)(2,1)}, bf16[6,16,128]{2,1,0:T(8,128)(2,1)}, bf16[6,16,128]{2,1,0:T(8,128)(2,1)},...) custom-call(s32[5,1,8]{2,1,0:T(1,128)} %bitcast.8, s32[1,2,5]{2,1,0:T(2,128)} %bitcast.11, ...), custom_call_target="tpu_custom_call" | custom-call | flops 10000000 | bytes 3000000 | tf_op jit(solution)/shard_map/up/pallas_call | solution.py:73
  3.4 4.1 %collective-permute-start.4 = (bf16[1,4,16,128]{3,2,1,0:T(8,128)(2,1)}, bf16[1,4,16,128]{3,2,1,0:T(8,128)(2,1)S(1)}, u32[]{:S(2)}, u32[]{:S(2)}) collective-permute-start(bf16[1,4,16,128]{3,2,1,0:T(8,128)(2,1)} %get-tuple-element.24.held_h), channel_id=1, source_target_pairs={{0,8},{2,10},{4,12},{6,14},{8,0},{10,2},{12,4},{14,6},{1,9},{3,11}... | collective-permute-start | bytes 49160 | tf_op jit(solution)/shard_map/ppermute | solution.py:424
  7.5 1.9 %collective-permute-done.4.got_h = bf16[1,4,16,128]{3,2,1,0:T(8,128)(2,1)S(1)} collective-permute-done((bf16[1,4,16,128]{3,2,1,0:T(8,128)(2,1)}, bf16[1,4,16,128]{3,2,1,0:T(8,128)(2,1)S(1)}, u32[]{:S(2)}, u32[]{:S(2)}) %collective-permute-start.4) | collective-permute-done | bytes 16416 | tf_op jit(solution)/shard_map/ppermute | solution.py:424
  9.4 0.0 copy-start.7
  9.4 0.6 %copy-done.7 = bf16[1,4,16,128]{3,2,1,0:T(8,128)(2,1)} copy-done((bf16[1,4,16,128]{3,2,1,0:T(8,128)(2,1)}, bf16[1,4,16,128]{3,2,1,0:T(8,128)(2,1)S(1)}, u32[]{:S(2)}) %copy-start.7) | copy-done | bytes 16408
  10.0 0.0 copy-start.9
  10.0 0.0 copy-start.8
  10.0 0.0 copy-start.11
  10.0 0.0 copy-start.10
  10.0 3.9 %near0.1 = (f32[16,48,64]{2,1,0:T(8,128)}, bf16[2,4,16,128]{3,2,1,0:T(8,128)(2,1)}) custom-call(s32[3,32]{1,0:T(4,128)} %bitcast.5, bf16[32,16,64]{2,1,0:T(8,128)(2,1)} %vec_h.5, bf16[3,32,3,64,64]{4,3,2,1,0:T(8,128)(2,1)} %near_h.1, bf16[1,4,16,128]{3,2,1,0:T(8,128)(2,1)} %get-tuple-element.24.held_h, bf16[1,4,16,128]{3,2,1,0:T(8,128)(2,1)} %copy-done.7), custom_call_target="tpu_custom_call" | custom-call | flops 20000000 | bytes 6000000 | tf_op jit(solution)/shard_map/near0/pallas_call | solution.py:73
  13.9 2.0 %collective-permute-start.5 = (bf16[2,4,16,128]{3,2,1,0:T(8,128)(2,1)}, bf16[2,4,16,128]{3,2,1,0:T(8,128)(2,1)S(1)}, u32[]{:S(2)}, u32[]{:S(2)}) collective-permute-start(bf16[2,4,16,128]{3,2,1,0:T(8,128)(2,1)} %get-tuple-element.25.held_h), channel_id=1, source_target_pairs={{0,4},{2,6},{4,0},{6,2},{8,12},{10,14},{12,8},{14,10},{1,5},{3,7},... | collective-permute-start | bytes 98312 | tf_op jit(solution)/shard_map/ppermute | solution.py:424
  15.9 2.2 %collective-permute-done.5.got_h = bf16[2,4,16,128]{3,2,1,0:T(8,128)(2,1)S(1)} collective-permute-done((bf16[2,4,16,128]{3,2,1,0:T(8,128)(2,1)}, bf16[2,4,16,128]{3,2,1,0:T(8,128)(2,1)S(1)}, u32[]{:S(2)}, u32[]{:S(2)}) %collective-permute-start.5) | collective-permute-done | bytes 32800 | tf_op jit(solution)/shard_map/ppermute | solution.py:424
  18.1 0.0 copy-start.6
  18.1 0.6 %copy-done.6 = bf16[2,4,16,128]{3,2,1,0:T(8,128)(2,1)} copy-done((bf16[2,4,16,128]{3,2,1,0:T(8,128)(2,1)}, bf16[2,4,16,128]{3,2,1,0:T(8,128)(2,1)S(1)}, u32[]{:S(2)}) %copy-start.6) | copy-done | bytes 32792
  18.7 4.6 %near1.1 = (f32[16,48,64]{2,1,0:T(8,128)}, bf16[4,4,16,128]{3,2,1,0:T(8,128)(2,1)}) custom-call(s32[3,32]{1,0:T(4,128)} %bitcast.6, bf16[32,16,64]{2,1,0:T(8,128)(2,1)} %vec_h.5, bf16[3,32,3,64,64]{4,3,2,1,0:T(8,128)(2,1)} %near_h.1, bf16[2,4,16,128]{3,2,1,0:T(8,128)(2,1)} %get-tuple-element.25.held_h, bf16[2,4,16,128]{3,2,1,0:T(8,128)(2,1)} %copy-done.6), custom_call_target="tpu_custom_call" | custom-call | flops 20000000 | bytes 6000000 | tf_op jit(solution)/shard_map/near1/pallas_call | solution.py:73
  23.3 2.0 %collective-permute-start.6 = (bf16[4,4,16,128]{3,2,1,0:T(8,128)(2,1)}, bf16[4,4,16,128]{3,2,1,0:T(8,128)(2,1)S(1)}, u32[]{:S(2)}, u32[]{:S(2)}) collective-permute-start(bf16[4,4,16,128]{3,2,1,0:T(8,128)(2,1)} %get-tuple-element.26.held_h), channel_id=1, source_target_pairs={{0,2},{2,0},{4,6},{6,4},{8,10},{10,8},{12,14},{14,12},{1,3},{3,1},... | collective-permute-start | bytes 196616 | tf_op jit(solution)/shard_map/ppermute | solution.py:424
  25.3 0.0 copy-done.9
  25.3 0.0 collective-permute-start
  25.3 0.0 copy-done.8
  25.3 3.7 %collective-permute-start.1 = (bf16[6,16,128]{2,1,0:T(8,128)(2,1)S(1)}, bf16[6,16,128]{2,1,0:T(8,128)(2,1)S(1)}, u32[]{:S(2)}, u32[]{:S(2)}) collective-permute-start(bf16[6,16,128]{2,1,0:T(8,128)(2,1)S(1)} %copy-done.8), channel_id=1, source_target_pairs={{0,15},{1,2},{2,1},{3,4},{4,3},{5,6},{6,5},{7,8},{8,7},{9,10},{10,... | collective-permute-start | bytes 73736 | tf_op jit(solution)/shard_map/ppermute | solution.py:430
  28.9 0.0 copy-done.11
  28.9 0.0 collective-permute-start.2
  28.9 0.0 copy-done.10
  28.9 4.7 %collective-permute-start.3 = (bf16[5,16,128]{2,1,0:T(8,128)(2,1)S(1)}, bf16[5,16,128]{2,1,0:T(8,128)(2,1)S(1)}, u32[]{:S(2)}, u32[]{:S(2)}) collective-permute-start(bf16[5,16,128]{2,1,0:T(8,128)(2,1)S(1)} %copy-done.10), channel_id=1, source_target_pairs={{0,14},{1,15},{2,0},{3,1},{4,2},{5,3},{6,4},{7,5},{8,6},{9,7},{10,... | collective-permute-start | bytes 61448 | tf_op jit(solution)/shard_map/ppermute | solution.py:432
  33.7 1.8 %collective-permute-done.2.fwd_h = bf16[5,16,128]{2,1,0:T(8,128)(2,1)S(1)} collective-permute-done((bf16[5,16,128]{2,1,0:T(8,128)(2,1)S(1)}, bf16[5,16,128]{2,1,0:T(8,128)(2,1)S(1)}, u32[]{:S(2)}, u32[]{:S(2)}) %collective-permute-start.2) | collective-permute-done | bytes 20512 | tf_op jit(solution)/shard_map/ppermute | solution.py:431
  35.4 0.0 copy-start.3
  35.4 0.0 collective-permute-done.3.back_h
  35.4 0.0 copy-start.4
  35.4 0.0 collective-permute-done.sib_h
  35.4 0.0 copy-start.1
  35.4 0.0 collective-permute-done.1.cross_h
  35.5 0.0 copy-start.2
  35.5 0.0 collective-permute-done.6.got_h
  35.5 0.0 copy-start.5
  35.5 0.5 copy-done.3
  36.0 0.0 copy-done.4
  36.0 0.0 copy-done.1
  36.0 0.0 copy-done.2
  36.1 0.0 copy-done.5
  36.1 6.7 %leaf.1 = (f32[32,48,64]{2,1,0:T(8,128)}, bf16[8,4,16,128]{3,2,1,0:T(8,128)(2,1)}) custom-call(s32[4,32]{1,0:T(4,128)} %bitcast.9, bf16[5,16,128]{2,1,0:T(8,128)(2,1)} %get-tuple-element.19.own_h, bf16[6,16,128]{2,1,0:T(8,128)(2,1)} %copy-done.1, bf16[6,16,128]{2,1,0:T(8,128)(2,1)} %copy-done.2, bf16[5,16,128]{2,1,0:T(8,128)(2,1)} %copy-done.3, ...), custom_call_target="tpu_custom_call" | custom-call | flops 50000000 | bytes 9000000 | tf_op jit(solution)/shard_map/leaf/pallas_call | solution.py:73
  42.8 0.1 collective-permute-start.7
  42.9 4.5 %pair.1 = (f32[16,48,64]{2,1,0:T(8,128)}, f32[4,48,64]{2,1,0:T(8,128)}) custom-call(s32[4,16]{1,0:T(4,128)} %bitcast.10, s32[3,32]{1,0:T(4,128)} %bitcast.7, bf16[5,16,128]{2,1,0:T(8,128)(2,1)} %get-tuple-element.19.own_h, bf16[6,16,128]{2,1,0:T(8,128)(2,1)} %copy-done.1, bf16[6,16,128]{2,1,0:T(8,128)(2,1)} %copy-done.2, bf16[5,16,128]{2,1,0:T(8,128)(2,1)} %copy-done.3, ...), custom_call_target="tpu_custom_call" | custom-call | flops 30000000 | bytes 5000000 | tf_op jit(solution)/shard_map/pair/pallas_call | solution.py:73
  47.5 0.0 collective-permute-done.7.theirs_h
  47.5 0.0 copy-start
  47.5 0.7 %copy-done = bf16[8,4,16,128]{3,2,1,0:T(8,128)(2,1)} copy-done((bf16[8,4,16,128]{3,2,1,0:T(8,128)(2,1)}, bf16[8,4,16,128]{3,2,1,0:T(8,128)(2,1)S(1)}, u32[]{:S(2)}) %copy-start) | copy-done | bytes 131096
  48.1 6.8 %down.1 = bf16[3,32,16,64]{3,2,1,0:T(8,128)(2,1)} custom-call(s32[8,8]{1,0:T(8,128)} %tlist.1, bf16[8,4,16,128]{3,2,1,0:T(8,128)(2,1)} %get-tuple-element.27.mine_h, bf16[8,4,16,128]{3,2,1,0:T(8,128)(2,1)} %copy-done, bf16[3,8,8,64,64]{4,3,2,1,0:T(8,128)(2,1)} %coupling_h.1, bf16[16,64,64]{2,1,0:T(8,128)(2,1)} %ptr_h.3, bf16[32,64,64]{2,1,0:T(8,128)(2,1)} %ltr_h.3, ...), custom_call_target="tpu_custom_call" | custom-call | flops 40000000 | bytes 8000000 | tf_op jit(solution)/shard_map/down/pallas_call | solution.py:73
Async XLA Ops:
  3.4 6.0 %collective-permute-start.4 = (bf16[1,4,16,128]{3,2,1,0:T(8,128)(2,1)}, bf16[1,4,16,128]{3,2,1,0:T(8,128)(2,1)S(1)}, u32[]{:S(2)}, u32[]{:S(2)}) collective-permute-start(bf16[1,4,16,128]{3,2,1,0:T(8,128)(2,1)} %get-tuple-element.24.held_h), channel_id=1, source_target_pairs={{0,8},{2,10},{4,12},{6,14},{8,0},{10,2},{12,4},{14,6},{1,9},{3,11}... | collective-permute-start | bytes 49160 | tf_op jit(solution)/shard_map/ppermute | solution.py:424
  9.4 0.6 %copy-start.7 = (bf16[1,4,16,128]{3,2,1,0:T(8,128)(2,1)}, bf16[1,4,16,128]{3,2,1,0:T(8,128)(2,1)S(1)}, u32[]{:S(2)}) copy-start(bf16[1,4,16,128]{3,2,1,0:T(8,128)(2,1)S(1)} %collective-permute-done.4.got_h) | copy-start | bytes 49156
  10.0 15.3 %copy-start.9 = (bf16[6,16,128]{2,1,0:T(8,128)(2,1)S(1)}, bf16[6,16,128]{2,1,0:T(8,128)(2,1)}, u32[]{:S(2)}) copy-start(bf16[6,16,128]{2,1,0:T(8,128)(2,1)} %get-tuple-element.20) | copy-start | bytes 73732
  10.0 15.3 %copy-start.8 = (bf16[6,16,128]{2,1,0:T(8,128)(2,1)S(1)}, bf16[6,16,128]{2,1,0:T(8,128)(2,1)}, u32[]{:S(2)}) copy-start(bf16[6,16,128]{2,1,0:T(8,128)(2,1)} %get-tuple-element.21) | copy-start | bytes 73732
  10.0 18.9 %copy-start.11 = (bf16[5,16,128]{2,1,0:T(8,128)(2,1)S(1)}, bf16[5,16,128]{2,1,0:T(8,128)(2,1)}, u32[]{:S(2)}) copy-start(bf16[5,16,128]{2,1,0:T(8,128)(2,1)} %get-tuple-element.22) | copy-start | bytes 61444
  10.0 18.9 %copy-start.10 = (bf16[5,16,128]{2,1,0:T(8,128)(2,1)S(1)}, bf16[5,16,128]{2,1,0:T(8,128)(2,1)}, u32[]{:S(2)}) copy-start(bf16[5,16,128]{2,1,0:T(8,128)(2,1)} %get-tuple-element.23) | copy-start | bytes 61444
  13.9 4.2 %collective-permute-start.5 = (bf16[2,4,16,128]{3,2,1,0:T(8,128)(2,1)}, bf16[2,4,16,128]{3,2,1,0:T(8,128)(2,1)S(1)}, u32[]{:S(2)}, u32[]{:S(2)}) collective-permute-start(bf16[2,4,16,128]{3,2,1,0:T(8,128)(2,1)} %get-tuple-element.25.held_h), channel_id=1, source_target_pairs={{0,4},{2,6},{4,0},{6,2},{8,12},{10,14},{12,8},{14,10},{1,5},{3,7},... | collective-permute-start | bytes 98312 | tf_op jit(solution)/shard_map/ppermute | solution.py:424
  18.1 0.6 %copy-start.6 = (bf16[2,4,16,128]{3,2,1,0:T(8,128)(2,1)}, bf16[2,4,16,128]{3,2,1,0:T(8,128)(2,1)S(1)}, u32[]{:S(2)}) copy-start(bf16[2,4,16,128]{3,2,1,0:T(8,128)(2,1)S(1)} %collective-permute-done.5.got_h) | copy-start | bytes 98308
  23.3 12.2 %collective-permute-start.6 = (bf16[4,4,16,128]{3,2,1,0:T(8,128)(2,1)}, bf16[4,4,16,128]{3,2,1,0:T(8,128)(2,1)S(1)}, u32[]{:S(2)}, u32[]{:S(2)}) collective-permute-start(bf16[4,4,16,128]{3,2,1,0:T(8,128)(2,1)} %get-tuple-element.26.held_h), channel_id=1, source_target_pairs={{0,2},{2,0},{4,6},{6,4},{8,10},{10,8},{12,14},{14,12},{1,3},{3,1},... | collective-permute-start | bytes 196616 | tf_op jit(solution)/shard_map/ppermute | solution.py:424
  25.3 10.2 %collective-permute-start = (bf16[6,16,128]{2,1,0:T(8,128)(2,1)S(1)}, bf16[6,16,128]{2,1,0:T(8,128)(2,1)S(1)}, u32[]{:S(2)}, u32[]{:S(2)}) collective-permute-start(bf16[6,16,128]{2,1,0:T(8,128)(2,1)S(1)} %copy-done.9), channel_id=1, source_target_pairs={{0,1},{1,0},{2,3},{3,2},{4,5},{5,4},{6,7},{7,6},{8,9},{9,8},{10,11... | collective-permute-start | bytes 73736 | tf_op jit(solution)/shard_map/ppermute | solution.py:429
  25.3 10.2 %collective-permute-start.1 = (bf16[6,16,128]{2,1,0:T(8,128)(2,1)S(1)}, bf16[6,16,128]{2,1,0:T(8,128)(2,1)S(1)}, u32[]{:S(2)}, u32[]{:S(2)}) collective-permute-start(bf16[6,16,128]{2,1,0:T(8,128)(2,1)S(1)} %copy-done.8), channel_id=1, source_target_pairs={{0,15},{1,2},{2,1},{3,4},{4,3},{5,6},{6,5},{7,8},{8,7},{9,10},{10,... | collective-permute-start | bytes 73736 | tf_op jit(solution)/shard_map/ppermute | solution.py:430
  28.9 6.5 %collective-permute-start.2 = (bf16[5,16,128]{2,1,0:T(8,128)(2,1)S(1)}, bf16[5,16,128]{2,1,0:T(8,128)(2,1)S(1)}, u32[]{:S(2)}, u32[]{:S(2)}) collective-permute-start(bf16[5,16,128]{2,1,0:T(8,128)(2,1)S(1)} %copy-done.11), channel_id=1, source_target_pairs={{0,2},{1,3},{2,4},{3,5},{4,6},{5,7},{6,8},{7,9},{8,10},{9,11},{10,... | collective-permute-start | bytes 61448 | tf_op jit(solution)/shard_map/ppermute | solution.py:431
  28.9 6.5 %collective-permute-start.3 = (bf16[5,16,128]{2,1,0:T(8,128)(2,1)S(1)}, bf16[5,16,128]{2,1,0:T(8,128)(2,1)S(1)}, u32[]{:S(2)}, u32[]{:S(2)}) collective-permute-start(bf16[5,16,128]{2,1,0:T(8,128)(2,1)S(1)} %copy-done.10), channel_id=1, source_target_pairs={{0,14},{1,15},{2,0},{3,1},{4,2},{5,3},{6,4},{7,5},{8,6},{9,7},{10,... | collective-permute-start | bytes 61448 | tf_op jit(solution)/shard_map/ppermute | solution.py:432
  35.4 0.6 %copy-start.3 = (bf16[5,16,128]{2,1,0:T(8,128)(2,1)}, bf16[5,16,128]{2,1,0:T(8,128)(2,1)S(1)}, u32[]{:S(2)}) copy-start(bf16[5,16,128]{2,1,0:T(8,128)(2,1)S(1)} %collective-permute-done.2.fwd_h) | copy-start | bytes 61444
  35.4 0.6 %copy-start.4 = (bf16[5,16,128]{2,1,0:T(8,128)(2,1)}, bf16[5,16,128]{2,1,0:T(8,128)(2,1)S(1)}, u32[]{:S(2)}) copy-start(bf16[5,16,128]{2,1,0:T(8,128)(2,1)S(1)} %collective-permute-done.3.back_h) | copy-start | bytes 61444
  35.4 0.6 %copy-start.1 = (bf16[6,16,128]{2,1,0:T(8,128)(2,1)}, bf16[6,16,128]{2,1,0:T(8,128)(2,1)S(1)}, u32[]{:S(2)}) copy-start(bf16[6,16,128]{2,1,0:T(8,128)(2,1)S(1)} %collective-permute-done.sib_h) | copy-start | bytes 73732
  35.5 0.6 %copy-start.2 = (bf16[6,16,128]{2,1,0:T(8,128)(2,1)}, bf16[6,16,128]{2,1,0:T(8,128)(2,1)S(1)}, u32[]{:S(2)}) copy-start(bf16[6,16,128]{2,1,0:T(8,128)(2,1)S(1)} %collective-permute-done.1.cross_h) | copy-start | bytes 73732
  35.5 0.6 %copy-start.5 = (bf16[4,4,16,128]{3,2,1,0:T(8,128)(2,1)}, bf16[4,4,16,128]{3,2,1,0:T(8,128)(2,1)S(1)}, u32[]{:S(2)}) copy-start(bf16[4,4,16,128]{3,2,1,0:T(8,128)(2,1)S(1)} %collective-permute-done.6.got_h) | copy-start | bytes 196612
  42.8 4.6 %collective-permute-start.7 = (bf16[8,4,16,128]{3,2,1,0:T(8,128)(2,1)}, bf16[8,4,16,128]{3,2,1,0:T(8,128)(2,1)S(1)}, u32[]{:S(2)}, u32[]{:S(2)}) collective-permute-start(bf16[8,4,16,128]{3,2,1,0:T(8,128)(2,1)} %get-tuple-element.27.mine_h), channel_id=1, source_target_pairs={{0,1},{1,0},{2,3},{3,2},{4,5},{5,4},{6,7},{7,6},{8,9},{9,8},{10,11... | collective-permute-start | bytes 393224 | tf_op jit(solution)/shard_map/ppermute | solution.py:438
  47.5 0.7 %copy-start = (bf16[8,4,16,128]{3,2,1,0:T(8,128)(2,1)}, bf16[8,4,16,128]{3,2,1,0:T(8,128)(2,1)S(1)}, u32[]{:S(2)}) copy-start(bf16[8,4,16,128]{3,2,1,0:T(8,128)(2,1)S(1)} %collective-permute-done.7.theirs_h) | copy-start | bytes 393220

commit v4 on v3

v4 whole, which is shorter than its diff:
```python
import jax
import jax.numpy as jnp
from jax import lax
from jax.experimental import pallas as pl
from jax.experimental.pallas import tpu as pltpu
from jax.sharding import PartitionSpec as P

REACH = 2
WIN = 2 * REACH + 1
HW = 2
AXES = ("row", "col")
F32 = jnp.float32
BF = jnp.bfloat16
LIMIT = 56 * 1024 * 1024

VMEM = pltpu.VMEM
SMEM = pltpu.SMEM
DMA = pltpu.SemaphoreType.DMA
FIXED = pl.BlockSpec(memory_space=pltpu.HBM)
WHOLE = pl.BlockSpec(memory_space=VMEM)


def dot(left, right):
    return jnp.dot(left, right, preferred_element_type=F32)


def beside(*parts):
    return jnp.concatenate(parts, axis=1)


def above(*parts):
    return jnp.concatenate(parts, axis=0)


def dot_t(left, right):
    return lax.dot_general(left, right, (((1,), (1,)), ((), ())), preferred_element_type=F32)


def row_of_blocks(ref, q):
    kernels, _, partners, _, _ = ref.shape
    return beside(*[above(*[ref[k, q, m] for k in range(kernels)]) for m in range(partners)])


def by_kernel(wide, rank):
    return above(*[wide[:, k * rank:(k + 1) * rank] for k in range(wide.shape[1] // rank)])


def copies(pairs, sems):
    made = [pltpu.make_async_copy(src, dst, sems.at[i]) for i, (src, dst) in enumerate(pairs)]
    for copy in made:
        copy.start()
    return made


def chunk_of(src, dst, sems, size):
    def chunk(c):
        part = pl.ds(c * size, size)
        return pltpu.make_async_copy(src.at[:, part], dst.at[:, part], sems.at[c])

    return chunk


def split(row, ref, at):
    rank = row.shape[1] // 2
    ref[at] = row[:, :rank]
    ref[at + 1] = row[:, rank:]


def call(body, name, params, arrays, out_shape, out_specs, scratch, cost, limit=LIMIT):
    return pl.pallas_call(
        body,
        out_shape=out_shape,
        in_specs=[FIXED] * len(params) + [WHOLE] * len(arrays),
        out_specs=out_specs,
        scratch_shapes=scratch,
        compiler_params=pltpu.CompilerParams(vmem_limit_bytes=limit),
        cost_estimate=pl.CostEstimate(flops=cost[0], bytes_accessed=cost[1], transcendentals=0),
        name=name,
    )(*params, *arrays)


def like(x):
    return VMEM(x.shape, x.dtype)


def held(x):
    return SMEM(x.shape, x.dtype)


def up_body(vec_h, basis_h, ltr_h, ptr_h, lsend_h, psend_h, tops, own, sib, cross, fwd, back,
            vec, basis, ltr, ptr, lsend, psend, low, mid, sems):
    leaves, vecs, rank = vec.shape
    col = lax.axis_index("col")
    cap0 = lsend.shape[2]
    cap1 = psend.shape[1]
    made = copies(
        [(vec_h, vec), (basis_h, basis), (ltr_h, ltr), (ptr_h, ptr), (lsend_h, lsend), (psend_h, psend)], sems
    )
    made[0].wait()
    made[1].wait()
    for t in range(leaves):
        low[t] = dot(vec[t], basis[t]).astype(BF)
    made[2].wait()
    for j in range(leaves // 2):
        mid[j] = dot(
            beside(low[2 * j], low[2 * j + 1]), ltr[2 * j:2 * j + 2].reshape(2 * rank, rank)
        ).astype(BF)
    made[3].wait()
    high = []
    for i in range(leaves // 4):
        high.append(
            dot(beside(mid[2 * i], mid[2 * i + 1]), ptr[2 * i:2 * i + 2].reshape(2 * rank, rank)).astype(BF)
        )
    for i in range(leaves // 8):
        both = beside(high[2 * i], high[2 * i + 1])
        for row in range(tops.shape[0]):
            tops[row, i] = both
    made[4].wait()
    made[5].wait()

    def pack(out, place):
        for c in range(cap0 // 2):
            out[c] = beside(low[lsend[place, 0, 2 * c]], low[lsend[place, 0, 2 * c + 1]])
        for c in range(cap1 // 2):
            out[cap0 // 2 + c] = beside(mid[psend[0, 2 * c, place]], mid[psend[0, 2 * c + 1, place]])

    def pack_halo(out, start):
        out[(cap0 + cap1) // 2] = beside(vec[start], vec[start + 1])

    pack(sib, 1 + 2 * col)
    pack_halo(sib, (1 - col) * (leaves - HW))
    pack(cross, 3 - 2 * col)
    pack_halo(cross, col * (leaves - HW))
    pack(fwd, 0)
    pack(back, 4)
    pack(own, REACH)


def up_pass(lsend, psend, vec, basis, ltr, ptr, rows):
    leaves, vecs, rank = vec.shape
    count = (lsend.shape[2] + psend.shape[1]) // 2
    shape = lambda *n: jax.ShapeDtypeStruct(n + (vecs, 2 * rank), BF)
    return call(
        up_body, "up", (vec, basis, ltr, ptr, lsend, psend), (),
        [shape(rows, leaves // 8), shape(count), shape(count + 1), shape(count + 1), shape(count), shape(count)],
        [WHOLE] * 6,
        [
            like(vec), like(basis), like(ltr), like(ptr), held(lsend), held(psend),
            VMEM((leaves, vecs, rank), BF), VMEM((leaves // 2, vecs, rank), BF), DMA((6,)),
        ],
        (10_000_000, 3_000_000),
    )


def near_body(vec_h, blocks_h, offsets_h, out, blocks, padded, offsets, sems, chunk_sems):
    leaves = blocks.shape[1]
    _, vecs, rank = padded.shape
    chunks = chunk_sems.shape[0]
    per = leaves // chunks
    made = copies([(vec_h, padded.at[pl.ds(HW, leaves)]), (offsets_h, offsets)], sems)
    chunk = chunk_of(blocks_h, blocks, chunk_sems, per)
    for c in range(chunks):
        chunk(c).start()
    zero = jnp.zeros((HW, vecs, rank), BF)
    padded[0:HW] = zero
    padded[HW + leaves:] = zero
    for copy in made:
        copy.wait()

    def body(c, _):
        chunk(c).wait()
        for q in range(per):
            t = c * per + q
            total = None
            for n in range(blocks.shape[2]):
                part = dot_t(padded[t + HW + offsets[n, t]], above(*[blocks[k, t, n] for k in range(blocks.shape[0])]))
                total = part if total is None else total + part
            out[t] = by_kernel(total, rank)
        return 0

    lax.fori_loop(0, chunks, body, 0)


def near_pass(offsets, vec, blocks, chunks):
    kernels, leaves, near, rank, _ = blocks.shape
    vecs = vec.shape[1]
    return call(
        near_body, "near", (vec, blocks, offsets), (),
        jax.ShapeDtypeStruct((leaves, kernels * vecs, rank), F32),
        WHOLE,
        [
            like(blocks), VMEM((leaves + 2 * HW, vecs, rank), BF), held(offsets), DMA((2,)), DMA((chunks,)),
        ],
        (40_000_000, 12_000_000),
    )


def rest_body(leaf_h, pair_h, coupling_h, near_h, ptr_h, ltr_h, basis_h, llist_h, plist_h, tlist_h, offsets_h,
              own, sib, cross, fwd, back, mine, theirs, near, out,
              leaf, pair, coupling, first, last, ptr, ltr, basis, llist, plist, tlist, offsets,
              wleaf, wpair, halo, tops, far0, far1, down, sems, leaf_sems, pair_sems, top_sems):
    kernels, leaves, partners, rank, _ = leaf.shape
    _, vecs, _ = wleaf.shape
    count = coupling.shape[1]
    cap0 = wleaf.shape[0] // WIN
    cap1 = wpair.shape[0] // WIN
    base = own.shape[0] - cap1 // 2
    heads = first.shape[1]
    chunks = leaf_sems.shape[0]
    per = leaves // chunks
    col = lax.axis_index("col")
    place = lax.axis_index("row") * lax.axis_size("col") + col
    last_place = lax.axis_size("row") * lax.axis_size("col") - 1
    lists = copies([(llist_h, llist), (plist_h, plist), (tlist_h, tlist), (offsets_h, offsets)], sems)
    leaf_chunk = chunk_of(leaf_h, leaf, leaf_sems, per)
    pair_chunk = chunk_of(pair_h, pair, pair_sems, per // 2)
    top_chunk = chunk_of(coupling_h, coupling, top_sems, 1)
    for c in range(chunks):
        leaf_chunk(c).start()
        pair_chunk(c).start()
    for c in range(count):
        top_chunk(c).start()
    others = copies(
        [
            (near_h.at[:, pl.ds(0, heads)], first), (near_h.at[:, pl.ds(leaves - heads, heads)], last),
            (ptr_h, ptr), (ltr_h, ltr), (basis_h, basis),
        ],
        sems.at[pl.ds(4, 5)],
    )

    for block, slot in ((own, REACH), (fwd, 0), (back, 4), (sib, 3 - 2 * col), (cross, 1 + 2 * col)):
        for c in range(cap0 // 2):
            split(block[c], wleaf, slot * cap0 + 2 * c)
        for c in range(cap1 // 2):
            split(block[base + c], wpair, slot * cap1 + 2 * c)
    zero = jnp.zeros((vecs, rank), BF)
    for block, slot in ((sib, HW - HW * col), (cross, HW * col)):
        row = block[base + cap1 // 2]
        outside = (place == 0) & (slot == 0) | (place == last_place) & (slot == HW)
        split(jnp.where(outside, jnp.zeros_like(row), row), halo, slot)
    halo[2 * HW] = zero
    for block, side in ((mine, col), (theirs, 1 - col)):
        for s in range(block.shape[0]):
            for i in range(block.shape[1]):
                split(block[s, i], tops, (s * 2 + side) * count + 2 * i)
    for copy in lists:
        copy.wait()

    def body(c, _):
        leaf_chunk(c).wait()
        pair_chunk(c).wait()
        for q in range(per):
            t = c * per + q
            rows = beside(*[wleaf[llist[m, t]] for m in range(partners)])
            far0[t] = by_kernel(dot_t(rows, row_of_blocks(leaf, t)), rank)
        for q in range(per // 2):
            j = c * (per // 2) + q
            rows = beside(*[wpair[plist[m, j]] for m in range(pair.shape[2])])
            far1[j] = by_kernel(dot_t(rows, row_of_blocks(pair, j)), rank)
        return 0

    lax.fori_loop(0, chunks, body, 0)

    for i in range(count):
        top_chunk(i).wait()
        rows = beside(*[tops[tlist[i, m]] for m in range(coupling.shape[2])])
        down[i] = by_kernel(dot_t(rows, row_of_blocks(coupling, i)), rank).astype(BF)
    for copy in others:
        copy.wait()

    def edge(t):
        if t < heads:
            ref, q = first, t
        else:
            ref, q = last, t - (leaves - heads)
        spots = [t + offsets[n, t] for n in range(ref.shape[2])]
        if t < heads:
            spots = [jnp.where(at < 0, at + HW, 2 * HW) for at in spots]
        else:
            spots = [jnp.where(at >= leaves, at - leaves + HW, 2 * HW) for at in spots]
        return by_kernel(dot_t(beside(*[halo[at] for at in spots]), row_of_blocks(ref, q)), rank)

    down1 = []
    for j in range(2 * count):
        down1.append((far1[j] + dot_t(down[j // 2], ptr[j])).astype(BF))
    down0 = []
    for t in range(leaves):
        down0.append((far0[t] + dot_t(down1[t // 2], ltr[t])).astype(BF))
    for t in range(leaves):
        points = dot_t(down0[t], basis[t]) + near[t]
        if t < heads or t >= leaves - heads:
            points = points + edge(t)
        points = points.astype(BF)
        for k in range(kernels):
            out[k, t] = points[k * vecs:(k + 1) * vecs]


def rest_pass(leaf, pair, coupling, near_blocks, ptr, ltr, basis, llist, plist, tlist, offsets,
              own, sib, cross, fwd, back, mine, theirs, near, cap0, cap1, chunks):
    kernels, leaves, _, rank, _ = leaf.shape
    count = coupling.shape[1]
    vecs = own.shape[1]
    ends = VMEM((kernels, HW) + near_blocks.shape[2:], BF)
    params = (leaf, pair, coupling, near_blocks, ptr, ltr, basis, llist, plist, tlist, offsets)
    return call(
        rest_body, "rest", params, (own, sib, cross, fwd, back, mine, theirs, near),
        jax.ShapeDtypeStruct((kernels, leaves, vecs, rank), BF),
        WHOLE,
        [like(leaf), like(pair), like(coupling), ends, ends, like(ptr), like(ltr), like(basis)]
        + [held(x) for x in (llist, plist, tlist, offsets)]
        + [VMEM((n, vecs, rank), BF) for n in (WIN * cap0, WIN * cap1, 2 * HW + 1, 2 * mine.shape[0] * count)]
        + [
            VMEM((leaves, kernels * vecs, rank), F32), VMEM((leaves // 2, kernels * vecs, rank), F32),
            VMEM((count, kernels * vecs, rank), BF), DMA((9,)), DMA((chunks,)), DMA((chunks,)), DMA((count,)),
        ],
        (100_000_000, 20_000_000),
    )


def on_device(
    vectors,
    leaf_basis,
    leaf_transfer,
    pair_transfer,
    near_blocks,
    near_offset,
    leaf_send,
    leaf_list,
    leaf_coupling,
    pair_send,
    pair_list,
    pair_coupling,
    top_list,
    top_coupling,
):
    rows = lax.axis_size("row")
    devs = rows * lax.axis_size("col")
    cap0, cap1 = leaf_send.shape[2], pair_send.shape[2]
    lsend = jnp.transpose(leaf_send, (1, 0, 2))
    psend = jnp.transpose(pair_send, (0, 2, 1))
    offsets = near_offset.T
    tops, own, sib, cross, fwd, back = up_pass(
        lsend, psend, vectors, leaf_basis, leaf_transfer, pair_transfer, rows
    )
    ring = range(devs)
    sibling = [(d, d ^ 1) for d in ring]
    mine = lax.all_to_all(tops, "row", split_axis=0, concat_axis=0)
    theirs = lax.ppermute(mine, AXES, sibling)
    sib = lax.ppermute(sib, AXES, sibling)
    cross = lax.ppermute(cross, AXES, [(d, (d + 1 if d % 2 else d - 1) % devs) for d in ring])
    fwd = lax.ppermute(fwd, AXES, [(d, (d + 2) % devs) for d in ring])
    back = lax.ppermute(back, AXES, [(d, (d - 2) % devs) for d in ring])
    near = near_pass(offsets, vectors, near_blocks, 4)
    return rest_pass(
        leaf_coupling, pair_coupling, top_coupling, near_blocks, pair_transfer, leaf_transfer, leaf_basis,
        leaf_list.T, pair_list.T, top_list, offsets,
        own, sib, cross, fwd, back, mine, theirs, near, cap0, cap1, 4,
    )


def solution(mesh):
    placed = P(("groups", "row", "col"))
    behind = P(None, ("groups", "row", "col"))
    return jax.shard_map(
        on_device,
        mesh=mesh,
        in_specs=(
            placed, placed, placed, placed, behind, placed, placed, placed, behind, placed, placed, behind, placed, behind,
        ),
        out_specs=behind,
        check_vma=False,
    )
```

time: 55.3 us -> 42.1 us (0.76)
  blocking collectives: 0 us -> 14.6 us
  starting transfers between devices: 16.5 us -> 5.93 us
  Pallas kernels: 29.9 us -> 20.5 us
  waiting for transfers between devices: 5.91 us -> 0.01 us
  local copies, waits for them, and re-layouts: 2.5 us -> 0.64 us
    all_to_all x0 -> x1, blocking collectives: none -> 14.6 us  [on_device(): mine = lax.all_to_all(tops, 'row', split_axis=0, concat_axis=0)]
    pallas_call x6 -> x3, Pallas kernels: 29.9 us -> 20.5 us  [call(): pl.pallas_call(body, out_shape=out_shape, in_specs=[FIXED] * len(params)...]
    ppermute x3 -> x0, starting transfers between devices: 8.05 us -> none  [exchanged(): return lax.ppermute(piece, 'row', [(r, r ^ mask) for r in range(rows)])]
    ppermute x3 -> x0, waiting for transfers between devices: 4.15 us -> none  [exchanged(): return lax.ppermute(piece, 'row', [(r, r ^ mask) for r in range(rows)])]
    ppermute x1, starting transfers between devices: 3.66 us -> 0.69 us  [on_device(): lax.ppermute(cross, AXES, [(d, (d + 1 if d % 2 else d - 1) % devs) for d...]
    unnamed x24 -> x12, local copies, waits for them, and re-layouts: 2.5 us -> 0.64 us
    ppermute x1, waiting for transfers between devices: 1.75 us -> 0.01 us  [on_device(): fwd = lax.ppermute(fwd, AXES, [(d, (d + 2) % devs) for d in ring])]
    ppermute x1, starting transfers between devices: 0.01 us -> 0.94 us  [on_device(): fwd = lax.ppermute(fwd, AXES, [(d, (d + 2) % devs) for d in ring])]
  transfers between devices with their start and end apart: 8 -> 5, of which waited for: 3 -> 0; matrix products, arithmetic and copies ran while one was open for 0% -> 0% of each run, Pallas kernels for 8% -> 14%
where the time goes in v4:
time: 42.1 us; the launch traced here: 41.8 us
  Pallas kernels  20.5 us (49%)
  blocking collectives  14.6 us (35%)
  starting transfers between devices  5.93 us (14%)
  local copies, waits for them, and re-layouts  0.64 us (2%)
    pallas_call x3, Pallas kernels, call(): pl.pallas_call(body, out_shape=out_shape, in_specs=[FIXED] * len(params)...  20.5 us
    all_to_all x1, blocking collectives, on_device(): mine = lax.all_to_all(tops, 'row', split_axis=0, concat_axis=0)  14.6 us
    ppermute x1, starting transfers between devices, on_device(): back = lax.ppermute(back, AXES, [(d, (d - 2) % devs) for d in ring])  3.78 us
    ppermute x1, starting transfers between devices, on_device(): fwd = lax.ppermute(fwd, AXES, [(d, (d + 2) % devs) for d in ring])  0.94 us
  transfers between devices with their start and end apart: 5, of which 0 were waited for; matrix products, arithmetic and copies ran while one was open for 0% of the time, Pallas kernels for 14%

profile of v4, /device:TPU:0, one launch (start us, length us, event | category | flops | bytes accessed | tf_op | source)
XLA Modules:
  0.0 41.8 jit_solution(16201673571307065459)
XLA Ops:
  0.0 2.8 %up.1 = (bf16[8,4,16,128]{3,2,1,0:T(8,128)(2,1)}, bf16[5,16,128]{2,1,0:T(8,128)(2,1)}, bf16[6,16,128]{2,1,0:T(8,128)(2,1)}, bf16[6,16,128]{2,1,0:T(8,128)(2,1)},...) custom-call(bf16[32,16,64]{2,1,0:T(8,128)(2,1)} %vec_h.3, bf16[32,64,64]{2,1,0:T(8,128)(2,1)} %basis_h.3, ...), custom_call_target="tpu_custom_call" | custom-call | flops 10000000 | bytes 3000000 | tf_op jit(solution)/shard_map/up/pallas_call | solution.py:70
  2.8 14.6 %all_to_all.5.mine = bf16[8,4,16,128]{3,2,1,0:T(8,128)(2,1)S(1)} all-to-all(bf16[8,4,16,128]{3,2,1,0:T(8,128)(2,1)} %get-tuple-element.16), channel_id=1, replica_groups=mesh['groups'=2,'row'=8,'col'=2] {'row'}, dimensions={0} | all-to-all | bytes 262144 | tf_op jit(solution)/shard_map/all_to_all | solution.py:347
  17.4 0.0 copy-start
  17.4 0.0 collective-permute-start.4
  17.4 0.5 %collective-permute-start = (bf16[6,16,128]{2,1,0:T(8,128)(2,1)}, bf16[6,16,128]{2,1,0:T(8,128)(2,1)S(1)}, u32[]{:S(2)}, u32[]{:S(2)}) collective-permute-start(bf16[6,16,128]{2,1,0:T(8,128)(2,1)} %get-tuple-element.12), channel_id=1, source_target_pairs={{0,1},{1,0},{2,3},{3,2},{4,5},{5,4},{6,7},{7,6},{8,9},{9,8},{10,11... | collective-permute-start | bytes 73736 | tf_op jit(solution)/shard_map/ppermute | solution.py:349
  17.9 0.7 %collective-permute-start.1 = (bf16[6,16,128]{2,1,0:T(8,128)(2,1)}, bf16[6,16,128]{2,1,0:T(8,128)(2,1)S(1)}, u32[]{:S(2)}, u32[]{:S(2)}) collective-permute-start(bf16[6,16,128]{2,1,0:T(8,128)(2,1)} %get-tuple-element.13), channel_id=1, source_target_pairs={{0,15},{1,2},{2,1},{3,4},{4,3},{5,6},{6,5},{7,8},{8,7},{9,10},{10,... | collective-permute-start | bytes 73736 | tf_op jit(solution)/shard_map/ppermute | solution.py:350
  18.6 0.9 %collective-permute-start.2 = (bf16[5,16,128]{2,1,0:T(8,128)(2,1)}, bf16[5,16,128]{2,1,0:T(8,128)(2,1)S(1)}, u32[]{:S(2)}, u32[]{:S(2)}) collective-permute-start(bf16[5,16,128]{2,1,0:T(8,128)(2,1)} %get-tuple-element.14), channel_id=1, source_target_pairs={{0,2},{1,3},{2,4},{3,5},{4,6},{5,7},{6,8},{7,9},{8,10},{9,11},{10,... | collective-permute-start | bytes 61448 | tf_op jit(solution)/shard_map/ppermute | solution.py:351
  19.6 3.8 %collective-permute-start.3 = (bf16[5,16,128]{2,1,0:T(8,128)(2,1)}, bf16[5,16,128]{2,1,0:T(8,128)(2,1)S(1)}, u32[]{:S(2)}, u32[]{:S(2)}) collective-permute-start(bf16[5,16,128]{2,1,0:T(8,128)(2,1)} %get-tuple-element.15), channel_id=1, source_target_pairs={{0,14},{1,15},{2,0},{3,1},{4,2},{5,3},{6,4},{7,5},{8,6},{9,7},{10,... | collective-permute-start | bytes 61448 | tf_op jit(solution)/shard_map/ppermute | solution.py:352
  23.4 5.8 %near.1 = f32[32,48,64]{2,1,0:T(8,128)} custom-call(bf16[32,16,64]{2,1,0:T(8,128)(2,1)} %vec_h.3, bf16[3,32,3,64,64]{4,3,2,1,0:T(8,128)(2,1)} %near_h.1, s32[3,32]{1,0:T(4,128)} %bitcast.5), custom_call_target="tpu_custom_call" | custom-call | flops 40000000 | bytes 12000000 | tf_op jit(solution)/shard_map/near/pallas_call | solution.py:70
  29.1 0.0 collective-permute-done.2.fwd
  29.1 0.0 copy-start.4
  29.1 0.0 collective-permute-done.3.back
  29.2 0.0 copy-start.5
  29.2 0.0 collective-permute-done.sib
  29.2 0.0 copy-start.2
  29.2 0.0 collective-permute-done.1.cross
  29.2 0.0 copy-start.3
  29.2 0.0 collective-permute-done.4.theirs
  29.2 0.0 copy-start.1
  29.2 0.0 copy-done
  29.2 0.5 %copy-done.4 = bf16[5,16,128]{2,1,0:T(8,128)(2,1)} copy-done((bf16[5,16,128]{2,1,0:T(8,128)(2,1)}, bf16[5,16,128]{2,1,0:T(8,128)(2,1)S(1)}, u32[]{:S(2)}) %copy-start.4) | copy-done | bytes 20504
  29.7 0.0 copy-done.5
  29.8 0.0 copy-done.2
  29.8 0.0 copy-done.3
  29.8 0.1 copy-done.1
  29.9 11.9 %rest.1 = bf16[3,32,16,64]{3,2,1,0:T(8,128)(2,1)} custom-call(bf16[3,32,4,64,64]{4,3,2,1,0:T(8,128)(2,1)} %leaf_h.1, bf16[3,16,4,64,64]{4,3,2,1,0:T(8,128)(2,1)} %pair_h.1, bf16[3,8,8,64,64]{4,3,2,1,0:T(8,128)(2,1)} %coupling_h.1, bf16[3,32,3,64,64]{4,3,2,1,0:T(8,128)(2,1)} %near_h.1, bf16[16,64,64]{2,1,0:T(8,128)(2,1)} %ptr_h.3, bf16[32,64,64]{2,1,0:T(8,128)(2,1)} %ltr_h.3, ...), custom_call_target="tpu_custom_call" | custom-call | flops 100000000 | bytes 20000000 | tf_op jit(solution)/shard_map/rest/pallas_call | solution.py:70
Async XLA Ops:
  17.4 11.8 %copy-start = (bf16[8,4,16,128]{3,2,1,0:T(8,128)(2,1)}, bf16[8,4,16,128]{3,2,1,0:T(8,128)(2,1)S(1)}, u32[]{:S(2)}) copy-start(bf16[8,4,16,128]{3,2,1,0:T(8,128)(2,1)S(1)} %all_to_all.5.mine) | copy-start | bytes 393220
  17.4 11.8 %collective-permute-start.4 = (bf16[8,4,16,128]{3,2,1,0:T(8,128)(2,1)S(1)}, bf16[8,4,16,128]{3,2,1,0:T(8,128)(2,1)S(1)}, u32[]{:S(2)}, u32[]{:S(2)}) collective-permute-start(bf16[8,4,16,128]{3,2,1,0:T(8,128)(2,1)S(1)} %all_to_all.5.mine), channel_id=1, source_target_pairs={{0,1},{1,0},{2,3},{3,2},{4,5},{5,4},{6,7},{7,6},{8,9},{9,8},{10,11... | collective-permute-start | bytes 393224 | tf_op jit(solution)/shard_map/ppermute | solution.py:348
  17.4 11.7 %collective-permute-start = (bf16[6,16,128]{2,1,0:T(8,128)(2,1)}, bf16[6,16,128]{2,1,0:T(8,128)(2,1)S(1)}, u32[]{:S(2)}, u32[]{:S(2)}) collective-permute-start(bf16[6,16,128]{2,1,0:T(8,128)(2,1)} %get-tuple-element.12), channel_id=1, source_target_pairs={{0,1},{1,0},{2,3},{3,2},{4,5},{5,4},{6,7},{7,6},{8,9},{9,8},{10,11... | collective-permute-start | bytes 73736 | tf_op jit(solution)/shard_map/ppermute | solution.py:349
  17.9 11.3 %collective-permute-start.1 = (bf16[6,16,128]{2,1,0:T(8,128)(2,1)}, bf16[6,16,128]{2,1,0:T(8,128)(2,1)S(1)}, u32[]{:S(2)}, u32[]{:S(2)}) collective-permute-start(bf16[6,16,128]{2,1,0:T(8,128)(2,1)} %get-tuple-element.13), channel_id=1, source_target_pairs={{0,15},{1,2},{2,1},{3,4},{4,3},{5,6},{6,5},{7,8},{8,7},{9,10},{10,... | collective-permute-start | bytes 73736 | tf_op jit(solution)/shard_map/ppermute | solution.py:350
  18.6 10.5 %collective-permute-start.2 = (bf16[5,16,128]{2,1,0:T(8,128)(2,1)}, bf16[5,16,128]{2,1,0:T(8,128)(2,1)S(1)}, u32[]{:S(2)}, u32[]{:S(2)}) collective-permute-start(bf16[5,16,128]{2,1,0:T(8,128)(2,1)} %get-tuple-element.14), channel_id=1, source_target_pairs={{0,2},{1,3},{2,4},{3,5},{4,6},{5,7},{6,8},{7,9},{8,10},{9,11},{10,... | collective-permute-start | bytes 61448 | tf_op jit(solution)/shard_map/ppermute | solution.py:351
  19.6 9.6 %collective-permute-start.3 = (bf16[5,16,128]{2,1,0:T(8,128)(2,1)}, bf16[5,16,128]{2,1,0:T(8,128)(2,1)S(1)}, u32[]{:S(2)}, u32[]{:S(2)}) collective-permute-start(bf16[5,16,128]{2,1,0:T(8,128)(2,1)} %get-tuple-element.15), channel_id=1, source_target_pairs={{0,14},{1,15},{2,0},{3,1},{4,2},{5,3},{6,4},{7,5},{8,6},{9,7},{10,... | collective-permute-start | bytes 61448 | tf_op jit(solution)/shard_map/ppermute | solution.py:352
  29.1 0.6 %copy-start.4 = (bf16[5,16,128]{2,1,0:T(8,128)(2,1)}, bf16[5,16,128]{2,1,0:T(8,128)(2,1)S(1)}, u32[]{:S(2)}) copy-start(bf16[5,16,128]{2,1,0:T(8,128)(2,1)S(1)} %collective-permute-done.2.fwd) | copy-start | bytes 61444
  29.2 0.6 %copy-start.5 = (bf16[5,16,128]{2,1,0:T(8,128)(2,1)}, bf16[5,16,128]{2,1,0:T(8,128)(2,1)S(1)}, u32[]{:S(2)}) copy-start(bf16[5,16,128]{2,1,0:T(8,128)(2,1)S(1)} %collective-permute-done.3.back) | copy-start | bytes 61444
  29.2 0.6 %copy-start.2 = (bf16[6,16,128]{2,1,0:T(8,128)(2,1)}, bf16[6,16,128]{2,1,0:T(8,128)(2,1)S(1)}, u32[]{:S(2)}) copy-start(bf16[6,16,128]{2,1,0:T(8,128)(2,1)S(1)} %collective-permute-done.sib) | copy-start | bytes 73732
  29.2 0.6 %copy-start.3 = (bf16[6,16,128]{2,1,0:T(8,128)(2,1)}, bf16[6,16,128]{2,1,0:T(8,128)(2,1)S(1)}, u32[]{:S(2)}) copy-start(bf16[6,16,128]{2,1,0:T(8,128)(2,1)S(1)} %collective-permute-done.1.cross) | copy-start | bytes 73732
  29.2 0.6 %copy-start.1 = (bf16[8,4,16,128]{3,2,1,0:T(8,128)(2,1)}, bf16[8,4,16,128]{3,2,1,0:T(8,128)(2,1)S(1)}, u32[]{:S(2)}) copy-start(bf16[8,4,16,128]{3,2,1,0:T(8,128)(2,1)S(1)} %collective-permute-done.4.theirs) | copy-start | bytes 393220

commit v5 on v4

--- a/solution.py
+++ b/solution.py
@@ -52,12 +52,23 @@
     return made
 
 
+class Chunk:
+    def __init__(self, src, dst, sems, size, c):
+        self.src, self.dst, self.sem = src, dst, sems.at[c]
+        self.part = pl.ds(c * size, size)
+
+    def start(self, turn):
+        for k in range(self.dst.shape[0]):
+            pltpu.make_async_copy(
+                self.src.at[k, self.part], self.dst.at[k, self.part], self.sem
+            ).start(priority=(turn + k) % 2)
+
+    def wait(self):
+        pltpu.make_async_copy(self.src.at[:, self.part], self.dst.at[:, self.part], self.sem).wait()
+
+
 def chunk_of(src, dst, sems, size):
-    def chunk(c):
-        part = pl.ds(c * size, size)
-        return pltpu.make_async_copy(src.at[:, part], dst.at[:, part], sems.at[c])
-
-    return chunk
+    return lambda c: Chunk(src, dst, sems, size, c)
 
 
 def split(row, ref, at):
@@ -160,7 +171,7 @@
     made = copies([(vec_h, padded.at[pl.ds(HW, leaves)]), (offsets_h, offsets)], sems)
     chunk = chunk_of(blocks_h, blocks, chunk_sems, per)
     for c in range(chunks):
-        chunk(c).start()
+        chunk(c).start(c)
     zero = jnp.zeros((HW, vecs, rank), BF)
     padded[0:HW] = zero
     padded[HW + leaves:] = zero
@@ -216,10 +227,10 @@
     pair_chunk = chunk_of(pair_h, pair, pair_sems, per // 2)
     top_chunk = chunk_of(coupling_h, coupling, top_sems, 1)
     for c in range(chunks):
-        leaf_chunk(c).start()
-        pair_chunk(c).start()
+        leaf_chunk(c).start(c)
+        pair_chunk(c).start(c + 1)
     for c in range(count):
-        top_chunk(c).start()
+        top_chunk(c).start(c)
     others = copies(
         [
             (near_h.at[:, pl.ds(0, heads)], first), (near_h.at[:, pl.ds(leaves - heads, heads)], last),

time: 42.1 us -> 42.9 us (1.019)
  Pallas kernels: 20.5 us -> 21.4 us
    pallas_call x3, Pallas kernels: 20.5 us -> 21.4 us  [call(): pl.pallas_call(body, out_shape=out_shape, in_specs=[FIXED] * len(params)...]
where the time goes in v5:
time: 42.9 us; the launch traced here: 42.7 us
  Pallas kernels  21.4 us (50%)
  blocking collectives  14.6 us (34%)
  starting transfers between devices  5.93 us (14%)
  local copies, waits for them, and re-layouts  0.64 us (1%)
    pallas_call x3, Pallas kernels, call(): pl.pallas_call(body, out_shape=out_shape, in_specs=[FIXED] * len(params)...  21.4 us
    all_to_all x1, blocking collectives, on_device(): mine = lax.all_to_all(tops, 'row', split_axis=0, concat_axis=0)  14.6 us
    ppermute x1, starting transfers between devices, on_device(): back = lax.ppermute(back, AXES, [(d, (d - 2) % devs) for d in ring])  3.78 us
    ppermute x1, starting transfers between devices, on_device(): fwd = lax.ppermute(fwd, AXES, [(d, (d + 2) % devs) for d in ring])  0.94 us
  transfers between devices with their start and end apart: 5, of which 0 were waited for; matrix products, arithmetic and copies ran while one was open for 0% of the time, Pallas kernels for 14%

profile of v5, /device:TPU:0, one launch (start us, length us, event | category | flops | bytes accessed | tf_op | source)
XLA Modules:
  0.0 42.7 jit_solution(12932470230844792765)
XLA Ops:
  0.0 2.8 %up.1 = (bf16[8,4,16,128]{3,2,1,0:T(8,128)(2,1)}, bf16[5,16,128]{2,1,0:T(8,128)(2,1)}, bf16[6,16,128]{2,1,0:T(8,128)(2,1)}, bf16[6,16,128]{2,1,0:T(8,128)(2,1)},...) custom-call(bf16[32,16,64]{2,1,0:T(8,128)(2,1)} %vec_h.3, bf16[32,64,64]{2,1,0:T(8,128)(2,1)} %basis_h.3, ...), custom_call_target="tpu_custom_call" | custom-call | flops 10000000 | bytes 3000000 | tf_op jit(solution)/shard_map/up/pallas_call | solution.py:81
  2.8 14.6 %all_to_all.5.mine = bf16[8,4,16,128]{3,2,1,0:T(8,128)(2,1)S(1)} all-to-all(bf16[8,4,16,128]{3,2,1,0:T(8,128)(2,1)} %get-tuple-element.16), channel_id=1, replica_groups=mesh['groups'=2,'row'=8,'col'=2] {'row'}, dimensions={0} | all-to-all | bytes 262144 | tf_op jit(solution)/shard_map/all_to_all | solution.py:358
  17.4 0.0 copy-start
  17.4 0.0 collective-permute-start.4
  17.4 0.5 %collective-permute-start = (bf16[6,16,128]{2,1,0:T(8,128)(2,1)}, bf16[6,16,128]{2,1,0:T(8,128)(2,1)S(1)}, u32[]{:S(2)}, u32[]{:S(2)}) collective-permute-start(bf16[6,16,128]{2,1,0:T(8,128)(2,1)} %get-tuple-element.12), channel_id=1, source_target_pairs={{0,1},{1,0},{2,3},{3,2},{4,5},{5,4},{6,7},{7,6},{8,9},{9,8},{10,11... | collective-permute-start | bytes 73736 | tf_op jit(solution)/shard_map/ppermute | solution.py:360
  17.9 0.7 %collective-permute-start.1 = (bf16[6,16,128]{2,1,0:T(8,128)(2,1)}, bf16[6,16,128]{2,1,0:T(8,128)(2,1)S(1)}, u32[]{:S(2)}, u32[]{:S(2)}) collective-permute-start(bf16[6,16,128]{2,1,0:T(8,128)(2,1)} %get-tuple-element.13), channel_id=1, source_target_pairs={{0,15},{1,2},{2,1},{3,4},{4,3},{5,6},{6,5},{7,8},{8,7},{9,10},{10,... | collective-permute-start | bytes 73736 | tf_op jit(solution)/shard_map/ppermute | solution.py:361
  18.6 0.9 %collective-permute-start.2 = (bf16[5,16,128]{2,1,0:T(8,128)(2,1)}, bf16[5,16,128]{2,1,0:T(8,128)(2,1)S(1)}, u32[]{:S(2)}, u32[]{:S(2)}) collective-permute-start(bf16[5,16,128]{2,1,0:T(8,128)(2,1)} %get-tuple-element.14), channel_id=1, source_target_pairs={{0,2},{1,3},{2,4},{3,5},{4,6},{5,7},{6,8},{7,9},{8,10},{9,11},{10,... | collective-permute-start | bytes 61448 | tf_op jit(solution)/shard_map/ppermute | solution.py:362
  19.6 3.8 %collective-permute-start.3 = (bf16[5,16,128]{2,1,0:T(8,128)(2,1)}, bf16[5,16,128]{2,1,0:T(8,128)(2,1)S(1)}, u32[]{:S(2)}, u32[]{:S(2)}) collective-permute-start(bf16[5,16,128]{2,1,0:T(8,128)(2,1)} %get-tuple-element.15), channel_id=1, source_target_pairs={{0,14},{1,15},{2,0},{3,1},{4,2},{5,3},{6,4},{7,5},{8,6},{9,7},{10,... | collective-permute-start | bytes 61448 | tf_op jit(solution)/shard_map/ppermute | solution.py:363
  23.4 5.9 %near.1 = f32[32,48,64]{2,1,0:T(8,128)} custom-call(bf16[32,16,64]{2,1,0:T(8,128)(2,1)} %vec_h.3, bf16[3,32,3,64,64]{4,3,2,1,0:T(8,128)(2,1)} %near_h.1, s32[3,32]{1,0:T(4,128)} %bitcast.5), custom_call_target="tpu_custom_call" | custom-call | flops 40000000 | bytes 12000000 | tf_op jit(solution)/shard_map/near/pallas_call | solution.py:81
  29.2 0.0 collective-permute-done.2.fwd
  29.3 0.0 copy-start.4
  29.3 0.0 collective-permute-done.3.back
  29.3 0.0 copy-start.5
  29.3 0.0 collective-permute-done.sib
  29.3 0.0 copy-start.2
  29.3 0.0 collective-permute-done.1.cross
  29.3 0.0 copy-start.3
  29.3 0.0 collective-permute-done.4.theirs
  29.3 0.0 copy-start.1
  29.3 0.0 copy-done
  29.4 0.5 %copy-done.4 = bf16[5,16,128]{2,1,0:T(8,128)(2,1)} copy-done((bf16[5,16,128]{2,1,0:T(8,128)(2,1)}, bf16[5,16,128]{2,1,0:T(8,128)(2,1)S(1)}, u32[]{:S(2)}) %copy-start.4) | copy-done | bytes 20504
  29.9 0.0 copy-done.5
  29.9 0.0 copy-done.2
  29.9 0.0 copy-done.3
  29.9 0.1 copy-done.1
  30.0 12.7 %rest.1 = bf16[3,32,16,64]{3,2,1,0:T(8,128)(2,1)} custom-call(bf16[3,32,4,64,64]{4,3,2,1,0:T(8,128)(2,1)} %leaf_h.1, bf16[3,16,4,64,64]{4,3,2,1,0:T(8,128)(2,1)} %pair_h.1, bf16[3,8,8,64,64]{4,3,2,1,0:T(8,128)(2,1)} %coupling_h.1, bf16[3,32,3,64,64]{4,3,2,1,0:T(8,128)(2,1)} %near_h.1, bf16[16,64,64]{2,1,0:T(8,128)(2,1)} %ptr_h.3, bf16[32,64,64]{2,1,0:T(8,128)(2,1)} %ltr_h.3, ...), custom_call_target="tpu_custom_call" | custom-call | flops 100000000 | bytes 20000000 | tf_op jit(solution)/shard_map/rest/pallas_call | solution.py:81
Async XLA Ops:
  17.4 11.9 %copy-start = (bf16[8,4,16,128]{3,2,1,0:T(8,128)(2,1)}, bf16[8,4,16,128]{3,2,1,0:T(8,128)(2,1)S(1)}, u32[]{:S(2)}) copy-start(bf16[8,4,16,128]{3,2,1,0:T(8,128)(2,1)S(1)} %all_to_all.5.mine) | copy-start | bytes 393220
  17.4 11.9 %collective-permute-start.4 = (bf16[8,4,16,128]{3,2,1,0:T(8,128)(2,1)S(1)}, bf16[8,4,16,128]{3,2,1,0:T(8,128)(2,1)S(1)}, u32[]{:S(2)}, u32[]{:S(2)}) collective-permute-start(bf16[8,4,16,128]{3,2,1,0:T(8,128)(2,1)S(1)} %all_to_all.5.mine), channel_id=1, source_target_pairs={{0,1},{1,0},{2,3},{3,2},{4,5},{5,4},{6,7},{7,6},{8,9},{9,8},{10,11... | collective-permute-start | bytes 393224 | tf_op jit(solution)/shard_map/ppermute | solution.py:359
  17.4 11.9 %collective-permute-start = (bf16[6,16,128]{2,1,0:T(8,128)(2,1)}, bf16[6,16,128]{2,1,0:T(8,128)(2,1)S(1)}, u32[]{:S(2)}, u32[]{:S(2)}) collective-permute-start(bf16[6,16,128]{2,1,0:T(8,128)(2,1)} %get-tuple-element.12), channel_id=1, source_target_pairs={{0,1},{1,0},{2,3},{3,2},{4,5},{5,4},{6,7},{7,6},{8,9},{9,8},{10,11... | collective-permute-start | bytes 73736 | tf_op jit(solution)/shard_map/ppermute | solution.py:360
  17.9 11.4 %collective-permute-start.1 = (bf16[6,16,128]{2,1,0:T(8,128)(2,1)}, bf16[6,16,128]{2,1,0:T(8,128)(2,1)S(1)}, u32[]{:S(2)}, u32[]{:S(2)}) collective-permute-start(bf16[6,16,128]{2,1,0:T(8,128)(2,1)} %get-tuple-element.13), channel_id=1, source_target_pairs={{0,15},{1,2},{2,1},{3,4},{4,3},{5,6},{6,5},{7,8},{8,7},{9,10},{10,... | collective-permute-start | bytes 73736 | tf_op jit(solution)/shard_map/ppermute | solution.py:361
  18.6 10.6 %collective-permute-start.2 = (bf16[5,16,128]{2,1,0:T(8,128)(2,1)}, bf16[5,16,128]{2,1,0:T(8,128)(2,1)S(1)}, u32[]{:S(2)}, u32[]{:S(2)}) collective-permute-start(bf16[5,16,128]{2,1,0:T(8,128)(2,1)} %get-tuple-element.14), channel_id=1, source_target_pairs={{0,2},{1,3},{2,4},{3,5},{4,6},{5,7},{6,8},{7,9},{8,10},{9,11},{10,... | collective-permute-start | bytes 61448 | tf_op jit(solution)/shard_map/ppermute | solution.py:362
  19.6 9.7 %collective-permute-start.3 = (bf16[5,16,128]{2,1,0:T(8,128)(2,1)}, bf16[5,16,128]{2,1,0:T(8,128)(2,1)S(1)}, u32[]{:S(2)}, u32[]{:S(2)}) collective-permute-start(bf16[5,16,128]{2,1,0:T(8,128)(2,1)} %get-tuple-element.15), channel_id=1, source_target_pairs={{0,14},{1,15},{2,0},{3,1},{4,2},{5,3},{6,4},{7,5},{8,6},{9,7},{10,... | collective-permute-start | bytes 61448 | tf_op jit(solution)/shard_map/ppermute | solution.py:363
  29.3 0.6 %copy-start.4 = (bf16[5,16,128]{2,1,0:T(8,128)(2,1)}, bf16[5,16,128]{2,1,0:T(8,128)(2,1)S(1)}, u32[]{:S(2)}) copy-start(bf16[5,16,128]{2,1,0:T(8,128)(2,1)S(1)} %collective-permute-done.2.fwd) | copy-start | bytes 61444
  29.3 0.6 %copy-start.5 = (bf16[5,16,128]{2,1,0:T(8,128)(2,1)}, bf16[5,16,128]{2,1,0:T(8,128)(2,1)S(1)}, u32[]{:S(2)}) copy-start(bf16[5,16,128]{2,1,0:T(8,128)(2,1)S(1)} %collective-permute-done.3.back) | copy-start | bytes 61444
  29.3 0.6 %copy-start.2 = (bf16[6,16,128]{2,1,0:T(8,128)(2,1)}, bf16[6,16,128]{2,1,0:T(8,128)(2,1)S(1)}, u32[]{:S(2)}) copy-start(bf16[6,16,128]{2,1,0:T(8,128)(2,1)S(1)} %collective-permute-done.sib) | copy-start | bytes 73732
  29.3 0.6 %copy-start.3 = (bf16[6,16,128]{2,1,0:T(8,128)(2,1)}, bf16[6,16,128]{2,1,0:T(8,128)(2,1)S(1)}, u32[]{:S(2)}) copy-start(bf16[6,16,128]{2,1,0:T(8,128)(2,1)S(1)} %collective-permute-done.1.cross) | copy-start | bytes 73732
  29.3 0.6 %copy-start.1 = (bf16[8,4,16,128]{3,2,1,0:T(8,128)(2,1)}, bf16[8,4,16,128]{3,2,1,0:T(8,128)(2,1)S(1)}, u32[]{:S(2)}) copy-start(bf16[8,4,16,128]{3,2,1,0:T(8,128)(2,1)S(1)} %collective-permute-done.4.theirs) | copy-start | bytes 393220

commit v6 on v4

v6 whole, which is shorter than its diff:
```python
import jax
import jax.numpy as jnp
from jax import lax
from jax.experimental import pallas as pl
from jax.experimental.pallas import tpu as pltpu
from jax.sharding import PartitionSpec as P

REACH = 2
WIN = 2 * REACH + 1
HW = 2
GROUP = 8
AXES = ("row", "col")
F32 = jnp.float32
BF = jnp.bfloat16
LIMIT = 56 * 1024 * 1024

VMEM = pltpu.VMEM
SMEM = pltpu.SMEM
DMA = pltpu.SemaphoreType.DMA
FIXED = pl.BlockSpec(memory_space=pltpu.HBM)
WHOLE = pl.BlockSpec(memory_space=VMEM)


def dot(left, right):
    return jnp.dot(left, right, preferred_element_type=F32)


def beside(*parts):
    return jnp.concatenate(parts, axis=1)


def above(*parts):
    return jnp.concatenate(parts, axis=0)


def dot_t(left, right):
    return lax.dot_general(left, right, (((1,), (1,)), ((), ())), preferred_element_type=F32)


def row_of_blocks(ref, q):
    kernels, _, partners, _, _ = ref.shape
    return beside(*[above(*[ref[k, q, m] for k in range(kernels)]) for m in range(partners)])


def by_kernel(wide, rank):
    return above(*[wide[:, k * rank:(k + 1) * rank] for k in range(wide.shape[1] // rank)])


def copies(pairs, sems):
    made = [pltpu.make_async_copy(src, dst, sems.at[i]) for i, (src, dst) in enumerate(pairs)]
    for copy in made:
        copy.start()
    return made


def split(row, ref, at):
    rank = row.shape[1] // 2
    ref[at] = row[:, :rank]
    ref[at + 1] = row[:, rank:]


def call(body, name, params, arrays, out_shape, out_specs, scratch, cost, limit=LIMIT):
    return pl.pallas_call(
        body,
        out_shape=out_shape,
        in_specs=[FIXED] * len(params) + [WHOLE] * len(arrays),
        out_specs=out_specs,
        scratch_shapes=scratch,
        compiler_params=pltpu.CompilerParams(vmem_limit_bytes=limit),
        cost_estimate=pl.CostEstimate(flops=cost[0], bytes_accessed=cost[1], transcendentals=0),
        name=name,
    )(*params, *arrays)


def like(x):
    return VMEM(x.shape, x.dtype)


def held(x):
    return SMEM(x.shape, x.dtype)


def up_body(vec_h, basis_h, ltr_h, ptr_h, lsend_h, psend_h, tops, own, sib, cross, fwd, back,
            vec, basis, ltr, ptr, lsend, psend, low, mid, sems):
    leaves, vecs, rank = vec.shape
    col = lax.axis_index("col")
    cap0 = lsend.shape[2]
    cap1 = psend.shape[1]
    made = copies(
        [(vec_h, vec), (basis_h, basis), (ltr_h, ltr), (ptr_h, ptr), (lsend_h, lsend), (psend_h, psend)], sems
    )
    made[0].wait()
    made[1].wait()
    for t in range(leaves):
        low[t] = dot(vec[t], basis[t]).astype(BF)
    made[2].wait()
    for j in range(leaves // 2):
        mid[j] = dot(
            beside(low[2 * j], low[2 * j + 1]), ltr[2 * j:2 * j + 2].reshape(2 * rank, rank)
        ).astype(BF)
    made[3].wait()
    high = []
    for i in range(leaves // 4):
        high.append(
            dot(beside(mid[2 * i], mid[2 * i + 1]), ptr[2 * i:2 * i + 2].reshape(2 * rank, rank)).astype(BF)
        )
    for i in range(leaves // 8):
        both = beside(high[2 * i], high[2 * i + 1])
        for row in range(tops.shape[0]):
            tops[row, i] = both
    made[4].wait()
    made[5].wait()

    def pack(out, place):
        for c in range(cap0 // 2):
            out[c] = beside(low[lsend[place, 0, 2 * c]], low[lsend[place, 0, 2 * c + 1]])
        for c in range(cap1 // 2):
            out[cap0 // 2 + c] = beside(mid[psend[0, 2 * c, place]], mid[psend[0, 2 * c + 1, place]])

    def pack_halo(out, start):
        out[(cap0 + cap1) // 2] = beside(vec[start], vec[start + 1])

    pack(sib, 1 + 2 * col)
    pack_halo(sib, (1 - col) * (leaves - HW))
    pack(cross, 3 - 2 * col)
    pack_halo(cross, col * (leaves - HW))
    pack(fwd, 0)
    pack(back, 4)
    pack(own, REACH)


def up_pass(lsend, psend, vec, basis, ltr, ptr, rows):
    leaves, vecs, rank = vec.shape
    count = (lsend.shape[2] + psend.shape[1]) // 2
    shape = lambda *n: jax.ShapeDtypeStruct(n + (vecs, 2 * rank), BF)
    return call(
        up_body, "up", (vec, basis, ltr, ptr, lsend, psend), (),
        [shape(rows, leaves // 8), shape(count), shape(count + 1), shape(count + 1), shape(count), shape(count)],
        [WHOLE] * 6,
        [
            like(vec), like(basis), like(ltr), like(ptr), held(lsend), held(psend),
            VMEM((leaves, vecs, rank), BF), VMEM((leaves // 2, vecs, rank), BF), DMA((6,)),
        ],
        (10_000_000, 3_000_000),
    )


def near_body(offsets_h, vec, near, close, ends, padded, offsets, sems):
    leaves, vecs, rank = vec.shape
    kernels = near.shape[0]
    made = copies([(offsets_h, offsets)], sems)
    ends[:, 0:HW] = near[:, 0:HW]
    ends[:, HW:] = near[:, leaves - HW:]
    zero = jnp.zeros((HW, vecs, rank), BF)
    padded[0:HW] = zero
    padded[HW:HW + leaves] = vec[...]
    padded[HW + leaves:] = zero
    made[0].wait()

    def body(c, _):
        for q in range(GROUP):
            t = c * GROUP + q
            total = None
            for n in range(near.shape[2]):
                part = dot_t(padded[t + HW + offsets[n, t]], above(*[near[k, t, n] for k in range(kernels)]))
                total = part if total is None else total + part
            close[t] = by_kernel(total, rank)
        return 0

    lax.fori_loop(0, leaves // GROUP, body, 0)


def near_pass(offsets, vec, blocks):
    kernels, leaves, near, rank, _ = blocks.shape
    vecs = vec.shape[1]
    return call(
        near_body, "near", (offsets,), (vec, blocks),
        [
            jax.ShapeDtypeStruct((leaves, kernels * vecs, rank), F32),
            jax.ShapeDtypeStruct((kernels, 2 * HW) + blocks.shape[2:], BF),
        ],
        [WHOLE] * 2,
        [VMEM((leaves + 2 * HW, vecs, rank), BF), held(offsets), DMA((1,))],
        (4_000_000_000, 60_000_000), 8 * 1024 * 1024,
    )


def far_sum(rows, blocks, q):
    return dot_t(beside(*rows), row_of_blocks(blocks, q))


def rest_body(llist_h, plist_h, tlist_h, offsets_h,
              leaf, pair, coupling, ends, ptr, ltr, basis, close, own, sib, cross, fwd, back, mine, theirs, out,
              llist, plist, tlist, offsets, wleaf, wpair, halo, tops, far0, far1, down, sems):
    kernels, leaves, partners, rank, _ = leaf.shape
    _, vecs, _ = wleaf.shape
    count = coupling.shape[1]
    cap0 = wleaf.shape[0] // WIN
    cap1 = wpair.shape[0] // WIN
    base = own.shape[0] - cap1 // 2
    col = lax.axis_index("col")
    place = lax.axis_index("row") * lax.axis_size("col") + col
    last_place = lax.axis_size("row") * lax.axis_size("col") - 1
    lists = copies([(llist_h, llist), (plist_h, plist), (tlist_h, tlist), (offsets_h, offsets)], sems)

    for block, slot in ((own, REACH), (fwd, 0), (back, 4), (sib, 3 - 2 * col), (cross, 1 + 2 * col)):
        for c in range(cap0 // 2):
            split(block[c], wleaf, slot * cap0 + 2 * c)
        for c in range(cap1 // 2):
            split(block[base + c], wpair, slot * cap1 + 2 * c)
    halo[2 * HW] = jnp.zeros((vecs, rank), BF)
    for block, upper in ((sib, 1 - col), (cross, col)):
        row = block[base + cap1 // 2]
        outside = (place == 0) & (upper == 0) | (place == last_place) & (upper == 1)
        split(jnp.where(outside, jnp.zeros_like(row), row), halo, upper * HW)
    for block, side in ((mine, col), (theirs, 1 - col)):
        for s in range(block.shape[0]):
            for i in range(block.shape[1]):
                split(block[s, i], tops, (s * 2 + side) * count + 2 * i)
    for copy in lists:
        copy.wait()

    def body(c, _):
        for q in range(GROUP):
            t = c * GROUP + q
            far0[t] = by_kernel(far_sum([wleaf[llist[m, t]] for m in range(partners)], leaf, t), rank)
        for q in range(GROUP // 2):
            j = c * (GROUP // 2) + q
            far1[j] = by_kernel(far_sum([wpair[plist[m, j]] for m in range(pair.shape[2])], pair, j), rank)
        for q in range(GROUP // 4):
            i = c * (GROUP // 4) + q
            rows = [tops[tlist[i, m]] for m in range(coupling.shape[2])]
            down[i] = by_kernel(far_sum(rows, coupling, i), rank).astype(BF)
        return 0

    lax.fori_loop(0, leaves // GROUP, body, 0)

    def edge(t):
        spots = [t + offsets[n, t] for n in range(ends.shape[2])]
        if t < HW:
            spots = [jnp.where(at < 0, at + HW, 2 * HW) for at in spots]
        else:
            spots = [jnp.where(at >= leaves, at - leaves + HW, 2 * HW) for at in spots]
        return by_kernel(far_sum([halo[at] for at in spots], ends, t if t < HW else t - (leaves - 2 * HW)), rank)

    down1 = []
    for j in range(2 * count):
        down1.append((far1[j] + dot_t(down[j // 2], ptr[j])).astype(BF))
    down0 = []
    for t in range(leaves):
        down0.append((far0[t] + dot_t(down1[t // 2], ltr[t])).astype(BF))
    for t in range(leaves):
        points = dot_t(down0[t], basis[t]) + close[t]
        if t < HW or t >= leaves - HW:
            points = points + edge(t)
        points = points.astype(BF)
        for k in range(kernels):
            out[k, t] = points[k * vecs:(k + 1) * vecs]


def rest_pass(lists, arrays, windows, cap0, cap1):
    leaf, pair, coupling = arrays[:3]
    kernels, leaves, _, rank, _ = leaf.shape
    count = coupling.shape[1]
    vecs = windows[0].shape[1]
    rows = kernels * vecs
    return call(
        rest_body, "rest", lists, arrays + windows,
        jax.ShapeDtypeStruct((kernels, leaves, vecs, rank), BF),
        WHOLE,
        [held(x) for x in lists]
        + [
            VMEM((n, vecs, rank), BF)
            for n in (WIN * cap0, WIN * cap1, 2 * HW + 1, 2 * windows[-1].shape[0] * count)
        ]
        + [
            VMEM((leaves, rows, rank), F32), VMEM((leaves // 2, rows, rank), F32),
            VMEM((count, rows, rank), BF), DMA((4,)),
        ],
        (150_000_000, 20_000_000), 16 * 1024 * 1024,
    )


def on_device(
    vectors,
    leaf_basis,
    leaf_transfer,
    pair_transfer,
    near_blocks,
    near_offset,
    leaf_send,
    leaf_list,
    leaf_coupling,
    pair_send,
    pair_list,
    pair_coupling,
    top_list,
    top_coupling,
):
    rows = lax.axis_size("row")
    devs = rows * lax.axis_size("col")
    cap0, cap1 = leaf_send.shape[2], pair_send.shape[2]
    lsend = jnp.transpose(leaf_send, (1, 0, 2))
    psend = jnp.transpose(pair_send, (0, 2, 1))
    tops, own, sib, cross, fwd, back = up_pass(
        lsend, psend, vectors, leaf_basis, leaf_transfer, pair_transfer, rows
    )
    ring = range(devs)
    sibling = [(d, d ^ 1) for d in ring]
    mine = lax.all_to_all(tops, "row", split_axis=0, concat_axis=0)
    theirs = lax.ppermute(mine, AXES, sibling)
    sib = lax.ppermute(sib, AXES, sibling)
    cross = lax.ppermute(cross, AXES, [(d, (d + 1 if d % 2 else d - 1) % devs) for d in ring])
    fwd = lax.ppermute(fwd, AXES, [(d, (d + 2) % devs) for d in ring])
    back = lax.ppermute(back, AXES, [(d, (d - 2) % devs) for d in ring])
    close, ends = near_pass(near_offset.T, vectors, near_blocks)
    return rest_pass(
        (leaf_list.T, pair_list.T, top_list, near_offset.T),
        (leaf_coupling, pair_coupling, top_coupling, ends, pair_transfer, leaf_transfer, leaf_basis, close),
        (own, sib, cross, fwd, back, mine, theirs), cap0, cap1,
    )


def solution(mesh):
    placed = P(("groups", "row", "col"))
    behind = P(None, ("groups", "row", "col"))
    return jax.shard_map(
        on_device,
        mesh=mesh,
        in_specs=(
            placed, placed, placed, placed, behind, placed, placed, placed, behind, placed, placed, behind, placed, behind,
        ),
        out_specs=behind,
        check_vma=False,
    )
```

time: 42.1 us -> 31.7 us (0.75)
  blocking collectives: 14.6 us -> 0 us
  Pallas kernels: 20.5 us -> 12 us
  starting transfers between devices: 5.93 us -> 14.3 us
  local copies, waits for them, and re-layouts: 0.64 us -> 4.37 us
  waiting for transfers between devices: 0.01 us -> 0.49 us
    all_to_all x1 -> x0, blocking collectives: 14.6 us -> none  [on_device(): mine = lax.all_to_all(tops, 'row', split_axis=0, concat_axis=0)]
    pallas_call x3, Pallas kernels: 20.5 us -> 12 us  [call(): pl.pallas_call(body, out_shape=out_shape, in_specs=[FIXED] * len(params)...]
    all_to_all x0 -> x1, starting transfers between devices: none -> 7.42 us  [on_device(): mine = lax.all_to_all(tops, 'row', split_axis=0, concat_axis=0)]
    unnamed x12 -> x30, local copies, waits for them, and re-layouts: 0.64 us -> 4.37 us
    ppermute x1, starting transfers between devices: 0.69 us -> 2.11 us  [on_device(): lax.ppermute(cross, AXES, [(d, (d + 1 if d % 2 else d - 1) % devs) for d...]
    ppermute x1, starting transfers between devices: 0.94 us -> 2.02 us  [on_device(): fwd = lax.ppermute(fwd, AXES, [(d, (d + 2) % devs) for d in ring])]
    ppermute x1, starting transfers between devices: 3.78 us -> 2.73 us  [on_device(): back = lax.ppermute(back, AXES, [(d, (d - 2) % devs) for d in ring])]
    ppermute x1, starting transfers between devices: 0.51 us -> 0.01 us  [on_device(): sib = lax.ppermute(sib, AXES, sibling)]
  transfers between devices with their start and end apart: 5 -> 6, of which waited for: 0 -> 1; matrix products, arithmetic and copies ran while one was open for 0% -> 0% of each run, Pallas kernels for 14% -> 12%
where the time goes in v6:
time: 31.7 us; the launch traced here: 31.3 us
  starting transfers between devices  14.3 us (45%)
  Pallas kernels  12 us (38%)
  local copies, waits for them, and re-layouts  4.37 us (14%)
  waiting for transfers between devices  0.49 us (2%)
    pallas_call x3, Pallas kernels, call(): pl.pallas_call(body, out_shape=out_shape, in_specs=[FIXED] * len(params)...  12 us
    all_to_all x1, starting transfers between devices, on_device(): mine = lax.all_to_all(tops, 'row', split_axis=0, concat_axis=0)  7.42 us
    unnamed x30, local copies, waits for them, and re-layouts  4.37 us
    ppermute x1, starting transfers between devices, on_device(): back = lax.ppermute(back, AXES, [(d, (d - 2) % devs) for d in ring])  2.73 us
    ppermute x1, starting transfers between devices, on_device(): lax.ppermute(cross, AXES, [(d, (d + 1 if d % 2 else d - 1) % devs) for d...  2.11 us
    ppermute x1, starting transfers between devices, on_device(): fwd = lax.ppermute(fwd, AXES, [(d, (d + 2) % devs) for d in ring])  2.02 us
  transfers between devices with their start and end apart: 6, of which 1 were waited for; matrix products, arithmetic and copies ran while one was open for 0% of the time, Pallas kernels for 12%

profile of v6, /device:TPU:0, one launch (start us, length us, event | category | flops | bytes accessed | tf_op | source)
XLA Modules:
  0.0 31.3 jit_solution(4388584046004297448)
XLA Ops:
  0.0 2.8 %up.1 = (bf16[8,4,16,128]{3,2,1,0:T(8,128)(2,1)}, bf16[5,16,128]{2,1,0:T(8,128)(2,1)}, bf16[6,16,128]{2,1,0:T(8,128)(2,1)}, bf16[6,16,128]{2,1,0:T(8,128)(2,1)},...) custom-call(bf16[32,16,64]{2,1,0:T(8,128)(2,1)} %vec_h.1, bf16[32,64,64]{2,1,0:T(8,128)(2,1)} %basis.1, ...), custom_call_target="tpu_custom_call" | custom-call | flops 10000000 | bytes 3000000 | tf_op jit(solution)/shard_map/up/pallas_call | solution.py:63
  2.8 0.0 slice-start
  2.8 7.4 %all-to-all-start = ((bf16[8,4,16,128]{3,2,1,0:T(8,128)(2,1)}), bf16[8,4,16,128]{3,2,1,0:T(8,128)(2,1)S(1)}, u32[]{:S(2)}, u32[]{:S(2)}) async-start(bf16[8,4,16,128]{3,2,1,0:T(8,128)(2,1)} %get-tuple-element.20), calls=%async_computation | async-start | bytes 262144 | tf_op jit(solution)/shard_map/all_to_all | solution.py:310
  10.2 2.0 %collective-permute-start.2 = (bf16[5,16,128]{2,1,0:T(8,128)(2,1)}, bf16[5,16,128]{2,1,0:T(8,128)(2,1)S(1)}, u32[]{:S(2)}, u32[]{:S(2)}) collective-permute-start(bf16[5,16,128]{2,1,0:T(8,128)(2,1)} %get-tuple-element.18), channel_id=1, source_target_pairs={{0,2},{1,3},{2,4},{3,5},{4,6},{5,7},{6,8},{7,9},{8,10},{9,11},{10,... | collective-permute-start | bytes 61448 | tf_op jit(solution)/shard_map/ppermute | solution.py:314
  12.3 2.7 %collective-permute-start.3 = (bf16[5,16,128]{2,1,0:T(8,128)(2,1)}, bf16[5,16,128]{2,1,0:T(8,128)(2,1)S(1)}, u32[]{:S(2)}, u32[]{:S(2)}) collective-permute-start(bf16[5,16,128]{2,1,0:T(8,128)(2,1)} %get-tuple-element.19), channel_id=1, source_target_pairs={{0,14},{1,15},{2,0},{3,1},{4,2},{5,3},{6,4},{7,5},{8,6},{9,7},{10,... | collective-permute-start | bytes 61448 | tf_op jit(solution)/shard_map/ppermute | solution.py:315
  15.0 0.0 collective-permute-start
  15.0 2.1 %collective-permute-start.1 = (bf16[6,16,128]{2,1,0:T(8,128)(2,1)}, bf16[6,16,128]{2,1,0:T(8,128)(2,1)S(1)}, u32[]{:S(2)}, u32[]{:S(2)}) collective-permute-start(bf16[6,16,128]{2,1,0:T(8,128)(2,1)} %get-tuple-element.17), channel_id=1, source_target_pairs={{0,15},{1,2},{2,1},{3,4},{4,3},{5,6},{6,5},{7,8},{8,7},{9,10},{10,... | collective-permute-start | bytes 73736 | tf_op jit(solution)/shard_map/ppermute | solution.py:313
  17.1 0.5 %all-to-all-done.mine = bf16[8,4,16,128]{3,2,1,0:T(8,128)(2,1)S(1)} async-done(((bf16[8,4,16,128]{3,2,1,0:T(8,128)(2,1)}), bf16[8,4,16,128]{3,2,1,0:T(8,128)(2,1)S(1)}, u32[]{:S(2)}, u32[]{:S(2)}) %all-to-all-start) | async-done | bytes 131104 | tf_op jit(solution)/shard_map/all_to_all | solution.py:310
  17.6 0.0 collective-permute-start.4
  17.6 0.0 copy-start.5
  17.6 0.9 %copy-done.5 = bf16[32,16,64]{2,1,0:T(8,128)(2,1)S(1)} copy-done((bf16[32,16,64]{2,1,0:T(8,128)(2,1)S(1)}, bf16[32,16,64]{2,1,0:T(8,128)(2,1)}, u32[]{:S(2)}) %copy-start.5) | copy-done | bytes 65560
  18.5 0.0 copy-start.10
  18.5 0.7 %copy-done.10 = s32[32,3]{0,1:T(4,128)S(1)} copy-done((s32[32,3]{0,1:T(4,128)S(1)}, s32[32,3]{0,1:T(4,128)}, u32[]{:S(2)}) %copy-start.10) | copy-done | bytes 408
  19.2 0.0 copy-start.12
  19.2 2.3 %copy-done.12 = bf16[3,32,3,64,64]{4,3,2,1,0:T(8,128)(2,1)S(1)} copy-done((bf16[3,32,3,64,64]{4,3,2,1,0:T(8,128)(2,1)S(1)}, bf16[3,32,3,64,64]{4,3,2,1,0:T(8,128)(2,1)}, u32[]{:S(2)}) %copy-start.12) | copy-done | bytes 2359320
  21.5 0.0 slice-start.1
  21.5 0.0 copy-start
  21.5 0.0 copy-start.1
  21.5 0.0 copy-start.2
  21.5 0.0 copy-start.3
  21.5 0.0 copy-start.4
  21.5 0.0 copy-start.6
  21.6 0.0 copy-start.7
  21.6 0.0 copy-start.8
  21.6 0.0 copy-start.9
  21.6 0.0 copy-start.11
  21.6 3.8 %near.2 = (f32[32,48,64]{2,1,0:T(8,128)S(1)}, bf16[3,4,3,64,64]{4,3,2,1,0:T(8,128)(2,1)S(1)}) custom-call(s32[3,32]{1,0:T(4,128)S(1)} %bitcast.9, bf16[32,16,64]{2,1,0:T(8,128)(2,1)S(1)} %copy-done.5, bf16[3,32,3,64,64]{4,3,2,1,0:T(8,128)(2,1)S(1)} %copy-done.12), custom_call_target="tpu_custom_call" | custom-call | flops 4000000000 | bytes 60000000 | tf_op jit(solution)/shard_map/near/pallas_call | solution.py:63
  25.4 0.0 collective-permute-done.2.fwd
  25.4 0.0 collective-permute-done.3.back
  25.4 0.0 collective-permute-done.sib
  25.4 0.0 collective-permute-done.1.cross
  25.4 0.0 collective-permute-done.4.theirs
  25.4 0.0 slice-done
  25.4 0.0 slice-done.1
  25.4 0.0 copy-done
  25.5 0.1 copy-done.1
  25.6 0.0 copy-done.2
  25.6 0.2 copy-done.3
  25.8 0.0 copy-done.4
  25.8 0.0 copy-done.6
  25.8 0.0 copy-done.7
  25.8 0.0 copy-done.8
  25.9 0.0 copy-done.9
  25.9 0.0 copy-done.11
  25.9 5.4 %rest.1 = bf16[3,32,16,64]{3,2,1,0:T(8,128)(2,1)} custom-call(s32[4,32]{1,0:T(4,128)S(1)} %bitcast.7, s32[4,16]{1,0:T(4,128)S(1)} %bitcast.8, s32[8,8]{1,0:T(8,128)S(1)} %copy-done.7, s32[3,32]{1,0:T(4,128)S(1)} %bitcast.10, bf16[3,32,4,64,64]{4,3,2,1,0:T(8,128)(2,1)S(1)} %bitcast.6, bf16[3,16,4,64,64]{4,3,2,1,0:T(8,128)(2,1)S(1)} %copy-done, ...), custom_call_target="tpu_custom_call" | custom-call | flops 150000000 | bytes 20000000 | tf_op jit(solution)/shard_map/rest/pallas_call | solution.py:63
  (1 shorter events, 0.0 us)
Async XLA Ops:
  2.8 22.6 %slice-start = ((s8[6291456]{0:T(1024)(128)(4,1)}), s8[2097152]{0:T(1024)(128)(4,1)S(1)}, s32[]{:S(2)}) async-start(s8[6291456]{0:T(1024)(128)(4,1)} %bitcast.5), calls=%async_computation.1 | async-start | bytes 4194304
  2.8 14.8 %all-to-all-start = ((bf16[8,4,16,128]{3,2,1,0:T(8,128)(2,1)}), bf16[8,4,16,128]{3,2,1,0:T(8,128)(2,1)S(1)}, u32[]{:S(2)}, u32[]{:S(2)}) async-start(bf16[8,4,16,128]{3,2,1,0:T(8,128)(2,1)} %get-tuple-element.20), calls=%async_computation | async-start | bytes 262144 | tf_op jit(solution)/shard_map/all_to_all | solution.py:310
  10.2 15.1 %collective-permute-start.2 = (bf16[5,16,128]{2,1,0:T(8,128)(2,1)}, bf16[5,16,128]{2,1,0:T(8,128)(2,1)S(1)}, u32[]{:S(2)}, u32[]{:S(2)}) collective-permute-start(bf16[5,16,128]{2,1,0:T(8,128)(2,1)} %get-tuple-element.18), channel_id=1, source_target_pairs={{0,2},{1,3},{2,4},{3,5},{4,6},{5,7},{6,8},{7,9},{8,10},{9,11},{10,... | collective-permute-start | bytes 61448 | tf_op jit(solution)/shard_map/ppermute | solution.py:314
  12.3 13.1 %collective-permute-start.3 = (bf16[5,16,128]{2,1,0:T(8,128)(2,1)}, bf16[5,16,128]{2,1,0:T(8,128)(2,1)S(1)}, u32[]{:S(2)}, u32[]{:S(2)}) collective-permute-start(bf16[5,16,128]{2,1,0:T(8,128)(2,1)} %get-tuple-element.19), channel_id=1, source_target_pairs={{0,14},{1,15},{2,0},{3,1},{4,2},{5,3},{6,4},{7,5},{8,6},{9,7},{10,... | collective-permute-start | bytes 61448 | tf_op jit(solution)/shard_map/ppermute | solution.py:315
  15.0 10.4 %collective-permute-start = (bf16[6,16,128]{2,1,0:T(8,128)(2,1)}, bf16[6,16,128]{2,1,0:T(8,128)(2,1)S(1)}, u32[]{:S(2)}, u32[]{:S(2)}) collective-permute-start(bf16[6,16,128]{2,1,0:T(8,128)(2,1)} %get-tuple-element.16), channel_id=1, source_target_pairs={{0,1},{1,0},{2,3},{3,2},{4,5},{5,4},{6,7},{7,6},{8,9},{9,8},{10,11... | collective-permute-start | bytes 73736 | tf_op jit(solution)/shard_map/ppermute | solution.py:312
  15.0 10.4 %collective-permute-start.1 = (bf16[6,16,128]{2,1,0:T(8,128)(2,1)}, bf16[6,16,128]{2,1,0:T(8,128)(2,1)S(1)}, u32[]{:S(2)}, u32[]{:S(2)}) collective-permute-start(bf16[6,16,128]{2,1,0:T(8,128)(2,1)} %get-tuple-element.17), channel_id=1, source_target_pairs={{0,15},{1,2},{2,1},{3,4},{4,3},{5,6},{6,5},{7,8},{8,7},{9,10},{10,... | collective-permute-start | bytes 73736 | tf_op jit(solution)/shard_map/ppermute | solution.py:313
  17.6 7.8 %collective-permute-start.4 = (bf16[8,4,16,128]{3,2,1,0:T(8,128)(2,1)S(1)}, bf16[8,4,16,128]{3,2,1,0:T(8,128)(2,1)S(1)}, u32[]{:S(2)}, u32[]{:S(2)}) collective-permute-start(bf16[8,4,16,128]{3,2,1,0:T(8,128)(2,1)S(1)} %all-to-all-done.mine), channel_id=1, source_target_pairs={{0,1},{1,0},{2,3},{3,2},{4,5},{5,4},{6,7},{7,6},{8,9},{9,8},{10,11... | collective-permute-start | bytes 393224 | tf_op jit(solution)/shard_map/ppermute | solution.py:311
  17.6 0.9 %copy-start.5 = (bf16[32,16,64]{2,1,0:T(8,128)(2,1)S(1)}, bf16[32,16,64]{2,1,0:T(8,128)(2,1)}, u32[]{:S(2)}) copy-start(bf16[32,16,64]{2,1,0:T(8,128)(2,1)} %vec_h.1) | copy-start | bytes 196612
  18.5 0.7 %copy-start.10 = (s32[32,3]{0,1:T(4,128)S(1)}, s32[32,3]{0,1:T(4,128)}, u32[]{:S(2)}) copy-start(s32[32,3]{0,1:T(4,128)} %param.19) | copy-start | bytes 1156
  19.2 2.3 %copy-start.12 = (bf16[3,32,3,64,64]{4,3,2,1,0:T(8,128)(2,1)S(1)}, bf16[3,32,3,64,64]{4,3,2,1,0:T(8,128)(2,1)}, u32[]{:S(2)}) copy-start(bf16[3,32,3,64,64]{4,3,2,1,0:T(8,128)(2,1)} %near.3) | copy-start | bytes 7077892
  21.5 3.9 %slice-start.1 = ((s8[6291456]{0:T(1024)(128)(4,1)}), s8[4194304]{0:T(1024)(128)(4,1)S(1)}, s32[]{:S(2)}) async-start(s8[6291456]{0:T(1024)(128)(4,1)} %bitcast.5), calls=%async_computation.2 | async-start | bytes 8388608
  21.5 3.9 %copy-start = (bf16[3,16,4,64,64]{4,3,2,1,0:T(8,128)(2,1)S(1)}, bf16[3,16,4,64,64]{4,3,2,1,0:T(8,128)(2,1)}, u32[]{:S(2)}) copy-start(bf16[3,16,4,64,64]{4,3,2,1,0:T(8,128)(2,1)} %pair.1) | copy-start | bytes 4718596
  21.5 4.1 %copy-start.1 = (bf16[3,8,8,64,64]{4,3,2,1,0:T(8,128)(2,1)S(1)}, bf16[3,8,8,64,64]{4,3,2,1,0:T(8,128)(2,1)}, u32[]{:S(2)}) copy-start(bf16[3,8,8,64,64]{4,3,2,1,0:T(8,128)(2,1)} %coupling.1) | copy-start | bytes 4718596
  21.5 4.1 %copy-start.2 = (bf16[32,64,64]{2,1,0:T(8,128)(2,1)S(1)}, bf16[32,64,64]{2,1,0:T(8,128)(2,1)}, u32[]{:S(2)}) copy-start(bf16[32,64,64]{2,1,0:T(8,128)(2,1)} %ltr.1) | copy-start | bytes 786436
  21.5 4.3 %copy-start.3 = (bf16[32,64,64]{2,1,0:T(8,128)(2,1)S(1)}, bf16[32,64,64]{2,1,0:T(8,128)(2,1)}, u32[]{:S(2)}) copy-start(bf16[32,64,64]{2,1,0:T(8,128)(2,1)} %basis.1) | copy-start | bytes 786436
  21.5 4.3 %copy-start.4 = (bf16[16,64,64]{2,1,0:T(8,128)(2,1)S(1)}, bf16[16,64,64]{2,1,0:T(8,128)(2,1)}, u32[]{:S(2)}) copy-start(bf16[16,64,64]{2,1,0:T(8,128)(2,1)} %ptr.1) | copy-start | bytes 393220
  21.5 4.3 %copy-start.6 = (bf16[5,16,128]{2,1,0:T(8,128)(2,1)S(1)}, bf16[5,16,128]{2,1,0:T(8,128)(2,1)}, u32[]{:S(2)}) copy-start(bf16[5,16,128]{2,1,0:T(8,128)(2,1)} %get-tuple-element.15.own) | copy-start | bytes 61444
  21.6 4.3 %copy-start.7 = (s32[8,8]{1,0:T(8,128)S(1)}, s32[8,8]{1,0:T(8,128)}, u32[]{:S(2)}) copy-start(s32[8,8]{1,0:T(8,128)} %tlist_h.1) | copy-start | bytes 772
  21.6 4.3 %copy-start.8 = (s32[32,4]{0,1:T(4,128)S(1)}, s32[32,4]{0,1:T(4,128)}, u32[]{:S(2)}) copy-start(s32[32,4]{0,1:T(4,128)} %param.21) | copy-start | bytes 1540
  21.6 4.3 %copy-start.9 = (s32[16,4]{0,1:T(4,128)S(1)}, s32[16,4]{0,1:T(4,128)}, u32[]{:S(2)}) copy-start(s32[16,4]{0,1:T(4,128)} %param.24) | copy-start | bytes 772
  21.6 4.3 %copy-start.11 = (s32[32,3]{0,1:T(4,128)S(1)}, s32[32,3]{0,1:T(4,128)}, u32[]{:S(2)}) copy-start(s32[32,3]{0,1:T(4,128)} %param.19) | copy-start | bytes 1156

commit v7 on v6

--- a/solution.py
+++ b/solution.py
@@ -105,9 +105,7 @@
             dot(beside(mid[2 * i], mid[2 * i + 1]), ptr[2 * i:2 * i + 2].reshape(2 * rank, rank)).astype(BF)
         )
     for i in range(leaves // 8):
-        both = beside(high[2 * i], high[2 * i + 1])
-        for row in range(tops.shape[0]):
-            tops[row, i] = both
+        tops[i] = beside(high[2 * i], high[2 * i + 1])
     made[4].wait()
     made[5].wait()
 
@@ -129,19 +127,31 @@
     pack(own, REACH)
 
 
-def up_pass(lsend, psend, vec, basis, ltr, ptr, rows):
+def up_pass(lsend, psend, vec, basis, ltr, ptr):
     leaves, vecs, rank = vec.shape
     count = (lsend.shape[2] + psend.shape[1]) // 2
     shape = lambda *n: jax.ShapeDtypeStruct(n + (vecs, 2 * rank), BF)
     return call(
         up_body, "up", (vec, basis, ltr, ptr, lsend, psend), (),
-        [shape(rows, leaves // 8), shape(count), shape(count + 1), shape(count + 1), shape(count), shape(count)],
+        [shape(leaves // 8), shape(count), shape(count + 1), shape(count + 1), shape(count), shape(count)],
         [WHOLE] * 6,
         [
             like(vec), like(basis), like(ltr), like(ptr), held(lsend), held(psend),
             VMEM((leaves, vecs, rank), BF), VMEM((leaves // 2, vecs, rank), BF), DMA((6,)),
         ],
         (10_000_000, 3_000_000),
+    )
+
+
+def spread_body(top, out):
+    for row in range(out.shape[0]):
+        out[row] = top[...]
+
+
+def spread_pass(top, rows):
+    return call(
+        spread_body, "spread", (), (top,), jax.ShapeDtypeStruct((rows,) + top.shape, top.dtype), WHOLE, [],
+        (4_000_000_000, 60_000_000), 4 * 1024 * 1024,
     )
 
 
@@ -303,11 +313,11 @@
     lsend = jnp.transpose(leaf_send, (1, 0, 2))
     psend = jnp.transpose(pair_send, (0, 2, 1))
     tops, own, sib, cross, fwd, back = up_pass(
-        lsend, psend, vectors, leaf_basis, leaf_transfer, pair_transfer, rows
+        lsend, psend, vectors, leaf_basis, leaf_transfer, pair_transfer
     )
     ring = range(devs)
     sibling = [(d, d ^ 1) for d in ring]
-    mine = lax.all_to_all(tops, "row", split_axis=0, concat_axis=0)
+    mine = lax.all_to_all(spread_pass(tops, rows), "row", split_axis=0, concat_axis=0)
     theirs = lax.ppermute(mine, AXES, sibling)
     sib = lax.ppermute(sib, AXES, sibling)
     cross = lax.ppermute(cross, AXES, [(d, (d + 1 if d % 2 else d - 1) % devs) for d in ring])

time: 31.7 us -> 33.8 us (1.066)
  local copies, waits for them, and re-layouts: 4.37 us -> 5.9 us
  Pallas kernels: 12 us -> 12.6 us
    unnamed x30 -> x36, local copies, waits for them, and re-layouts: 4.37 us -> 5.9 us
    pallas_call x3 -> x4, Pallas kernels: 12 us -> 12.6 us  [call(): pl.pallas_call(body, out_shape=out_shape, in_specs=[FIXED] * len(params)...]
  transfers between devices with their start and end apart: 6 -> 6, of which waited for: 1 -> 1; matrix products, arithmetic and copies ran while one was open for 0% -> 0% of each run, Pallas kernels for 12% -> 11%
where the time goes in v7:
time: 33.8 us; the launch traced here: 33.3 us
  starting transfers between devices  14.1 us (42%)
  Pallas kernels  12.6 us (37%)
  local copies, waits for them, and re-layouts  5.9 us (17%)
  waiting for transfers between devices  0.48 us (1%)
    pallas_call x4, Pallas kernels, call(): pl.pallas_call(body, out_shape=out_shape, in_specs=[FIXED] * len(params)...  12.6 us
    all_to_all x1, starting transfers between devices, on_device(): lax.all_to_all(spread_pass(tops, rows), 'row', split_axis=0, concat_axis=0)  7.28 us
    unnamed x36, local copies, waits for them, and re-layouts  5.9 us
    ppermute x1, starting transfers between devices, on_device(): back = lax.ppermute(back, AXES, [(d, (d - 2) % devs) for d in ring])  2.77 us
    ppermute x1, starting transfers between devices, on_device(): lax.ppermute(cross, AXES, [(d, (d + 1 if d % 2 else d - 1) % devs) for d...  2.07 us
    ppermute x1, starting transfers between devices, on_device(): fwd = lax.ppermute(fwd, AXES, [(d, (d + 2) % devs) for d in ring])  2.02 us
  transfers between devices with their start and end apart: 6, of which 1 were waited for; matrix products, arithmetic and copies ran while one was open for 0% of the time, Pallas kernels for 11%

profile of v7, /device:TPU:0, one launch (start us, length us, event | category | flops | bytes accessed | tf_op | source)
XLA Modules:
  0.0 33.3 jit_solution(17249363682271247921)
XLA Ops:
  0.0 2.8 %up.1 = (bf16[4,16,128]{2,1,0:T(8,128)(2,1)}, bf16[5,16,128]{2,1,0:T(8,128)(2,1)}, bf16[6,16,128]{2,1,0:T(8,128)(2,1)}, bf16[6,16,128]{2,1,0:T(8,128)(2,1)}, bf1...) custom-call(bf16[32,16,64]{2,1,0:T(8,128)(2,1)} %vec_h.1, bf16[32,64,64]{2,1,0:T(8,128)(2,1)} %basis.1, ...), custom_call_target="tpu_custom_call" | custom-call | flops 10000000 | bytes 3000000 | tf_op jit(solution)/shard_map/up/pallas_call | solution.py:63
  2.8 0.0 copy-start.13
  2.8 0.7 %copy-done.13 = bf16[4,16,128]{2,1,0:T(8,128)(2,1)S(1)} copy-done((bf16[4,16,128]{2,1,0:T(8,128)(2,1)S(1)}, bf16[4,16,128]{2,1,0:T(8,128)(2,1)}, u32[]{:S(2)}) %copy-start.13) | copy-done | bytes 16408
  3.5 0.0 copy-start.17
  3.5 0.0 copy-start.15
  3.5 0.0 copy-start.14
  3.5 0.0 copy-start.6
  3.5 0.0 copy-start.11
  3.6 0.7 %spread.1 = bf16[8,4,16,128]{3,2,1,0:T(8,128)(2,1)} custom-call(bf16[4,16,128]{2,1,0:T(8,128)(2,1)S(1)} %copy-done.13), custom_call_target="tpu_custom_call" | custom-call | flops 4000000000 | bytes 60000000 | tf_op jit(solution)/shard_map/spread/pallas_call | solution.py:63
  4.2 7.3 %all-to-all-start = ((bf16[8,4,16,128]{3,2,1,0:T(8,128)(2,1)}), bf16[8,4,16,128]{3,2,1,0:T(8,128)(2,1)S(1)}, u32[]{:S(2)}, u32[]{:S(2)}) async-start(bf16[8,4,16,128]{3,2,1,0:T(8,128)(2,1)} %spread.1), calls=%async_computation | async-start | bytes 262144 | tf_op jit(solution)/shard_map/all_to_all | solution.py:320
  11.5 0.0 copy-done.17
  11.5 2.0 %collective-permute-start.2 = (bf16[5,16,128]{2,1,0:T(8,128)(2,1)S(1)}, bf16[5,16,128]{2,1,0:T(8,128)(2,1)S(1)}, u32[]{:S(2)}, u32[]{:S(2)}) collective-permute-start(bf16[5,16,128]{2,1,0:T(8,128)(2,1)S(1)} %copy-done.17), channel_id=1, source_target_pairs={{0,2},{1,3},{2,4},{3,5},{4,6},{5,7},{6,8},{7,9},{8,10},{9,11},{10,... | collective-permute-start | bytes 61448 | tf_op jit(solution)/shard_map/ppermute | solution.py:324
  13.5 0.0 copy-done.16
  13.5 2.8 %collective-permute-start.3 = (bf16[5,16,128]{2,1,0:T(8,128)(2,1)S(1)}, bf16[5,16,128]{2,1,0:T(8,128)(2,1)S(1)}, u32[]{:S(2)}, u32[]{:S(2)}) collective-permute-start(bf16[5,16,128]{2,1,0:T(8,128)(2,1)S(1)} %copy-done.16), channel_id=1, source_target_pairs={{0,14},{1,15},{2,0},{3,1},{4,2},{5,3},{6,4},{7,5},{8,6},{9,7},{10,... | collective-permute-start | bytes 61448 | tf_op jit(solution)/shard_map/ppermute | solution.py:325
  16.3 0.0 copy-done.15
  16.3 0.0 collective-permute-start
  16.3 0.0 copy-done.14
  16.3 2.1 %collective-permute-start.1 = (bf16[6,16,128]{2,1,0:T(8,128)(2,1)S(1)}, bf16[6,16,128]{2,1,0:T(8,128)(2,1)S(1)}, u32[]{:S(2)}, u32[]{:S(2)}) collective-permute-start(bf16[6,16,128]{2,1,0:T(8,128)(2,1)S(1)} %copy-done.14), channel_id=1, source_target_pairs={{0,15},{1,2},{2,1},{3,4},{4,3},{5,6},{6,5},{7,8},{8,7},{9,10},{10,... | collective-permute-start | bytes 73736 | tf_op jit(solution)/shard_map/ppermute | solution.py:323
  18.4 0.5 %all-to-all-done.mine = bf16[8,4,16,128]{3,2,1,0:T(8,128)(2,1)S(1)} async-done(((bf16[8,4,16,128]{3,2,1,0:T(8,128)(2,1)}), bf16[8,4,16,128]{3,2,1,0:T(8,128)(2,1)S(1)}, u32[]{:S(2)}, u32[]{:S(2)}) %all-to-all-start) | async-done | bytes 131104 | tf_op jit(solution)/shard_map/all_to_all | solution.py:320
  18.9 0.0 collective-permute-start.4
  18.9 0.0 copy-done.6
  18.9 0.0 copy-done.11
  18.9 0.0 copy-start.12
  18.9 2.3 %copy-done.12 = bf16[3,32,3,64,64]{4,3,2,1,0:T(8,128)(2,1)S(1)} copy-done((bf16[3,32,3,64,64]{4,3,2,1,0:T(8,128)(2,1)S(1)}, bf16[3,32,3,64,64]{4,3,2,1,0:T(8,128)(2,1)}, u32[]{:S(2)}) %copy-start.12) | copy-done | bytes 2359320
  21.2 0.0 copy-start.1
  21.2 0.0 copy-start.5
  21.2 0.0 copy-start.7
  21.2 0.0 copy-start.8
  21.2 0.0 copy-start.9
  21.3 0.0 copy-start.10
  21.3 3.8 %near.2 = (f32[32,48,64]{2,1,0:T(8,128)S(1)}, bf16[3,4,3,64,64]{4,3,2,1,0:T(8,128)(2,1)S(1)}) custom-call(s32[3,32]{1,0:T(4,128)S(1)} %bitcast.7, bf16[32,16,64]{2,1,0:T(8,128)(2,1)S(1)} %copy-done.6, bf16[3,32,3,64,64]{4,3,2,1,0:T(8,128)(2,1)S(1)} %copy-done.12), custom_call_target="tpu_custom_call" | custom-call | flops 4000000000 | bytes 60000000 | tf_op jit(solution)/shard_map/near/pallas_call | solution.py:63
  25.0 0.0 collective-permute-done.2.fwd
  25.1 0.0 collective-permute-done.3.back
  25.1 0.0 collective-permute-done.sib
  25.1 0.0 collective-permute-done.1.cross
  25.1 0.0 collective-permute-done.4.theirs
  25.1 0.0 copy-done.1
  25.1 0.0 copy-done.2
  25.1 0.0 copy-done.3
  25.1 0.0 copy-done.4
  25.1 0.0 copy-done.5
  25.1 0.0 copy-done.7
  25.2 0.0 copy-done.8
  25.2 0.0 copy-done.9
  25.2 0.0 copy-done.10
  25.2 0.0 copy-start
  25.2 2.8 %copy-done = bf16[3,32,4,64,64]{4,3,2,1,0:T(8,128)(2,1)S(1)} copy-done((bf16[3,32,4,64,64]{4,3,2,1,0:T(8,128)(2,1)S(1)}, bf16[3,32,4,64,64]{4,3,2,1,0:T(8,128)(2,1)}, u32[]{:S(2)}) %copy-start) | copy-done | bytes 3145752
  28.0 5.4 %rest.1 = bf16[3,32,16,64]{3,2,1,0:T(8,128)(2,1)} custom-call(s32[4,32]{1,0:T(4,128)S(1)} %bitcast.5, s32[4,16]{1,0:T(4,128)S(1)} %bitcast.6, s32[8,8]{1,0:T(8,128)S(1)} %copy-done.8, s32[3,32]{1,0:T(4,128)S(1)} %bitcast.8, bf16[3,32,4,64,64]{4,3,2,1,0:T(8,128)(2,1)S(1)} %copy-done, bf16[3,16,4,64,64]{4,3,2,1,0:T(8,128)(2,1)S(1)} %copy-done.1, ...), custom_call_target="tpu_custom_call" | custom-call | flops 150000000 | bytes 20000000 | tf_op jit(solution)/shard_map/rest/pallas_call | solution.py:63
  (4 shorter events, 0.0 us)
Async XLA Ops:
  2.8 0.7 %copy-start.13 = (bf16[4,16,128]{2,1,0:T(8,128)(2,1)S(1)}, bf16[4,16,128]{2,1,0:T(8,128)(2,1)}, u32[]{:S(2)}) copy-start(bf16[4,16,128]{2,1,0:T(8,128)(2,1)} %get-tuple-element.20.top) | copy-start | bytes 49156
  3.5 8.0 %copy-start.17 = (bf16[5,16,128]{2,1,0:T(8,128)(2,1)S(1)}, bf16[5,16,128]{2,1,0:T(8,128)(2,1)}, u32[]{:S(2)}) copy-start(bf16[5,16,128]{2,1,0:T(8,128)(2,1)} %get-tuple-element.18) | copy-start | bytes 61444
  3.5 10.0 %copy-start.16 = (bf16[5,16,128]{2,1,0:T(8,128)(2,1)S(1)}, bf16[5,16,128]{2,1,0:T(8,128)(2,1)}, u32[]{:S(2)}) copy-start(bf16[5,16,128]{2,1,0:T(8,128)(2,1)} %get-tuple-element.19) | copy-start | bytes 61444
  3.5 12.8 %copy-start.15 = (bf16[6,16,128]{2,1,0:T(8,128)(2,1)S(1)}, bf16[6,16,128]{2,1,0:T(8,128)(2,1)}, u32[]{:S(2)}) copy-start(bf16[6,16,128]{2,1,0:T(8,128)(2,1)} %get-tuple-element.16) | copy-start | bytes 73732
  3.5 12.8 %copy-start.14 = (bf16[6,16,128]{2,1,0:T(8,128)(2,1)S(1)}, bf16[6,16,128]{2,1,0:T(8,128)(2,1)}, u32[]{:S(2)}) copy-start(bf16[6,16,128]{2,1,0:T(8,128)(2,1)} %get-tuple-element.17) | copy-start | bytes 73732
  3.5 15.3 %copy-start.6 = (bf16[32,16,64]{2,1,0:T(8,128)(2,1)S(1)}, bf16[32,16,64]{2,1,0:T(8,128)(2,1)}, u32[]{:S(2)}) copy-start(bf16[32,16,64]{2,1,0:T(8,128)(2,1)} %vec_h.1) | copy-start | bytes 196612
  3.5 15.3 %copy-start.11 = (s32[32,3]{0,1:T(4,128)S(1)}, s32[32,3]{0,1:T(4,128)}, u32[]{:S(2)}) copy-start(s32[32,3]{0,1:T(4,128)} %param.19) | copy-start | bytes 1156
  4.2 14.6 %all-to-all-start = ((bf16[8,4,16,128]{3,2,1,0:T(8,128)(2,1)}), bf16[8,4,16,128]{3,2,1,0:T(8,128)(2,1)S(1)}, u32[]{:S(2)}, u32[]{:S(2)}) async-start(bf16[8,4,16,128]{3,2,1,0:T(8,128)(2,1)} %spread.1), calls=%async_computation | async-start | bytes 262144 | tf_op jit(solution)/shard_map/all_to_all | solution.py:320
  11.5 13.5 %collective-permute-start.2 = (bf16[5,16,128]{2,1,0:T(8,128)(2,1)S(1)}, bf16[5,16,128]{2,1,0:T(8,128)(2,1)S(1)}, u32[]{:S(2)}, u32[]{:S(2)}) collective-permute-start(bf16[5,16,128]{2,1,0:T(8,128)(2,1)S(1)} %copy-done.17), channel_id=1, source_target_pairs={{0,2},{1,3},{2,4},{3,5},{4,6},{5,7},{6,8},{7,9},{8,10},{9,11},{10,... | collective-permute-start | bytes 61448 | tf_op jit(solution)/shard_map/ppermute | solution.py:324
  13.5 11.5 %collective-permute-start.3 = (bf16[5,16,128]{2,1,0:T(8,128)(2,1)S(1)}, bf16[5,16,128]{2,1,0:T(8,128)(2,1)S(1)}, u32[]{:S(2)}, u32[]{:S(2)}) collective-permute-start(bf16[5,16,128]{2,1,0:T(8,128)(2,1)S(1)} %copy-done.16), channel_id=1, source_target_pairs={{0,14},{1,15},{2,0},{3,1},{4,2},{5,3},{6,4},{7,5},{8,6},{9,7},{10,... | collective-permute-start | bytes 61448 | tf_op jit(solution)/shard_map/ppermute | solution.py:325
  16.3 8.8 %collective-permute-start = (bf16[6,16,128]{2,1,0:T(8,128)(2,1)S(1)}, bf16[6,16,128]{2,1,0:T(8,128)(2,1)S(1)}, u32[]{:S(2)}, u32[]{:S(2)}) collective-permute-start(bf16[6,16,128]{2,1,0:T(8,128)(2,1)S(1)} %copy-done.15), channel_id=1, source_target_pairs={{0,1},{1,0},{2,3},{3,2},{4,5},{5,4},{6,7},{7,6},{8,9},{9,8},{10,11... | collective-permute-start | bytes 73736 | tf_op jit(solution)/shard_map/ppermute | solution.py:322
  16.3 8.8 %collective-permute-start.1 = (bf16[6,16,128]{2,1,0:T(8,128)(2,1)S(1)}, bf16[6,16,128]{2,1,0:T(8,128)(2,1)S(1)}, u32[]{:S(2)}, u32[]{:S(2)}) collective-permute-start(bf16[6,16,128]{2,1,0:T(8,128)(2,1)S(1)} %copy-done.14), channel_id=1, source_target_pairs={{0,15},{1,2},{2,1},{3,4},{4,3},{5,6},{6,5},{7,8},{8,7},{9,10},{10,... | collective-permute-start | bytes 73736 | tf_op jit(solution)/shard_map/ppermute | solution.py:323
  18.9 6.2 %collective-permute-start.4 = (bf16[8,4,16,128]{3,2,1,0:T(8,128)(2,1)S(1)}, bf16[8,4,16,128]{3,2,1,0:T(8,128)(2,1)S(1)}, u32[]{:S(2)}, u32[]{:S(2)}) collective-permute-start(bf16[8,4,16,128]{3,2,1,0:T(8,128)(2,1)S(1)} %all-to-all-done.mine), channel_id=1, source_target_pairs={{0,1},{1,0},{2,3},{3,2},{4,5},{5,4},{6,7},{7,6},{8,9},{9,8},{10,11... | collective-permute-start | bytes 393224 | tf_op jit(solution)/shard_map/ppermute | solution.py:321
  18.9 2.3 %copy-start.12 = (bf16[3,32,3,64,64]{4,3,2,1,0:T(8,128)(2,1)S(1)}, bf16[3,32,3,64,64]{4,3,2,1,0:T(8,128)(2,1)}, u32[]{:S(2)}) copy-start(bf16[3,32,3,64,64]{4,3,2,1,0:T(8,128)(2,1)} %near.3) | copy-start | bytes 7077892
  21.2 3.9 %copy-start.1 = (bf16[3,16,4,64,64]{4,3,2,1,0:T(8,128)(2,1)S(1)}, bf16[3,16,4,64,64]{4,3,2,1,0:T(8,128)(2,1)}, u32[]{:S(2)}) copy-start(bf16[3,16,4,64,64]{4,3,2,1,0:T(8,128)(2,1)} %pair.1) | copy-start | bytes 4718596
  21.2 3.9 %copy-start.2 = (bf16[3,8,8,64,64]{4,3,2,1,0:T(8,128)(2,1)S(1)}, bf16[3,8,8,64,64]{4,3,2,1,0:T(8,128)(2,1)}, u32[]{:S(2)}) copy-start(bf16[3,8,8,64,64]{4,3,2,1,0:T(8,128)(2,1)} %coupling.1) | copy-start | bytes 4718596
  21.2 3.9 %copy-start.3 = (bf16[32,64,64]{2,1,0:T(8,128)(2,1)S(1)}, bf16[32,64,64]{2,1,0:T(8,128)(2,1)}, u32[]{:S(2)}) copy-start(bf16[32,64,64]{2,1,0:T(8,128)(2,1)} %ltr.1) | copy-start | bytes 786436
  21.2 3.9 %copy-start.4 = (bf16[32,64,64]{2,1,0:T(8,128)(2,1)S(1)}, bf16[32,64,64]{2,1,0:T(8,128)(2,1)}, u32[]{:S(2)}) copy-start(bf16[32,64,64]{2,1,0:T(8,128)(2,1)} %basis.1) | copy-start | bytes 786436
  21.2 3.9 %copy-start.5 = (bf16[16,64,64]{2,1,0:T(8,128)(2,1)S(1)}, bf16[16,64,64]{2,1,0:T(8,128)(2,1)}, u32[]{:S(2)}) copy-start(bf16[16,64,64]{2,1,0:T(8,128)(2,1)} %ptr.1) | copy-start | bytes 393220
  21.2 3.9 %copy-start.7 = (bf16[5,16,128]{2,1,0:T(8,128)(2,1)S(1)}, bf16[5,16,128]{2,1,0:T(8,128)(2,1)}, u32[]{:S(2)}) copy-start(bf16[5,16,128]{2,1,0:T(8,128)(2,1)} %get-tuple-element.15.own) | copy-start | bytes 61444
  21.2 3.9 %copy-start.8 = (s32[8,8]{1,0:T(8,128)S(1)}, s32[8,8]{1,0:T(8,128)}, u32[]{:S(2)}) copy-start(s32[8,8]{1,0:T(8,128)} %tlist_h.1) | copy-start | bytes 772
  21.2 3.9 %copy-start.9 = (s32[32,4]{0,1:T(4,128)S(1)}, s32[32,4]{0,1:T(4,128)}, u32[]{:S(2)}) copy-start(s32[32,4]{0,1:T(4,128)} %param.21) | copy-start | bytes 1540
  21.3 3.9 %copy-start.10 = (s32[16,4]{0,1:T(4,128)S(1)}, s32[16,4]{0,1:T(4,128)}, u32[]{:S(2)}) copy-start(s32[16,4]{0,1:T(4,128)} %param.24) | copy-start | bytes 772
  25.2 2.8 %copy-start = (bf16[3,32,4,64,64]{4,3,2,1,0:T(8,128)(2,1)S(1)}, bf16[3,32,4,64,64]{4,3,2,1,0:T(8,128)(2,1)}, u32[]{:S(2)}) copy-start(bf16[3,32,4,64,64]{4,3,2,1,0:T(8,128)(2,1)} %leaf.1) | copy-start | bytes 9437188

commit v8 on v6

--- a/solution.py
+++ b/solution.py
@@ -80,7 +80,7 @@
     return SMEM(x.shape, x.dtype)
 
 
-def up_body(vec_h, basis_h, ltr_h, ptr_h, lsend_h, psend_h, tops, own, sib, cross, fwd, back,
+def up_body(vec_h, basis_h, ltr_h, ptr_h, lsend_h, psend_h, tops, own, windows,
             vec, basis, ltr, ptr, lsend, psend, low, mid, sems):
     leaves, vecs, rank = vec.shape
     col = lax.axis_index("col")
@@ -111,6 +111,8 @@
     made[4].wait()
     made[5].wait()
 
+    sib, cross, fwd, back = [windows.at[i] for i in range(4)]
+
     def pack(out, place):
         for c in range(cap0 // 2):
             out[c] = beside(low[lsend[place, 0, 2 * c]], low[lsend[place, 0, 2 * c + 1]])
@@ -135,8 +137,8 @@
     shape = lambda *n: jax.ShapeDtypeStruct(n + (vecs, 2 * rank), BF)
     return call(
         up_body, "up", (vec, basis, ltr, ptr, lsend, psend), (),
-        [shape(rows, leaves // 8), shape(count), shape(count + 1), shape(count + 1), shape(count), shape(count)],
-        [WHOLE] * 6,
+        [shape(rows, leaves // 8), shape(count), shape(4, count + 1)],
+        [WHOLE] * 3,
         [
             like(vec), like(basis), like(ltr), like(ptr), held(lsend), held(psend),
             VMEM((leaves, vecs, rank), BF), VMEM((leaves // 2, vecs, rank), BF), DMA((6,)),
@@ -145,43 +147,17 @@
     )
 
 
-def near_body(offsets_h, vec, near, close, ends, padded, offsets, sems):
-    leaves, vecs, rank = vec.shape
-    kernels = near.shape[0]
-    made = copies([(offsets_h, offsets)], sems)
-    ends[:, 0:HW] = near[:, 0:HW]
-    ends[:, HW:] = near[:, leaves - HW:]
-    zero = jnp.zeros((HW, vecs, rank), BF)
-    padded[0:HW] = zero
-    padded[HW:HW + leaves] = vec[...]
-    padded[HW + leaves:] = zero
-    made[0].wait()
-
-    def body(c, _):
-        for q in range(GROUP):
-            t = c * GROUP + q
-            total = None
-            for n in range(near.shape[2]):
-                part = dot_t(padded[t + HW + offsets[n, t]], above(*[near[k, t, n] for k in range(kernels)]))
-                total = part if total is None else total + part
-            close[t] = by_kernel(total, rank)
-        return 0
-
-    lax.fori_loop(0, leaves // GROUP, body, 0)
-
-
-def near_pass(offsets, vec, blocks):
-    kernels, leaves, near, rank, _ = blocks.shape
-    vecs = vec.shape[1]
+def hand_body(windows, *outs):
+    for i, out in enumerate(outs):
+        out[...] = windows[i, :out.shape[0]]
+
+
+def hand_pass(windows, counts):
+    shape = windows.shape[2:]
     return call(
-        near_body, "near", (offsets,), (vec, blocks),
-        [
-            jax.ShapeDtypeStruct((leaves, kernels * vecs, rank), F32),
-            jax.ShapeDtypeStruct((kernels, 2 * HW) + blocks.shape[2:], BF),
-        ],
-        [WHOLE] * 2,
-        [VMEM((leaves + 2 * HW, vecs, rank), BF), held(offsets), DMA((1,))],
-        (4_000_000_000, 60_000_000), 8 * 1024 * 1024,
+        hand_body, "hand", (), (windows,),
+        [jax.ShapeDtypeStruct((n,) + shape, windows.dtype) for n in counts],
+        [WHOLE] * len(counts), [], (8_000_000_000, 100_000_000), 2 * 1024 * 1024,
     )
 
 
@@ -190,8 +166,8 @@
 
 
 def rest_body(llist_h, plist_h, tlist_h, offsets_h,
-              leaf, pair, coupling, ends, ptr, ltr, basis, close, own, sib, cross, fwd, back, mine, theirs, out,
-              llist, plist, tlist, offsets, wleaf, wpair, halo, tops, far0, far1, down, sems):
+              leaf, pair, coupling, near, ptr, ltr, basis, vec, own, sib, cross, fwd, back, mine, theirs, out,
+              llist, plist, tlist, offsets, wleaf, wpair, padded, tops, far0, far1, close, down, sems):
     kernels, leaves, partners, rank, _ = leaf.shape
     _, vecs, _ = wleaf.shape
     count = coupling.shape[1]
@@ -208,11 +184,11 @@
             split(block[c], wleaf, slot * cap0 + 2 * c)
         for c in range(cap1 // 2):
             split(block[base + c], wpair, slot * cap1 + 2 * c)
-    halo[2 * HW] = jnp.zeros((vecs, rank), BF)
+    padded[HW:HW + leaves] = vec[...]
     for block, upper in ((sib, 1 - col), (cross, col)):
         row = block[base + cap1 // 2]
         outside = (place == 0) & (upper == 0) | (place == last_place) & (upper == 1)
-        split(jnp.where(outside, jnp.zeros_like(row), row), halo, upper * HW)
+        split(jnp.where(outside, jnp.zeros_like(row), row), padded, upper * (HW + leaves))
     for block, side in ((mine, col), (theirs, 1 - col)):
         for s in range(block.shape[0]):
             for i in range(block.shape[1]):
@@ -223,6 +199,8 @@
     def body(c, _):
         for q in range(GROUP):
             t = c * GROUP + q
+            rows = [padded[t + HW + offsets[n, t]] for n in range(near.shape[2])]
+            close[t] = by_kernel(far_sum(rows, near, t), rank)
             far0[t] = by_kernel(far_sum([wleaf[llist[m, t]] for m in range(partners)], leaf, t), rank)
         for q in range(GROUP // 2):
             j = c * (GROUP // 2) + q
@@ -235,14 +213,6 @@
 
     lax.fori_loop(0, leaves // GROUP, body, 0)
 
-    def edge(t):
-        spots = [t + offsets[n, t] for n in range(ends.shape[2])]
-        if t < HW:
-            spots = [jnp.where(at < 0, at + HW, 2 * HW) for at in spots]
-        else:
-            spots = [jnp.where(at >= leaves, at - leaves + HW, 2 * HW) for at in spots]
-        return by_kernel(far_sum([halo[at] for at in spots], ends, t if t < HW else t - (leaves - 2 * HW)), rank)
-
     down1 = []
     for j in range(2 * count):
         down1.append((far1[j] + dot_t(down[j // 2], ptr[j])).astype(BF))
@@ -250,10 +220,7 @@
     for t in range(leaves):
         down0.append((far0[t] + dot_t(down1[t // 2], ltr[t])).astype(BF))
     for t in range(leaves):
-        points = dot_t(down0[t], basis[t]) + close[t]
-        if t < HW or t >= leaves - HW:
-            points = points + edge(t)
-        points = points.astype(BF)
+        points = (dot_t(down0[t], basis[t]) + close[t]).astype(BF)
         for k in range(kernels):
             out[k, t] = points[k * vecs:(k + 1) * vecs]
 
@@ -271,10 +238,10 @@
         [held(x) for x in lists]
         + [
             VMEM((n, vecs, rank), BF)
-            for n in (WIN * cap0, WIN * cap1, 2 * HW + 1, 2 * windows[-1].shape[0] * count)
+            for n in (WIN * cap0, WIN * cap1, 2 * HW + leaves, 2 * windows[-1].shape[0] * count)
         ]
         + [
-            VMEM((leaves, rows, rank), F32), VMEM((leaves // 2, rows, rank), F32),
+            VMEM((leaves, rows, rank), F32), VMEM((leaves // 2, rows, rank), F32), VMEM((leaves, rows, rank), F32),
             VMEM((count, rows, rank), BF), DMA((4,)),
         ],
         (150_000_000, 20_000_000), 16 * 1024 * 1024,
@@ -302,9 +269,11 @@
     cap0, cap1 = leaf_send.shape[2], pair_send.shape[2]
     lsend = jnp.transpose(leaf_send, (1, 0, 2))
     psend = jnp.transpose(pair_send, (0, 2, 1))
-    tops, own, sib, cross, fwd, back = up_pass(
+    tops, own, windows = up_pass(
         lsend, psend, vectors, leaf_basis, leaf_transfer, pair_transfer, rows
     )
+    count = own.shape[0]
+    sib, cross, fwd, back = hand_pass(windows, (count + 1, count + 1, count, count))
     ring = range(devs)
     sibling = [(d, d ^ 1) for d in ring]
     mine = lax.all_to_all(tops, "row", split_axis=0, concat_axis=0)
@@ -313,10 +282,9 @@
     cross = lax.ppermute(cross, AXES, [(d, (d + 1 if d % 2 else d - 1) % devs) for d in ring])
     fwd = lax.ppermute(fwd, AXES, [(d, (d + 2) % devs) for d in ring])
     back = lax.ppermute(back, AXES, [(d, (d - 2) % devs) for d in ring])
-    close, ends = near_pass(near_offset.T, vectors, near_blocks)
     return rest_pass(
         (leaf_list.T, pair_list.T, top_list, near_offset.T),
-        (leaf_coupling, pair_coupling, top_coupling, ends, pair_transfer, leaf_transfer, leaf_basis, close),
+        (leaf_coupling, pair_coupling, top_coupling, near_blocks, pair_transfer, leaf_transfer, leaf_basis, vectors),
         (own, sib, cross, fwd, back, mine, theirs), cap0, cap1,
     )
 

time: 31.7 us -> 32.8 us (1.035)
  blocking collectives: 0 us -> 14.6 us
  starting transfers between devices: 14.3 us -> 6.07 us
  local copies, waits for them, and re-layouts: 4.37 us -> 0.97 us
  Pallas kernels: 12 us -> 8.9 us
  waiting for transfers between devices: 0.49 us -> 1.77 us
    all_to_all x0 -> x1, blocking collectives: none -> 14.6 us  [on_device(): mine = lax.all_to_all(tops, 'row', split_axis=0, concat_axis=0)]
    all_to_all x1 -> x0, starting transfers between devices: 7.42 us -> none  [on_device(): mine = lax.all_to_all(tops, 'row', split_axis=0, concat_axis=0)]
    unnamed x30 -> x32, local copies, waits for them, and re-layouts: 4.37 us -> 0.97 us
    pallas_call x3, Pallas kernels: 12 us -> 8.9 us  [call(): pl.pallas_call(body, out_shape=out_shape, in_specs=[FIXED] * len(params)...]
    ppermute x1, waiting for transfers between devices: 0.01 us -> 1.76 us  [on_device(): fwd = lax.ppermute(fwd, AXES, [(d, (d + 2) % devs) for d in ring])]
    ppermute x1, starting transfers between devices: 2.11 us -> 0.77 us  [on_device(): lax.ppermute(cross, AXES, [(d, (d + 1 if d % 2 else d - 1) % devs) for d...]
    ppermute x1, starting transfers between devices: 2.02 us -> 0.94 us  [on_device(): fwd = lax.ppermute(fwd, AXES, [(d, (d + 2) % devs) for d in ring])]
    ppermute x1, starting transfers between devices: 2.73 us -> 3.78 us  [on_device(): back = lax.ppermute(back, AXES, [(d, (d - 2) % devs) for d in ring])]
  transfers between devices with their start and end apart: 6 -> 5, of which waited for: 1 -> 1; matrix products, arithmetic and copies ran while one was open for 0% -> 0% of each run, Pallas kernels for 12% -> 0%
where the time goes in v8:
time: 32.8 us; the launch traced here: 32.6 us
  blocking collectives  14.6 us (45%)
  Pallas kernels  8.9 us (27%)
  starting transfers between devices  6.07 us (19%)
  waiting for transfers between devices  1.77 us (5%)
  local copies, waits for them, and re-layouts  0.97 us (3%)
    all_to_all x1, blocking collectives, on_device(): mine = lax.all_to_all(tops, 'row', split_axis=0, concat_axis=0)  14.6 us
    pallas_call x3, Pallas kernels, call(): pl.pallas_call(body, out_shape=out_shape, in_specs=[FIXED] * len(params)...  8.9 us
    ppermute x1, starting transfers between devices, on_device(): back = lax.ppermute(back, AXES, [(d, (d - 2) % devs) for d in ring])  3.78 us
    ppermute x1, waiting for transfers between devices, on_device(): fwd = lax.ppermute(fwd, AXES, [(d, (d + 2) % devs) for d in ring])  1.76 us
    unnamed x32, local copies, waits for them, and re-layouts  0.97 us
    ppermute x1, starting transfers between devices, on_device(): fwd = lax.ppermute(fwd, AXES, [(d, (d + 2) % devs) for d in ring])  0.94 us
    ppermute x1, starting transfers between devices, on_device(): lax.ppermute(cross, AXES, [(d, (d + 1 if d % 2 else d - 1) % devs) for d...  0.77 us
  transfers between devices with their start and end apart: 5, of which 1 were waited for; matrix products, arithmetic and copies ran while one was open for 0% of the time, Pallas kernels for 0%

profile of v8, /device:TPU:0, one launch (start us, length us, event | category | flops | bytes accessed | tf_op | source)
XLA Modules:
  0.0 32.6 jit_solution(14934746997889222910)
XLA Ops:
  0.0 0.0 slice-start
  0.0 0.0 slice-start.2
  0.0 2.9 %up.1 = (bf16[8,4,16,128]{3,2,1,0:T(8,128)(2,1)}, bf16[5,16,128]{2,1,0:T(8,128)(2,1)}, bf16[4,6,16,128]{3,2,1,0:T(8,128)(2,1)}) custom-call(bf16[32,16,64]{2,1,0:T(8,128)(2,1)} %vec.1, bf16[32,64,64]{2,1,0:T(8,128)(2,1)} %basis.1, bf16[32,64,64]{2,1,0:T(8,128)(2,1)} %ltr.1, bf16[16,64,64]{2,1,0:T(8,128)(2,1)} %ptr.1, s32[5,1,8]{2,1,0:T(1,128)} %bitcast.12, ...), custom_call_target="tpu_custom_call" | custom-call | flops 10000000 | bytes 3000000 | tf_op jit(solution)/shard_map/up/pallas_call | solution.py:63
  2.9 14.6 %all_to_all.5.mine = bf16[8,4,16,128]{3,2,1,0:T(8,128)(2,1)S(1)} all-to-all(bf16[8,4,16,128]{3,2,1,0:T(8,128)(2,1)} %get-tuple-element.18), channel_id=1, replica_groups=mesh['groups'=2,'row'=8,'col'=2] {'row'}, dimensions={0} | all-to-all | bytes 262144 | tf_op jit(solution)/shard_map/all_to_all | solution.py:279
  17.6 0.0 collective-permute-start.4
  17.6 0.0 copy-start.11
  17.6 0.9 %copy-done.11 = bf16[4,6,16,128]{3,2,1,0:T(8,128)(2,1)S(1)} copy-done((bf16[4,6,16,128]{3,2,1,0:T(8,128)(2,1)S(1)}, bf16[4,6,16,128]{3,2,1,0:T(8,128)(2,1)}, u32[]{:S(2)}) %copy-start.11) | copy-done | bytes 98328
  18.5 0.0 slice-start.1
  18.5 0.0 slice-start.3
  18.5 0.0 copy-start
  18.5 0.0 copy-start.1
  18.5 0.0 copy-start.2
  18.5 0.0 copy-start.3
  18.5 0.0 copy-start.4
  18.5 0.0 copy-start.5
  18.5 0.0 copy-start.6
  18.5 0.0 copy-start.7
  18.6 0.0 copy-start.8
  18.6 0.0 copy-start.9
  18.6 0.0 copy-start.10
  18.6 0.6 %collective-permute-start = (bf16[6,16,128]{2,1,0:T(8,128)(2,1)S(1)}, bf16[6,16,128]{2,1,0:T(8,128)(2,1)S(1)}, u32[]{:S(2)}, u32[]{:S(2)}) collective-permute-start(bf16[6,16,128]{2,1,0:T(8,128)(2,1)S(1)} %get-tuple-element.14), channel_id=1, source_target_pairs={{0,1},{1,0},{2,3},{3,2},{4,5},{5,4},{6,7},{7,6},{8,9},{9,8},{10,11... | collective-permute-start | bytes 73736 | tf_op jit(solution)/shard_map/ppermute | solution.py:281
  19.2 0.8 %collective-permute-start.1 = (bf16[6,16,128]{2,1,0:T(8,128)(2,1)S(1)}, bf16[6,16,128]{2,1,0:T(8,128)(2,1)S(1)}, u32[]{:S(2)}, u32[]{:S(2)}) collective-permute-start(bf16[6,16,128]{2,1,0:T(8,128)(2,1)S(1)} %get-tuple-element.15), channel_id=1, source_target_pairs={{0,15},{1,2},{2,1},{3,4},{4,3},{5,6},{6,5},{7,8},{8,7},{9,10},{10,... | collective-permute-start | bytes 73736 | tf_op jit(solution)/shard_map/ppermute | solution.py:282
  20.0 0.9 %collective-permute-start.2 = (bf16[5,16,128]{2,1,0:T(8,128)(2,1)S(1)}, bf16[5,16,128]{2,1,0:T(8,128)(2,1)S(1)}, u32[]{:S(2)}, u32[]{:S(2)}) collective-permute-start(bf16[5,16,128]{2,1,0:T(8,128)(2,1)S(1)} %get-tuple-element.16), channel_id=1, source_target_pairs={{0,2},{1,3},{2,4},{3,5},{4,6},{5,7},{6,8},{7,9},{8,10},{9,11},{10,... | collective-permute-start | bytes 61448 | tf_op jit(solution)/shard_map/ppermute | solution.py:283
  20.9 3.8 %collective-permute-start.3 = (bf16[5,16,128]{2,1,0:T(8,128)(2,1)S(1)}, bf16[5,16,128]{2,1,0:T(8,128)(2,1)S(1)}, u32[]{:S(2)}, u32[]{:S(2)}) collective-permute-start(bf16[5,16,128]{2,1,0:T(8,128)(2,1)S(1)} %get-tuple-element.17), channel_id=1, source_target_pairs={{0,14},{1,15},{2,0},{3,1},{4,2},{5,3},{6,4},{7,5},{8,6},{9,7},{10,... | collective-permute-start | bytes 61448 | tf_op jit(solution)/shard_map/ppermute | solution.py:284
  24.7 1.8 %collective-permute-done.2.fwd = bf16[5,16,128]{2,1,0:T(8,128)(2,1)S(1)} collective-permute-done((bf16[5,16,128]{2,1,0:T(8,128)(2,1)S(1)}, bf16[5,16,128]{2,1,0:T(8,128)(2,1)S(1)}, u32[]{:S(2)}, u32[]{:S(2)}) %collective-permute-start.2) | collective-permute-done | bytes 20512 | tf_op jit(solution)/shard_map/ppermute | solution.py:283
  26.4 0.0 collective-permute-done.3.back
  26.4 0.0 collective-permute-done.sib
  26.4 0.0 collective-permute-done.1.cross
  26.4 0.0 collective-permute-done.4.theirs
  26.5 0.0 slice-done
  26.5 0.0 slice-done.2
  26.5 0.0 slice-done.1
  26.5 0.0 slice-done.3
  26.5 0.0 copy-done
  26.5 0.0 copy-done.1
  26.5 0.0 copy-done.2
  26.5 0.0 copy-done.3
  26.5 0.0 copy-done.4
  26.5 0.0 copy-done.5
  26.6 0.0 copy-done.6
  26.6 0.0 copy-done.7
  26.6 0.0 copy-done.8
  26.6 0.0 copy-done.9
  26.6 0.0 copy-done.10
  26.6 6.0 %rest.1 = bf16[3,32,16,64]{3,2,1,0:T(8,128)(2,1)} custom-call(s32[4,32]{1,0:T(4,128)S(1)} %bitcast.9, s32[4,16]{1,0:T(4,128)S(1)} %bitcast.10, s32[8,8]{1,0:T(8,128)S(1)} %copy-done.7, s32[3,32]{1,0:T(4,128)S(1)} %bitcast.11, bf16[3,32,4,64,64]{4,3,2,1,0:T(8,128)(2,1)S(1)} %bitcast.6, bf16[3,16,4,64,64]{4,3,2,1,0:T(8,128)(2,1)S(1)} %copy-done, ...), custom_call_target="tpu_custom_call" | custom-call | flops 150000000 | bytes 20000000 | tf_op jit(solution)/shard_map/rest/pallas_call | solution.py:63
  (3 shorter events, 0.0 us)
Async XLA Ops:
  0.0 26.5 %slice-start = ((s8[6291456]{0:T(1024)(128)(4,1)}), s8[2097152]{0:T(1024)(128)(4,1)S(1)}, s32[]{:S(2)}) async-start(s8[6291456]{0:T(1024)(128)(4,1)} %bitcast.5), calls=%async_computation.1 | async-start | bytes 4194304
  0.0 26.5 %slice-start.2 = ((s8[4718592]{0:T(1024)(128)(4,1)}), s8[4194304]{0:T(1024)(128)(4,1)S(1)}, s32[]{:S(2)}) async-start(s8[4718592]{0:T(1024)(128)(4,1)} %bitcast.7), calls=%async_computation.3 | async-start | bytes 8388608
  17.6 8.9 %collective-permute-start.4 = (bf16[8,4,16,128]{3,2,1,0:T(8,128)(2,1)S(1)}, bf16[8,4,16,128]{3,2,1,0:T(8,128)(2,1)S(1)}, u32[]{:S(2)}, u32[]{:S(2)}) collective-permute-start(bf16[8,4,16,128]{3,2,1,0:T(8,128)(2,1)S(1)} %all_to_all.5.mine), channel_id=1, source_target_pairs={{0,1},{1,0},{2,3},{3,2},{4,5},{5,4},{6,7},{7,6},{8,9},{9,8},{10,11... | collective-permute-start | bytes 393224 | tf_op jit(solution)/shard_map/ppermute | solution.py:280
  17.6 0.9 %copy-start.11 = (bf16[4,6,16,128]{3,2,1,0:T(8,128)(2,1)S(1)}, bf16[4,6,16,128]{3,2,1,0:T(8,128)(2,1)}, u32[]{:S(2)}) copy-start(bf16[4,6,16,128]{3,2,1,0:T(8,128)(2,1)} %get-tuple-element.13.windows) | copy-start | bytes 294916
  18.5 8.0 %slice-start.1 = ((s8[6291456]{0:T(1024)(128)(4,1)}), s8[4194304]{0:T(1024)(128)(4,1)S(1)}, s32[]{:S(2)}) async-start(s8[6291456]{0:T(1024)(128)(4,1)} %bitcast.5), calls=%async_computation.2 | async-start | bytes 8388608
  18.5 8.0 %slice-start.3 = ((s8[4718592]{0:T(1024)(128)(4,1)}), s8[524288]{0:T(1024)(128)(4,1)S(1)}, s32[]{:S(2)}) async-start(s8[4718592]{0:T(1024)(128)(4,1)} %bitcast.7), calls=%async_computation.4 | async-start | bytes 1048576
  18.5 8.0 %copy-start = (bf16[3,16,4,64,64]{4,3,2,1,0:T(8,128)(2,1)S(1)}, bf16[3,16,4,64,64]{4,3,2,1,0:T(8,128)(2,1)}, u32[]{:S(2)}) copy-start(bf16[3,16,4,64,64]{4,3,2,1,0:T(8,128)(2,1)} %pair.1) | copy-start | bytes 4718596
  18.5 8.0 %copy-start.1 = (bf16[3,8,8,64,64]{4,3,2,1,0:T(8,128)(2,1)S(1)}, bf16[3,8,8,64,64]{4,3,2,1,0:T(8,128)(2,1)}, u32[]{:S(2)}) copy-start(bf16[3,8,8,64,64]{4,3,2,1,0:T(8,128)(2,1)} %coupling.1) | copy-start | bytes 4718596
  18.5 8.0 %copy-start.2 = (bf16[32,64,64]{2,1,0:T(8,128)(2,1)S(1)}, bf16[32,64,64]{2,1,0:T(8,128)(2,1)}, u32[]{:S(2)}) copy-start(bf16[32,64,64]{2,1,0:T(8,128)(2,1)} %ltr.1) | copy-start | bytes 786436
  18.5 8.0 %copy-start.3 = (bf16[32,64,64]{2,1,0:T(8,128)(2,1)S(1)}, bf16[32,64,64]{2,1,0:T(8,128)(2,1)}, u32[]{:S(2)}) copy-start(bf16[32,64,64]{2,1,0:T(8,128)(2,1)} %basis.1) | copy-start | bytes 786436
  18.5 8.0 %copy-start.4 = (bf16[16,64,64]{2,1,0:T(8,128)(2,1)S(1)}, bf16[16,64,64]{2,1,0:T(8,128)(2,1)}, u32[]{:S(2)}) copy-start(bf16[16,64,64]{2,1,0:T(8,128)(2,1)} %ptr.1) | copy-start | bytes 393220
  18.5 8.0 %copy-start.5 = (bf16[32,16,64]{2,1,0:T(8,128)(2,1)S(1)}, bf16[32,16,64]{2,1,0:T(8,128)(2,1)}, u32[]{:S(2)}) copy-start(bf16[32,16,64]{2,1,0:T(8,128)(2,1)} %vec.1) | copy-start | bytes 196612
  18.5 8.0 %copy-start.6 = (bf16[5,16,128]{2,1,0:T(8,128)(2,1)S(1)}, bf16[5,16,128]{2,1,0:T(8,128)(2,1)}, u32[]{:S(2)}) copy-start(bf16[5,16,128]{2,1,0:T(8,128)(2,1)} %get-tuple-element.12.own) | copy-start | bytes 61444
  18.5 8.0 %copy-start.7 = (s32[8,8]{1,0:T(8,128)S(1)}, s32[8,8]{1,0:T(8,128)}, u32[]{:S(2)}) copy-start(s32[8,8]{1,0:T(8,128)} %tlist_h.1) | copy-start | bytes 772
  18.6 8.0 %copy-start.8 = (s32[32,4]{0,1:T(4,128)S(1)}, s32[32,4]{0,1:T(4,128)}, u32[]{:S(2)}) copy-start(s32[32,4]{0,1:T(4,128)} %param.21) | copy-start | bytes 1540
  18.6 8.0 %copy-start.9 = (s32[16,4]{0,1:T(4,128)S(1)}, s32[16,4]{0,1:T(4,128)}, u32[]{:S(2)}) copy-start(s32[16,4]{0,1:T(4,128)} %param.24) | copy-start | bytes 772
  18.6 8.0 %copy-start.10 = (s32[32,3]{0,1:T(4,128)S(1)}, s32[32,3]{0,1:T(4,128)}, u32[]{:S(2)}) copy-start(s32[32,3]{0,1:T(4,128)} %param.19) | copy-start | bytes 1156
  18.6 7.8 %collective-permute-start = (bf16[6,16,128]{2,1,0:T(8,128)(2,1)S(1)}, bf16[6,16,128]{2,1,0:T(8,128)(2,1)S(1)}, u32[]{:S(2)}, u32[]{:S(2)}) collective-permute-start(bf16[6,16,128]{2,1,0:T(8,128)(2,1)S(1)} %get-tuple-element.14), channel_id=1, source_target_pairs={{0,1},{1,0},{2,3},{3,2},{4,5},{5,4},{6,7},{7,6},{8,9},{9,8},{10,11... | collective-permute-start | bytes 73736 | tf_op jit(solution)/shard_map/ppermute | solution.py:281
  19.2 7.3 %collective-permute-start.1 = (bf16[6,16,128]{2,1,0:T(8,128)(2,1)S(1)}, bf16[6,16,128]{2,1,0:T(8,128)(2,1)S(1)}, u32[]{:S(2)}, u32[]{:S(2)}) collective-permute-start(bf16[6,16,128]{2,1,0:T(8,128)(2,1)S(1)} %get-tuple-element.15), channel_id=1, source_target_pairs={{0,15},{1,2},{2,1},{3,4},{4,3},{5,6},{6,5},{7,8},{8,7},{9,10},{10,... | collective-permute-start | bytes 73736 | tf_op jit(solution)/shard_map/ppermute | solution.py:282
  20.0 6.5 %collective-permute-start.2 = (bf16[5,16,128]{2,1,0:T(8,128)(2,1)S(1)}, bf16[5,16,128]{2,1,0:T(8,128)(2,1)S(1)}, u32[]{:S(2)}, u32[]{:S(2)}) collective-permute-start(bf16[5,16,128]{2,1,0:T(8,128)(2,1)S(1)} %get-tuple-element.16), channel_id=1, source_target_pairs={{0,2},{1,3},{2,4},{3,5},{4,6},{5,7},{6,8},{7,9},{8,10},{9,11},{10,... | collective-permute-start | bytes 61448 | tf_op jit(solution)/shard_map/ppermute | solution.py:283
  20.9 5.5 %collective-permute-start.3 = (bf16[5,16,128]{2,1,0:T(8,128)(2,1)S(1)}, bf16[5,16,128]{2,1,0:T(8,128)(2,1)S(1)}, u32[]{:S(2)}, u32[]{:S(2)}) collective-permute-start(bf16[5,16,128]{2,1,0:T(8,128)(2,1)S(1)} %get-tuple-element.17), channel_id=1, source_target_pairs={{0,14},{1,15},{2,0},{3,1},{4,2},{5,3},{6,4},{7,5},{8,6},{9,7},{10,... | collective-permute-start | bytes 61448 | tf_op jit(solution)/shard_map/ppermute | solution.py:284

commit v9 on v6

--- a/solution.py
+++ b/solution.py
@@ -80,7 +80,7 @@
     return SMEM(x.shape, x.dtype)
 
 
-def up_body(vec_h, basis_h, ltr_h, ptr_h, lsend_h, psend_h, tops, own, sib, cross, fwd, back,
+def up_body(vec_h, basis_h, ltr_h, ptr_h, lsend_h, psend_h, tops, own, windows,
             vec, basis, ltr, ptr, lsend, psend, low, mid, sems):
     leaves, vecs, rank = vec.shape
     col = lax.axis_index("col")
@@ -111,6 +111,8 @@
     made[4].wait()
     made[5].wait()
 
+    sib, cross, fwd, back = [windows.at[i] for i in range(4)]
+
     def pack(out, place):
         for c in range(cap0 // 2):
             out[c] = beside(low[lsend[place, 0, 2 * c]], low[lsend[place, 0, 2 * c + 1]])
@@ -135,13 +137,27 @@
     shape = lambda *n: jax.ShapeDtypeStruct(n + (vecs, 2 * rank), BF)
     return call(
         up_body, "up", (vec, basis, ltr, ptr, lsend, psend), (),
-        [shape(rows, leaves // 8), shape(count), shape(count + 1), shape(count + 1), shape(count), shape(count)],
-        [WHOLE] * 6,
+        [shape(rows, leaves // 8), shape(count), shape(4, count + 1)],
+        [WHOLE] * 3,
         [
             like(vec), like(basis), like(ltr), like(ptr), held(lsend), held(psend),
             VMEM((leaves, vecs, rank), BF), VMEM((leaves // 2, vecs, rank), BF), DMA((6,)),
         ],
         (10_000_000, 3_000_000),
+    )
+
+
+def hand_body(windows, *outs):
+    for i, out in enumerate(outs):
+        out[...] = windows[i, :out.shape[0]]
+
+
+def hand_pass(windows, counts):
+    shape = windows.shape[2:]
+    return call(
+        hand_body, "hand", (), (windows,),
+        [jax.ShapeDtypeStruct((n,) + shape, windows.dtype) for n in counts],
+        [WHOLE] * len(counts), [], (8_000_000_000, 100_000_000), 2 * 1024 * 1024,
     )
 
 
@@ -160,11 +176,8 @@
     def body(c, _):
         for q in range(GROUP):
             t = c * GROUP + q
-            total = None
-            for n in range(near.shape[2]):
-                part = dot_t(padded[t + HW + offsets[n, t]], above(*[near[k, t, n] for k in range(kernels)]))
-                total = part if total is None else total + part
-            close[t] = by_kernel(total, rank)
+            rows = [padded[t + HW + offsets[n, t]] for n in range(near.shape[2])]
+            close[t] = by_kernel(far_sum(rows, near, t), rank)
         return 0
 
     lax.fori_loop(0, leaves // GROUP, body, 0)
@@ -302,9 +315,11 @@
     cap0, cap1 = leaf_send.shape[2], pair_send.shape[2]
     lsend = jnp.transpose(leaf_send, (1, 0, 2))
     psend = jnp.transpose(pair_send, (0, 2, 1))
-    tops, own, sib, cross, fwd, back = up_pass(
+    tops, own, windows = up_pass(
         lsend, psend, vectors, leaf_basis, leaf_transfer, pair_transfer, rows
     )
+    count = own.shape[0]
+    sib, cross, fwd, back = hand_pass(windows, (count + 1, count + 1, count, count))
     ring = range(devs)
     sibling = [(d, d ^ 1) for d in ring]
     mine = lax.all_to_all(tops, "row", split_axis=0, concat_axis=0)

time: 31.7 us -> 31 us (0.978)
  Pallas kernels: 12 us -> 10.6 us
  local copies, waits for them, and re-layouts: 4.37 us -> 5.74 us
  waiting for transfers between devices: 0.49 us -> 0.02 us
    pallas_call x3 -> x4, Pallas kernels: 12 us -> 10.6 us  [call(): pl.pallas_call(body, out_shape=out_shape, in_specs=[FIXED] * len(params)...]
    unnamed x30 -> x28, local copies, waits for them, and re-layouts: 4.37 us -> 5.74 us
    all_to_all x1, waiting for transfers between devices: 0.48 us -> 0.01 us  [on_device(): mine = lax.all_to_all(tops, 'row', split_axis=0, concat_axis=0)]
  transfers between devices with their start and end apart: 6 -> 6, of which waited for: 1 -> 0; matrix products, arithmetic and copies ran while one was open for 0% -> 0% of each run, Pallas kernels for 12% -> 8%
where the time goes in v9:
time: 31 us; the launch traced here: 30.7 us
  starting transfers between devices  14.2 us (46%)
  Pallas kernels  10.6 us (34%)
  local copies, waits for them, and re-layouts  5.74 us (19%)
    pallas_call x4, Pallas kernels, call(): pl.pallas_call(body, out_shape=out_shape, in_specs=[FIXED] * len(params)...  10.6 us
    all_to_all x1, starting transfers between devices, on_device(): mine = lax.all_to_all(tops, 'row', split_axis=0, concat_axis=0)  7.29 us
    unnamed x28, local copies, waits for them, and re-layouts  5.74 us
    ppermute x1, starting transfers between devices, on_device(): back = lax.ppermute(back, AXES, [(d, (d - 2) % devs) for d in ring])  2.77 us
    ppermute x1, starting transfers between devices, on_device(): fwd = lax.ppermute(fwd, AXES, [(d, (d + 2) % devs) for d in ring])  2.07 us
    ppermute x1, starting transfers between devices, on_device(): lax.ppermute(cross, AXES, [(d, (d + 1 if d % 2 else d - 1) % devs) for d...  2.07 us
  transfers between devices with their start and end apart: 6, of which 0 were waited for; matrix products, arithmetic and copies ran while one was open for 0% of the time, Pallas kernels for 8%

profile of v9, /device:TPU:0, one launch (start us, length us, event | category | flops | bytes accessed | tf_op | source)
XLA Modules:
  0.0 30.7 jit_solution(7432995521680519505)
XLA Ops:
  0.0 2.8 %up.1 = (bf16[8,4,16,128]{3,2,1,0:T(8,128)(2,1)}, bf16[5,16,128]{2,1,0:T(8,128)(2,1)}, bf16[4,6,16,128]{3,2,1,0:T(8,128)(2,1)}) custom-call(bf16[32,16,64]{2,1,0:T(8,128)(2,1)} %vec_h.1, bf16[32,64,64]{2,1,0:T(8,128)(2,1)} %basis.1, bf16[32,64,64]{2,1,0:T(8,128)(2,1)} %ltr.1, bf16[16,64,64]{2,1,0:T(8,128)(2,1)} %ptr.1, s32[5,1,8]{2,1,0:T(1,128)} %bitcast.9, ...), custom_call_target="tpu_custom_call" | custom-call | flops 10000000 | bytes 3000000 | tf_op jit(solution)/shard_map/up/pallas_call | solution.py:63
  2.8 7.3 %all-to-all-start = ((bf16[8,4,16,128]{3,2,1,0:T(8,128)(2,1)}), bf16[8,4,16,128]{3,2,1,0:T(8,128)(2,1)S(1)}, u32[]{:S(2)}, u32[]{:S(2)}) async-start(bf16[8,4,16,128]{3,2,1,0:T(8,128)(2,1)} %get-tuple-element.22), calls=%async_computation | async-start | bytes 262144 | tf_op jit(solution)/shard_map/all_to_all | solution.py:325
  10.1 0.0 copy-start.13
  10.1 0.9 %copy-done.13 = bf16[4,6,16,128]{3,2,1,0:T(8,128)(2,1)S(1)} copy-done((bf16[4,6,16,128]{3,2,1,0:T(8,128)(2,1)S(1)}, bf16[4,6,16,128]{3,2,1,0:T(8,128)(2,1)}, u32[]{:S(2)}) %copy-start.13) | copy-done | bytes 98328
  11.0 0.0 copy-start.6
  11.0 0.0 copy-start.11
  11.0 2.1 %collective-permute-start.2 = (bf16[5,16,128]{2,1,0:T(8,128)(2,1)S(1)}, bf16[5,16,128]{2,1,0:T(8,128)(2,1)S(1)}, u32[]{:S(2)}, u32[]{:S(2)}) collective-permute-start(bf16[5,16,128]{2,1,0:T(8,128)(2,1)S(1)} %get-tuple-element.20), channel_id=1, source_target_pairs={{0,2},{1,3},{2,4},{3,5},{4,6},{5,7},{6,8},{7,9},{8,10},{9,11},{10,... | collective-permute-start | bytes 61448 | tf_op jit(solution)/shard_map/ppermute | solution.py:329
  13.1 2.8 %collective-permute-start.3 = (bf16[5,16,128]{2,1,0:T(8,128)(2,1)S(1)}, bf16[5,16,128]{2,1,0:T(8,128)(2,1)S(1)}, u32[]{:S(2)}, u32[]{:S(2)}) collective-permute-start(bf16[5,16,128]{2,1,0:T(8,128)(2,1)S(1)} %get-tuple-element.21), channel_id=1, source_target_pairs={{0,14},{1,15},{2,0},{3,1},{4,2},{5,3},{6,4},{7,5},{8,6},{9,7},{10,... | collective-permute-start | bytes 61448 | tf_op jit(solution)/shard_map/ppermute | solution.py:330
  15.8 0.0 collective-permute-start
  15.8 2.1 %collective-permute-start.1 = (bf16[6,16,128]{2,1,0:T(8,128)(2,1)S(1)}, bf16[6,16,128]{2,1,0:T(8,128)(2,1)S(1)}, u32[]{:S(2)}, u32[]{:S(2)}) collective-permute-start(bf16[6,16,128]{2,1,0:T(8,128)(2,1)S(1)} %get-tuple-element.19), channel_id=1, source_target_pairs={{0,15},{1,2},{2,1},{3,4},{4,3},{5,6},{6,5},{7,8},{8,7},{9,10},{10,... | collective-permute-start | bytes 73736 | tf_op jit(solution)/shard_map/ppermute | solution.py:328
  17.9 0.0 all-to-all-done.mine
  17.9 0.0 collective-permute-start.4
  17.9 0.0 copy-done.6
  17.9 0.0 copy-done.11
  17.9 0.0 copy-start.12
  18.0 2.3 %copy-done.12 = bf16[3,32,3,64,64]{4,3,2,1,0:T(8,128)(2,1)S(1)} copy-done((bf16[3,32,3,64,64]{4,3,2,1,0:T(8,128)(2,1)S(1)}, bf16[3,32,3,64,64]{4,3,2,1,0:T(8,128)(2,1)}, u32[]{:S(2)}) %copy-start.12) | copy-done | bytes 2359320
  20.3 0.0 copy-start
  20.3 0.0 copy-start.1
  20.3 0.0 copy-start.2
  20.3 0.0 copy-start.3
  20.3 0.0 copy-start.4
  20.3 0.0 copy-start.5
  20.3 0.0 copy-start.7
  20.3 0.0 copy-start.8
  20.3 0.0 copy-start.9
  20.4 0.0 copy-start.10
  20.4 2.4 %near.2 = (f32[32,48,64]{2,1,0:T(8,128)S(1)}, bf16[3,4,3,64,64]{4,3,2,1,0:T(8,128)(2,1)S(1)}) custom-call(s32[3,32]{1,0:T(4,128)S(1)} %bitcast.7, bf16[32,16,64]{2,1,0:T(8,128)(2,1)S(1)} %copy-done.6, bf16[3,32,3,64,64]{4,3,2,1,0:T(8,128)(2,1)S(1)} %copy-done.12), custom_call_target="tpu_custom_call" | custom-call | flops 4000000000 | bytes 60000000 | tf_op jit(solution)/shard_map/near/pallas_call | solution.py:63
  22.8 0.0 collective-permute-done.2.fwd
  22.8 0.0 collective-permute-done.3.back
  22.8 0.0 collective-permute-done.sib
  22.8 0.0 collective-permute-done.1.cross
  22.8 0.0 collective-permute-done.4.theirs
  22.8 0.2 copy-done
  23.1 0.9 %copy-done.1 = bf16[3,16,4,64,64]{4,3,2,1,0:T(8,128)(2,1)S(1)} copy-done((bf16[3,16,4,64,64]{4,3,2,1,0:T(8,128)(2,1)S(1)}, bf16[3,16,4,64,64]{4,3,2,1,0:T(8,128)(2,1)}, u32[]{:S(2)}) %copy-start.1) | copy-done | bytes 1572888
  24.0 0.9 %copy-done.2 = bf16[3,8,8,64,64]{4,3,2,1,0:T(8,128)(2,1)S(1)} copy-done((bf16[3,8,8,64,64]{4,3,2,1,0:T(8,128)(2,1)S(1)}, bf16[3,8,8,64,64]{4,3,2,1,0:T(8,128)(2,1)}, u32[]{:S(2)}) %copy-start.2) | copy-done | bytes 1572888
  24.9 0.2 copy-done.3
  25.1 0.2 copy-done.4
  25.2 0.1 copy-done.5
  25.3 0.0 copy-done.7
  25.3 0.0 copy-done.8
  25.3 0.0 copy-done.9
  25.3 0.0 copy-done.10
  25.3 5.4 %rest.1 = bf16[3,32,16,64]{3,2,1,0:T(8,128)(2,1)} custom-call(s32[4,32]{1,0:T(4,128)S(1)} %bitcast.5, s32[4,16]{1,0:T(4,128)S(1)} %bitcast.6, s32[8,8]{1,0:T(8,128)S(1)} %copy-done.8, s32[3,32]{1,0:T(4,128)S(1)} %bitcast.8, bf16[3,32,4,64,64]{4,3,2,1,0:T(8,128)(2,1)S(1)} %copy-done, bf16[3,16,4,64,64]{4,3,2,1,0:T(8,128)(2,1)S(1)} %copy-done.1, ...), custom_call_target="tpu_custom_call" | custom-call | flops 150000000 | bytes 20000000 | tf_op jit(solution)/shard_map/rest/pallas_call | solution.py:63
  (1 shorter events, 0.0 us)
Async XLA Ops:
  2.8 15.1 %all-to-all-start = ((bf16[8,4,16,128]{3,2,1,0:T(8,128)(2,1)}), bf16[8,4,16,128]{3,2,1,0:T(8,128)(2,1)S(1)}, u32[]{:S(2)}, u32[]{:S(2)}) async-start(bf16[8,4,16,128]{3,2,1,0:T(8,128)(2,1)} %get-tuple-element.22), calls=%async_computation | async-start | bytes 262144 | tf_op jit(solution)/shard_map/all_to_all | solution.py:325
  10.1 0.9 %copy-start.13 = (bf16[4,6,16,128]{3,2,1,0:T(8,128)(2,1)S(1)}, bf16[4,6,16,128]{3,2,1,0:T(8,128)(2,1)}, u32[]{:S(2)}) copy-start(bf16[4,6,16,128]{3,2,1,0:T(8,128)(2,1)} %get-tuple-element.17.windows) | copy-start | bytes 294916
  11.0 6.9 %copy-start.6 = (bf16[32,16,64]{2,1,0:T(8,128)(2,1)S(1)}, bf16[32,16,64]{2,1,0:T(8,128)(2,1)}, u32[]{:S(2)}) copy-start(bf16[32,16,64]{2,1,0:T(8,128)(2,1)} %vec_h.1) | copy-start | bytes 196612
  11.0 6.9 %copy-start.11 = (s32[32,3]{0,1:T(4,128)S(1)}, s32[32,3]{0,1:T(4,128)}, u32[]{:S(2)}) copy-start(s32[32,3]{0,1:T(4,128)} %param.19) | copy-start | bytes 1156
  11.0 11.8 %collective-permute-start.2 = (bf16[5,16,128]{2,1,0:T(8,128)(2,1)S(1)}, bf16[5,16,128]{2,1,0:T(8,128)(2,1)S(1)}, u32[]{:S(2)}, u32[]{:S(2)}) collective-permute-start(bf16[5,16,128]{2,1,0:T(8,128)(2,1)S(1)} %get-tuple-element.20), channel_id=1, source_target_pairs={{0,2},{1,3},{2,4},{3,5},{4,6},{5,7},{6,8},{7,9},{8,10},{9,11},{10,... | collective-permute-start | bytes 61448 | tf_op jit(solution)/shard_map/ppermute | solution.py:329
  13.1 9.7 %collective-permute-start.3 = (bf16[5,16,128]{2,1,0:T(8,128)(2,1)S(1)}, bf16[5,16,128]{2,1,0:T(8,128)(2,1)S(1)}, u32[]{:S(2)}, u32[]{:S(2)}) collective-permute-start(bf16[5,16,128]{2,1,0:T(8,128)(2,1)S(1)} %get-tuple-element.21), channel_id=1, source_target_pairs={{0,14},{1,15},{2,0},{3,1},{4,2},{5,3},{6,4},{7,5},{8,6},{9,7},{10,... | collective-permute-start | bytes 61448 | tf_op jit(solution)/shard_map/ppermute | solution.py:330
  15.8 7.0 %collective-permute-start = (bf16[6,16,128]{2,1,0:T(8,128)(2,1)S(1)}, bf16[6,16,128]{2,1,0:T(8,128)(2,1)S(1)}, u32[]{:S(2)}, u32[]{:S(2)}) collective-permute-start(bf16[6,16,128]{2,1,0:T(8,128)(2,1)S(1)} %get-tuple-element.18), channel_id=1, source_target_pairs={{0,1},{1,0},{2,3},{3,2},{4,5},{5,4},{6,7},{7,6},{8,9},{9,8},{10,11... | collective-permute-start | bytes 73736 | tf_op jit(solution)/shard_map/ppermute | solution.py:327
  15.8 7.0 %collective-permute-start.1 = (bf16[6,16,128]{2,1,0:T(8,128)(2,1)S(1)}, bf16[6,16,128]{2,1,0:T(8,128)(2,1)S(1)}, u32[]{:S(2)}, u32[]{:S(2)}) collective-permute-start(bf16[6,16,128]{2,1,0:T(8,128)(2,1)S(1)} %get-tuple-element.19), channel_id=1, source_target_pairs={{0,15},{1,2},{2,1},{3,4},{4,3},{5,6},{6,5},{7,8},{8,7},{9,10},{10,... | collective-permute-start | bytes 73736 | tf_op jit(solution)/shard_map/ppermute | solution.py:328
  17.9 4.9 %collective-permute-start.4 = (bf16[8,4,16,128]{3,2,1,0:T(8,128)(2,1)S(1)}, bf16[8,4,16,128]{3,2,1,0:T(8,128)(2,1)S(1)}, u32[]{:S(2)}, u32[]{:S(2)}) collective-permute-start(bf16[8,4,16,128]{3,2,1,0:T(8,128)(2,1)S(1)} %all-to-all-done.mine), channel_id=1, source_target_pairs={{0,1},{1,0},{2,3},{3,2},{4,5},{5,4},{6,7},{7,6},{8,9},{9,8},{10,11... | collective-permute-start | bytes 393224 | tf_op jit(solution)/shard_map/ppermute | solution.py:326
  17.9 2.3 %copy-start.12 = (bf16[3,32,3,64,64]{4,3,2,1,0:T(8,128)(2,1)S(1)}, bf16[3,32,3,64,64]{4,3,2,1,0:T(8,128)(2,1)}, u32[]{:S(2)}) copy-start(bf16[3,32,3,64,64]{4,3,2,1,0:T(8,128)(2,1)} %near.3) | copy-start | bytes 7077892
  20.3 2.8 %copy-start = (bf16[3,32,4,64,64]{4,3,2,1,0:T(8,128)(2,1)S(1)}, bf16[3,32,4,64,64]{4,3,2,1,0:T(8,128)(2,1)}, u32[]{:S(2)}) copy-start(bf16[3,32,4,64,64]{4,3,2,1,0:T(8,128)(2,1)} %leaf.1) | copy-start | bytes 9437188
  20.3 3.7 %copy-start.1 = (bf16[3,16,4,64,64]{4,3,2,1,0:T(8,128)(2,1)S(1)}, bf16[3,16,4,64,64]{4,3,2,1,0:T(8,128)(2,1)}, u32[]{:S(2)}) copy-start(bf16[3,16,4,64,64]{4,3,2,1,0:T(8,128)(2,1)} %pair.1) | copy-start | bytes 4718596
  20.3 4.6 %copy-start.2 = (bf16[3,8,8,64,64]{4,3,2,1,0:T(8,128)(2,1)S(1)}, bf16[3,8,8,64,64]{4,3,2,1,0:T(8,128)(2,1)}, u32[]{:S(2)}) copy-start(bf16[3,8,8,64,64]{4,3,2,1,0:T(8,128)(2,1)} %coupling.1) | copy-start | bytes 4718596
  20.3 4.8 %copy-start.3 = (bf16[32,64,64]{2,1,0:T(8,128)(2,1)S(1)}, bf16[32,64,64]{2,1,0:T(8,128)(2,1)}, u32[]{:S(2)}) copy-start(bf16[32,64,64]{2,1,0:T(8,128)(2,1)} %ltr.1) | copy-start | bytes 786436
  20.3 5.0 %copy-start.4 = (bf16[32,64,64]{2,1,0:T(8,128)(2,1)S(1)}, bf16[32,64,64]{2,1,0:T(8,128)(2,1)}, u32[]{:S(2)}) copy-start(bf16[32,64,64]{2,1,0:T(8,128)(2,1)} %basis.1) | copy-start | bytes 786436
  20.3 5.0 %copy-start.5 = (bf16[16,64,64]{2,1,0:T(8,128)(2,1)S(1)}, bf16[16,64,64]{2,1,0:T(8,128)(2,1)}, u32[]{:S(2)}) copy-start(bf16[16,64,64]{2,1,0:T(8,128)(2,1)} %ptr.1) | copy-start | bytes 393220
  20.3 5.0 %copy-start.7 = (bf16[5,16,128]{2,1,0:T(8,128)(2,1)S(1)}, bf16[5,16,128]{2,1,0:T(8,128)(2,1)}, u32[]{:S(2)}) copy-start(bf16[5,16,128]{2,1,0:T(8,128)(2,1)} %get-tuple-element.16.own) | copy-start | bytes 61444
  20.3 5.0 %copy-start.8 = (s32[8,8]{1,0:T(8,128)S(1)}, s32[8,8]{1,0:T(8,128)}, u32[]{:S(2)}) copy-start(s32[8,8]{1,0:T(8,128)} %tlist_h.1) | copy-start | bytes 772
  20.3 5.0 %copy-start.9 = (s32[32,4]{0,1:T(4,128)S(1)}, s32[32,4]{0,1:T(4,128)}, u32[]{:S(2)}) copy-start(s32[32,4]{0,1:T(4,128)} %param.21) | copy-start | bytes 1540
  20.4 5.0 %copy-start.10 = (s32[16,4]{0,1:T(4,128)S(1)}, s32[16,4]{0,1:T(4,128)}, u32[]{:S(2)}) copy-start(s32[16,4]{0,1:T(4,128)} %param.24) | copy-start | bytes 772

commit v10 on v9

--- a/solution.py
+++ b/solution.py
@@ -161,6 +161,17 @@
     )
 
 
+def pass_body(src, out):
+    out[...] = src[...]
+
+
+def pass_on(x):
+    return call(
+        pass_body, "pass", (), (x,), jax.ShapeDtypeStruct(x.shape, x.dtype), WHOLE, [],
+        (8_000_000_000, 100_000_000), 2 * 1024 * 1024,
+    )
+
+
 def near_body(offsets_h, vec, near, close, ends, padded, offsets, sems):
     leaves, vecs, rank = vec.shape
     kernels = near.shape[0]
@@ -194,7 +205,7 @@
         ],
         [WHOLE] * 2,
         [VMEM((leaves + 2 * HW, vecs, rank), BF), held(offsets), DMA((1,))],
-        (4_000_000_000, 60_000_000), 8 * 1024 * 1024,
+        (1_000_000_000, 20_000_000), 8 * 1024 * 1024,
     )
 
 
@@ -323,6 +334,7 @@
     ring = range(devs)
     sibling = [(d, d ^ 1) for d in ring]
     mine = lax.all_to_all(tops, "row", split_axis=0, concat_axis=0)
+    mine = pass_on(mine)
     theirs = lax.ppermute(mine, AXES, sibling)
     sib = lax.ppermute(sib, AXES, sibling)
     cross = lax.ppermute(cross, AXES, [(d, (d + 1 if d % 2 else d - 1) % devs) for d in ring])

time: 31 us -> 34.9 us (1.13)
  blocking collectives: 0 us -> 14.6 us
  starting transfers between devices: 14.2 us -> 4.96 us
  local copies, waits for them, and re-layouts: 5.74 us -> 0.87 us
  waiting for transfers between devices: 0.02 us -> 3.38 us
    all_to_all x0 -> x1, blocking collectives: none -> 14.6 us  [on_device(): mine = lax.all_to_all(tops, 'row', split_axis=0, concat_axis=0)]
    all_to_all x1 -> x0, starting transfers between devices: 7.29 us -> none  [on_device(): mine = lax.all_to_all(tops, 'row', split_axis=0, concat_axis=0)]
    unnamed x28 -> x32, local copies, waits for them, and re-layouts: 5.74 us -> 0.87 us
    ppermute x1, waiting for transfers between devices: 0.01 us -> 3.37 us  [on_device(): lax.ppermute(cross, AXES, [(d, (d + 1 if d % 2 else d - 1) % devs) for d...]
    ppermute x1, starting transfers between devices: 2.07 us -> 0.11 us  [on_device(): lax.ppermute(cross, AXES, [(d, (d + 1 if d % 2 else d - 1) % devs) for d...]
    ppermute x1, starting transfers between devices: 2.07 us -> 0.27 us  [on_device(): fwd = lax.ppermute(fwd, AXES, [(d, (d + 2) % devs) for d in ring])]
    ppermute x1, starting transfers between devices: 2.77 us -> 4.51 us  [on_device(): back = lax.ppermute(back, AXES, [(d, (d - 2) % devs) for d in ring])]
    pallas_call x4 -> x5, Pallas kernels: 10.6 us -> 10.6 us  [call(): pl.pallas_call(body, out_shape=out_shape, in_specs=[FIXED] * len(params)...]
  transfers between devices with their start and end apart: 6 -> 5, of which waited for: 0 -> 1; matrix products, arithmetic and copies ran while one was open for 0% -> 0% of each run, Pallas kernels for 8% -> 7%
where the time goes in v10:
time: 34.9 us; the launch traced here: 34.7 us
  blocking collectives  14.6 us (42%)
  Pallas kernels  10.6 us (30%)
  starting transfers between devices  4.96 us (14%)
  waiting for transfers between devices  3.38 us (10%)
  local copies, waits for them, and re-layouts  0.87 us (2%)
    all_to_all x1, blocking collectives, on_device(): mine = lax.all_to_all(tops, 'row', split_axis=0, concat_axis=0)  14.6 us
    pallas_call x5, Pallas kernels, call(): pl.pallas_call(body, out_shape=out_shape, in_specs=[FIXED] * len(params)...  10.6 us
    ppermute x1, starting transfers between devices, on_device(): back = lax.ppermute(back, AXES, [(d, (d - 2) % devs) for d in ring])  4.51 us
    ppermute x1, waiting for transfers between devices, on_device(): lax.ppermute(cross, AXES, [(d, (d + 1 if d % 2 else d - 1) % devs) for d...  3.37 us
    unnamed x32, local copies, waits for them, and re-layouts  0.87 us
  transfers between devices with their start and end apart: 5, of which 1 were waited for; matrix products, arithmetic and copies ran while one was open for 0% of the time, Pallas kernels for 7%

profile of v10, /device:TPU:0, one launch (start us, length us, event | category | flops | bytes accessed | tf_op | source)
XLA Modules:
  0.0 34.7 jit_solution(10850410893483336004)
XLA Ops:
  0.0 2.8 %up.1 = (bf16[8,4,16,128]{3,2,1,0:T(8,128)(2,1)}, bf16[5,16,128]{2,1,0:T(8,128)(2,1)}, bf16[4,6,16,128]{3,2,1,0:T(8,128)(2,1)}) custom-call(bf16[32,16,64]{2,1,0:T(8,128)(2,1)} %vec_h.1, bf16[32,64,64]{2,1,0:T(8,128)(2,1)} %basis.1, bf16[32,64,64]{2,1,0:T(8,128)(2,1)} %ltr.1, bf16[16,64,64]{2,1,0:T(8,128)(2,1)} %ptr.1, s32[5,1,8]{2,1,0:T(1,128)} %bitcast.13, ...), custom_call_target="tpu_custom_call" | custom-call | flops 10000000 | bytes 3000000 | tf_op jit(solution)/shard_map/up/pallas_call | solution.py:63
  2.8 14.6 %all_to_all.5.src = bf16[8,4,16,128]{3,2,1,0:T(8,128)(2,1)S(1)} all-to-all(bf16[8,4,16,128]{3,2,1,0:T(8,128)(2,1)} %get-tuple-element.22), channel_id=1, replica_groups=mesh['groups'=2,'row'=8,'col'=2] {'row'}, dimensions={0} | all-to-all | bytes 262144 | tf_op jit(solution)/shard_map/all_to_all | solution.py:336
  17.4 0.0 copy-start.11
  17.4 0.0 slice-start.2
  17.5 0.1 collective-permute-start.4
  17.5 0.0 slice-start
  17.5 0.8 %copy-done.11 = bf16[4,6,16,128]{3,2,1,0:T(8,128)(2,1)S(1)} copy-done((bf16[4,6,16,128]{3,2,1,0:T(8,128)(2,1)S(1)}, bf16[4,6,16,128]{3,2,1,0:T(8,128)(2,1)}, u32[]{:S(2)}) %copy-start.11) | copy-done | bytes 98328
  18.3 0.0 slice-start.3
  18.3 0.0 copy-start.5
  18.3 0.0 copy-start.7
  18.3 0.0 slice-start.1
  18.3 0.0 copy-start.1
  18.4 0.0 copy-start
  18.4 0.0 copy-start.2
  18.4 0.0 copy-start.3
  18.4 0.0 copy-start.4
  18.4 0.0 copy-start.6
  18.4 0.0 copy-start.8
  18.4 0.0 copy-start.9
  18.5 0.0 copy-start.10
  18.5 0.3 collective-permute-start.2
  18.7 4.5 %collective-permute-start.3 = (bf16[5,16,128]{2,1,0:T(8,128)(2,1)S(1)}, bf16[5,16,128]{2,1,0:T(8,128)(2,1)S(1)}, u32[]{:S(2)}, u32[]{:S(2)}) collective-permute-start(bf16[5,16,128]{2,1,0:T(8,128)(2,1)S(1)} %get-tuple-element.21), channel_id=1, source_target_pairs={{0,14},{1,15},{2,0},{3,1},{4,2},{5,3},{6,4},{7,5},{8,6},{9,7},{10,... | collective-permute-start | bytes 61448 | tf_op jit(solution)/shard_map/ppermute | solution.py:342
  23.2 0.0 collective-permute-start
  23.2 0.1 collective-permute-start.1
  23.4 0.0 slice-done.2
  23.4 0.0 slice-done.3
  23.4 0.0 copy-done.5
  23.4 0.0 copy-done.7
  23.4 2.4 %near.2 = (f32[32,48,64]{2,1,0:T(8,128)S(1)}, bf16[3,4,3,64,64]{4,3,2,1,0:T(8,128)(2,1)S(1)}) custom-call(s32[3,32]{1,0:T(4,128)S(1)} %bitcast.9, bf16[32,16,64]{2,1,0:T(8,128)(2,1)S(1)} %copy-done.5, bf16[3,32,3,64,64]{4,3,2,1,0:T(8,128)(2,1)S(1)} %bitcast.8), custom_call_target="tpu_custom_call" | custom-call | flops 1000000000 | bytes 20000000 | tf_op jit(solution)/shard_map/near/pallas_call | solution.py:63
  25.8 0.0 collective-permute-done.2.fwd
  25.8 0.0 collective-permute-done.3.back
  25.8 0.0 collective-permute-done.sib
  25.8 3.4 %collective-permute-done.1.cross = bf16[6,16,128]{2,1,0:T(8,128)(2,1)S(1)} collective-permute-done((bf16[6,16,128]{2,1,0:T(8,128)(2,1)S(1)}, bf16[6,16,128]{2,1,0:T(8,128)(2,1)S(1)}, u32[]{:S(2)}, u32[]{:S(2)}) %collective-permute-start.1) | collective-permute-done | bytes 24608 | tf_op jit(solution)/shard_map/ppermute | solution.py:340
  29.2 0.0 collective-permute-done.4.theirs
  29.2 0.0 slice-done
  29.2 0.0 slice-done.1
  29.2 0.0 copy-done.1
  29.2 0.0 copy-done
  29.2 0.0 copy-done.2
  29.2 0.0 copy-done.3
  29.2 0.0 copy-done.4
  29.3 0.0 copy-done.6
  29.3 0.0 copy-done.8
  29.3 0.0 copy-done.9
  29.3 0.0 copy-done.10
  29.3 5.4 %rest.1 = bf16[3,32,16,64]{3,2,1,0:T(8,128)(2,1)} custom-call(s32[4,32]{1,0:T(4,128)S(1)} %bitcast.11, s32[4,16]{1,0:T(4,128)S(1)} %bitcast.12, s32[8,8]{1,0:T(8,128)S(1)} %copy-done.8, s32[3,32]{1,0:T(4,128)S(1)} %bitcast.10, bf16[3,32,4,64,64]{4,3,2,1,0:T(8,128)(2,1)S(1)} %bitcast.6, bf16[3,16,4,64,64]{4,3,2,1,0:T(8,128)(2,1)S(1)} %copy-done, ...), custom_call_target="tpu_custom_call" | custom-call | flops 150000000 | bytes 20000000 | tf_op jit(solution)/shard_map/rest/pallas_call | solution.py:63
  (4 shorter events, 0.0 us)
Async XLA Ops:
  17.4 0.9 %copy-start.11 = (bf16[4,6,16,128]{3,2,1,0:T(8,128)(2,1)S(1)}, bf16[4,6,16,128]{3,2,1,0:T(8,128)(2,1)}, u32[]{:S(2)}) copy-start(bf16[4,6,16,128]{3,2,1,0:T(8,128)(2,1)} %get-tuple-element.17.windows) | copy-start | bytes 294916
  17.4 5.9 %slice-start.2 = ((s8[4718592]{0:T(1024)(128)(4,1)}), s8[4194304]{0:T(1024)(128)(4,1)S(1)}, s32[]{:S(2)}) async-start(s8[4718592]{0:T(1024)(128)(4,1)} %bitcast.7), calls=%async_computation.3 | async-start | bytes 8388608
  17.5 11.7 %collective-permute-start.4 = (bf16[8,4,16,128]{3,2,1,0:T(8,128)(2,1)S(1)}, bf16[8,4,16,128]{3,2,1,0:T(8,128)(2,1)S(1)}, u32[]{:S(2)}, u32[]{:S(2)}) collective-permute-start(bf16[8,4,16,128]{3,2,1,0:T(8,128)(2,1)S(1)} %pass.1.mine), channel_id=1, source_target_pairs={{0,1},{1,0},{2,3},{3,2},{4,5},{5,4},{6,7},{7,6},{8,9},{9,8},{10,11... | collective-permute-start | bytes 393224 | tf_op jit(solution)/shard_map/ppermute | solution.py:338
  17.5 11.7 %slice-start = ((s8[6291456]{0:T(1024)(128)(4,1)}), s8[4194304]{0:T(1024)(128)(4,1)S(1)}, s32[]{:S(2)}) async-start(s8[6291456]{0:T(1024)(128)(4,1)} %bitcast.5), calls=%async_computation.1 | async-start | bytes 8388608
  18.3 5.0 %slice-start.3 = ((s8[4718592]{0:T(1024)(128)(4,1)}), s8[524288]{0:T(1024)(128)(4,1)S(1)}, s32[]{:S(2)}) async-start(s8[4718592]{0:T(1024)(128)(4,1)} %bitcast.7), calls=%async_computation.4 | async-start | bytes 1048576
  18.3 5.0 %copy-start.5 = (bf16[32,16,64]{2,1,0:T(8,128)(2,1)S(1)}, bf16[32,16,64]{2,1,0:T(8,128)(2,1)}, u32[]{:S(2)}) copy-start(bf16[32,16,64]{2,1,0:T(8,128)(2,1)} %vec_h.1) | copy-start | bytes 196612
  18.3 5.0 %copy-start.7 = (s32[32,3]{0,1:T(4,128)S(1)}, s32[32,3]{0,1:T(4,128)}, u32[]{:S(2)}) copy-start(s32[32,3]{0,1:T(4,128)} %param.19) | copy-start | bytes 1156
  18.3 10.9 %slice-start.1 = ((s8[6291456]{0:T(1024)(128)(4,1)}), s8[2097152]{0:T(1024)(128)(4,1)S(1)}, s32[]{:S(2)}) async-start(s8[6291456]{0:T(1024)(128)(4,1)} %bitcast.5), calls=%async_computation.2 | async-start | bytes 4194304
  18.3 10.9 %copy-start.1 = (bf16[3,8,8,64,64]{4,3,2,1,0:T(8,128)(2,1)S(1)}, bf16[3,8,8,64,64]{4,3,2,1,0:T(8,128)(2,1)}, u32[]{:S(2)}) copy-start(bf16[3,8,8,64,64]{4,3,2,1,0:T(8,128)(2,1)} %coupling.1) | copy-start | bytes 4718596
  18.4 10.8 %copy-start = (bf16[3,16,4,64,64]{4,3,2,1,0:T(8,128)(2,1)S(1)}, bf16[3,16,4,64,64]{4,3,2,1,0:T(8,128)(2,1)}, u32[]{:S(2)}) copy-start(bf16[3,16,4,64,64]{4,3,2,1,0:T(8,128)(2,1)} %pair.1) | copy-start | bytes 4718596
  18.4 10.8 %copy-start.2 = (bf16[32,64,64]{2,1,0:T(8,128)(2,1)S(1)}, bf16[32,64,64]{2,1,0:T(8,128)(2,1)}, u32[]{:S(2)}) copy-start(bf16[32,64,64]{2,1,0:T(8,128)(2,1)} %ltr.1) | copy-start | bytes 786436
  18.4 10.8 %copy-start.3 = (bf16[32,64,64]{2,1,0:T(8,128)(2,1)S(1)}, bf16[32,64,64]{2,1,0:T(8,128)(2,1)}, u32[]{:S(2)}) copy-start(bf16[32,64,64]{2,1,0:T(8,128)(2,1)} %basis.1) | copy-start | bytes 786436
  18.4 10.8 %copy-start.4 = (bf16[16,64,64]{2,1,0:T(8,128)(2,1)S(1)}, bf16[16,64,64]{2,1,0:T(8,128)(2,1)}, u32[]{:S(2)}) copy-start(bf16[16,64,64]{2,1,0:T(8,128)(2,1)} %ptr.1) | copy-start | bytes 393220
  18.4 10.8 %copy-start.6 = (bf16[5,16,128]{2,1,0:T(8,128)(2,1)S(1)}, bf16[5,16,128]{2,1,0:T(8,128)(2,1)}, u32[]{:S(2)}) copy-start(bf16[5,16,128]{2,1,0:T(8,128)(2,1)} %get-tuple-element.16.own) | copy-start | bytes 61444
  18.4 10.8 %copy-start.8 = (s32[8,8]{1,0:T(8,128)S(1)}, s32[8,8]{1,0:T(8,128)}, u32[]{:S(2)}) copy-start(s32[8,8]{1,0:T(8,128)} %tlist_h.1) | copy-start | bytes 772
  18.4 10.8 %copy-start.9 = (s32[32,4]{0,1:T(4,128)S(1)}, s32[32,4]{0,1:T(4,128)}, u32[]{:S(2)}) copy-start(s32[32,4]{0,1:T(4,128)} %param.21) | copy-start | bytes 1540
  18.5 10.8 %copy-start.10 = (s32[16,4]{0,1:T(4,128)S(1)}, s32[16,4]{0,1:T(4,128)}, u32[]{:S(2)}) copy-start(s32[16,4]{0,1:T(4,128)} %param.24) | copy-start | bytes 772
  18.5 7.3 %collective-permute-start.2 = (bf16[5,16,128]{2,1,0:T(8,128)(2,1)S(1)}, bf16[5,16,128]{2,1,0:T(8,128)(2,1)S(1)}, u32[]{:S(2)}, u32[]{:S(2)}) collective-permute-start(bf16[5,16,128]{2,1,0:T(8,128)(2,1)S(1)} %get-tuple-element.20), channel_id=1, source_target_pairs={{0,2},{1,3},{2,4},{3,5},{4,6},{5,7},{6,8},{7,9},{8,10},{9,11},{10,... | collective-permute-start | bytes 61448 | tf_op jit(solution)/shard_map/ppermute | solution.py:341
  18.7 7.1 %collective-permute-start.3 = (bf16[5,16,128]{2,1,0:T(8,128)(2,1)S(1)}, bf16[5,16,128]{2,1,0:T(8,128)(2,1)S(1)}, u32[]{:S(2)}, u32[]{:S(2)}) collective-permute-start(bf16[5,16,128]{2,1,0:T(8,128)(2,1)S(1)} %get-tuple-element.21), channel_id=1, source_target_pairs={{0,14},{1,15},{2,0},{3,1},{4,2},{5,3},{6,4},{7,5},{8,6},{9,7},{10,... | collective-permute-start | bytes 61448 | tf_op jit(solution)/shard_map/ppermute | solution.py:342
  23.2 2.6 %collective-permute-start = (bf16[6,16,128]{2,1,0:T(8,128)(2,1)S(1)}, bf16[6,16,128]{2,1,0:T(8,128)(2,1)S(1)}, u32[]{:S(2)}, u32[]{:S(2)}) collective-permute-start(bf16[6,16,128]{2,1,0:T(8,128)(2,1)S(1)} %get-tuple-element.18), channel_id=1, source_target_pairs={{0,1},{1,0},{2,3},{3,2},{4,5},{5,4},{6,7},{7,6},{8,9},{9,8},{10,11... | collective-permute-start | bytes 73736 | tf_op jit(solution)/shard_map/ppermute | solution.py:339
  23.2 5.9 %collective-permute-start.1 = (bf16[6,16,128]{2,1,0:T(8,128)(2,1)S(1)}, bf16[6,16,128]{2,1,0:T(8,128)(2,1)S(1)}, u32[]{:S(2)}, u32[]{:S(2)}) collective-permute-start(bf16[6,16,128]{2,1,0:T(8,128)(2,1)S(1)} %get-tuple-element.19), channel_id=1, source_target_pairs={{0,15},{1,2},{2,1},{3,4},{4,3},{5,6},{6,5},{7,8},{8,7},{9,10},{10,... | collective-permute-start | bytes 73736 | tf_op jit(solution)/shard_map/ppermute | solution.py:340

commit v11 on v9

--- a/solution.py
+++ b/solution.py
@@ -1,3 +1,5 @@
+import functools
+
 import jax
 import jax.numpy as jnp
 from jax import lax
@@ -105,9 +107,7 @@
             dot(beside(mid[2 * i], mid[2 * i + 1]), ptr[2 * i:2 * i + 2].reshape(2 * rank, rank)).astype(BF)
         )
     for i in range(leaves // 8):
-        both = beside(high[2 * i], high[2 * i + 1])
-        for row in range(tops.shape[0]):
-            tops[row, i] = both
+        tops[0, i] = beside(high[2 * i], high[2 * i + 1])
     made[4].wait()
     made[5].wait()
 
@@ -131,13 +131,13 @@
     pack(own, REACH)
 
 
-def up_pass(lsend, psend, vec, basis, ltr, ptr, rows):
+def up_pass(lsend, psend, vec, basis, ltr, ptr):
     leaves, vecs, rank = vec.shape
     count = (lsend.shape[2] + psend.shape[1]) // 2
     shape = lambda *n: jax.ShapeDtypeStruct(n + (vecs, 2 * rank), BF)
     return call(
         up_body, "up", (vec, basis, ltr, ptr, lsend, psend), (),
-        [shape(rows, leaves // 8), shape(count), shape(4, count + 1)],
+        [shape(1, leaves // 8), shape(count), shape(4, count + 1)],
         [WHOLE] * 3,
         [
             like(vec), like(basis), like(ltr), like(ptr), held(lsend), held(psend),
@@ -147,17 +147,31 @@
     )
 
 
-def hand_body(windows, *outs):
-    for i, out in enumerate(outs):
+def hand_body(windows, top, *outs):
+    for i, out in enumerate(outs[:-1]):
         out[...] = windows[i, :out.shape[0]]
-
-
-def hand_pass(windows, counts):
+    outs[-1][...] = top[...]
+
+
+def hand_pass(windows, top, counts):
     shape = windows.shape[2:]
     return call(
-        hand_body, "hand", (), (windows,),
-        [jax.ShapeDtypeStruct((n,) + shape, windows.dtype) for n in counts],
-        [WHOLE] * len(counts), [], (8_000_000_000, 100_000_000), 2 * 1024 * 1024,
+        hand_body, "hand", (), (windows, top),
+        [jax.ShapeDtypeStruct((n,) + shape, windows.dtype) for n in counts] + [jax.ShapeDtypeStruct(top.shape, top.dtype)],
+        [WHOLE] * (len(counts) + 1), [], (8_000_000_000, 100_000_000), 2 * 1024 * 1024,
+    )
+
+
+def join_body(first, second, out):
+    out[:first.shape[0]] = first[...]
+    out[first.shape[0]:] = second[...]
+
+
+def join_pass(first, second):
+    return call(
+        join_body, "join", (), (first, second),
+        jax.ShapeDtypeStruct((2 * first.shape[0],) + first.shape[1:], first.dtype), WHOLE, [],
+        (100_000, 500_000), 2 * 1024 * 1024,
     )
 
 
@@ -194,7 +208,7 @@
         ],
         [WHOLE] * 2,
         [VMEM((leaves + 2 * HW, vecs, rank), BF), held(offsets), DMA((1,))],
-        (4_000_000_000, 60_000_000), 8 * 1024 * 1024,
+        (1_000_000_000, 20_000_000), 8 * 1024 * 1024,
     )
 
 
@@ -202,8 +216,8 @@
     return dot_t(beside(*rows), row_of_blocks(blocks, q))
 
 
-def rest_body(llist_h, plist_h, tlist_h, offsets_h,
-              leaf, pair, coupling, ends, ptr, ltr, basis, close, own, sib, cross, fwd, back, mine, theirs, out,
+def rest_body(offs, llist_h, plist_h, tlist_h, offsets_h,
+              leaf, pair, coupling, ends, ptr, ltr, basis, close, own, sib, cross, fwd, back, held0, held1, held2, held3, out,
               llist, plist, tlist, offsets, wleaf, wpair, halo, tops, far0, far1, down, sems):
     kernels, leaves, partners, rank, _ = leaf.shape
     _, vecs, _ = wleaf.shape
@@ -226,10 +240,12 @@
         row = block[base + cap1 // 2]
         outside = (place == 0) & (upper == 0) | (place == last_place) & (upper == 1)
         split(jnp.where(outside, jnp.zeros_like(row), row), halo, upper * HW)
-    for block, side in ((mine, col), (theirs, 1 - col)):
-        for s in range(block.shape[0]):
+    row = lax.axis_index("row")
+    for h, block in enumerate((held0, held1, held2, held3)):
+        side = col if h < 2 else 1 - col
+        for s, off in enumerate(offs):
             for i in range(block.shape[1]):
-                split(block[s, i], tops, (s * 2 + side) * count + 2 * i)
+                split(block[s, i], tops, (((row ^ (off + h % 2)) * 2) + side) * count + 2 * i)
     for copy in lists:
         copy.wait()
 
@@ -271,20 +287,20 @@
             out[k, t] = points[k * vecs:(k + 1) * vecs]
 
 
-def rest_pass(lists, arrays, windows, cap0, cap1):
+def rest_pass(lists, arrays, windows, offs, cap0, cap1):
     leaf, pair, coupling = arrays[:3]
     kernels, leaves, _, rank, _ = leaf.shape
     count = coupling.shape[1]
     vecs = windows[0].shape[1]
     rows = kernels * vecs
     return call(
-        rest_body, "rest", lists, arrays + windows,
+        functools.partial(rest_body, offs), "rest", lists, arrays + windows,
         jax.ShapeDtypeStruct((kernels, leaves, vecs, rank), BF),
         WHOLE,
         [held(x) for x in lists]
         + [
             VMEM((n, vecs, rank), BF)
-            for n in (WIN * cap0, WIN * cap1, 2 * HW + 1, 2 * windows[-1].shape[0] * count)
+            for n in (WIN * cap0, WIN * cap1, 2 * HW + 1, 4 * windows[-1].shape[0] * count)
         ]
         + [
             VMEM((leaves, rows, rank), F32), VMEM((leaves // 2, rows, rank), F32),
@@ -315,24 +331,30 @@
     cap0, cap1 = leaf_send.shape[2], pair_send.shape[2]
     lsend = jnp.transpose(leaf_send, (1, 0, 2))
     psend = jnp.transpose(pair_send, (0, 2, 1))
-    tops, own, windows = up_pass(
-        lsend, psend, vectors, leaf_basis, leaf_transfer, pair_transfer, rows
-    )
+    held, own, windows = up_pass(lsend, psend, vectors, leaf_basis, leaf_transfer, pair_transfer)
     count = own.shape[0]
-    sib, cross, fwd, back = hand_pass(windows, (count + 1, count + 1, count, count))
+    sib, cross, fwd, back, held = hand_pass(windows, held, (count + 1, count + 1, count, count))
     ring = range(devs)
-    sibling = [(d, d ^ 1) for d in ring]
-    mine = lax.all_to_all(tops, "row", split_axis=0, concat_axis=0)
-    theirs = lax.ppermute(mine, AXES, sibling)
-    sib = lax.ppermute(sib, AXES, sibling)
-    cross = lax.ppermute(cross, AXES, [(d, (d + 1 if d % 2 else d - 1) % devs) for d in ring])
-    fwd = lax.ppermute(fwd, AXES, [(d, (d + 2) % devs) for d in ring])
-    back = lax.ppermute(back, AXES, [(d, (d - 2) % devs) for d in ring])
+
+    def sent(piece, target):
+        return lax.ppermute(piece, AXES, [(d, target(d)) for d in ring])
+
+    offs = [0]
+    mask = rows // 2
+    while mask > 1:
+        held = join_pass(held, sent(held, lambda d: d ^ (2 * mask)))
+        offs = offs + [off ^ mask for off in offs]
+        mask //= 2
+    sib = sent(sib, lambda d: d ^ 1)
+    cross = sent(cross, lambda d: (d + 1 if d % 2 else d - 1) % devs)
+    fwd = sent(fwd, lambda d: (d + 2) % devs)
+    back = sent(back, lambda d: (d - 2) % devs)
+    pieces = (held, sent(held, lambda d: d ^ 2), sent(held, lambda d: d ^ 1), sent(held, lambda d: d ^ 3))
     close, ends = near_pass(near_offset.T, vectors, near_blocks)
     return rest_pass(
         (leaf_list.T, pair_list.T, top_list, near_offset.T),
         (leaf_coupling, pair_coupling, top_coupling, ends, pair_transfer, leaf_transfer, leaf_basis, close),
-        (own, sib, cross, fwd, back, mine, theirs), cap0, cap1,
+        (own, sib, cross, fwd, back) + pieces, offs, cap0, cap1,
     )
 
 

time: 31 us -> 30.3 us (0.977)
  waiting for transfers between devices: 0.02 us -> 4.03 us
  local copies, waits for them, and re-layouts: 5.74 us -> 2.09 us
  starting transfers between devices: 14.2 us -> 13 us
    all_to_all x1 -> x0, starting transfers between devices: 7.29 us -> none  [on_device(): mine = lax.all_to_all(tops, 'row', split_axis=0, concat_axis=0)]
    ppermute x5 -> x9, starting transfers between devices: 6.92 us -> 13 us  [sent(): return lax.ppermute(piece, AXES, [(d, target(d)) for d in ring])]
    ppermute x5 -> x9, waiting for transfers between devices: 0.01 us -> 4.03 us  [sent(): return lax.ppermute(piece, AXES, [(d, target(d)) for d in ring])]
    unnamed x28 -> x34, local copies, waits for them, and re-layouts: 5.74 us -> 2.09 us
    pallas_call x4 -> x6, Pallas kernels: 10.6 us -> 10.7 us  [call(): pl.pallas_call(body, out_shape=out_shape, in_specs=[FIXED] * len(params)...]
  transfers between devices with their start and end apart: 6 -> 9, of which waited for: 0 -> 4; matrix products, arithmetic and copies ran while one was open for 0% -> 0% of each run, Pallas kernels for 8% -> 8%
where the time goes in v11:
time: 30.3 us; the launch traced here: 30 us
  starting transfers between devices  13 us (43%)
  Pallas kernels  10.7 us (35%)
  waiting for transfers between devices  4.03 us (13%)
  local copies, waits for them, and re-layouts  2.09 us (7%)
    ppermute x9, starting transfers between devices, sent(): return lax.ppermute(piece, AXES, [(d, target(d)) for d in ring])  13 us
    pallas_call x6, Pallas kernels, call(): pl.pallas_call(body, out_shape=out_shape, in_specs=[FIXED] * len(params)...  10.7 us
    ppermute x9, waiting for transfers between devices, sent(): return lax.ppermute(piece, AXES, [(d, target(d)) for d in ring])  4.03 us
    unnamed x34, local copies, waits for them, and re-layouts  2.09 us
  transfers between devices with their start and end apart: 9, of which 4 were waited for; matrix products, arithmetic and copies ran while one was open for 0% of the time, Pallas kernels for 8%

profile of v11, /device:TPU:0, one launch (start us, length us, event | category | flops | bytes accessed | tf_op | source)
XLA Modules:
  0.0 30.0 jit_solution(64697857826401791)
XLA Ops:
  0.0 2.8 %up.1 = (bf16[1,4,16,128]{3,2,1,0:T(8,128)(2,1)}, bf16[5,16,128]{2,1,0:T(8,128)(2,1)}, bf16[4,6,16,128]{3,2,1,0:T(8,128)(2,1)}) custom-call(bf16[32,16,64]{2,1,0:T(8,128)(2,1)} %vec_h.1, bf16[32,64,64]{2,1,0:T(8,128)(2,1)} %basis.1, bf16[32,64,64]{2,1,0:T(8,128)(2,1)} %ltr.1, bf16[16,64,64]{2,1,0:T(8,128)(2,1)} %ptr.1, s32[5,1,8]{2,1,0:T(1,128)} %bitcast.13, ...), custom_call_target="tpu_custom_call" | custom-call | flops 10000000 | bytes 3000000 | tf_op jit(solution)/shard_map/up/pallas_call | solution.py:65
  2.9 0.0 slice-start
  2.9 0.0 copy-start.11
  2.9 1.0 %copy-done.11 = bf16[4,6,16,128]{3,2,1,0:T(8,128)(2,1)S(1)} copy-done((bf16[4,6,16,128]{3,2,1,0:T(8,128)(2,1)S(1)}, bf16[4,6,16,128]{3,2,1,0:T(8,128)(2,1)}, u32[]{:S(2)}) %copy-start.11) | copy-done | bytes 98328
  3.9 1.0 %copy-done.12 = bf16[1,4,16,128]{3,2,1,0:T(8,128)(2,1)S(1)} copy-done((bf16[1,4,16,128]{3,2,1,0:T(8,128)(2,1)S(1)}, bf16[1,4,16,128]{3,2,1,0:T(8,128)(2,1)}, u32[]{:S(2)}) %copy-start.12) | copy-done | bytes 16408
  4.9 0.0 copy-start.1
  4.9 0.0 copy-start
  4.9 0.0 copy-start.2
  5.0 0.0 copy-start.3
  5.0 0.0 copy-start.4
  5.0 0.0 copy-start.6
  5.0 0.0 copy-start.8
  5.0 0.0 copy-start.9
  5.0 0.0 copy-start.10
  5.0 4.1 %collective-permute-start.4 = (bf16[1,4,16,128]{3,2,1,0:T(8,128)(2,1)S(1)}, bf16[1,4,16,128]{3,2,1,0:T(8,128)(2,1)S(1)}, u32[]{:S(2)}, u32[]{:S(2)}) collective-permute-start(bf16[1,4,16,128]{3,2,1,0:T(8,128)(2,1)S(1)} %get-tuple-element.24.first), channel_id=1, source_target_pairs={{0,8},{1,9},{2,10},{3,11},{4,12},{5,13},{6,14},{7,15},{8,0},{9,1},... | collective-permute-start | bytes 49160 | tf_op jit(solution)/shard_map/ppermute | solution.py:340
  9.1 1.7 %collective-permute-done.4.second = bf16[1,4,16,128]{3,2,1,0:T(8,128)(2,1)S(1)} collective-permute-done((bf16[1,4,16,128]{3,2,1,0:T(8,128)(2,1)S(1)}, bf16[1,4,16,128]{3,2,1,0:T(8,128)(2,1)S(1)}, u32[]{:S(2)}, u32[]{:S(2)}) %collective-permute-start.4) | collective-permute-done | bytes 16416 | tf_op jit(solution)/shard_map/ppermute | solution.py:340
  10.9 1.9 %collective-permute-start.5 = (bf16[2,4,16,128]{3,2,1,0:T(8,128)(2,1)S(1)}, bf16[2,4,16,128]{3,2,1,0:T(8,128)(2,1)S(1)}, u32[]{:S(2)}, u32[]{:S(2)}) collective-permute-start(bf16[2,4,16,128]{3,2,1,0:T(8,128)(2,1)S(1)} %join.2.first), channel_id=1, source_target_pairs={{0,4},{1,5},{2,6},{3,7},{4,0},{5,1},{6,2},{7,3},{8,12},{9,13},{10,... | collective-permute-start | bytes 98312 | tf_op jit(solution)/shard_map/ppermute | solution.py:340
  12.8 1.5 %collective-permute-start.2 = (bf16[5,16,128]{2,1,0:T(8,128)(2,1)S(1)}, bf16[5,16,128]{2,1,0:T(8,128)(2,1)S(1)}, u32[]{:S(2)}, u32[]{:S(2)}) collective-permute-start(bf16[5,16,128]{2,1,0:T(8,128)(2,1)S(1)} %get-tuple-element.22), channel_id=1, source_target_pairs={{0,2},{1,3},{2,4},{3,5},{4,6},{5,7},{6,8},{7,9},{8,10},{9,11},{10,... | collective-permute-start | bytes 61448 | tf_op jit(solution)/shard_map/ppermute | solution.py:340
  14.3 3.2 %collective-permute-start.3 = (bf16[5,16,128]{2,1,0:T(8,128)(2,1)S(1)}, bf16[5,16,128]{2,1,0:T(8,128)(2,1)S(1)}, u32[]{:S(2)}, u32[]{:S(2)}) collective-permute-start(bf16[5,16,128]{2,1,0:T(8,128)(2,1)S(1)} %get-tuple-element.23), channel_id=1, source_target_pairs={{0,14},{1,15},{2,0},{3,1},{4,2},{5,3},{6,4},{7,5},{8,6},{9,7},{10,... | collective-permute-start | bytes 61448 | tf_op jit(solution)/shard_map/ppermute | solution.py:340
  17.5 0.0 collective-permute-start
  17.5 0.9 %collective-permute-start.1 = (bf16[6,16,128]{2,1,0:T(8,128)(2,1)S(1)}, bf16[6,16,128]{2,1,0:T(8,128)(2,1)S(1)}, u32[]{:S(2)}, u32[]{:S(2)}) collective-permute-start(bf16[6,16,128]{2,1,0:T(8,128)(2,1)S(1)} %get-tuple-element.21), channel_id=1, source_target_pairs={{0,15},{1,2},{2,1},{3,4},{4,3},{5,6},{6,5},{7,8},{8,7},{9,10},{10,... | collective-permute-start | bytes 73736 | tf_op jit(solution)/shard_map/ppermute | solution.py:340
  18.3 0.0 collective-permute-done.5.second
  18.3 0.1 collective-permute-start.8
  18.4 0.8 %collective-permute-done.2.fwd = bf16[5,16,128]{2,1,0:T(8,128)(2,1)S(1)} collective-permute-done((bf16[5,16,128]{2,1,0:T(8,128)(2,1)S(1)}, bf16[5,16,128]{2,1,0:T(8,128)(2,1)S(1)}, u32[]{:S(2)}, u32[]{:S(2)}) %collective-permute-start.2) | collective-permute-done | bytes 20512 | tf_op jit(solution)/shard_map/ppermute | solution.py:340
  19.2 0.6 %collective-permute-start.7 = (bf16[4,4,16,128]{3,2,1,0:T(8,128)(2,1)S(1)}, bf16[4,4,16,128]{3,2,1,0:T(8,128)(2,1)S(1)}, u32[]{:S(2)}, u32[]{:S(2)}) collective-permute-start(bf16[4,4,16,128]{3,2,1,0:T(8,128)(2,1)S(1)} %join.3.held0), channel_id=1, source_target_pairs={{0,1},{1,0},{2,3},{3,2},{4,5},{5,4},{6,7},{7,6},{8,9},{9,8},{10,11... | collective-permute-start | bytes 196616 | tf_op jit(solution)/shard_map/ppermute | solution.py:340
  19.8 0.0 collective-permute-done.3.back
  19.8 0.7 %collective-permute-start.6 = (bf16[4,4,16,128]{3,2,1,0:T(8,128)(2,1)S(1)}, bf16[4,4,16,128]{3,2,1,0:T(8,128)(2,1)S(1)}, u32[]{:S(2)}, u32[]{:S(2)}) collective-permute-start(bf16[4,4,16,128]{3,2,1,0:T(8,128)(2,1)S(1)} %join.3.held0), channel_id=1, source_target_pairs={{0,2},{1,3},{2,0},{3,1},{4,6},{5,7},{6,4},{7,5},{8,10},{9,11},{10,... | collective-permute-start | bytes 196616 | tf_op jit(solution)/shard_map/ppermute | solution.py:340
  20.6 0.0 slice-done.2
  20.6 0.0 slice-done.3
  20.6 0.0 copy-done.5
  20.6 0.0 copy-done.7
  20.6 2.4 %near.2 = (f32[32,48,64]{2,1,0:T(8,128)S(1)}, bf16[3,4,3,64,64]{4,3,2,1,0:T(8,128)(2,1)S(1)}) custom-call(s32[3,32]{1,0:T(4,128)S(1)} %bitcast.9, bf16[32,16,64]{2,1,0:T(8,128)(2,1)S(1)} %copy-done.5, bf16[3,32,3,64,64]{4,3,2,1,0:T(8,128)(2,1)S(1)} %bitcast.8), custom_call_target="tpu_custom_call" | custom-call | flops 1000000000 | bytes 20000000 | tf_op jit(solution)/shard_map/near/pallas_call | solution.py:65
  23.0 0.0 collective-permute-done.sib
  23.0 0.5 %collective-permute-done.1.cross = bf16[6,16,128]{2,1,0:T(8,128)(2,1)S(1)} collective-permute-done((bf16[6,16,128]{2,1,0:T(8,128)(2,1)S(1)}, bf16[6,16,128]{2,1,0:T(8,128)(2,1)S(1)}, u32[]{:S(2)}, u32[]{:S(2)}) %collective-permute-start.1) | collective-permute-done | bytes 24608 | tf_op jit(solution)/shard_map/ppermute | solution.py:340
  23.5 0.0 collective-permute-done.8.held3
  23.5 0.0 collective-permute-done.7.held2
  23.5 0.9 %collective-permute-done.6.held1 = bf16[4,4,16,128]{3,2,1,0:T(8,128)(2,1)S(1)} collective-permute-done((bf16[4,4,16,128]{3,2,1,0:T(8,128)(2,1)S(1)}, bf16[4,4,16,128]{3,2,1,0:T(8,128)(2,1)S(1)}, u32[]{:S(2)}, u32[]{:S(2)}) %collective-permute-start.6) | collective-permute-done | bytes 65568 | tf_op jit(solution)/shard_map/ppermute | solution.py:340
  24.5 0.0 slice-done
  24.5 0.0 slice-done.1
  24.5 0.0 copy-done.1
  24.5 0.0 copy-done
  24.5 0.0 copy-done.2
  24.5 0.0 copy-done.3
  24.5 0.0 copy-done.4
  24.5 0.0 copy-done.6
  24.6 0.0 copy-done.8
  24.6 0.0 copy-done.9
  24.6 5.4 %rest.1 = bf16[3,32,16,64]{3,2,1,0:T(8,128)(2,1)} custom-call(s32[4,32]{1,0:T(4,128)S(1)} %bitcast.11, s32[4,16]{1,0:T(4,128)S(1)} %bitcast.12, s32[8,8]{1,0:T(8,128)S(1)} %copy-done.8, s32[3,32]{1,0:T(4,128)S(1)} %bitcast.10, bf16[3,32,4,64,64]{4,3,2,1,0:T(8,128)(2,1)S(1)} %bitcast.6, bf16[3,16,4,64,64]{4,3,2,1,0:T(8,128)(2,1)S(1)} %copy-done, ...), custom_call_target="tpu_custom_call" | custom-call | flops 150000000 | bytes 20000000 | tf_op jit(solution)/shard_map/rest/pallas_call | solution.py:65
  (12 shorter events, 0.0 us)
Async XLA Ops:
  0.0 20.6 %slice-start.2 = ((s8[4718592]{0:T(1024)(128)(4,1)}), s8[524288]{0:T(1024)(128)(4,1)S(1)}, s32[]{:S(2)}) async-start(s8[4718592]{0:T(1024)(128)(4,1)} %bitcast.7), calls=%async_computation.2 | async-start | bytes 1048576
  2.9 21.6 %slice-start = ((s8[6291456]{0:T(1024)(128)(4,1)}), s8[4194304]{0:T(1024)(128)(4,1)S(1)}, s32[]{:S(2)}) async-start(s8[6291456]{0:T(1024)(128)(4,1)} %bitcast.5), calls=%async_computation | async-start | bytes 8388608
  2.9 1.0 %copy-start.11 = (bf16[4,6,16,128]{3,2,1,0:T(8,128)(2,1)S(1)}, bf16[4,6,16,128]{3,2,1,0:T(8,128)(2,1)}, u32[]{:S(2)}) copy-start(bf16[4,6,16,128]{3,2,1,0:T(8,128)(2,1)} %get-tuple-element.18.windows) | copy-start | bytes 294916
  3.9 1.0 %copy-start.12 = (bf16[1,4,16,128]{3,2,1,0:T(8,128)(2,1)S(1)}, bf16[1,4,16,128]{3,2,1,0:T(8,128)(2,1)}, u32[]{:S(2)}) copy-start(bf16[1,4,16,128]{3,2,1,0:T(8,128)(2,1)} %get-tuple-element.19.top) | copy-start | bytes 49156
  4.9 15.7 %slice-start.3 = ((s8[4718592]{0:T(1024)(128)(4,1)}), s8[4194304]{0:T(1024)(128)(4,1)S(1)}, s32[]{:S(2)}) async-start(s8[4718592]{0:T(1024)(128)(4,1)} %bitcast.7), calls=%async_computation.3 | async-start | bytes 8388608
  4.9 15.7 %copy-start.5 = (bf16[32,16,64]{2,1,0:T(8,128)(2,1)S(1)}, bf16[32,16,64]{2,1,0:T(8,128)(2,1)}, u32[]{:S(2)}) copy-start(bf16[32,16,64]{2,1,0:T(8,128)(2,1)} %vec_h.1) | copy-start | bytes 196612
  4.9 15.7 %copy-start.7 = (s32[32,3]{0,1:T(4,128)S(1)}, s32[32,3]{0,1:T(4,128)}, u32[]{:S(2)}) copy-start(s32[32,3]{0,1:T(4,128)} %param.19) | copy-start | bytes 1156
  4.9 19.6 %slice-start.1 = ((s8[6291456]{0:T(1024)(128)(4,1)}), s8[2097152]{0:T(1024)(128)(4,1)S(1)}, s32[]{:S(2)}) async-start(s8[6291456]{0:T(1024)(128)(4,1)} %bitcast.5), calls=%async_computation.1 | async-start | bytes 4194304
  4.9 19.6 %copy-start.1 = (bf16[3,8,8,64,64]{4,3,2,1,0:T(8,128)(2,1)S(1)}, bf16[3,8,8,64,64]{4,3,2,1,0:T(8,128)(2,1)}, u32[]{:S(2)}) copy-start(bf16[3,8,8,64,64]{4,3,2,1,0:T(8,128)(2,1)} %coupling.1) | copy-start | bytes 4718596
  4.9 19.6 %copy-start = (bf16[3,16,4,64,64]{4,3,2,1,0:T(8,128)(2,1)S(1)}, bf16[3,16,4,64,64]{4,3,2,1,0:T(8,128)(2,1)}, u32[]{:S(2)}) copy-start(bf16[3,16,4,64,64]{4,3,2,1,0:T(8,128)(2,1)} %pair.1) | copy-start | bytes 4718596
  4.9 19.6 %copy-start.2 = (bf16[32,64,64]{2,1,0:T(8,128)(2,1)S(1)}, bf16[32,64,64]{2,1,0:T(8,128)(2,1)}, u32[]{:S(2)}) copy-start(bf16[32,64,64]{2,1,0:T(8,128)(2,1)} %ltr.1) | copy-start | bytes 786436
  5.0 19.6 %copy-start.3 = (bf16[32,64,64]{2,1,0:T(8,128)(2,1)S(1)}, bf16[32,64,64]{2,1,0:T(8,128)(2,1)}, u32[]{:S(2)}) copy-start(bf16[32,64,64]{2,1,0:T(8,128)(2,1)} %basis.1) | copy-start | bytes 786436
  5.0 19.6 %copy-start.4 = (bf16[16,64,64]{2,1,0:T(8,128)(2,1)S(1)}, bf16[16,64,64]{2,1,0:T(8,128)(2,1)}, u32[]{:S(2)}) copy-start(bf16[16,64,64]{2,1,0:T(8,128)(2,1)} %ptr.1) | copy-start | bytes 393220
  5.0 19.6 %copy-start.6 = (bf16[5,16,128]{2,1,0:T(8,128)(2,1)S(1)}, bf16[5,16,128]{2,1,0:T(8,128)(2,1)}, u32[]{:S(2)}) copy-start(bf16[5,16,128]{2,1,0:T(8,128)(2,1)} %get-tuple-element.17.own) | copy-start | bytes 61444
  5.0 19.6 %copy-start.8 = (s32[8,8]{1,0:T(8,128)S(1)}, s32[8,8]{1,0:T(8,128)}, u32[]{:S(2)}) copy-start(s32[8,8]{1,0:T(8,128)} %tlist_h.1) | copy-start | bytes 772
  5.0 19.6 %copy-start.9 = (s32[32,4]{0,1:T(4,128)S(1)}, s32[32,4]{0,1:T(4,128)}, u32[]{:S(2)}) copy-start(s32[32,4]{0,1:T(4,128)} %param.21) | copy-start | bytes 1540
  5.0 19.6 %copy-start.10 = (s32[16,4]{0,1:T(4,128)S(1)}, s32[16,4]{0,1:T(4,128)}, u32[]{:S(2)}) copy-start(s32[16,4]{0,1:T(4,128)} %param.24) | copy-start | bytes 772
  5.0 5.8 %collective-permute-start.4 = (bf16[1,4,16,128]{3,2,1,0:T(8,128)(2,1)S(1)}, bf16[1,4,16,128]{3,2,1,0:T(8,128)(2,1)S(1)}, u32[]{:S(2)}, u32[]{:S(2)}) collective-permute-start(bf16[1,4,16,128]{3,2,1,0:T(8,128)(2,1)S(1)} %get-tuple-element.24.first), channel_id=1, source_target_pairs={{0,8},{1,9},{2,10},{3,11},{4,12},{5,13},{6,14},{7,15},{8,0},{9,1},... | collective-permute-start | bytes 49160 | tf_op jit(solution)/shard_map/ppermute | solution.py:340
  10.9 7.5 %collective-permute-start.5 = (bf16[2,4,16,128]{3,2,1,0:T(8,128)(2,1)S(1)}, bf16[2,4,16,128]{3,2,1,0:T(8,128)(2,1)S(1)}, u32[]{:S(2)}, u32[]{:S(2)}) collective-permute-start(bf16[2,4,16,128]{3,2,1,0:T(8,128)(2,1)S(1)} %join.2.first), channel_id=1, source_target_pairs={{0,4},{1,5},{2,6},{3,7},{4,0},{5,1},{6,2},{7,3},{8,12},{9,13},{10,... | collective-permute-start | bytes 98312 | tf_op jit(solution)/shard_map/ppermute | solution.py:340
  12.8 6.5 %collective-permute-start.2 = (bf16[5,16,128]{2,1,0:T(8,128)(2,1)S(1)}, bf16[5,16,128]{2,1,0:T(8,128)(2,1)S(1)}, u32[]{:S(2)}, u32[]{:S(2)}) collective-permute-start(bf16[5,16,128]{2,1,0:T(8,128)(2,1)S(1)} %get-tuple-element.22), channel_id=1, source_target_pairs={{0,2},{1,3},{2,4},{3,5},{4,6},{5,7},{6,8},{7,9},{8,10},{9,11},{10,... | collective-permute-start | bytes 61448 | tf_op jit(solution)/shard_map/ppermute | solution.py:340
  14.3 5.5 %collective-permute-start.3 = (bf16[5,16,128]{2,1,0:T(8,128)(2,1)S(1)}, bf16[5,16,128]{2,1,0:T(8,128)(2,1)S(1)}, u32[]{:S(2)}, u32[]{:S(2)}) collective-permute-start(bf16[5,16,128]{2,1,0:T(8,128)(2,1)S(1)} %get-tuple-element.23), channel_id=1, source_target_pairs={{0,14},{1,15},{2,0},{3,1},{4,2},{5,3},{6,4},{7,5},{8,6},{9,7},{10,... | collective-permute-start | bytes 61448 | tf_op jit(solution)/shard_map/ppermute | solution.py:340
  17.5 5.5 %collective-permute-start = (bf16[6,16,128]{2,1,0:T(8,128)(2,1)S(1)}, bf16[6,16,128]{2,1,0:T(8,128)(2,1)S(1)}, u32[]{:S(2)}, u32[]{:S(2)}) collective-permute-start(bf16[6,16,128]{2,1,0:T(8,128)(2,1)S(1)} %get-tuple-element.20), channel_id=1, source_target_pairs={{0,1},{1,0},{2,3},{3,2},{4,5},{5,4},{6,7},{7,6},{8,9},{9,8},{10,11... | collective-permute-start | bytes 73736 | tf_op jit(solution)/shard_map/ppermute | solution.py:340
  17.5 6.1 %collective-permute-start.1 = (bf16[6,16,128]{2,1,0:T(8,128)(2,1)S(1)}, bf16[6,16,128]{2,1,0:T(8,128)(2,1)S(1)}, u32[]{:S(2)}, u32[]{:S(2)}) collective-permute-start(bf16[6,16,128]{2,1,0:T(8,128)(2,1)S(1)} %get-tuple-element.21), channel_id=1, source_target_pairs={{0,15},{1,2},{2,1},{3,4},{4,3},{5,6},{6,5},{7,8},{8,7},{9,10},{10,... | collective-permute-start | bytes 73736 | tf_op jit(solution)/shard_map/ppermute | solution.py:340
  18.3 5.2 %collective-permute-start.8 = (bf16[4,4,16,128]{3,2,1,0:T(8,128)(2,1)S(1)}, bf16[4,4,16,128]{3,2,1,0:T(8,128)(2,1)S(1)}, u32[]{:S(2)}, u32[]{:S(2)}) collective-permute-start(bf16[4,4,16,128]{3,2,1,0:T(8,128)(2,1)S(1)} %join.3.held0), channel_id=1, source_target_pairs={{0,3},{1,2},{2,1},{3,0},{4,7},{5,6},{6,5},{7,4},{8,11},{9,10},{10,... | collective-permute-start | bytes 196616 | tf_op jit(solution)/shard_map/ppermute | solution.py:340
  19.2 4.3 %collective-permute-start.7 = (bf16[4,4,16,128]{3,2,1,0:T(8,128)(2,1)S(1)}, bf16[4,4,16,128]{3,2,1,0:T(8,128)(2,1)S(1)}, u32[]{:S(2)}, u32[]{:S(2)}) collective-permute-start(bf16[4,4,16,128]{3,2,1,0:T(8,128)(2,1)S(1)} %join.3.held0), channel_id=1, source_target_pairs={{0,1},{1,0},{2,3},{3,2},{4,5},{5,4},{6,7},{7,6},{8,9},{9,8},{10,11... | collective-permute-start | bytes 196616 | tf_op jit(solution)/shard_map/ppermute | solution.py:340
  19.8 4.7 %collective-permute-start.6 = (bf16[4,4,16,128]{3,2,1,0:T(8,128)(2,1)S(1)}, bf16[4,4,16,128]{3,2,1,0:T(8,128)(2,1)S(1)}, u32[]{:S(2)}, u32[]{:S(2)}) collective-permute-start(bf16[4,4,16,128]{3,2,1,0:T(8,128)(2,1)S(1)} %join.3.held0), channel_id=1, source_target_pairs={{0,2},{1,3},{2,0},{3,1},{4,6},{5,7},{6,4},{7,5},{8,10},{9,11},{10,... | collective-permute-start | bytes 196616 | tf_op jit(solution)/shard_map/ppermute | solution.py:340

commit v12 on v11

--- a/solution.py
+++ b/solution.py
@@ -10,7 +10,7 @@
 REACH = 2
 WIN = 2 * REACH + 1
 HW = 2
-GROUP = 8
+GROUP = 16
 AXES = ("row", "col")
 F32 = jnp.float32
 BF = jnp.bfloat16
@@ -82,7 +82,7 @@
     return SMEM(x.shape, x.dtype)
 
 
-def up_body(vec_h, basis_h, ltr_h, ptr_h, lsend_h, psend_h, tops, own, windows,
+def up_body(vec_h, basis_h, ltr_h, ptr_h, lsend_h, psend_h, tops, own, sib, cross, fwd, back,
             vec, basis, ltr, ptr, lsend, psend, low, mid, sems):
     leaves, vecs, rank = vec.shape
     col = lax.axis_index("col")
@@ -111,8 +111,6 @@
     made[4].wait()
     made[5].wait()
 
-    sib, cross, fwd, back = [windows.at[i] for i in range(4)]
-
     def pack(out, place):
         for c in range(cap0 // 2):
             out[c] = beside(low[lsend[place, 0, 2 * c]], low[lsend[place, 0, 2 * c + 1]])
@@ -137,8 +135,8 @@
     shape = lambda *n: jax.ShapeDtypeStruct(n + (vecs, 2 * rank), BF)
     return call(
         up_body, "up", (vec, basis, ltr, ptr, lsend, psend), (),
-        [shape(1, leaves // 8), shape(count), shape(4, count + 1)],
-        [WHOLE] * 3,
+        [shape(1, leaves // 8), shape(count), shape(count + 1), shape(count + 1), shape(count), shape(count)],
+        [WHOLE] * 6,
         [
             like(vec), like(basis), like(ltr), like(ptr), held(lsend), held(psend),
             VMEM((leaves, vecs, rank), BF), VMEM((leaves // 2, vecs, rank), BF), DMA((6,)),
@@ -147,31 +145,17 @@
     )
 
 
-def hand_body(windows, top, *outs):
-    for i, out in enumerate(outs[:-1]):
-        out[...] = windows[i, :out.shape[0]]
-    outs[-1][...] = top[...]
-
-
-def hand_pass(windows, top, counts):
-    shape = windows.shape[2:]
-    return call(
-        hand_body, "hand", (), (windows, top),
-        [jax.ShapeDtypeStruct((n,) + shape, windows.dtype) for n in counts] + [jax.ShapeDtypeStruct(top.shape, top.dtype)],
-        [WHOLE] * (len(counts) + 1), [], (8_000_000_000, 100_000_000), 2 * 1024 * 1024,
-    )
-
-
-def join_body(first, second, out):
+def join_body(first, second, *rest):
+    out = rest[-1]
     out[:first.shape[0]] = first[...]
     out[first.shape[0]:] = second[...]
 
 
-def join_pass(first, second):
+def join_pass(first, second, *others):
     return call(
-        join_body, "join", (), (first, second),
+        join_body, "join", (), (first, second) + others,
         jax.ShapeDtypeStruct((2 * first.shape[0],) + first.shape[1:], first.dtype), WHOLE, [],
-        (100_000, 500_000), 2 * 1024 * 1024,
+        (8_000_000_000, 100_000_000) if others else (100_000, 500_000), 2 * 1024 * 1024,
     )
 
 
@@ -331,9 +315,9 @@
     cap0, cap1 = leaf_send.shape[2], pair_send.shape[2]
     lsend = jnp.transpose(leaf_send, (1, 0, 2))
     psend = jnp.transpose(pair_send, (0, 2, 1))
-    held, own, windows = up_pass(lsend, psend, vectors, leaf_basis, leaf_transfer, pair_transfer)
-    count = own.shape[0]
-    sib, cross, fwd, back, held = hand_pass(windows, held, (count + 1, count + 1, count, count))
+    held, own, sib, cross, fwd, back = up_pass(
+        lsend, psend, vectors, leaf_basis, leaf_transfer, pair_transfer
+    )
     ring = range(devs)
 
     def sent(piece, target):
@@ -341,15 +325,19 @@
 
     offs = [0]
     mask = rows // 2
+    got = sent(held, lambda d: d ^ (2 * mask))
+    fwd = sent(fwd, lambda d: (d + 2) % devs)
+    back = sent(back, lambda d: (d - 2) % devs)
+    others = (fwd, back)
     while mask > 1:
-        held = join_pass(held, sent(held, lambda d: d ^ (2 * mask)))
+        held = join_pass(held, got, *others)
         offs = offs + [off ^ mask for off in offs]
         mask //= 2
+        got = sent(held, lambda d: d ^ (2 * mask))
+        others = ()
     sib = sent(sib, lambda d: d ^ 1)
     cross = sent(cross, lambda d: (d + 1 if d % 2 else d - 1) % devs)
-    fwd = sent(fwd, lambda d: (d + 2) % devs)
-    back = sent(back, lambda d: (d - 2) % devs)
-    pieces = (held, sent(held, lambda d: d ^ 2), sent(held, lambda d: d ^ 1), sent(held, lambda d: d ^ 3))
+    pieces = (held, got, sent(held, lambda d: d ^ 1), sent(held, lambda d: d ^ 3))
     close, ends = near_pass(near_offset.T, vectors, near_blocks)
     return rest_pass(
         (leaf_list.T, pair_list.T, top_list, near_offset.T),

time: 30.3 us -> 29 us (0.957)
  waiting for transfers between devices: 4.03 us -> 6.15 us
  starting transfers between devices: 13 us -> 11.4 us
  Pallas kernels: 10.7 us -> 9.63 us
  local copies, waits for them, and re-layouts: 2.09 us -> 1.36 us
    ppermute x9, waiting for transfers between devices: 4.03 us -> 6.15 us  [sent(): return lax.ppermute(piece, AXES, [(d, target(d)) for d in ring])]
    ppermute x9, starting transfers between devices: 13 us -> 11.4 us  [sent(): return lax.ppermute(piece, AXES, [(d, target(d)) for d in ring])]
    pallas_call x6 -> x5, Pallas kernels: 10.7 us -> 9.63 us  [call(): pl.pallas_call(body, out_shape=out_shape, in_specs=[FIXED] * len(params)...]
    unnamed x34 -> x36, local copies, waits for them, and re-layouts: 2.09 us -> 1.36 us
  transfers between devices with their start and end apart: 9 -> 9, of which waited for: 4 -> 3; matrix products, arithmetic and copies ran while one was open for 0% -> 0% of each run, Pallas kernels for 8% -> 7%
where the time goes in v12:
time: 29 us; the launch traced here: 28.8 us
  starting transfers between devices  11.4 us (39%)
  Pallas kernels  9.63 us (33%)
  waiting for transfers between devices  6.15 us (21%)
  local copies, waits for them, and re-layouts  1.36 us (5%)
    ppermute x9, starting transfers between devices, sent(): return lax.ppermute(piece, AXES, [(d, target(d)) for d in ring])  11.4 us
    pallas_call x5, Pallas kernels, call(): pl.pallas_call(body, out_shape=out_shape, in_specs=[FIXED] * len(params)...  9.63 us
    ppermute x9, waiting for transfers between devices, sent(): return lax.ppermute(piece, AXES, [(d, target(d)) for d in ring])  6.15 us
    unnamed x36, local copies, waits for them, and re-layouts  1.36 us
  transfers between devices with their start and end apart: 9, of which 3 were waited for; matrix products, arithmetic and copies ran while one was open for 0% of the time, Pallas kernels for 7%

profile of v12, /device:TPU:0, one launch (start us, length us, event | category | flops | bytes accessed | tf_op | source)
XLA Modules:
  0.0 28.8 jit_solution(3033869374795409082)
XLA Ops:
  0.0 2.8 %up.1 = (bf16[1,4,16,128]{3,2,1,0:T(8,128)(2,1)}, bf16[5,16,128]{2,1,0:T(8,128)(2,1)}, bf16[6,16,128]{2,1,0:T(8,128)(2,1)}, bf16[6,16,128]{2,1,0:T(8,128)(2,1)},...) custom-call(bf16[32,16,64]{2,1,0:T(8,128)(2,1)} %vec_h.1, bf16[32,64,64]{2,1,0:T(8,128)(2,1)} %basis.1, ...), custom_call_target="tpu_custom_call" | custom-call | flops 10000000 | bytes 3000000 | tf_op jit(solution)/shard_map/up/pallas_call | solution.py:65
  2.8 3.0 %collective-permute-start.2 = (bf16[5,16,128]{2,1,0:T(8,128)(2,1)}, bf16[5,16,128]{2,1,0:T(8,128)(2,1)S(1)}, u32[]{:S(2)}, u32[]{:S(2)}) collective-permute-start(bf16[5,16,128]{2,1,0:T(8,128)(2,1)} %get-tuple-element.18), channel_id=1, source_target_pairs={{0,2},{1,3},{2,4},{3,5},{4,6},{5,7},{6,8},{7,9},{8,10},{9,11},{10,... | collective-permute-start | bytes 61448 | tf_op jit(solution)/shard_map/ppermute | solution.py:324
  5.8 3.1 %collective-permute-start.3 = (bf16[5,16,128]{2,1,0:T(8,128)(2,1)}, bf16[5,16,128]{2,1,0:T(8,128)(2,1)S(1)}, u32[]{:S(2)}, u32[]{:S(2)}) collective-permute-start(bf16[5,16,128]{2,1,0:T(8,128)(2,1)} %get-tuple-element.19), channel_id=1, source_target_pairs={{0,14},{1,15},{2,0},{3,1},{4,2},{5,3},{6,4},{7,5},{8,6},{9,7},{10,... | collective-permute-start | bytes 61448 | tf_op jit(solution)/shard_map/ppermute | solution.py:324
  8.9 0.0 copy-start.7
  8.9 0.0 slice-start.1
  8.9 1.0 %collective-permute-start.4 = (bf16[1,4,16,128]{3,2,1,0:T(8,128)(2,1)}, bf16[1,4,16,128]{3,2,1,0:T(8,128)(2,1)S(1)}, u32[]{:S(2)}, u32[]{:S(2)}) collective-permute-start(bf16[1,4,16,128]{3,2,1,0:T(8,128)(2,1)} %get-tuple-element.20.first), channel_id=1, source_target_pairs={{0,8},{1,9},{2,10},{3,11},{4,12},{5,13},{6,14},{7,15},{8,0},{9,1},... | collective-permute-start | bytes 49160 | tf_op jit(solution)/shard_map/ppermute | solution.py:324
  9.9 4.0 %collective-permute-done.4.second = bf16[1,4,16,128]{3,2,1,0:T(8,128)(2,1)S(1)} collective-permute-done((bf16[1,4,16,128]{3,2,1,0:T(8,128)(2,1)}, bf16[1,4,16,128]{3,2,1,0:T(8,128)(2,1)S(1)}, u32[]{:S(2)}, u32[]{:S(2)}) %collective-permute-start.4) | collective-permute-done | bytes 16416 | tf_op jit(solution)/shard_map/ppermute | solution.py:324
  13.9 0.0 collective-permute-done.2.rest_0_.fwd
  13.9 0.0 collective-permute-done.3.rest_1_.back
  13.9 0.7 %copy-done.11 = bf16[1,4,16,128]{3,2,1,0:T(8,128)(2,1)S(1)} copy-done((bf16[1,4,16,128]{3,2,1,0:T(8,128)(2,1)S(1)}, bf16[1,4,16,128]{3,2,1,0:T(8,128)(2,1)}, u32[]{:S(2)}) %copy-start.11) | copy-done | bytes 16408
  14.6 0.0 copy-start
  14.6 0.0 copy-start.2
  14.6 0.0 copy-start.3
  14.6 0.0 copy-start.4
  14.7 0.0 copy-start.6
  14.7 0.0 copy-start.8
  14.7 0.0 copy-start.9
  14.7 0.0 copy-start.10
  14.7 0.1 collective-permute-start.5
  14.8 0.6 %copy-done.13 = bf16[6,16,128]{2,1,0:T(8,128)(2,1)S(1)} copy-done((bf16[6,16,128]{2,1,0:T(8,128)(2,1)S(1)}, bf16[6,16,128]{2,1,0:T(8,128)(2,1)}, u32[]{:S(2)}) %copy-start.13) | copy-done | bytes 24600
  15.3 0.0 collective-permute-start
  15.3 0.0 copy-done.12
  15.3 2.1 %collective-permute-start.1 = (bf16[6,16,128]{2,1,0:T(8,128)(2,1)S(1)}, bf16[6,16,128]{2,1,0:T(8,128)(2,1)S(1)}, u32[]{:S(2)}, u32[]{:S(2)}) collective-permute-start(bf16[6,16,128]{2,1,0:T(8,128)(2,1)S(1)} %copy-done.12), channel_id=1, source_target_pairs={{0,15},{1,2},{2,1},{3,4},{4,3},{5,6},{6,5},{7,8},{8,7},{9,10},{10,... | collective-permute-start | bytes 73736 | tf_op jit(solution)/shard_map/ppermute | solution.py:324
  17.5 1.2 %collective-permute-done.5.second = bf16[2,4,16,128]{3,2,1,0:T(8,128)(2,1)S(1)} collective-permute-done((bf16[2,4,16,128]{3,2,1,0:T(8,128)(2,1)S(1)}, bf16[2,4,16,128]{3,2,1,0:T(8,128)(2,1)S(1)}, u32[]{:S(2)}, u32[]{:S(2)}) %collective-permute-start.5) | collective-permute-done | bytes 32800 | tf_op jit(solution)/shard_map/ppermute | solution.py:324
  18.7 0.0 collective-permute-start.8
  18.7 0.1 collective-permute-start.7
  18.8 2.1 %collective-permute-start.6 = (bf16[4,4,16,128]{3,2,1,0:T(8,128)(2,1)S(1)}, bf16[4,4,16,128]{3,2,1,0:T(8,128)(2,1)S(1)}, u32[]{:S(2)}, u32[]{:S(2)}) collective-permute-start(bf16[4,4,16,128]{3,2,1,0:T(8,128)(2,1)S(1)} %join.3.held0), channel_id=1, source_target_pairs={{0,2},{1,3},{2,0},{3,1},{4,6},{5,7},{6,4},{7,5},{8,10},{9,11},{10,... | collective-permute-start | bytes 196616 | tf_op jit(solution)/shard_map/ppermute | solution.py:324
  20.8 0.0 slice-done.2
  20.8 0.0 slice-done.3
  20.8 0.0 copy-done.5
  20.8 0.0 copy-done.7
  20.8 1.9 %near.2 = (f32[32,48,64]{2,1,0:T(8,128)S(1)}, bf16[3,4,3,64,64]{4,3,2,1,0:T(8,128)(2,1)S(1)}) custom-call(s32[3,32]{1,0:T(4,128)S(1)} %bitcast.9, bf16[32,16,64]{2,1,0:T(8,128)(2,1)S(1)} %copy-done.5, bf16[3,32,3,64,64]{4,3,2,1,0:T(8,128)(2,1)S(1)} %bitcast.8), custom_call_target="tpu_custom_call" | custom-call | flops 1000000000 | bytes 20000000 | tf_op jit(solution)/shard_map/near/pallas_call | solution.py:65
  22.8 0.0 collective-permute-done.sib
  22.8 0.0 collective-permute-done.1.cross
  22.8 0.0 collective-permute-done.8.held3
  22.8 0.0 collective-permute-done.7.held2
  22.8 1.0 %collective-permute-done.6.held1 = bf16[4,4,16,128]{3,2,1,0:T(8,128)(2,1)S(1)} collective-permute-done((bf16[4,4,16,128]{3,2,1,0:T(8,128)(2,1)S(1)}, bf16[4,4,16,128]{3,2,1,0:T(8,128)(2,1)S(1)}, u32[]{:S(2)}, u32[]{:S(2)}) %collective-permute-start.6) | collective-permute-done | bytes 65568 | tf_op jit(solution)/shard_map/ppermute | solution.py:324
  23.8 0.0 slice-done
  23.8 0.0 slice-done.1
  23.8 0.0 copy-done.1
  23.8 0.0 copy-done
  23.8 0.0 copy-done.2
  23.8 0.0 copy-done.3
  23.8 0.0 copy-done.4
  23.8 0.0 copy-done.6
  23.8 0.0 copy-done.8
  23.8 0.0 copy-done.9
  23.9 4.9 %rest.1 = bf16[3,32,16,64]{3,2,1,0:T(8,128)(2,1)} custom-call(s32[4,32]{1,0:T(4,128)S(1)} %bitcast.11, s32[4,16]{1,0:T(4,128)S(1)} %bitcast.12, s32[8,8]{1,0:T(8,128)S(1)} %copy-done.8, s32[3,32]{1,0:T(4,128)S(1)} %bitcast.10, bf16[3,32,4,64,64]{4,3,2,1,0:T(8,128)(2,1)S(1)} %bitcast.6, bf16[3,16,4,64,64]{4,3,2,1,0:T(8,128)(2,1)S(1)} %copy-done, ...), custom_call_target="tpu_custom_call" | custom-call | flops 150000000 | bytes 20000000 | tf_op jit(solution)/shard_map/rest/pallas_call | solution.py:65
  (13 shorter events, 0.0 us)
Async XLA Ops:
  2.8 11.1 %collective-permute-start.2 = (bf16[5,16,128]{2,1,0:T(8,128)(2,1)}, bf16[5,16,128]{2,1,0:T(8,128)(2,1)S(1)}, u32[]{:S(2)}, u32[]{:S(2)}) collective-permute-start(bf16[5,16,128]{2,1,0:T(8,128)(2,1)} %get-tuple-element.18), channel_id=1, source_target_pairs={{0,2},{1,3},{2,4},{3,5},{4,6},{5,7},{6,8},{7,9},{8,10},{9,11},{10,... | collective-permute-start | bytes 61448 | tf_op jit(solution)/shard_map/ppermute | solution.py:324
  5.8 8.1 %collective-permute-start.3 = (bf16[5,16,128]{2,1,0:T(8,128)(2,1)}, bf16[5,16,128]{2,1,0:T(8,128)(2,1)S(1)}, u32[]{:S(2)}, u32[]{:S(2)}) collective-permute-start(bf16[5,16,128]{2,1,0:T(8,128)(2,1)} %get-tuple-element.19), channel_id=1, source_target_pairs={{0,14},{1,15},{2,0},{3,1},{4,2},{5,3},{6,4},{7,5},{8,6},{9,7},{10,... | collective-permute-start | bytes 61448 | tf_op jit(solution)/shard_map/ppermute | solution.py:324
  8.9 11.9 %slice-start.2 = ((s8[4718592]{0:T(1024)(128)(4,1)}), s8[4194304]{0:T(1024)(128)(4,1)S(1)}, s32[]{:S(2)}) async-start(s8[4718592]{0:T(1024)(128)(4,1)} %bitcast.7), calls=%async_computation.2 | async-start | bytes 8388608
  8.9 14.8 %slice-start = ((s8[6291456]{0:T(1024)(128)(4,1)}), s8[4194304]{0:T(1024)(128)(4,1)S(1)}, s32[]{:S(2)}) async-start(s8[6291456]{0:T(1024)(128)(4,1)} %bitcast.5), calls=%async_computation | async-start | bytes 8388608
  8.9 11.9 %slice-start.3 = ((s8[4718592]{0:T(1024)(128)(4,1)}), s8[524288]{0:T(1024)(128)(4,1)S(1)}, s32[]{:S(2)}) async-start(s8[4718592]{0:T(1024)(128)(4,1)} %bitcast.7), calls=%async_computation.3 | async-start | bytes 1048576
  8.9 11.9 %copy-start.5 = (bf16[32,16,64]{2,1,0:T(8,128)(2,1)S(1)}, bf16[32,16,64]{2,1,0:T(8,128)(2,1)}, u32[]{:S(2)}) copy-start(bf16[32,16,64]{2,1,0:T(8,128)(2,1)} %vec_h.1) | copy-start | bytes 196612
  8.9 11.9 %copy-start.7 = (s32[32,3]{0,1:T(4,128)S(1)}, s32[32,3]{0,1:T(4,128)}, u32[]{:S(2)}) copy-start(s32[32,3]{0,1:T(4,128)} %param.19) | copy-start | bytes 1156
  8.9 14.8 %slice-start.1 = ((s8[6291456]{0:T(1024)(128)(4,1)}), s8[2097152]{0:T(1024)(128)(4,1)S(1)}, s32[]{:S(2)}) async-start(s8[6291456]{0:T(1024)(128)(4,1)} %bitcast.5), calls=%async_computation.1 | async-start | bytes 4194304
  8.9 4.9 %collective-permute-start.4 = (bf16[1,4,16,128]{3,2,1,0:T(8,128)(2,1)}, bf16[1,4,16,128]{3,2,1,0:T(8,128)(2,1)S(1)}, u32[]{:S(2)}, u32[]{:S(2)}) collective-permute-start(bf16[1,4,16,128]{3,2,1,0:T(8,128)(2,1)} %get-tuple-element.20.first), channel_id=1, source_target_pairs={{0,8},{1,9},{2,10},{3,11},{4,12},{5,13},{6,14},{7,15},{8,0},{9,1},... | collective-permute-start | bytes 49160 | tf_op jit(solution)/shard_map/ppermute | solution.py:324
  13.9 0.7 %copy-start.11 = (bf16[1,4,16,128]{3,2,1,0:T(8,128)(2,1)S(1)}, bf16[1,4,16,128]{3,2,1,0:T(8,128)(2,1)}, u32[]{:S(2)}) copy-start(bf16[1,4,16,128]{3,2,1,0:T(8,128)(2,1)} %get-tuple-element.20.first) | copy-start | bytes 49156
  14.6 0.7 %copy-start.13 = (bf16[6,16,128]{2,1,0:T(8,128)(2,1)S(1)}, bf16[6,16,128]{2,1,0:T(8,128)(2,1)}, u32[]{:S(2)}) copy-start(bf16[6,16,128]{2,1,0:T(8,128)(2,1)} %get-tuple-element.16) | copy-start | bytes 73732
  14.6 0.8 %copy-start.12 = (bf16[6,16,128]{2,1,0:T(8,128)(2,1)S(1)}, bf16[6,16,128]{2,1,0:T(8,128)(2,1)}, u32[]{:S(2)}) copy-start(bf16[6,16,128]{2,1,0:T(8,128)(2,1)} %get-tuple-element.17) | copy-start | bytes 73732
  14.6 9.2 %copy-start.1 = (bf16[3,8,8,64,64]{4,3,2,1,0:T(8,128)(2,1)S(1)}, bf16[3,8,8,64,64]{4,3,2,1,0:T(8,128)(2,1)}, u32[]{:S(2)}) copy-start(bf16[3,8,8,64,64]{4,3,2,1,0:T(8,128)(2,1)} %coupling.1) | copy-start | bytes 4718596
  14.6 9.2 %copy-start = (bf16[3,16,4,64,64]{4,3,2,1,0:T(8,128)(2,1)S(1)}, bf16[3,16,4,64,64]{4,3,2,1,0:T(8,128)(2,1)}, u32[]{:S(2)}) copy-start(bf16[3,16,4,64,64]{4,3,2,1,0:T(8,128)(2,1)} %pair.1) | copy-start | bytes 4718596
  14.6 9.2 %copy-start.2 = (bf16[32,64,64]{2,1,0:T(8,128)(2,1)S(1)}, bf16[32,64,64]{2,1,0:T(8,128)(2,1)}, u32[]{:S(2)}) copy-start(bf16[32,64,64]{2,1,0:T(8,128)(2,1)} %ltr.1) | copy-start | bytes 786436
  14.6 9.2 %copy-start.3 = (bf16[32,64,64]{2,1,0:T(8,128)(2,1)S(1)}, bf16[32,64,64]{2,1,0:T(8,128)(2,1)}, u32[]{:S(2)}) copy-start(bf16[32,64,64]{2,1,0:T(8,128)(2,1)} %basis.1) | copy-start | bytes 786436
  14.6 9.2 %copy-start.4 = (bf16[16,64,64]{2,1,0:T(8,128)(2,1)S(1)}, bf16[16,64,64]{2,1,0:T(8,128)(2,1)}, u32[]{:S(2)}) copy-start(bf16[16,64,64]{2,1,0:T(8,128)(2,1)} %ptr.1) | copy-start | bytes 393220
  14.7 9.2 %copy-start.6 = (bf16[5,16,128]{2,1,0:T(8,128)(2,1)S(1)}, bf16[5,16,128]{2,1,0:T(8,128)(2,1)}, u32[]{:S(2)}) copy-start(bf16[5,16,128]{2,1,0:T(8,128)(2,1)} %get-tuple-element.15.own) | copy-start | bytes 61444
  14.7 9.2 %copy-start.8 = (s32[8,8]{1,0:T(8,128)S(1)}, s32[8,8]{1,0:T(8,128)}, u32[]{:S(2)}) copy-start(s32[8,8]{1,0:T(8,128)} %tlist_h.1) | copy-start | bytes 772
  14.7 9.2 %copy-start.9 = (s32[32,4]{0,1:T(4,128)S(1)}, s32[32,4]{0,1:T(4,128)}, u32[]{:S(2)}) copy-start(s32[32,4]{0,1:T(4,128)} %param.21) | copy-start | bytes 1540
  14.7 9.2 %copy-start.10 = (s32[16,4]{0,1:T(4,128)S(1)}, s32[16,4]{0,1:T(4,128)}, u32[]{:S(2)}) copy-start(s32[16,4]{0,1:T(4,128)} %param.24) | copy-start | bytes 772
  14.7 4.0 %collective-permute-start.5 = (bf16[2,4,16,128]{3,2,1,0:T(8,128)(2,1)S(1)}, bf16[2,4,16,128]{3,2,1,0:T(8,128)(2,1)S(1)}, u32[]{:S(2)}, u32[]{:S(2)}) collective-permute-start(bf16[2,4,16,128]{3,2,1,0:T(8,128)(2,1)S(1)} %join.2.first), channel_id=1, source_target_pairs={{0,4},{1,5},{2,6},{3,7},{4,0},{5,1},{6,2},{7,3},{8,12},{9,13},{10,... | collective-permute-start | bytes 98312 | tf_op jit(solution)/shard_map/ppermute | solution.py:324
  15.3 7.4 %collective-permute-start = (bf16[6,16,128]{2,1,0:T(8,128)(2,1)S(1)}, bf16[6,16,128]{2,1,0:T(8,128)(2,1)S(1)}, u32[]{:S(2)}, u32[]{:S(2)}) collective-permute-start(bf16[6,16,128]{2,1,0:T(8,128)(2,1)S(1)} %copy-done.13), channel_id=1, source_target_pairs={{0,1},{1,0},{2,3},{3,2},{4,5},{5,4},{6,7},{7,6},{8,9},{9,8},{10,11... | collective-permute-start | bytes 73736 | tf_op jit(solution)/shard_map/ppermute | solution.py:324
  15.3 7.4 %collective-permute-start.1 = (bf16[6,16,128]{2,1,0:T(8,128)(2,1)S(1)}, bf16[6,16,128]{2,1,0:T(8,128)(2,1)S(1)}, u32[]{:S(2)}, u32[]{:S(2)}) collective-permute-start(bf16[6,16,128]{2,1,0:T(8,128)(2,1)S(1)} %copy-done.12), channel_id=1, source_target_pairs={{0,15},{1,2},{2,1},{3,4},{4,3},{5,6},{6,5},{7,8},{8,7},{9,10},{10,... | collective-permute-start | bytes 73736 | tf_op jit(solution)/shard_map/ppermute | solution.py:324
  18.7 4.1 %collective-permute-start.8 = (bf16[4,4,16,128]{3,2,1,0:T(8,128)(2,1)S(1)}, bf16[4,4,16,128]{3,2,1,0:T(8,128)(2,1)S(1)}, u32[]{:S(2)}, u32[]{:S(2)}) collective-permute-start(bf16[4,4,16,128]{3,2,1,0:T(8,128)(2,1)S(1)} %join.3.held0), channel_id=1, source_target_pairs={{0,3},{1,2},{2,1},{3,0},{4,7},{5,6},{6,5},{7,4},{8,11},{9,10},{10,... | collective-permute-start | bytes 196616 | tf_op jit(solution)/shard_map/ppermute | solution.py:324
  18.7 4.1 %collective-permute-start.7 = (bf16[4,4,16,128]{3,2,1,0:T(8,128)(2,1)S(1)}, bf16[4,4,16,128]{3,2,1,0:T(8,128)(2,1)S(1)}, u32[]{:S(2)}, u32[]{:S(2)}) collective-permute-start(bf16[4,4,16,128]{3,2,1,0:T(8,128)(2,1)S(1)} %join.3.held0), channel_id=1, source_target_pairs={{0,1},{1,0},{2,3},{3,2},{4,5},{5,4},{6,7},{7,6},{8,9},{9,8},{10,11... | collective-permute-start | bytes 196616 | tf_op jit(solution)/shard_map/ppermute | solution.py:324
  18.8 5.0 %collective-permute-start.6 = (bf16[4,4,16,128]{3,2,1,0:T(8,128)(2,1)S(1)}, bf16[4,4,16,128]{3,2,1,0:T(8,128)(2,1)S(1)}, u32[]{:S(2)}, u32[]{:S(2)}) collective-permute-start(bf16[4,4,16,128]{3,2,1,0:T(8,128)(2,1)S(1)} %join.3.held0), channel_id=1, source_target_pairs={{0,2},{1,3},{2,0},{3,1},{4,6},{5,7},{6,4},{7,5},{8,10},{9,11},{10,... | collective-permute-start | bytes 196616 | tf_op jit(solution)/shard_map/ppermute | solution.py:324

commit v13 on v12

--- a/solution.py
+++ b/solution.py
@@ -10,7 +10,6 @@
 REACH = 2
 WIN = 2 * REACH + 1
 HW = 2
-GROUP = 16
 AXES = ("row", "col")
 F32 = jnp.float32
 BF = jnp.bfloat16
@@ -159,137 +158,98 @@
     )
 
 
-def near_body(offsets_h, vec, near, close, ends, padded, offsets, sems):
-    leaves, vecs, rank = vec.shape
-    kernels = near.shape[0]
-    made = copies([(offsets_h, offsets)], sems)
-    ends[:, 0:HW] = near[:, 0:HW]
-    ends[:, HW:] = near[:, leaves - HW:]
-    zero = jnp.zeros((HW, vecs, rank), BF)
-    padded[0:HW] = zero
-    padded[HW:HW + leaves] = vec[...]
-    padded[HW + leaves:] = zero
-    made[0].wait()
-
-    def body(c, _):
-        for q in range(GROUP):
-            t = c * GROUP + q
-            rows = [padded[t + HW + offsets[n, t]] for n in range(near.shape[2])]
-            close[t] = by_kernel(far_sum(rows, near, t), rank)
-        return 0
-
-    lax.fori_loop(0, leaves // GROUP, body, 0)
-
-
-def near_pass(offsets, vec, blocks):
-    kernels, leaves, near, rank, _ = blocks.shape
-    vecs = vec.shape[1]
-    return call(
-        near_body, "near", (offsets,), (vec, blocks),
-        [
-            jax.ShapeDtypeStruct((leaves, kernels * vecs, rank), F32),
-            jax.ShapeDtypeStruct((kernels, 2 * HW) + blocks.shape[2:], BF),
-        ],
-        [WHOLE] * 2,
-        [VMEM((leaves + 2 * HW, vecs, rank), BF), held(offsets), DMA((1,))],
-        (1_000_000_000, 20_000_000), 8 * 1024 * 1024,
-    )
-
-
 def far_sum(rows, blocks, q):
     return dot_t(beside(*rows), row_of_blocks(blocks, q))
 
 
-def rest_body(offs, llist_h, plist_h, tlist_h, offsets_h,
-              leaf, pair, coupling, ends, ptr, ltr, basis, close, own, sib, cross, fwd, back, held0, held1, held2, held3, out,
-              llist, plist, tlist, offsets, wleaf, wpair, halo, tops, far0, far1, down, sems):
-    kernels, leaves, partners, rank, _ = leaf.shape
-    _, vecs, _ = wleaf.shape
-    count = coupling.shape[1]
+def near_body(offsets_h, llist_h, plist_h, vec, near, leaf, pair, own, sib, cross, fwd, back, close, far0, far1,
+              offsets, llist, plist, padded, wleaf, wpair, sems):
+    leaves, vecs, rank = vec.shape
+    partners = leaf.shape[2]
     cap0 = wleaf.shape[0] // WIN
     cap1 = wpair.shape[0] // WIN
     base = own.shape[0] - cap1 // 2
     col = lax.axis_index("col")
     place = lax.axis_index("row") * lax.axis_size("col") + col
     last_place = lax.axis_size("row") * lax.axis_size("col") - 1
-    lists = copies([(llist_h, llist), (plist_h, plist), (tlist_h, tlist), (offsets_h, offsets)], sems)
+    made = copies([(offsets_h, offsets), (llist_h, llist), (plist_h, plist)], sems)
 
     for block, slot in ((own, REACH), (fwd, 0), (back, 4), (sib, 3 - 2 * col), (cross, 1 + 2 * col)):
         for c in range(cap0 // 2):
             split(block[c], wleaf, slot * cap0 + 2 * c)
         for c in range(cap1 // 2):
             split(block[base + c], wpair, slot * cap1 + 2 * c)
-    halo[2 * HW] = jnp.zeros((vecs, rank), BF)
+    padded[HW:HW + leaves] = vec[...]
     for block, upper in ((sib, 1 - col), (cross, col)):
         row = block[base + cap1 // 2]
         outside = (place == 0) & (upper == 0) | (place == last_place) & (upper == 1)
-        split(jnp.where(outside, jnp.zeros_like(row), row), halo, upper * HW)
+        split(jnp.where(outside, jnp.zeros_like(row), row), padded, upper * (HW + leaves))
+    for copy in made:
+        copy.wait()
+
+    for t in range(leaves):
+        rows = [padded[t + HW + offsets[n, t]] for n in range(near.shape[2])]
+        close[t] = by_kernel(far_sum(rows, near, t), rank)
+        far0[t] = by_kernel(far_sum([wleaf[llist[m, t]] for m in range(partners)], leaf, t), rank)
+        if t % 2:
+            j = t // 2
+            far1[j] = by_kernel(far_sum([wpair[plist[m, j]] for m in range(pair.shape[2])], pair, j), rank)
+
+
+def near_pass(lists, arrays, windows, cap0, cap1):
+    vec, blocks = arrays[:2]
+    leaves, vecs, rank = vec.shape
+    rows = blocks.shape[0] * vecs
+    sums = [jax.ShapeDtypeStruct((n, rows, rank), F32) for n in (leaves, leaves, leaves // 2)]
+    return call(
+        near_body, "near", lists, arrays + windows, sums, [WHOLE] * 3,
+        [held(x) for x in lists]
+        + [VMEM((n, vecs, rank), BF) for n in (leaves + 2 * HW, WIN * cap0, WIN * cap1)] + [DMA((3,))],
+        (1_000_000_000, 20_000_000), 8 * 1024 * 1024,
+    )
+
+
+def rest_body(offs, tlist_h, coupling, ptr, ltr, basis, close, far0, far1, held0, held1, held2, held3, out,
+              tlist, tops, sems):
+    kernels, count, partners, rank, _ = coupling.shape
+    leaves = basis.shape[0]
+    vecs = tops.shape[1]
+    col = lax.axis_index("col")
     row = lax.axis_index("row")
+    made = copies([(tlist_h, tlist)], sems)
     for h, block in enumerate((held0, held1, held2, held3)):
         side = col if h < 2 else 1 - col
         for s, off in enumerate(offs):
             for i in range(block.shape[1]):
                 split(block[s, i], tops, (((row ^ (off + h % 2)) * 2) + side) * count + 2 * i)
-    for copy in lists:
-        copy.wait()
-
-    def body(c, _):
-        for q in range(GROUP):
-            t = c * GROUP + q
-            far0[t] = by_kernel(far_sum([wleaf[llist[m, t]] for m in range(partners)], leaf, t), rank)
-        for q in range(GROUP // 2):
-            j = c * (GROUP // 2) + q
-            far1[j] = by_kernel(far_sum([wpair[plist[m, j]] for m in range(pair.shape[2])], pair, j), rank)
-        for q in range(GROUP // 4):
-            i = c * (GROUP // 4) + q
-            rows = [tops[tlist[i, m]] for m in range(coupling.shape[2])]
-            down[i] = by_kernel(far_sum(rows, coupling, i), rank).astype(BF)
-        return 0
-
-    lax.fori_loop(0, leaves // GROUP, body, 0)
-
-    def edge(t):
-        spots = [t + offsets[n, t] for n in range(ends.shape[2])]
-        if t < HW:
-            spots = [jnp.where(at < 0, at + HW, 2 * HW) for at in spots]
-        else:
-            spots = [jnp.where(at >= leaves, at - leaves + HW, 2 * HW) for at in spots]
-        return by_kernel(far_sum([halo[at] for at in spots], ends, t if t < HW else t - (leaves - 2 * HW)), rank)
-
+    made[0].wait()
+
+    down2 = []
+    for i in range(count):
+        rows = [tops[tlist[i, m]] for m in range(partners)]
+        down2.append(by_kernel(far_sum(rows, coupling, i), rank).astype(BF))
     down1 = []
     for j in range(2 * count):
-        down1.append((far1[j] + dot_t(down[j // 2], ptr[j])).astype(BF))
+        down1.append((far1[j] + dot_t(down2[j // 2], ptr[j])).astype(BF))
     down0 = []
     for t in range(leaves):
         down0.append((far0[t] + dot_t(down1[t // 2], ltr[t])).astype(BF))
     for t in range(leaves):
-        points = dot_t(down0[t], basis[t]) + close[t]
-        if t < HW or t >= leaves - HW:
-            points = points + edge(t)
-        points = points.astype(BF)
+        points = (dot_t(down0[t], basis[t]) + close[t]).astype(BF)
         for k in range(kernels):
             out[k, t] = points[k * vecs:(k + 1) * vecs]
 
 
-def rest_pass(lists, arrays, windows, offs, cap0, cap1):
-    leaf, pair, coupling = arrays[:3]
-    kernels, leaves, _, rank, _ = leaf.shape
-    count = coupling.shape[1]
-    vecs = windows[0].shape[1]
-    rows = kernels * vecs
+def rest_pass(tlist, arrays, pieces, offs):
+    coupling = arrays[0]
+    kernels, count, _, rank, _ = coupling.shape
+    leaves = arrays[3].shape[0]
+    vecs = pieces[0].shape[2]
     return call(
-        functools.partial(rest_body, offs), "rest", lists, arrays + windows,
+        functools.partial(rest_body, offs), "rest", (tlist,), arrays + pieces,
         jax.ShapeDtypeStruct((kernels, leaves, vecs, rank), BF),
         WHOLE,
-        [held(x) for x in lists]
-        + [
-            VMEM((n, vecs, rank), BF)
-            for n in (WIN * cap0, WIN * cap1, 2 * HW + 1, 4 * windows[-1].shape[0] * count)
-        ]
-        + [
-            VMEM((leaves, rows, rank), F32), VMEM((leaves // 2, rows, rank), F32),
-            VMEM((count, rows, rank), BF), DMA((4,)),
-        ],
+        [held(tlist), VMEM((4 * pieces[0].shape[0] * count, vecs, rank), BF), DMA((1,))],
         (150_000_000, 20_000_000), 16 * 1024 * 1024,
     )
 
@@ -338,11 +298,12 @@
     sib = sent(sib, lambda d: d ^ 1)
     cross = sent(cross, lambda d: (d + 1 if d % 2 else d - 1) % devs)
     pieces = (held, got, sent(held, lambda d: d ^ 1), sent(held, lambda d: d ^ 3))
-    close, ends = near_pass(near_offset.T, vectors, near_blocks)
+    close, far0, far1 = near_pass(
+        (near_offset.T, leaf_list.T, pair_list.T),
+        (vectors, near_blocks, leaf_coupling, pair_coupling), (own, sib, cross, fwd, back), cap0, cap1,
+    )
     return rest_pass(
-        (leaf_list.T, pair_list.T, top_list, near_offset.T),
-        (leaf_coupling, pair_coupling, top_coupling, ends, pair_transfer, leaf_transfer, leaf_basis, close),
-        (own, sib, cross, fwd, back) + pieces, offs, cap0, cap1,
+        top_list, (top_coupling, pair_transfer, leaf_transfer, leaf_basis, close, far0, far1), pieces, offs
     )
 
 

time: 29 us -> 27.8 us (0.959)
  Pallas kernels: 9.63 us -> 8.76 us
  waiting for transfers between devices: 6.15 us -> 5.65 us
    pallas_call x5, Pallas kernels: 9.63 us -> 8.76 us  [call(): pl.pallas_call(body, out_shape=out_shape, in_specs=[FIXED] * len(params)...]
    ppermute x9, waiting for transfers between devices: 6.15 us -> 5.65 us  [sent(): return lax.ppermute(piece, AXES, [(d, target(d)) for d in ring])]
  transfers between devices with their start and end apart: 9 -> 9, of which waited for: 3 -> 3; matrix products, arithmetic and copies ran while one was open for 0% -> 0% of each run, Pallas kernels for 7% -> 11%
where the time goes in v13:
time: 27.8 us; the launch traced here: 27.6 us
  starting transfers between devices  11.4 us (41%)
  Pallas kernels  8.76 us (32%)
  waiting for transfers between devices  5.65 us (20%)
  local copies, waits for them, and re-layouts  1.47 us (5%)
  between operations  0.28 us (1%)
    ppermute x9, starting transfers between devices, sent(): return lax.ppermute(piece, AXES, [(d, target(d)) for d in ring])  11.4 us
    pallas_call x5, Pallas kernels, call(): pl.pallas_call(body, out_shape=out_shape, in_specs=[FIXED] * len(params)...  8.76 us
    ppermute x9, waiting for transfers between devices, sent(): return lax.ppermute(piece, AXES, [(d, target(d)) for d in ring])  5.65 us
    unnamed x36, local copies, waits for them, and re-layouts  1.47 us
  transfers between devices with their start and end apart: 9, of which 3 were waited for; matrix products, arithmetic and copies ran while one was open for 0% of the time, Pallas kernels for 11%

profile of v13, /device:TPU:0, one launch (start us, length us, event | category | flops | bytes accessed | tf_op | source)
XLA Modules:
  0.0 27.6 jit_solution(15342878189173352109)
XLA Ops:
  0.0 2.8 %up.1 = (bf16[1,4,16,128]{3,2,1,0:T(8,128)(2,1)}, bf16[5,16,128]{2,1,0:T(8,128)(2,1)}, bf16[6,16,128]{2,1,0:T(8,128)(2,1)}, bf16[6,16,128]{2,1,0:T(8,128)(2,1)},...) custom-call(bf16[32,16,64]{2,1,0:T(8,128)(2,1)} %vec.1, bf16[32,64,64]{2,1,0:T(8,128)(2,1)} %basis.1, ...), custom_call_target="tpu_custom_call" | custom-call | flops 10000000 | bytes 3000000 | tf_op jit(solution)/shard_map/up/pallas_call | solution.py:64
  2.8 3.0 %collective-permute-start.2 = (bf16[5,16,128]{2,1,0:T(8,128)(2,1)}, bf16[5,16,128]{2,1,0:T(8,128)(2,1)S(1)}, u32[]{:S(2)}, u32[]{:S(2)}) collective-permute-start(bf16[5,16,128]{2,1,0:T(8,128)(2,1)} %get-tuple-element.17), channel_id=1, source_target_pairs={{0,2},{1,3},{2,4},{3,5},{4,6},{5,7},{6,8},{7,9},{8,10},{9,11},{10,... | collective-permute-start | bytes 61448 | tf_op jit(solution)/shard_map/ppermute | solution.py:284
  5.8 3.1 %collective-permute-start.3 = (bf16[5,16,128]{2,1,0:T(8,128)(2,1)}, bf16[5,16,128]{2,1,0:T(8,128)(2,1)S(1)}, u32[]{:S(2)}, u32[]{:S(2)}) collective-permute-start(bf16[5,16,128]{2,1,0:T(8,128)(2,1)} %get-tuple-element.18), channel_id=1, source_target_pairs={{0,14},{1,15},{2,0},{3,1},{4,2},{5,3},{6,4},{7,5},{8,6},{9,7},{10,... | collective-permute-start | bytes 61448 | tf_op jit(solution)/shard_map/ppermute | solution.py:284
  8.9 0.0 copy-start.1
  8.9 0.0 copy-start.5
  9.0 0.0 copy-start.6
  9.0 0.0 copy-start.8
  9.0 0.0 copy-start.9
  9.0 0.0 copy-start.10
  9.0 1.0 %collective-permute-start.4 = (bf16[1,4,16,128]{3,2,1,0:T(8,128)(2,1)}, bf16[1,4,16,128]{3,2,1,0:T(8,128)(2,1)S(1)}, u32[]{:S(2)}, u32[]{:S(2)}) collective-permute-start(bf16[1,4,16,128]{3,2,1,0:T(8,128)(2,1)} %get-tuple-element.22.first), channel_id=1, source_target_pairs={{0,8},{1,9},{2,10},{3,11},{4,12},{5,13},{6,14},{7,15},{8,0},{9,1},... | collective-permute-start | bytes 49160 | tf_op jit(solution)/shard_map/ppermute | solution.py:284
  10.0 4.0 %collective-permute-done.4.second = bf16[1,4,16,128]{3,2,1,0:T(8,128)(2,1)S(1)} collective-permute-done((bf16[1,4,16,128]{3,2,1,0:T(8,128)(2,1)}, bf16[1,4,16,128]{3,2,1,0:T(8,128)(2,1)S(1)}, u32[]{:S(2)}, u32[]{:S(2)}) %collective-permute-start.4) | collective-permute-done | bytes 16416 | tf_op jit(solution)/shard_map/ppermute | solution.py:284
  13.9 0.0 collective-permute-done.2.fwd.rest_0_
  13.9 0.0 collective-permute-done.3.back.rest_1_
  13.9 0.7 %copy-done.11 = bf16[1,4,16,128]{3,2,1,0:T(8,128)(2,1)S(1)} copy-done((bf16[1,4,16,128]{3,2,1,0:T(8,128)(2,1)S(1)}, bf16[1,4,16,128]{3,2,1,0:T(8,128)(2,1)}, u32[]{:S(2)}) %copy-start.11) | copy-done | bytes 16408
  14.6 0.1 collective-permute-start.5
  14.7 0.7 %copy-done.13 = bf16[6,16,128]{2,1,0:T(8,128)(2,1)S(1)} copy-done((bf16[6,16,128]{2,1,0:T(8,128)(2,1)S(1)}, bf16[6,16,128]{2,1,0:T(8,128)(2,1)}, u32[]{:S(2)}) %copy-start.13) | copy-done | bytes 24600
  15.4 0.0 collective-permute-start
  15.4 0.0 copy-done.12
  15.4 2.1 %collective-permute-start.1 = (bf16[6,16,128]{2,1,0:T(8,128)(2,1)S(1)}, bf16[6,16,128]{2,1,0:T(8,128)(2,1)S(1)}, u32[]{:S(2)}, u32[]{:S(2)}) collective-permute-start(bf16[6,16,128]{2,1,0:T(8,128)(2,1)S(1)} %copy-done.12), channel_id=1, source_target_pairs={{0,15},{1,2},{2,1},{3,4},{4,3},{5,6},{6,5},{7,8},{8,7},{9,10},{10,... | collective-permute-start | bytes 73736 | tf_op jit(solution)/shard_map/ppermute | solution.py:284
  17.5 1.1 %collective-permute-done.5.second = bf16[2,4,16,128]{3,2,1,0:T(8,128)(2,1)S(1)} collective-permute-done((bf16[2,4,16,128]{3,2,1,0:T(8,128)(2,1)S(1)}, bf16[2,4,16,128]{3,2,1,0:T(8,128)(2,1)S(1)}, u32[]{:S(2)}, u32[]{:S(2)}) %collective-permute-start.5) | collective-permute-done | bytes 32800 | tf_op jit(solution)/shard_map/ppermute | solution.py:284
  18.6 0.0 collective-permute-start.8
  18.6 0.1 collective-permute-start.7
  18.7 2.1 %collective-permute-start.6 = (bf16[4,4,16,128]{3,2,1,0:T(8,128)(2,1)S(1)}, bf16[4,4,16,128]{3,2,1,0:T(8,128)(2,1)S(1)}, u32[]{:S(2)}, u32[]{:S(2)}) collective-permute-start(bf16[4,4,16,128]{3,2,1,0:T(8,128)(2,1)S(1)} %join.3.held0), channel_id=1, source_target_pairs={{0,2},{1,3},{2,0},{3,1},{4,6},{5,7},{6,4},{7,5},{8,10},{9,11},{10,... | collective-permute-start | bytes 196616 | tf_op jit(solution)/shard_map/ppermute | solution.py:284
  20.8 0.0 collective-permute-done.sib
  20.8 0.6 %collective-permute-done.1.cross = bf16[6,16,128]{2,1,0:T(8,128)(2,1)S(1)} collective-permute-done((bf16[6,16,128]{2,1,0:T(8,128)(2,1)S(1)}, bf16[6,16,128]{2,1,0:T(8,128)(2,1)S(1)}, u32[]{:S(2)}, u32[]{:S(2)}) %collective-permute-start.1) | collective-permute-done | bytes 24608 | tf_op jit(solution)/shard_map/ppermute | solution.py:284
  21.3 0.0 slice-done
  21.3 0.0 slice-done.2
  21.3 0.0 slice-done.1
  21.4 0.0 slice-done.3
  21.4 0.0 copy-done.1
  21.4 0.0 copy-done.5
  21.4 0.0 copy-done.6
  21.4 0.0 copy-done.8
  21.4 0.0 copy-done.9
  21.4 0.0 copy-done.10
  21.4 0.0 copy-start
  21.5 0.0 copy-start.2
  21.5 0.0 copy-start.3
  21.5 0.0 copy-start.4
  21.5 0.0 copy-start.7
  21.5 3.1 %near.2 = (f32[32,48,64]{2,1,0:T(8,128)S(1)}, f32[32,48,64]{2,1,0:T(8,128)S(1)}, f32[16,48,64]{2,1,0:T(8,128)S(1)}) custom-call(s32[3,32]{1,0:T(4,128)S(1)} %bitcast.9, s32[4,32]{1,0:T(4,128)S(1)} %bitcast.10, s32[4,16]{1,0:T(4,128)S(1)} %bitcast.11, bf16[32,16,64]{2,1,0:T(8,128)(2,1)S(1)} %copy-done.5, bf16[3,32,3,64,64]{4,3,2,1,0:T(8,128)(2,1)S(1)} %bitcast.8, ...), custom_call_target="tpu_custom_call" | custom-call | flops 1000000000 | bytes 20000000 | tf_op jit(solution)/shard_map/near/pallas_call | solution.py:64
  24.6 0.0 collective-permute-done.8.held3
  24.6 0.0 collective-permute-done.7.held2
  24.6 0.0 collective-permute-done.6.held1
  24.6 0.0 copy-done
  24.6 0.0 copy-done.2
  24.6 0.0 copy-done.3
  24.7 2.9 %rest.1 = bf16[3,32,16,64]{3,2,1,0:T(8,128)(2,1)} custom-call(s32[8,8]{1,0:T(8,128)S(1)} %copy-done.7, bf16[3,8,8,64,64]{4,3,2,1,0:T(8,128)(2,1)S(1)} %copy-done, bf16[16,64,64]{2,1,0:T(8,128)(2,1)S(1)} %copy-done.4, bf16[32,64,64]{2,1,0:T(8,128)(2,1)S(1)} %copy-done.2, bf16[32,64,64]{2,1,0:T(8,128)(2,1)S(1)} %copy-done.3, ...), custom_call_target="tpu_custom_call" | custom-call | flops 150000000 | bytes 20000000 | tf_op jit(solution)/shard_map/rest/pallas_call | solution.py:64
  (13 shorter events, 0.0 us)
Async XLA Ops:
  2.8 11.1 %collective-permute-start.2 = (bf16[5,16,128]{2,1,0:T(8,128)(2,1)}, bf16[5,16,128]{2,1,0:T(8,128)(2,1)S(1)}, u32[]{:S(2)}, u32[]{:S(2)}) collective-permute-start(bf16[5,16,128]{2,1,0:T(8,128)(2,1)} %get-tuple-element.17), channel_id=1, source_target_pairs={{0,2},{1,3},{2,4},{3,5},{4,6},{5,7},{6,8},{7,9},{8,10},{9,11},{10,... | collective-permute-start | bytes 61448 | tf_op jit(solution)/shard_map/ppermute | solution.py:284
  5.8 8.1 %collective-permute-start.3 = (bf16[5,16,128]{2,1,0:T(8,128)(2,1)}, bf16[5,16,128]{2,1,0:T(8,128)(2,1)S(1)}, u32[]{:S(2)}, u32[]{:S(2)}) collective-permute-start(bf16[5,16,128]{2,1,0:T(8,128)(2,1)} %get-tuple-element.18), channel_id=1, source_target_pairs={{0,14},{1,15},{2,0},{3,1},{4,2},{5,3},{6,4},{7,5},{8,6},{9,7},{10,... | collective-permute-start | bytes 61448 | tf_op jit(solution)/shard_map/ppermute | solution.py:284
  8.9 12.4 %slice-start = ((s8[6291456]{0:T(1024)(128)(4,1)}), s8[4194304]{0:T(1024)(128)(4,1)S(1)}, s32[]{:S(2)}) async-start(s8[6291456]{0:T(1024)(128)(4,1)} %bitcast.5), calls=%async_computation | async-start | bytes 8388608
  8.9 12.4 %slice-start.2 = ((s8[4718592]{0:T(1024)(128)(4,1)}), s8[4194304]{0:T(1024)(128)(4,1)S(1)}, s32[]{:S(2)}) async-start(s8[4718592]{0:T(1024)(128)(4,1)} %bitcast.7), calls=%async_computation.2 | async-start | bytes 8388608
  8.9 12.4 %slice-start.1 = ((s8[6291456]{0:T(1024)(128)(4,1)}), s8[2097152]{0:T(1024)(128)(4,1)S(1)}, s32[]{:S(2)}) async-start(s8[6291456]{0:T(1024)(128)(4,1)} %bitcast.5), calls=%async_computation.1 | async-start | bytes 4194304
  8.9 12.4 %slice-start.3 = ((s8[4718592]{0:T(1024)(128)(4,1)}), s8[524288]{0:T(1024)(128)(4,1)S(1)}, s32[]{:S(2)}) async-start(s8[4718592]{0:T(1024)(128)(4,1)} %bitcast.7), calls=%async_computation.3 | async-start | bytes 1048576
  8.9 12.4 %copy-start.1 = (bf16[3,16,4,64,64]{4,3,2,1,0:T(8,128)(2,1)S(1)}, bf16[3,16,4,64,64]{4,3,2,1,0:T(8,128)(2,1)}, u32[]{:S(2)}) copy-start(bf16[3,16,4,64,64]{4,3,2,1,0:T(8,128)(2,1)} %pair.1) | copy-start | bytes 4718596
  8.9 12.4 %copy-start.5 = (bf16[32,16,64]{2,1,0:T(8,128)(2,1)S(1)}, bf16[32,16,64]{2,1,0:T(8,128)(2,1)}, u32[]{:S(2)}) copy-start(bf16[32,16,64]{2,1,0:T(8,128)(2,1)} %vec.1) | copy-start | bytes 196612
  9.0 12.4 %copy-start.6 = (bf16[5,16,128]{2,1,0:T(8,128)(2,1)S(1)}, bf16[5,16,128]{2,1,0:T(8,128)(2,1)}, u32[]{:S(2)}) copy-start(bf16[5,16,128]{2,1,0:T(8,128)(2,1)} %get-tuple-element.14.own) | copy-start | bytes 61444
  9.0 12.4 %copy-start.8 = (s32[32,3]{0,1:T(4,128)S(1)}, s32[32,3]{0,1:T(4,128)}, u32[]{:S(2)}) copy-start(s32[32,3]{0,1:T(4,128)} %param.19) | copy-start | bytes 1156
  9.0 12.4 %copy-start.9 = (s32[32,4]{0,1:T(4,128)S(1)}, s32[32,4]{0,1:T(4,128)}, u32[]{:S(2)}) copy-start(s32[32,4]{0,1:T(4,128)} %param.21) | copy-start | bytes 1540
  9.0 12.4 %copy-start.10 = (s32[16,4]{0,1:T(4,128)S(1)}, s32[16,4]{0,1:T(4,128)}, u32[]{:S(2)}) copy-start(s32[16,4]{0,1:T(4,128)} %param.24) | copy-start | bytes 772
  9.0 4.9 %collective-permute-start.4 = (bf16[1,4,16,128]{3,2,1,0:T(8,128)(2,1)}, bf16[1,4,16,128]{3,2,1,0:T(8,128)(2,1)S(1)}, u32[]{:S(2)}, u32[]{:S(2)}) collective-permute-start(bf16[1,4,16,128]{3,2,1,0:T(8,128)(2,1)} %get-tuple-element.22.first), channel_id=1, source_target_pairs={{0,8},{1,9},{2,10},{3,11},{4,12},{5,13},{6,14},{7,15},{8,0},{9,1},... | collective-permute-start | bytes 49160 | tf_op jit(solution)/shard_map/ppermute | solution.py:284
  13.9 0.7 %copy-start.11 = (bf16[1,4,16,128]{3,2,1,0:T(8,128)(2,1)S(1)}, bf16[1,4,16,128]{3,2,1,0:T(8,128)(2,1)}, u32[]{:S(2)}) copy-start(bf16[1,4,16,128]{3,2,1,0:T(8,128)(2,1)} %get-tuple-element.22.first) | copy-start | bytes 49156
  14.6 0.7 %copy-start.13 = (bf16[6,16,128]{2,1,0:T(8,128)(2,1)S(1)}, bf16[6,16,128]{2,1,0:T(8,128)(2,1)}, u32[]{:S(2)}) copy-start(bf16[6,16,128]{2,1,0:T(8,128)(2,1)} %get-tuple-element.15) | copy-start | bytes 73732
  14.6 0.8 %copy-start.12 = (bf16[6,16,128]{2,1,0:T(8,128)(2,1)S(1)}, bf16[6,16,128]{2,1,0:T(8,128)(2,1)}, u32[]{:S(2)}) copy-start(bf16[6,16,128]{2,1,0:T(8,128)(2,1)} %get-tuple-element.16) | copy-start | bytes 73732
  14.6 4.0 %collective-permute-start.5 = (bf16[2,4,16,128]{3,2,1,0:T(8,128)(2,1)S(1)}, bf16[2,4,16,128]{3,2,1,0:T(8,128)(2,1)S(1)}, u32[]{:S(2)}, u32[]{:S(2)}) collective-permute-start(bf16[2,4,16,128]{3,2,1,0:T(8,128)(2,1)S(1)} %join.2.first), channel_id=1, source_target_pairs={{0,4},{1,5},{2,6},{3,7},{4,0},{5,1},{6,2},{7,3},{8,12},{9,13},{10,... | collective-permute-start | bytes 98312 | tf_op jit(solution)/shard_map/ppermute | solution.py:284
  15.4 5.4 %collective-permute-start = (bf16[6,16,128]{2,1,0:T(8,128)(2,1)S(1)}, bf16[6,16,128]{2,1,0:T(8,128)(2,1)S(1)}, u32[]{:S(2)}, u32[]{:S(2)}) collective-permute-start(bf16[6,16,128]{2,1,0:T(8,128)(2,1)S(1)} %copy-done.13), channel_id=1, source_target_pairs={{0,1},{1,0},{2,3},{3,2},{4,5},{5,4},{6,7},{7,6},{8,9},{9,8},{10,11... | collective-permute-start | bytes 73736 | tf_op jit(solution)/shard_map/ppermute | solution.py:284
  15.4 5.9 %collective-permute-start.1 = (bf16[6,16,128]{2,1,0:T(8,128)(2,1)S(1)}, bf16[6,16,128]{2,1,0:T(8,128)(2,1)S(1)}, u32[]{:S(2)}, u32[]{:S(2)}) collective-permute-start(bf16[6,16,128]{2,1,0:T(8,128)(2,1)S(1)} %copy-done.12), channel_id=1, source_target_pairs={{0,15},{1,2},{2,1},{3,4},{4,3},{5,6},{6,5},{7,8},{8,7},{9,10},{10,... | collective-permute-start | bytes 73736 | tf_op jit(solution)/shard_map/ppermute | solution.py:284
  18.6 6.0 %collective-permute-start.8 = (bf16[4,4,16,128]{3,2,1,0:T(8,128)(2,1)S(1)}, bf16[4,4,16,128]{3,2,1,0:T(8,128)(2,1)S(1)}, u32[]{:S(2)}, u32[]{:S(2)}) collective-permute-start(bf16[4,4,16,128]{3,2,1,0:T(8,128)(2,1)S(1)} %join.3.held0), channel_id=1, source_target_pairs={{0,3},{1,2},{2,1},{3,0},{4,7},{5,6},{6,5},{7,4},{8,11},{9,10},{10,... | collective-permute-start | bytes 196616 | tf_op jit(solution)/shard_map/ppermute | solution.py:284
  18.6 6.0 %collective-permute-start.7 = (bf16[4,4,16,128]{3,2,1,0:T(8,128)(2,1)S(1)}, bf16[4,4,16,128]{3,2,1,0:T(8,128)(2,1)S(1)}, u32[]{:S(2)}, u32[]{:S(2)}) collective-permute-start(bf16[4,4,16,128]{3,2,1,0:T(8,128)(2,1)S(1)} %join.3.held0), channel_id=1, source_target_pairs={{0,1},{1,0},{2,3},{3,2},{4,5},{5,4},{6,7},{7,6},{8,9},{9,8},{10,11... | collective-permute-start | bytes 196616 | tf_op jit(solution)/shard_map/ppermute | solution.py:284
  18.7 5.9 %collective-permute-start.6 = (bf16[4,4,16,128]{3,2,1,0:T(8,128)(2,1)S(1)}, bf16[4,4,16,128]{3,2,1,0:T(8,128)(2,1)S(1)}, u32[]{:S(2)}, u32[]{:S(2)}) collective-permute-start(bf16[4,4,16,128]{3,2,1,0:T(8,128)(2,1)S(1)} %join.3.held0), channel_id=1, source_target_pairs={{0,2},{1,3},{2,0},{3,1},{4,6},{5,7},{6,4},{7,5},{8,10},{9,11},{10,... | collective-permute-start | bytes 196616 | tf_op jit(solution)/shard_map/ppermute | solution.py:284
  21.4 3.2 %copy-start = (bf16[3,8,8,64,64]{4,3,2,1,0:T(8,128)(2,1)S(1)}, bf16[3,8,8,64,64]{4,3,2,1,0:T(8,128)(2,1)}, u32[]{:S(2)}) copy-start(bf16[3,8,8,64,64]{4,3,2,1,0:T(8,128)(2,1)} %coupling.1) | copy-start | bytes 4718596
  21.5 3.2 %copy-start.2 = (bf16[32,64,64]{2,1,0:T(8,128)(2,1)S(1)}, bf16[32,64,64]{2,1,0:T(8,128)(2,1)}, u32[]{:S(2)}) copy-start(bf16[32,64,64]{2,1,0:T(8,128)(2,1)} %ltr.1) | copy-start | bytes 786436
  21.5 3.2 %copy-start.3 = (bf16[32,64,64]{2,1,0:T(8,128)(2,1)S(1)}, bf16[32,64,64]{2,1,0:T(8,128)(2,1)}, u32[]{:S(2)}) copy-start(bf16[32,64,64]{2,1,0:T(8,128)(2,1)} %basis.1) | copy-start | bytes 786436
  21.5 3.2 %copy-start.4 = (bf16[16,64,64]{2,1,0:T(8,128)(2,1)S(1)}, bf16[16,64,64]{2,1,0:T(8,128)(2,1)}, u32[]{:S(2)}) copy-start(bf16[16,64,64]{2,1,0:T(8,128)(2,1)} %ptr.1) | copy-start | bytes 393220
  21.5 3.2 %copy-start.7 = (s32[8,8]{1,0:T(8,128)S(1)}, s32[8,8]{1,0:T(8,128)}, u32[]{:S(2)}) copy-start(s32[8,8]{1,0:T(8,128)} %tlist_h.1) | copy-start | bytes 772

commit v14 on v13

--- a/solution.py
+++ b/solution.py
@@ -141,6 +141,17 @@
             VMEM((leaves, vecs, rank), BF), VMEM((leaves // 2, vecs, rank), BF), DMA((6,)),
         ],
         (10_000_000, 3_000_000),
+    )
+
+
+def pass_body(src, out):
+    out[...] = src[...]
+
+
+def pass_on(x):
+    return call(
+        pass_body, "pass", (), (x,), jax.ShapeDtypeStruct(x.shape, x.dtype), WHOLE, [],
+        (8_000_000_000, 100_000_000), 2 * 1024 * 1024,
     )
 
 
@@ -288,15 +299,16 @@
     got = sent(held, lambda d: d ^ (2 * mask))
     fwd = sent(fwd, lambda d: (d + 2) % devs)
     back = sent(back, lambda d: (d - 2) % devs)
-    others = (fwd, back)
+    sib = sent(sib, lambda d: d ^ 1)
+    cross = sent(cross, lambda d: (d + 1 if d % 2 else d - 1) % devs)
+    others = (sib, cross, fwd, back)
+    held = pass_on(held)
     while mask > 1:
         held = join_pass(held, got, *others)
         offs = offs + [off ^ mask for off in offs]
         mask //= 2
         got = sent(held, lambda d: d ^ (2 * mask))
         others = ()
-    sib = sent(sib, lambda d: d ^ 1)
-    cross = sent(cross, lambda d: (d + 1 if d % 2 else d - 1) % devs)
     pieces = (held, got, sent(held, lambda d: d ^ 1), sent(held, lambda d: d ^ 3))
     close, far0, far1 = near_pass(
         (near_offset.T, leaf_list.T, pair_list.T),

time: 27.8 us -> 30.4 us (1.094)
  waiting for transfers between devices: 5.65 us -> 9.25 us
  local copies, waits for them, and re-layouts: 1.47 us -> 0.8 us
    ppermute x9, waiting for transfers between devices: 5.65 us -> 9.25 us  [sent(): return lax.ppermute(piece, AXES, [(d, target(d)) for d in ring])]
    unnamed x36 -> x32, local copies, waits for them, and re-layouts: 1.47 us -> 0.8 us
    ppermute x9, starting transfers between devices: 11.4 us -> 11.1 us  [sent(): return lax.ppermute(piece, AXES, [(d, target(d)) for d in ring])]
    pallas_call x5 -> x6, Pallas kernels: 8.76 us -> 8.76 us  [call(): pl.pallas_call(body, out_shape=out_shape, in_specs=[FIXED] * len(params)...]
  transfers between devices with their start and end apart: 9 -> 9, of which waited for: 3 -> 3; matrix products, arithmetic and copies ran while one was open for 0% -> 0% of each run, Pallas kernels for 11% -> 10%
where the time goes in v14:
time: 30.4 us; the launch traced here: 30.2 us
  starting transfers between devices  11.1 us (37%)
  waiting for transfers between devices  9.25 us (30%)
  Pallas kernels  8.76 us (29%)
  local copies, waits for them, and re-layouts  0.8 us (3%)
    ppermute x9, starting transfers between devices, sent(): return lax.ppermute(piece, AXES, [(d, target(d)) for d in ring])  11.1 us
    ppermute x9, waiting for transfers between devices, sent(): return lax.ppermute(piece, AXES, [(d, target(d)) for d in ring])  9.25 us
    pallas_call x6, Pallas kernels, call(): pl.pallas_call(body, out_shape=out_shape, in_specs=[FIXED] * len(params)...  8.76 us
    unnamed x32, local copies, waits for them, and re-layouts  0.8 us
  transfers between devices with their start and end apart: 9, of which 3 were waited for; matrix products, arithmetic and copies ran while one was open for 0% of the time, Pallas kernels for 10%

profile of v14, /device:TPU:0, one launch (start us, length us, event | category | flops | bytes accessed | tf_op | source)
XLA Modules:
  0.0 30.2 jit_solution(17562264097943396864)
XLA Ops:
  0.0 2.8 %up.1 = (bf16[1,4,16,128]{3,2,1,0:T(8,128)(2,1)}, bf16[5,16,128]{2,1,0:T(8,128)(2,1)}, bf16[6,16,128]{2,1,0:T(8,128)(2,1)}, bf16[6,16,128]{2,1,0:T(8,128)(2,1)},...) custom-call(bf16[32,16,64]{2,1,0:T(8,128)(2,1)} %vec.1, bf16[32,64,64]{2,1,0:T(8,128)(2,1)} %basis.1, ...), custom_call_target="tpu_custom_call" | custom-call | flops 10000000 | bytes 3000000 | tf_op jit(solution)/shard_map/up/pallas_call | solution.py:64
  2.8 4.1 %collective-permute-start.4 = (bf16[1,4,16,128]{3,2,1,0:T(8,128)(2,1)}, bf16[1,4,16,128]{3,2,1,0:T(8,128)(2,1)S(1)}, u32[]{:S(2)}, u32[]{:S(2)}) collective-permute-start(bf16[1,4,16,128]{3,2,1,0:T(8,128)(2,1)} %get-tuple-element.22.src), channel_id=1, source_target_pairs={{0,8},{1,9},{2,10},{3,11},{4,12},{5,13},{6,14},{7,15},{8,0},{9,1},... | collective-permute-start | bytes 49160 | tf_op jit(solution)/shard_map/ppermute | solution.py:295
  6.9 1.5 %collective-permute-start.2 = (bf16[5,16,128]{2,1,0:T(8,128)(2,1)}, bf16[5,16,128]{2,1,0:T(8,128)(2,1)S(1)}, u32[]{:S(2)}, u32[]{:S(2)}) collective-permute-start(bf16[5,16,128]{2,1,0:T(8,128)(2,1)} %get-tuple-element.17), channel_id=1, source_target_pairs={{0,2},{1,3},{2,4},{3,5},{4,6},{5,7},{6,8},{7,9},{8,10},{9,11},{10,... | collective-permute-start | bytes 61448 | tf_op jit(solution)/shard_map/ppermute | solution.py:295
  8.4 3.2 %collective-permute-start.3 = (bf16[5,16,128]{2,1,0:T(8,128)(2,1)}, bf16[5,16,128]{2,1,0:T(8,128)(2,1)S(1)}, u32[]{:S(2)}, u32[]{:S(2)}) collective-permute-start(bf16[5,16,128]{2,1,0:T(8,128)(2,1)} %get-tuple-element.18), channel_id=1, source_target_pairs={{0,14},{1,15},{2,0},{3,1},{4,2},{5,3},{6,4},{7,5},{8,6},{9,7},{10,... | collective-permute-start | bytes 61448 | tf_op jit(solution)/shard_map/ppermute | solution.py:295
  11.6 0.0 collective-permute-start
  11.6 0.1 collective-permute-start.1
  11.7 0.7 %copy-done.11 = bf16[1,4,16,128]{3,2,1,0:T(8,128)(2,1)S(1)} copy-done((bf16[1,4,16,128]{3,2,1,0:T(8,128)(2,1)S(1)}, bf16[1,4,16,128]{3,2,1,0:T(8,128)(2,1)}, u32[]{:S(2)}) %copy-start.11) | copy-done | bytes 16408
  12.5 0.0 slice-start.3
  12.5 0.0 copy-start.1
  12.5 0.0 copy-start.5
  12.5 0.0 copy-start.6
  12.5 0.0 copy-start.8
  12.5 0.0 copy-start.9
  12.5 0.0 copy-start.10
  12.5 0.0 collective-permute-done.4.second
  12.6 1.0 %collective-permute-done.2.fwd.rest_2_ = bf16[5,16,128]{2,1,0:T(8,128)(2,1)S(1)} collective-permute-done((bf16[5,16,128]{2,1,0:T(8,128)(2,1)}, bf16[5,16,128]{2,1,0:T(8,128)(2,1)S(1)}, u32[]{:S(2)}, u32[]{:S(2)}) %collective-permute-start.2) | collective-permute-done | bytes 20512 | tf_op jit(solution)/shard_map/ppermute | solution.py:295
  13.6 0.0 collective-permute-done.3.back.rest_3_
  13.6 0.0 collective-permute-done.sib.rest_0_
  13.6 4.3 %collective-permute-done.1.cross.rest_1_ = bf16[6,16,128]{2,1,0:T(8,128)(2,1)S(1)} collective-permute-done((bf16[6,16,128]{2,1,0:T(8,128)(2,1)}, bf16[6,16,128]{2,1,0:T(8,128)(2,1)S(1)}, u32[]{:S(2)}, u32[]{:S(2)}) %collective-permute-start.1) | collective-permute-done | bytes 24608 | tf_op jit(solution)/shard_map/ppermute | solution.py:295
  17.9 0.0 collective-permute-start.5
  17.9 3.9 %collective-permute-done.5.second = bf16[2,4,16,128]{3,2,1,0:T(8,128)(2,1)S(1)} collective-permute-done((bf16[2,4,16,128]{3,2,1,0:T(8,128)(2,1)S(1)}, bf16[2,4,16,128]{3,2,1,0:T(8,128)(2,1)S(1)}, u32[]{:S(2)}, u32[]{:S(2)}) %collective-permute-start.5) | collective-permute-done | bytes 32800 | tf_op jit(solution)/shard_map/ppermute | solution.py:295
  21.8 0.0 collective-permute-start.8
  21.8 0.1 collective-permute-start.7
  21.9 2.1 %collective-permute-start.6 = (bf16[4,4,16,128]{3,2,1,0:T(8,128)(2,1)S(1)}, bf16[4,4,16,128]{3,2,1,0:T(8,128)(2,1)S(1)}, u32[]{:S(2)}, u32[]{:S(2)}) collective-permute-start(bf16[4,4,16,128]{3,2,1,0:T(8,128)(2,1)S(1)} %join.3.held0), channel_id=1, source_target_pairs={{0,2},{1,3},{2,0},{3,1},{4,6},{5,7},{6,4},{7,5},{8,10},{9,11},{10,... | collective-permute-start | bytes 196616 | tf_op jit(solution)/shard_map/ppermute | solution.py:295
  24.0 0.0 slice-done
  24.0 0.0 slice-done.2
  24.0 0.0 slice-done.1
  24.0 0.0 slice-done.3
  24.0 0.0 copy-done.1
  24.0 0.0 copy-done.5
  24.0 0.0 copy-done.6
  24.0 0.0 copy-done.8
  24.0 0.0 copy-done.9
  24.0 0.0 copy-done.10
  24.0 0.0 copy-start
  24.1 0.0 copy-start.2
  24.1 0.0 copy-start.3
  24.1 0.0 copy-start.4
  24.1 0.0 copy-start.7
  24.1 3.1 %near.2 = (f32[32,48,64]{2,1,0:T(8,128)S(1)}, f32[32,48,64]{2,1,0:T(8,128)S(1)}, f32[16,48,64]{2,1,0:T(8,128)S(1)}) custom-call(s32[3,32]{1,0:T(4,128)S(1)} %bitcast.9, s32[4,32]{1,0:T(4,128)S(1)} %bitcast.10, s32[4,16]{1,0:T(4,128)S(1)} %bitcast.11, bf16[32,16,64]{2,1,0:T(8,128)(2,1)S(1)} %copy-done.5, bf16[3,32,3,64,64]{4,3,2,1,0:T(8,128)(2,1)S(1)} %bitcast.8, ...), custom_call_target="tpu_custom_call" | custom-call | flops 1000000000 | bytes 20000000 | tf_op jit(solution)/shard_map/near/pallas_call | solution.py:64
  27.2 0.0 collective-permute-done.8.held3
  27.2 0.0 collective-permute-done.7.held2
  27.2 0.0 collective-permute-done.6.held1
  27.2 0.0 copy-done
  27.2 0.0 copy-done.2
  27.3 0.0 copy-done.3
  27.3 0.0 copy-done.4
  27.3 2.9 %rest.1 = bf16[3,32,16,64]{3,2,1,0:T(8,128)(2,1)} custom-call(s32[8,8]{1,0:T(8,128)S(1)} %copy-done.7, bf16[3,8,8,64,64]{4,3,2,1,0:T(8,128)(2,1)S(1)} %copy-done, bf16[16,64,64]{2,1,0:T(8,128)(2,1)S(1)} %copy-done.4, bf16[32,64,64]{2,1,0:T(8,128)(2,1)S(1)} %copy-done.2, bf16[32,64,64]{2,1,0:T(8,128)(2,1)S(1)} %copy-done.3, ...), custom_call_target="tpu_custom_call" | custom-call | flops 150000000 | bytes 20000000 | tf_op jit(solution)/shard_map/rest/pallas_call | solution.py:64
  (10 shorter events, 0.0 us)
Async XLA Ops:
  2.8 9.8 %collective-permute-start.4 = (bf16[1,4,16,128]{3,2,1,0:T(8,128)(2,1)}, bf16[1,4,16,128]{3,2,1,0:T(8,128)(2,1)S(1)}, u32[]{:S(2)}, u32[]{:S(2)}) collective-permute-start(bf16[1,4,16,128]{3,2,1,0:T(8,128)(2,1)} %get-tuple-element.22.src), channel_id=1, source_target_pairs={{0,8},{1,9},{2,10},{3,11},{4,12},{5,13},{6,14},{7,15},{8,0},{9,1},... | collective-permute-start | bytes 49160 | tf_op jit(solution)/shard_map/ppermute | solution.py:295
  6.9 6.7 %collective-permute-start.2 = (bf16[5,16,128]{2,1,0:T(8,128)(2,1)}, bf16[5,16,128]{2,1,0:T(8,128)(2,1)S(1)}, u32[]{:S(2)}, u32[]{:S(2)}) collective-permute-start(bf16[5,16,128]{2,1,0:T(8,128)(2,1)} %get-tuple-element.17), channel_id=1, source_target_pairs={{0,2},{1,3},{2,4},{3,5},{4,6},{5,7},{6,8},{7,9},{8,10},{9,11},{10,... | collective-permute-start | bytes 61448 | tf_op jit(solution)/shard_map/ppermute | solution.py:295
  8.4 5.2 %collective-permute-start.3 = (bf16[5,16,128]{2,1,0:T(8,128)(2,1)}, bf16[5,16,128]{2,1,0:T(8,128)(2,1)S(1)}, u32[]{:S(2)}, u32[]{:S(2)}) collective-permute-start(bf16[5,16,128]{2,1,0:T(8,128)(2,1)} %get-tuple-element.18), channel_id=1, source_target_pairs={{0,14},{1,15},{2,0},{3,1},{4,2},{5,3},{6,4},{7,5},{8,6},{9,7},{10,... | collective-permute-start | bytes 61448 | tf_op jit(solution)/shard_map/ppermute | solution.py:295
  11.6 2.0 %collective-permute-start = (bf16[6,16,128]{2,1,0:T(8,128)(2,1)}, bf16[6,16,128]{2,1,0:T(8,128)(2,1)S(1)}, u32[]{:S(2)}, u32[]{:S(2)}) collective-permute-start(bf16[6,16,128]{2,1,0:T(8,128)(2,1)} %get-tuple-element.15), channel_id=1, source_target_pairs={{0,1},{1,0},{2,3},{3,2},{4,5},{5,4},{6,7},{7,6},{8,9},{9,8},{10,11... | collective-permute-start | bytes 73736 | tf_op jit(solution)/shard_map/ppermute | solution.py:295
  11.6 6.3 %collective-permute-start.1 = (bf16[6,16,128]{2,1,0:T(8,128)(2,1)}, bf16[6,16,128]{2,1,0:T(8,128)(2,1)S(1)}, u32[]{:S(2)}, u32[]{:S(2)}) collective-permute-start(bf16[6,16,128]{2,1,0:T(8,128)(2,1)} %get-tuple-element.16), channel_id=1, source_target_pairs={{0,15},{1,2},{2,1},{3,4},{4,3},{5,6},{6,5},{7,8},{8,7},{9,10},{10,... | collective-permute-start | bytes 73736 | tf_op jit(solution)/shard_map/ppermute | solution.py:295
  11.7 0.7 %copy-start.11 = (bf16[1,4,16,128]{3,2,1,0:T(8,128)(2,1)S(1)}, bf16[1,4,16,128]{3,2,1,0:T(8,128)(2,1)}, u32[]{:S(2)}) copy-start(bf16[1,4,16,128]{3,2,1,0:T(8,128)(2,1)} %get-tuple-element.22.src) | copy-start | bytes 49156
  12.5 11.5 %slice-start = ((s8[6291456]{0:T(1024)(128)(4,1)}), s8[4194304]{0:T(1024)(128)(4,1)S(1)}, s32[]{:S(2)}) async-start(s8[6291456]{0:T(1024)(128)(4,1)} %bitcast.5), calls=%async_computation | async-start | bytes 8388608
  12.5 11.5 %slice-start.2 = ((s8[4718592]{0:T(1024)(128)(4,1)}), s8[4194304]{0:T(1024)(128)(4,1)S(1)}, s32[]{:S(2)}) async-start(s8[4718592]{0:T(1024)(128)(4,1)} %bitcast.7), calls=%async_computation.2 | async-start | bytes 8388608
  12.5 11.5 %slice-start.1 = ((s8[6291456]{0:T(1024)(128)(4,1)}), s8[2097152]{0:T(1024)(128)(4,1)S(1)}, s32[]{:S(2)}) async-start(s8[6291456]{0:T(1024)(128)(4,1)} %bitcast.5), calls=%async_computation.1 | async-start | bytes 4194304
  12.5 11.5 %slice-start.3 = ((s8[4718592]{0:T(1024)(128)(4,1)}), s8[524288]{0:T(1024)(128)(4,1)S(1)}, s32[]{:S(2)}) async-start(s8[4718592]{0:T(1024)(128)(4,1)} %bitcast.7), calls=%async_computation.3 | async-start | bytes 1048576
  12.5 11.5 %copy-start.1 = (bf16[3,16,4,64,64]{4,3,2,1,0:T(8,128)(2,1)S(1)}, bf16[3,16,4,64,64]{4,3,2,1,0:T(8,128)(2,1)}, u32[]{:S(2)}) copy-start(bf16[3,16,4,64,64]{4,3,2,1,0:T(8,128)(2,1)} %pair.1) | copy-start | bytes 4718596
  12.5 11.5 %copy-start.5 = (bf16[32,16,64]{2,1,0:T(8,128)(2,1)S(1)}, bf16[32,16,64]{2,1,0:T(8,128)(2,1)}, u32[]{:S(2)}) copy-start(bf16[32,16,64]{2,1,0:T(8,128)(2,1)} %vec.1) | copy-start | bytes 196612
  12.5 11.5 %copy-start.6 = (bf16[5,16,128]{2,1,0:T(8,128)(2,1)S(1)}, bf16[5,16,128]{2,1,0:T(8,128)(2,1)}, u32[]{:S(2)}) copy-start(bf16[5,16,128]{2,1,0:T(8,128)(2,1)} %get-tuple-element.14.own) | copy-start | bytes 61444
  12.5 11.5 %copy-start.8 = (s32[32,3]{0,1:T(4,128)S(1)}, s32[32,3]{0,1:T(4,128)}, u32[]{:S(2)}) copy-start(s32[32,3]{0,1:T(4,128)} %param.19) | copy-start | bytes 1156
  12.5 11.5 %copy-start.9 = (s32[32,4]{0,1:T(4,128)S(1)}, s32[32,4]{0,1:T(4,128)}, u32[]{:S(2)}) copy-start(s32[32,4]{0,1:T(4,128)} %param.21) | copy-start | bytes 1540
  12.5 11.5 %copy-start.10 = (s32[16,4]{0,1:T(4,128)S(1)}, s32[16,4]{0,1:T(4,128)}, u32[]{:S(2)}) copy-start(s32[16,4]{0,1:T(4,128)} %param.24) | copy-start | bytes 772
  17.9 3.9 %collective-permute-start.5 = (bf16[2,4,16,128]{3,2,1,0:T(8,128)(2,1)S(1)}, bf16[2,4,16,128]{3,2,1,0:T(8,128)(2,1)S(1)}, u32[]{:S(2)}, u32[]{:S(2)}) collective-permute-start(bf16[2,4,16,128]{3,2,1,0:T(8,128)(2,1)S(1)} %join.2.first), channel_id=1, source_target_pairs={{0,4},{1,5},{2,6},{3,7},{4,0},{5,1},{6,2},{7,3},{8,12},{9,13},{10,... | collective-permute-start | bytes 98312 | tf_op jit(solution)/shard_map/ppermute | solution.py:295
  21.8 5.4 %collective-permute-start.8 = (bf16[4,4,16,128]{3,2,1,0:T(8,128)(2,1)S(1)}, bf16[4,4,16,128]{3,2,1,0:T(8,128)(2,1)S(1)}, u32[]{:S(2)}, u32[]{:S(2)}) collective-permute-start(bf16[4,4,16,128]{3,2,1,0:T(8,128)(2,1)S(1)} %join.3.held0), channel_id=1, source_target_pairs={{0,3},{1,2},{2,1},{3,0},{4,7},{5,6},{6,5},{7,4},{8,11},{9,10},{10,... | collective-permute-start | bytes 196616 | tf_op jit(solution)/shard_map/ppermute | solution.py:295
  21.8 5.4 %collective-permute-start.7 = (bf16[4,4,16,128]{3,2,1,0:T(8,128)(2,1)S(1)}, bf16[4,4,16,128]{3,2,1,0:T(8,128)(2,1)S(1)}, u32[]{:S(2)}, u32[]{:S(2)}) collective-permute-start(bf16[4,4,16,128]{3,2,1,0:T(8,128)(2,1)S(1)} %join.3.held0), channel_id=1, source_target_pairs={{0,1},{1,0},{2,3},{3,2},{4,5},{5,4},{6,7},{7,6},{8,9},{9,8},{10,11... | collective-permute-start | bytes 196616 | tf_op jit(solution)/shard_map/ppermute | solution.py:295
  21.9 5.3 %collective-permute-start.6 = (bf16[4,4,16,128]{3,2,1,0:T(8,128)(2,1)S(1)}, bf16[4,4,16,128]{3,2,1,0:T(8,128)(2,1)S(1)}, u32[]{:S(2)}, u32[]{:S(2)}) collective-permute-start(bf16[4,4,16,128]{3,2,1,0:T(8,128)(2,1)S(1)} %join.3.held0), channel_id=1, source_target_pairs={{0,2},{1,3},{2,0},{3,1},{4,6},{5,7},{6,4},{7,5},{8,10},{9,11},{10,... | collective-permute-start | bytes 196616 | tf_op jit(solution)/shard_map/ppermute | solution.py:295
  24.0 3.2 %copy-start = (bf16[3,8,8,64,64]{4,3,2,1,0:T(8,128)(2,1)S(1)}, bf16[3,8,8,64,64]{4,3,2,1,0:T(8,128)(2,1)}, u32[]{:S(2)}) copy-start(bf16[3,8,8,64,64]{4,3,2,1,0:T(8,128)(2,1)} %coupling.1) | copy-start | bytes 4718596
  24.1 3.2 %copy-start.2 = (bf16[32,64,64]{2,1,0:T(8,128)(2,1)S(1)}, bf16[32,64,64]{2,1,0:T(8,128)(2,1)}, u32[]{:S(2)}) copy-start(bf16[32,64,64]{2,1,0:T(8,128)(2,1)} %ltr.1) | copy-start | bytes 786436
  24.1 3.2 %copy-start.3 = (bf16[32,64,64]{2,1,0:T(8,128)(2,1)S(1)}, bf16[32,64,64]{2,1,0:T(8,128)(2,1)}, u32[]{:S(2)}) copy-start(bf16[32,64,64]{2,1,0:T(8,128)(2,1)} %basis.1) | copy-start | bytes 786436
  24.1 3.2 %copy-start.4 = (bf16[16,64,64]{2,1,0:T(8,128)(2,1)S(1)}, bf16[16,64,64]{2,1,0:T(8,128)(2,1)}, u32[]{:S(2)}) copy-start(bf16[16,64,64]{2,1,0:T(8,128)(2,1)} %ptr.1) | copy-start | bytes 393220
  24.1 3.2 %copy-start.7 = (s32[8,8]{1,0:T(8,128)S(1)}, s32[8,8]{1,0:T(8,128)}, u32[]{:S(2)}) copy-start(s32[8,8]{1,0:T(8,128)} %tlist_h.1) | copy-start | bytes 772

commit v15 on v14

--- a/solution.py
+++ b/solution.py
@@ -299,9 +299,7 @@
     got = sent(held, lambda d: d ^ (2 * mask))
     fwd = sent(fwd, lambda d: (d + 2) % devs)
     back = sent(back, lambda d: (d - 2) % devs)
-    sib = sent(sib, lambda d: d ^ 1)
-    cross = sent(cross, lambda d: (d + 1 if d % 2 else d - 1) % devs)
-    others = (sib, cross, fwd, back)
+    others = (fwd, back)
     held = pass_on(held)
     while mask > 1:
         held = join_pass(held, got, *others)
@@ -309,6 +307,8 @@
         mask //= 2
         got = sent(held, lambda d: d ^ (2 * mask))
         others = ()
+    sib = sent(sib, lambda d: d ^ 1)
+    cross = sent(cross, lambda d: (d + 1 if d % 2 else d - 1) % devs)
     pieces = (held, got, sent(held, lambda d: d ^ 1), sent(held, lambda d: d ^ 3))
     close, far0, far1 = near_pass(
         (near_offset.T, leaf_list.T, pair_list.T),

time: 30.4 us -> 27.2 us (0.89)
  waiting for transfers between devices: 9.25 us -> 1.14 us
  starting transfers between devices: 11.1 us -> 15.9 us
    ppermute x9, waiting for transfers between devices: 9.25 us -> 1.14 us  [sent(): return lax.ppermute(piece, AXES, [(d, target(d)) for d in ring])]
    ppermute x9, starting transfers between devices: 11.1 us -> 15.9 us  [sent(): return lax.ppermute(piece, AXES, [(d, target(d)) for d in ring])]
    unnamed x32 -> x36, local copies, waits for them, and re-layouts: 0.8 us -> 0.82 us
  transfers between devices with their start and end apart: 9 -> 9, of which waited for: 3 -> 1; matrix products, arithmetic and copies ran while one was open for 0% -> 0% of each run, Pallas kernels for 10% -> 11%
where the time goes in v15:
time: 27.2 us; the launch traced here: 27 us
  starting transfers between devices  15.9 us (58%)
  Pallas kernels  8.76 us (32%)
  waiting for transfers between devices  1.14 us (4%)
  local copies, waits for them, and re-layouts  0.82 us (3%)
  between operations  0.32 us (1%)
    ppermute x9, starting transfers between devices, sent(): return lax.ppermute(piece, AXES, [(d, target(d)) for d in ring])  15.9 us
    pallas_call x6, Pallas kernels, call(): pl.pallas_call(body, out_shape=out_shape, in_specs=[FIXED] * len(params)...  8.76 us
    ppermute x9, waiting for transfers between devices, sent(): return lax.ppermute(piece, AXES, [(d, target(d)) for d in ring])  1.14 us
    unnamed x36, local copies, waits for them, and re-layouts  0.82 us
  transfers between devices with their start and end apart: 9, of which 1 were waited for; matrix products, arithmetic and copies ran while one was open for 0% of the time, Pallas kernels for 11%

profile of v15, /device:TPU:0, one launch (start us, length us, event | category | flops | bytes accessed | tf_op | source)
XLA Modules:
  0.0 27.0 jit_solution(6597811044284661913)
XLA Ops:
  0.0 2.8 %up.1 = (bf16[1,4,16,128]{3,2,1,0:T(8,128)(2,1)}, bf16[5,16,128]{2,1,0:T(8,128)(2,1)}, bf16[6,16,128]{2,1,0:T(8,128)(2,1)}, bf16[6,16,128]{2,1,0:T(8,128)(2,1)},...) custom-call(bf16[32,16,64]{2,1,0:T(8,128)(2,1)} %vec.1, bf16[32,64,64]{2,1,0:T(8,128)(2,1)} %basis.1, ...), custom_call_target="tpu_custom_call" | custom-call | flops 10000000 | bytes 3000000 | tf_op jit(solution)/shard_map/up/pallas_call | solution.py:64
  2.8 4.1 %collective-permute-start.4 = (bf16[1,4,16,128]{3,2,1,0:T(8,128)(2,1)}, bf16[1,4,16,128]{3,2,1,0:T(8,128)(2,1)S(1)}, u32[]{:S(2)}, u32[]{:S(2)}) collective-permute-start(bf16[1,4,16,128]{3,2,1,0:T(8,128)(2,1)} %get-tuple-element.22.src), channel_id=1, source_target_pairs={{0,8},{1,9},{2,10},{3,11},{4,12},{5,13},{6,14},{7,15},{8,0},{9,1},... | collective-permute-start | bytes 49160 | tf_op jit(solution)/shard_map/ppermute | solution.py:295
  6.9 1.5 %collective-permute-start.2 = (bf16[5,16,128]{2,1,0:T(8,128)(2,1)}, bf16[5,16,128]{2,1,0:T(8,128)(2,1)S(1)}, u32[]{:S(2)}, u32[]{:S(2)}) collective-permute-start(bf16[5,16,128]{2,1,0:T(8,128)(2,1)} %get-tuple-element.17), channel_id=1, source_target_pairs={{0,2},{1,3},{2,4},{3,5},{4,6},{5,7},{6,8},{7,9},{8,10},{9,11},{10,... | collective-permute-start | bytes 61448 | tf_op jit(solution)/shard_map/ppermute | solution.py:295
  8.4 3.2 %collective-permute-start.3 = (bf16[5,16,128]{2,1,0:T(8,128)(2,1)}, bf16[5,16,128]{2,1,0:T(8,128)(2,1)S(1)}, u32[]{:S(2)}, u32[]{:S(2)}) collective-permute-start(bf16[5,16,128]{2,1,0:T(8,128)(2,1)} %get-tuple-element.18), channel_id=1, source_target_pairs={{0,14},{1,15},{2,0},{3,1},{4,2},{5,3},{6,4},{7,5},{8,6},{9,7},{10,... | collective-permute-start | bytes 61448 | tf_op jit(solution)/shard_map/ppermute | solution.py:295
  11.6 0.7 %copy-done.11 = bf16[1,4,16,128]{3,2,1,0:T(8,128)(2,1)S(1)} copy-done((bf16[1,4,16,128]{3,2,1,0:T(8,128)(2,1)S(1)}, bf16[1,4,16,128]{3,2,1,0:T(8,128)(2,1)}, u32[]{:S(2)}) %copy-start.11) | copy-done | bytes 16408
  12.3 0.0 copy-start.12
  12.4 0.0 slice-start.1
  12.4 0.0 slice-start.3
  12.4 0.0 copy-start.1
  12.4 0.0 copy-start.5
  12.4 0.0 copy-start.6
  12.4 0.0 copy-start.8
  12.4 0.0 copy-start.9
  12.4 0.0 copy-start.10
  12.5 0.0 collective-permute-done.4.second
  12.5 1.1 %collective-permute-done.2.fwd.rest_0_ = bf16[5,16,128]{2,1,0:T(8,128)(2,1)S(1)} collective-permute-done((bf16[5,16,128]{2,1,0:T(8,128)(2,1)}, bf16[5,16,128]{2,1,0:T(8,128)(2,1)S(1)}, u32[]{:S(2)}, u32[]{:S(2)}) %collective-permute-start.2) | collective-permute-done | bytes 20512 | tf_op jit(solution)/shard_map/ppermute | solution.py:295
  13.6 0.0 collective-permute-done.3.back.rest_1_
  13.6 0.4 %collective-permute-start.5 = (bf16[2,4,16,128]{3,2,1,0:T(8,128)(2,1)S(1)}, bf16[2,4,16,128]{3,2,1,0:T(8,128)(2,1)S(1)}, u32[]{:S(2)}, u32[]{:S(2)}) collective-permute-start(bf16[2,4,16,128]{3,2,1,0:T(8,128)(2,1)S(1)} %join.2.first), channel_id=1, source_target_pairs={{0,4},{1,5},{2,6},{3,7},{4,0},{5,1},{6,2},{7,3},{8,12},{9,13},{10,... | collective-permute-start | bytes 98312 | tf_op jit(solution)/shard_map/ppermute | solution.py:295
  14.0 0.0 copy-done.13
  14.0 0.0 collective-permute-start
  14.0 0.0 copy-done.12
  14.0 4.5 %collective-permute-start.1 = (bf16[6,16,128]{2,1,0:T(8,128)(2,1)S(1)}, bf16[6,16,128]{2,1,0:T(8,128)(2,1)S(1)}, u32[]{:S(2)}, u32[]{:S(2)}) collective-permute-start(bf16[6,16,128]{2,1,0:T(8,128)(2,1)S(1)} %copy-done.12), channel_id=1, source_target_pairs={{0,15},{1,2},{2,1},{3,4},{4,3},{5,6},{6,5},{7,8},{8,7},{9,10},{10,... | collective-permute-start | bytes 73736 | tf_op jit(solution)/shard_map/ppermute | solution.py:295
  18.5 0.0 collective-permute-done.5.second
  18.5 0.1 collective-permute-start.8
  18.6 0.3 %collective-permute-start.7 = (bf16[4,4,16,128]{3,2,1,0:T(8,128)(2,1)S(1)}, bf16[4,4,16,128]{3,2,1,0:T(8,128)(2,1)S(1)}, u32[]{:S(2)}, u32[]{:S(2)}) collective-permute-start(bf16[4,4,16,128]{3,2,1,0:T(8,128)(2,1)S(1)} %join.3.held0), channel_id=1, source_target_pairs={{0,1},{1,0},{2,3},{3,2},{4,5},{5,4},{6,7},{7,6},{8,9},{9,8},{10,11... | collective-permute-start | bytes 196616 | tf_op jit(solution)/shard_map/ppermute | solution.py:295
  18.9 1.9 %collective-permute-start.6 = (bf16[4,4,16,128]{3,2,1,0:T(8,128)(2,1)S(1)}, bf16[4,4,16,128]{3,2,1,0:T(8,128)(2,1)S(1)}, u32[]{:S(2)}, u32[]{:S(2)}) collective-permute-start(bf16[4,4,16,128]{3,2,1,0:T(8,128)(2,1)S(1)} %join.3.held0), channel_id=1, source_target_pairs={{0,2},{1,3},{2,0},{3,1},{4,6},{5,7},{6,4},{7,5},{8,10},{9,11},{10,... | collective-permute-start | bytes 196616 | tf_op jit(solution)/shard_map/ppermute | solution.py:295
  20.7 0.0 collective-permute-done.sib
  20.7 0.0 collective-permute-done.1.cross
  20.7 0.0 slice-done
  20.7 0.0 slice-done.2
  20.7 0.0 slice-done.1
  20.8 0.0 slice-done.3
  20.8 0.0 copy-done.1
  20.8 0.0 copy-done.5
  20.8 0.0 copy-done.6
  20.8 0.0 copy-done.8
  20.8 0.0 copy-done.9
  20.8 0.0 copy-done.10
  20.8 0.0 copy-start
  20.9 0.0 copy-start.2
  20.9 0.0 copy-start.3
  20.9 0.0 copy-start.4
  20.9 0.0 copy-start.7
  20.9 3.1 %near.2 = (f32[32,48,64]{2,1,0:T(8,128)S(1)}, f32[32,48,64]{2,1,0:T(8,128)S(1)}, f32[16,48,64]{2,1,0:T(8,128)S(1)}) custom-call(s32[3,32]{1,0:T(4,128)S(1)} %bitcast.9, s32[4,32]{1,0:T(4,128)S(1)} %bitcast.10, s32[4,16]{1,0:T(4,128)S(1)} %bitcast.11, bf16[32,16,64]{2,1,0:T(8,128)(2,1)S(1)} %copy-done.5, bf16[3,32,3,64,64]{4,3,2,1,0:T(8,128)(2,1)S(1)} %bitcast.8, ...), custom_call_target="tpu_custom_call" | custom-call | flops 1000000000 | bytes 20000000 | tf_op jit(solution)/shard_map/near/pallas_call | solution.py:64
  24.0 0.0 collective-permute-done.8.held3
  24.0 0.0 collective-permute-done.7.held2
  24.0 0.0 collective-permute-done.6.held1
  24.1 2.9 %rest.1 = bf16[3,32,16,64]{3,2,1,0:T(8,128)(2,1)} custom-call(s32[8,8]{1,0:T(8,128)S(1)} %copy-done.7, bf16[3,8,8,64,64]{4,3,2,1,0:T(8,128)(2,1)S(1)} %copy-done, bf16[16,64,64]{2,1,0:T(8,128)(2,1)S(1)} %copy-done.4, bf16[32,64,64]{2,1,0:T(8,128)(2,1)S(1)} %copy-done.2, bf16[32,64,64]{2,1,0:T(8,128)(2,1)S(1)} %copy-done.3, ...), custom_call_target="tpu_custom_call" | custom-call | flops 150000000 | bytes 20000000 | tf_op jit(solution)/shard_map/rest/pallas_call | solution.py:64
  (14 shorter events, 0.0 us)
Async XLA Ops:
  2.8 9.7 %collective-permute-start.4 = (bf16[1,4,16,128]{3,2,1,0:T(8,128)(2,1)}, bf16[1,4,16,128]{3,2,1,0:T(8,128)(2,1)S(1)}, u32[]{:S(2)}, u32[]{:S(2)}) collective-permute-start(bf16[1,4,16,128]{3,2,1,0:T(8,128)(2,1)} %get-tuple-element.22.src), channel_id=1, source_target_pairs={{0,8},{1,9},{2,10},{3,11},{4,12},{5,13},{6,14},{7,15},{8,0},{9,1},... | collective-permute-start | bytes 49160 | tf_op jit(solution)/shard_map/ppermute | solution.py:295
  6.9 6.7 %collective-permute-start.2 = (bf16[5,16,128]{2,1,0:T(8,128)(2,1)}, bf16[5,16,128]{2,1,0:T(8,128)(2,1)S(1)}, u32[]{:S(2)}, u32[]{:S(2)}) collective-permute-start(bf16[5,16,128]{2,1,0:T(8,128)(2,1)} %get-tuple-element.17), channel_id=1, source_target_pairs={{0,2},{1,3},{2,4},{3,5},{4,6},{5,7},{6,8},{7,9},{8,10},{9,11},{10,... | collective-permute-start | bytes 61448 | tf_op jit(solution)/shard_map/ppermute | solution.py:295
  8.4 5.2 %collective-permute-start.3 = (bf16[5,16,128]{2,1,0:T(8,128)(2,1)}, bf16[5,16,128]{2,1,0:T(8,128)(2,1)S(1)}, u32[]{:S(2)}, u32[]{:S(2)}) collective-permute-start(bf16[5,16,128]{2,1,0:T(8,128)(2,1)} %get-tuple-element.18), channel_id=1, source_target_pairs={{0,14},{1,15},{2,0},{3,1},{4,2},{5,3},{6,4},{7,5},{8,6},{9,7},{10,... | collective-permute-start | bytes 61448 | tf_op jit(solution)/shard_map/ppermute | solution.py:295
  11.6 0.7 %copy-start.11 = (bf16[1,4,16,128]{3,2,1,0:T(8,128)(2,1)S(1)}, bf16[1,4,16,128]{3,2,1,0:T(8,128)(2,1)}, u32[]{:S(2)}) copy-start(bf16[1,4,16,128]{3,2,1,0:T(8,128)(2,1)} %get-tuple-element.22.src) | copy-start | bytes 49156
  12.3 8.4 %slice-start = ((s8[6291456]{0:T(1024)(128)(4,1)}), s8[4194304]{0:T(1024)(128)(4,1)S(1)}, s32[]{:S(2)}) async-start(s8[6291456]{0:T(1024)(128)(4,1)} %bitcast.5), calls=%async_computation | async-start | bytes 8388608
  12.3 8.4 %slice-start.2 = ((s8[4718592]{0:T(1024)(128)(4,1)}), s8[4194304]{0:T(1024)(128)(4,1)S(1)}, s32[]{:S(2)}) async-start(s8[4718592]{0:T(1024)(128)(4,1)} %bitcast.7), calls=%async_computation.2 | async-start | bytes 8388608
  12.3 1.6 %copy-start.13 = (bf16[6,16,128]{2,1,0:T(8,128)(2,1)S(1)}, bf16[6,16,128]{2,1,0:T(8,128)(2,1)}, u32[]{:S(2)}) copy-start(bf16[6,16,128]{2,1,0:T(8,128)(2,1)} %get-tuple-element.15) | copy-start | bytes 73732
  12.3 1.6 %copy-start.12 = (bf16[6,16,128]{2,1,0:T(8,128)(2,1)S(1)}, bf16[6,16,128]{2,1,0:T(8,128)(2,1)}, u32[]{:S(2)}) copy-start(bf16[6,16,128]{2,1,0:T(8,128)(2,1)} %get-tuple-element.16) | copy-start | bytes 73732
  12.4 8.4 %slice-start.1 = ((s8[6291456]{0:T(1024)(128)(4,1)}), s8[2097152]{0:T(1024)(128)(4,1)S(1)}, s32[]{:S(2)}) async-start(s8[6291456]{0:T(1024)(128)(4,1)} %bitcast.5), calls=%async_computation.1 | async-start | bytes 4194304
  12.4 8.4 %slice-start.3 = ((s8[4718592]{0:T(1024)(128)(4,1)}), s8[524288]{0:T(1024)(128)(4,1)S(1)}, s32[]{:S(2)}) async-start(s8[4718592]{0:T(1024)(128)(4,1)} %bitcast.7), calls=%async_computation.3 | async-start | bytes 1048576
  12.4 8.4 %copy-start.1 = (bf16[3,16,4,64,64]{4,3,2,1,0:T(8,128)(2,1)S(1)}, bf16[3,16,4,64,64]{4,3,2,1,0:T(8,128)(2,1)}, u32[]{:S(2)}) copy-start(bf16[3,16,4,64,64]{4,3,2,1,0:T(8,128)(2,1)} %pair.1) | copy-start | bytes 4718596
  12.4 8.4 %copy-start.5 = (bf16[32,16,64]{2,1,0:T(8,128)(2,1)S(1)}, bf16[32,16,64]{2,1,0:T(8,128)(2,1)}, u32[]{:S(2)}) copy-start(bf16[32,16,64]{2,1,0:T(8,128)(2,1)} %vec.1) | copy-start | bytes 196612
  12.4 8.4 %copy-start.6 = (bf16[5,16,128]{2,1,0:T(8,128)(2,1)S(1)}, bf16[5,16,128]{2,1,0:T(8,128)(2,1)}, u32[]{:S(2)}) copy-start(bf16[5,16,128]{2,1,0:T(8,128)(2,1)} %get-tuple-element.14.own) | copy-start | bytes 61444
  12.4 8.4 %copy-start.8 = (s32[32,3]{0,1:T(4,128)S(1)}, s32[32,3]{0,1:T(4,128)}, u32[]{:S(2)}) copy-start(s32[32,3]{0,1:T(4,128)} %param.19) | copy-start | bytes 1156
  12.4 8.4 %copy-start.9 = (s32[32,4]{0,1:T(4,128)S(1)}, s32[32,4]{0,1:T(4,128)}, u32[]{:S(2)}) copy-start(s32[32,4]{0,1:T(4,128)} %param.21) | copy-start | bytes 1540
  12.4 8.4 %copy-start.10 = (s32[16,4]{0,1:T(4,128)S(1)}, s32[16,4]{0,1:T(4,128)}, u32[]{:S(2)}) copy-start(s32[16,4]{0,1:T(4,128)} %param.24) | copy-start | bytes 772
  13.6 4.9 %collective-permute-start.5 = (bf16[2,4,16,128]{3,2,1,0:T(8,128)(2,1)S(1)}, bf16[2,4,16,128]{3,2,1,0:T(8,128)(2,1)S(1)}, u32[]{:S(2)}, u32[]{:S(2)}) collective-permute-start(bf16[2,4,16,128]{3,2,1,0:T(8,128)(2,1)S(1)} %join.2.first), channel_id=1, source_target_pairs={{0,4},{1,5},{2,6},{3,7},{4,0},{5,1},{6,2},{7,3},{8,12},{9,13},{10,... | collective-permute-start | bytes 98312 | tf_op jit(solution)/shard_map/ppermute | solution.py:295
  14.0 6.7 %collective-permute-start = (bf16[6,16,128]{2,1,0:T(8,128)(2,1)S(1)}, bf16[6,16,128]{2,1,0:T(8,128)(2,1)S(1)}, u32[]{:S(2)}, u32[]{:S(2)}) collective-permute-start(bf16[6,16,128]{2,1,0:T(8,128)(2,1)S(1)} %copy-done.13), channel_id=1, source_target_pairs={{0,1},{1,0},{2,3},{3,2},{4,5},{5,4},{6,7},{7,6},{8,9},{9,8},{10,11... | collective-permute-start | bytes 73736 | tf_op jit(solution)/shard_map/ppermute | solution.py:295
  14.0 6.7 %collective-permute-start.1 = (bf16[6,16,128]{2,1,0:T(8,128)(2,1)S(1)}, bf16[6,16,128]{2,1,0:T(8,128)(2,1)S(1)}, u32[]{:S(2)}, u32[]{:S(2)}) collective-permute-start(bf16[6,16,128]{2,1,0:T(8,128)(2,1)S(1)} %copy-done.12), channel_id=1, source_target_pairs={{0,15},{1,2},{2,1},{3,4},{4,3},{5,6},{6,5},{7,8},{8,7},{9,10},{10,... | collective-permute-start | bytes 73736 | tf_op jit(solution)/shard_map/ppermute | solution.py:295
  18.5 5.5 %collective-permute-start.8 = (bf16[4,4,16,128]{3,2,1,0:T(8,128)(2,1)S(1)}, bf16[4,4,16,128]{3,2,1,0:T(8,128)(2,1)S(1)}, u32[]{:S(2)}, u32[]{:S(2)}) collective-permute-start(bf16[4,4,16,128]{3,2,1,0:T(8,128)(2,1)S(1)} %join.3.held0), channel_id=1, source_target_pairs={{0,3},{1,2},{2,1},{3,0},{4,7},{5,6},{6,5},{7,4},{8,11},{9,10},{10,... | collective-permute-start | bytes 196616 | tf_op jit(solution)/shard_map/ppermute | solution.py:295
  18.6 5.4 %collective-permute-start.7 = (bf16[4,4,16,128]{3,2,1,0:T(8,128)(2,1)S(1)}, bf16[4,4,16,128]{3,2,1,0:T(8,128)(2,1)S(1)}, u32[]{:S(2)}, u32[]{:S(2)}) collective-permute-start(bf16[4,4,16,128]{3,2,1,0:T(8,128)(2,1)S(1)} %join.3.held0), channel_id=1, source_target_pairs={{0,1},{1,0},{2,3},{3,2},{4,5},{5,4},{6,7},{7,6},{8,9},{9,8},{10,11... | collective-permute-start | bytes 196616 | tf_op jit(solution)/shard_map/ppermute | solution.py:295
  18.9 5.2 %collective-permute-start.6 = (bf16[4,4,16,128]{3,2,1,0:T(8,128)(2,1)S(1)}, bf16[4,4,16,128]{3,2,1,0:T(8,128)(2,1)S(1)}, u32[]{:S(2)}, u32[]{:S(2)}) collective-permute-start(bf16[4,4,16,128]{3,2,1,0:T(8,128)(2,1)S(1)} %join.3.held0), channel_id=1, source_target_pairs={{0,2},{1,3},{2,0},{3,1},{4,6},{5,7},{6,4},{7,5},{8,10},{9,11},{10,... | collective-permute-start | bytes 196616 | tf_op jit(solution)/shard_map/ppermute | solution.py:295
  20.8 3.2 %copy-start = (bf16[3,8,8,64,64]{4,3,2,1,0:T(8,128)(2,1)S(1)}, bf16[3,8,8,64,64]{4,3,2,1,0:T(8,128)(2,1)}, u32[]{:S(2)}) copy-start(bf16[3,8,8,64,64]{4,3,2,1,0:T(8,128)(2,1)} %coupling.1) | copy-start | bytes 4718596
  20.9 3.2 %copy-start.2 = (bf16[32,64,64]{2,1,0:T(8,128)(2,1)S(1)}, bf16[32,64,64]{2,1,0:T(8,128)(2,1)}, u32[]{:S(2)}) copy-start(bf16[32,64,64]{2,1,0:T(8,128)(2,1)} %ltr.1) | copy-start | bytes 786436
  20.9 3.2 %copy-start.3 = (bf16[32,64,64]{2,1,0:T(8,128)(2,1)S(1)}, bf16[32,64,64]{2,1,0:T(8,128)(2,1)}, u32[]{:S(2)}) copy-start(bf16[32,64,64]{2,1,0:T(8,128)(2,1)} %basis.1) | copy-start | bytes 786436
  20.9 3.2 %copy-start.4 = (bf16[16,64,64]{2,1,0:T(8,128)(2,1)S(1)}, bf16[16,64,64]{2,1,0:T(8,128)(2,1)}, u32[]{:S(2)}) copy-start(bf16[16,64,64]{2,1,0:T(8,128)(2,1)} %ptr.1) | copy-start | bytes 393220
  20.9 3.2 %copy-start.7 = (s32[8,8]{1,0:T(8,128)S(1)}, s32[8,8]{1,0:T(8,128)}, u32[]{:S(2)}) copy-start(s32[8,8]{1,0:T(8,128)} %tlist_h.1) | copy-start | bytes 772
